TPU v7x, 32 devices: a whole 2x2x4 slice. The times are simulated.
32 devices in a mesh: dp: 16 (over z, y, x), seq: 2 (over core).
Axes of the slice: x: 2, y: 2, z: 4, core: 2. Of those that a mesh axis runs over, the one named last changes fastest.
Arguments:
- dec_in: bfloat16 [2, 32, 256, 512], P(None, 'dp', 'seq'), may hold values from -6 to 6
- enc_out: bfloat16 [2, 32, 256, 512], P(None, 'dp', 'seq'), may hold values from -6 to 6
- out_grad: bfloat16 [2, 32, 256, 512], P(None, 'dp', 'seq'), may hold values from -6 to 6
- tgt_len: int32 [2, 32], P(None, 'dp'), may hold values from 4 to 256, as said below
- src_len: int32 [2, 32], P(None, 'dp'), may hold values from 4 to 256, as said below
- pair_id: int32 [2], replicated, may hold values from 0 to 7
- self_qkv: bfloat16 [512, 1536], replicated, may hold values from -0.25 to 0.25
- self_out: bfloat16 [512, 512], replicated, may hold values from -1 to 1
- cross_q: bfloat16 [512, 512], replicated, may hold values from -0.25 to 0.25
- cross_kv: bfloat16 [512, 1024], replicated, may hold values from -0.25 to 0.25
- cross_out: bfloat16 [512, 512], replicated, may hold values from -1 to 1
- ff_in: bfloat16 [512, 2048], replicated, may hold values from -0.25 to 0.25
- ff_out: bfloat16 [2048, 512], replicated, may hold values from -0.125 to 0.125
- norm_gain: bfloat16 [3, 512], replicated, may hold values from 0.5 to 1.5
- norm_bias: bfloat16 [3, 512], replicated, may hold values from -2 to 2
- lang_table: bfloat16 [8, 512], replicated, may hold values from -3 to 3
Outputs:
- output: bfloat16 [2, 32, 256, 512], P(None, 'dp', 'seq')
- grad_input: bfloat16 [2, 32, 256, 512], P(None, 'dp', 'seq')
- grad_encoder: bfloat16 [2, 32, 256, 512], P(None, 'dp', 'seq')
- grad_self_qkv: float32 [512, 1536], P(None, 'seq')
- grad_self_out: float32 [512, 512], P(None, 'seq')
- grad_cross_q: float32 [512, 512], P(None, 'seq')
- grad_cross_kv: float32 [512, 1024], P(None, 'seq')
- grad_cross_out: float32 [512, 512], P(None, 'seq')
- grad_ff_in: float32 [512, 2048], P(None, 'seq')
- grad_ff_out: float32 [2048, 512], P(None, 'seq')
- grad_norm_gain: float32 [3, 512], P(None, 'seq')
- grad_norm_bias: float32 [3, 512], P(None, 'seq')
- grad_lang_table: float32 [8, 512], P(None, 'seq')
Inputs may be any that keep to these rules, and one draw needn't show every extreme that they name: `tgt_len`: in each group of sentences on one index of dp (all micro-batches together) one sentence has exactly 256 positions. `src_len`: in each group of sentences on one index of dp (all micro-batches together) one sentence has exactly 256 positions.
All inputs are finite; a program needn't handle non-finite values.
Results may differ from a plain program's by a relative error of at most 0.02.
Values may be sent and summed in bfloat16 or wider, within the bound.
No kernel may reach another device: no remote copies, remote signals or barrier semaphores. Data moves between devices by JAX's collectives and lax.ppermute only.
A program may use at most 128 MiB of HBM per device.

v0:
```python
import math

import jax
import jax.numpy as jnp
from jax import lax
from jax.sharding import PartitionSpec as P

HEADS = 8


NORM_EPS = 1e-05
NEG_FILL = -1e30


def layer_norm(values, gain_row, bias_row):
    center = values - jnp.mean(values, -1, keepdims=True)
    spread = jnp.mean(center * center, -1, keepdims=True)
    return center * lax.rsqrt(spread + NORM_EPS) * gain_row + bias_row


def norm_backward(values, gain_row, bias_row, upstream):
    result, pullback = jax.vjp(layer_norm, values, gain_row, bias_row)
    grad_values, grad_gain, grad_bias = pullback(upstream)
    return (grad_values, grad_gain, grad_bias)


def smooth_gelu(values):
    return (
        0.5
        * values
        * (1.0 + jnp.tanh(0.7978845608028654 * (values + 0.044715 * values * values * values)))
    )


def split_heads(values):
    return values.reshape(values.shape[:-1] + (HEADS, values.shape[-1] // HEADS))


def project(values, weight):
    return jnp.einsum("btd,de->bte", values, weight, preferred_element_type=jnp.float32)


def project_back(grads, weight):
    return jnp.einsum("bte,de->btd", grads, weight, preferred_element_type=jnp.float32)


def weight_grad(inputs, grads):
    return jnp.einsum("btd,bte->de", inputs, grads, preferred_element_type=jnp.float32)


def scores_of(queries, keys, key_mask):
    head_scale = 1.0 / math.sqrt(queries.shape[-1] // HEADS)
    raw_scores = (
        jnp.einsum(
            "bqhd,bkhd->bhqk",
            split_heads(queries),
            split_heads(keys),
            preferred_element_type=jnp.float32,
        )
        * head_scale
    )
    return jnp.where(key_mask[:, None], raw_scores, NEG_FILL)


def attend_forward(queries, keys, values, key_mask):
    scores = scores_of(queries, keys, key_mask)
    row_top = jnp.max(scores, -1, keepdims=True)
    exp_scores = jnp.exp(scores - row_top)
    totals = jnp.sum(exp_scores, -1, keepdims=True)
    probability = (exp_scores / totals).astype(jnp.bfloat16)
    mixed_out = jnp.einsum(
        "bhqk,bkhd->bqhd", probability, split_heads(values), preferred_element_type=jnp.float32
    )
    return (mixed_out.reshape(queries.shape), row_top + jnp.log(totals))


def attend_backward(queries, keys, values, key_mask, log_sums, grad_mixed):
    head_scale = 1.0 / math.sqrt(queries.shape[-1] // HEADS)
    probability = jnp.exp(scores_of(queries, keys, key_mask) - log_sums)
    grad_probs = jnp.einsum(
        "bqhd,bkhd->bhqk",
        split_heads(grad_mixed),
        split_heads(values),
        preferred_element_type=jnp.float32,
    )
    row_dot = jnp.sum(probability * grad_probs, -1, keepdims=True)
    grad_scores = (probability * (grad_probs - row_dot)).astype(jnp.bfloat16)
    grad_queries = (
        jnp.einsum(
            "bhqk,bkhd->bqhd", grad_scores, split_heads(keys), preferred_element_type=jnp.float32
        )
        * head_scale
    )
    grad_keys = (
        jnp.einsum(
            "bhqk,bqhd->bkhd", grad_scores, split_heads(queries), preferred_element_type=jnp.float32
        )
        * head_scale
    )
    grad_values = jnp.einsum(
        "bhqk,bqhd->bkhd",
        probability.astype(jnp.bfloat16),
        split_heads(grad_mixed),
        preferred_element_type=jnp.float32,
    )
    return (
        grad_queries.reshape(queries.shape),
        grad_keys.reshape(keys.shape),
        grad_values.reshape(values.shape),
    )


def local(
    dec_in,
    enc_out,
    out_grad,
    tgt_len,
    src_len,
    pair_id,
    self_qkv,
    self_out,
    cross_q,
    cross_kv,
    cross_out,
    ff_in,
    ff_out,
    norm_gain,
    norm_bias,
    lang_table,
):
    micro_count, sent_count, local_len, model_width = dec_in.shape
    src_local = enc_out.shape[2]
    seq_count = lax.axis_size("seq")
    seq_place = lax.axis_index("seq")
    query_pos = seq_place * local_len + jnp.arange(local_len)
    self_pos = jnp.arange(local_len * seq_count)
    cross_pos = jnp.arange(src_local * seq_count)
    norm_gains = norm_gain.astype(jnp.float32)
    biases = norm_bias.astype(jnp.float32)
    pair_table = lang_table.astype(jnp.float32)
    weights_list = (
        self_qkv,
        self_out,
        cross_q,
        cross_kv,
        cross_out,
        ff_in,
        ff_out,
        norm_gain,
        norm_bias,
        lang_table,
    )
    grad_totals = [jnp.zeros(weight.shape, jnp.float32) for weight in weights_list]
    outputs = []
    input_grads = []
    encoder_grads = []
    for micro_index in range(micro_count):
        choose = (jnp.arange(pair_table.shape[0]) == pair_id[micro_index]).astype(jnp.float32)
        pair_row = jnp.sum(choose[:, None] * pair_table, 0)
        embedded = dec_in[micro_index].astype(jnp.float32) + pair_row
        embedded_low = embedded.astype(jnp.bfloat16)
        packed = project(embedded_low, self_qkv).astype(jnp.bfloat16)
        queries = packed[..., :model_width]
        keys_local = packed[..., model_width : 2 * model_width]
        values_local = packed[..., 2 * model_width :]
        keys_all, values_all = (
            lax.all_gather(keys_local, "seq", axis=1, tiled=True),
            lax.all_gather(values_local, "seq", axis=1, tiled=True),
        )
        self_mask = (self_pos[None, None, :] <= query_pos[None, :, None]) & (
            self_pos[None, None, :] < tgt_len[micro_index][:, None, None]
        )
        attended, self_lse = attend_forward(queries, keys_all, values_all, self_mask)
        attended_low = attended.astype(jnp.bfloat16)
        first_sum = embedded + project(attended_low, self_out)
        first_norm = layer_norm(first_sum, norm_gains[0], biases[0])
        first_low = first_norm.astype(jnp.bfloat16)
        cross_queries = project(first_low, cross_q).astype(jnp.bfloat16)
        encoded = enc_out[micro_index]
        cross_packed = project(encoded, cross_kv).astype(jnp.bfloat16)
        cross_keys_all, cross_values_all = (
            lax.all_gather(cross_packed[..., :model_width], "seq", axis=1, tiled=True),
            lax.all_gather(cross_packed[..., model_width:], "seq", axis=1, tiled=True),
        )
        cross_mask = jnp.broadcast_to(
            cross_pos[None, None, :] < src_len[micro_index][:, None, None],
            (sent_count, local_len, cross_pos.shape[0]),
        )
        crossed, cross_lse = attend_forward(
            cross_queries, cross_keys_all, cross_values_all, cross_mask
        )
        crossed_low = crossed.astype(jnp.bfloat16)
        second_sum = first_norm + project(crossed_low, cross_out)
        second_norm = layer_norm(second_sum, norm_gains[1], biases[1])
        second_low = second_norm.astype(jnp.bfloat16)
        ff_inner = project(second_low, ff_in)
        hidden = smooth_gelu(ff_inner).astype(jnp.bfloat16)
        third_sum = second_norm + project(hidden, ff_out)
        outputs.append(layer_norm(third_sum, norm_gains[2], biases[2]).astype(jnp.bfloat16))
        upstream = out_grad[micro_index].astype(jnp.float32)
        grad_third, gain_three, bias_three = norm_backward(
            third_sum, norm_gains[2], biases[2], upstream
        )
        grad_ff = grad_third.astype(jnp.bfloat16)
        grad_totals[6] = grad_totals[6] + weight_grad(hidden, grad_ff)
        grad_hidden = project_back(grad_ff, ff_out).astype(jnp.bfloat16)
        gelu_value, gelu_pull = jax.vjp(smooth_gelu, ff_inner)
        grad_inner = gelu_pull(grad_hidden.astype(jnp.float32))[0].astype(jnp.bfloat16)
        grad_totals[5] = grad_totals[5] + weight_grad(second_low, grad_inner)
        grad_second = grad_third + project_back(grad_inner, ff_in)
        grad_second_sum, gain_two, bias_two = norm_backward(
            second_sum, norm_gains[1], biases[1], grad_second
        )
        grad_cross_branch = grad_second_sum.astype(jnp.bfloat16)
        grad_totals[4] = grad_totals[4] + weight_grad(crossed_low, grad_cross_branch)
        grad_crossed = project_back(grad_cross_branch, cross_out).astype(jnp.bfloat16)
        grad_cross_queries, grad_cross_keys_all, grad_cross_values_all = attend_backward(
            cross_queries, cross_keys_all, cross_values_all, cross_mask, cross_lse, grad_crossed
        )
        grad_cross_keys, grad_cross_values = (
            lax.psum_scatter(
                grad_cross_keys_all.astype(jnp.bfloat16), "seq", scatter_dimension=1, tiled=True
            ).astype(jnp.float32),
            lax.psum_scatter(
                grad_cross_values_all.astype(jnp.bfloat16), "seq", scatter_dimension=1, tiled=True
            ).astype(jnp.float32),
        )
        grad_cross_packed = jnp.concatenate([grad_cross_keys, grad_cross_values], -1).astype(
            jnp.bfloat16
        )
        grad_totals[3] = grad_totals[3] + weight_grad(encoded, grad_cross_packed)
        encoder_grads.append(project_back(grad_cross_packed, cross_kv).astype(jnp.bfloat16))
        grad_cross_low = grad_cross_queries.astype(jnp.bfloat16)
        grad_totals[2] = grad_totals[2] + weight_grad(first_low, grad_cross_low)
        grad_first = grad_second_sum + project_back(grad_cross_low, cross_q)
        grad_first_sum, gain_one, bias_one = norm_backward(
            first_sum, norm_gains[0], biases[0], grad_first
        )
        grad_self_branch = grad_first_sum.astype(jnp.bfloat16)
        grad_totals[1] = grad_totals[1] + weight_grad(attended_low, grad_self_branch)
        grad_attended = project_back(grad_self_branch, self_out).astype(jnp.bfloat16)
        keys_back, values_back = (keys_all, values_all)
        grad_queries, grad_keys_all, grad_values_all = attend_backward(
            queries, keys_back, values_back, self_mask, self_lse, grad_attended
        )
        grad_keys, grad_values = (
            lax.psum_scatter(
                grad_keys_all.astype(jnp.bfloat16), "seq", scatter_dimension=1, tiled=True
            ).astype(jnp.float32),
            lax.psum_scatter(
                grad_values_all.astype(jnp.bfloat16), "seq", scatter_dimension=1, tiled=True
            ).astype(jnp.float32),
        )
        grad_packed = jnp.concatenate([grad_queries, grad_keys, grad_values], -1).astype(
            jnp.bfloat16
        )
        grad_totals[0] = grad_totals[0] + weight_grad(embedded_low, grad_packed)
        grad_start = grad_first_sum + project_back(grad_packed, self_qkv)
        input_grads.append(grad_start.astype(jnp.bfloat16))
        grad_totals[9] = grad_totals[9] + choose[:, None] * jnp.sum(grad_start, (0, 1))[None, :]
        grad_totals[7] = grad_totals[7] + jnp.stack([gain_one, gain_two, gain_three])
        grad_totals[8] = grad_totals[8] + jnp.stack([bias_one, bias_two, bias_three])
    summed = lax.psum(
        (
            grad_totals[0],
            grad_totals[1],
            grad_totals[2],
            grad_totals[3],
            grad_totals[4],
            grad_totals[5],
            grad_totals[6],
            grad_totals[7],
            grad_totals[8],
            grad_totals[9],
        ),
        ("dp", "seq"),
    )

    def own_half(whole_grad):
        part_cols = whole_grad.shape[1] // seq_count
        return lax.dynamic_slice_in_dim(whole_grad, seq_place * part_cols, part_cols, 1)

    reduced = tuple((own_half(whole_grad) for whole_grad in summed))
    return (
        jnp.stack(outputs),
        jnp.stack(input_grads),
        jnp.stack(encoder_grads),
        reduced[0],
        reduced[1],
        reduced[2],
        reduced[3],
        reduced[4],
        reduced[5],
        reduced[6],
        reduced[7],
        reduced[8],
        reduced[9],
    )


def solution(mesh):
    return jax.shard_map(
        local,
        mesh=mesh,
        in_specs=(
            P(None, "dp", "seq", None),
            P(None, "dp", "seq", None),
            P(None, "dp", "seq", None),
            P(None, "dp"),
            P(None, "dp"),
            P(),
            P(),
            P(),
            P(),
            P(),
            P(),
            P(),
            P(),
            P(),
            P(),
            P(),
        ),
        out_specs=(
            P(None, "dp", "seq", None),
            P(None, "dp", "seq", None),
            P(None, "dp", "seq", None),
            P(None, "seq"),
            P(None, "seq"),
            P(None, "seq"),
            P(None, "seq"),
            P(None, "seq"),
            P(None, "seq"),
            P(None, "seq"),
            P(None, "seq"),
            P(None, "seq"),
            P(None, "seq"),
        ),
        check_vma=False,
    )
```

profile of v0, /device:TPU:0, one launch (start us, length us, event | category | flops | bytes accessed | tf_op | source)
XLA Modules:
  0.0 508.2 jit_solution(16442411260155045281)
XLA Ops:
  7.3 1.9 convolution_convert_fusion.8
  9.2 1.8 convolution_convert_fusion.9
  13.0 2.3 all_gather.31
  16.3 2.2 all_gather.30
  19.6 2.3 all_gather.27
  22.9 2.2 all_gather.26
  27.5 2.0 convolution_convert_fusion.3
  30.3 2.2 all_gather.25
  34.6 2.4 all_gather.24
  38.0 2.0 convolution_convert_fusion.2
  40.9 2.2 all_gather.29
  44.6 4.1 all_gather.28
  48.6 2.0 copy.98
  55.6 1.8 copy.103
  57.4 1.7 fusion.177
  64.3 1.7 fusion.179
  77.4 1.9 fusion.105
  79.3 2.8 fusion.10
  83.2 2.5 fusion.5
  85.8 1.8 multiply_reduce_fusion.6
  87.6 1.7 fusion.165
  91.2 1.8 copy.112
  93.0 2.0 multiply_reduce_fusion.1
  97.9 2.2 copy.120
  100.2 2.2 convolution_convert_fusion.15
  102.4 1.8 copy.106
  104.2 2.0 multiply_reduce_fusion.3
  109.1 2.1 copy.118
  111.2 3.1 convolution_convert_fusion.4
  114.3 2.0 copy.121
  116.4 1.4 convolution_convert_fusion.5
  117.8 2.2 copy.119
  120.5 1.9 fusion.79
  124.9 1.7 fusion.164
  128.5 1.8 copy.114
  130.3 2.3 convolution_convert_fusion.6
  132.6 2.1 copy.116
  134.7 2.0 multiply_reduce_fusion
  139.6 2.2 copy.115
  141.9 2.2 convolution_convert_fusion.14
  144.1 1.8 copy.108
  146.0 2.3 convolution_convert_fusion.7
  148.3 2.1 copy.110
  150.4 2.0 multiply_reduce_fusion.2
  156.7 1.6 convolution_bitcast_fusion.6
  160.8 3.1 fusion.140
  163.9 2.8 fusion.147
  168.1 1.4 fusion.53
  172.9 5.8 %bitcast_add_fusion = f32[2048,512]{1,0:T(8,128)} fusion(f32[2048,512,1]{1,0,2:T(8,128)} %fusion.140, f32[2,128]{1,0:T(2,128)S(1)} %copy-done.116, f32[2,128,512]{2,1,0:T(8,128)} %copy-done.45, f32[2,128]{1,0:T(2,128)S(1)} %get-tuple-element.117, f32[2,128]{1,0:T(2,128)S(1)} %copy-done.98, f32[2,128]{1,0:T(2,128)S(1)} %broadcast_multiply_fusion, ...), kind=kOutput, calls=%fused_computation | convolution fusion | flops 543817728 | bytes 11278336 | tf_op jit(solution)/shard_map/btd,bte->de/dot_general | solution.py:48
  178.7 2.9 bitcast_add_fusion.1
  186.6 1.8 convolution_bitcast_fusion
  188.5 1.5 fusion.129
  190.0 1.8 fusion.19
  192.5 3.4 fusion
  198.1 2.5 fusion.171
  202.0 43.5 %all-reduce = (f32[3,512]{1,0:T(4,128)S(1)}, f32[3,512]{1,0:T(4,128)S(1)}, f32[8,512]{1,0:T(8,128)S(1)}) all-reduce(f32[3,512]{1,0:T(4,128)S(1)} %maximum_add_fusion, f32[3,512]{1,0:T(4,128)S(1)} %maximum_add_fusion.1, f32[8,512]{1,0:T(8,128)S(1)} %multiply_add_fusion.8), channel_id=1, replica_groups=mesh['dp'=16,'seq'=2] {'dp','seq'}, use_global_device_ids=true, to_apply=%region_59.60 | all-reduce | flops 7168 | bytes 57344 | tf_op jit(solution)/shard_map/psum | solution.py:263
  247.4 1.6 fusion.82
  249.0 1.5 fusion.81
  252.2 234.0 %all-reduce.4.cloned.1.call-done = (f32[512,1536]{1,0:T(8,128)}, f32[512,512]{1,0:T(8,128)}, f32[512,512]{1,0:T(8,128)}, f32[512,1024]{0,1:T(8,128)}, f32[512,51...) async-done(((f32[512,1536]{1,0:T(8,128)}, f32[512,512]{1,0:T(8,128)}, f32[512,512]{1,0:T(8,128)}, f32[512,1024]{0,1:T(8,128)}, f32[512,512]{1,0:T(8,128)}, ...) | async-done | bytes 16777232 | tf_op jit(solution)/shard_map/psum | solution.py:263
  486.2 2.0 constant_dynamic-slice_fusion.8
  488.2 1.9 constant_dynamic-slice_fusion.7
  490.9 3.2 constant_dynamic-slice_fusion.3
  495.5 2.7 constant_dynamic-slice_fusion.9
  498.1 3.3 constant_dynamic-slice_fusion.4
  (413 shorter events, 77.4 us)
Async XLA Ops:
  7.2 61.2 %copy-start = (bf16[512,2048]{1,0:T(8,128)(2,1)S(1)}, bf16[512,2048]{1,0:T(8,128)(2,1)}, u32[]{:S(2)}) copy-start(bf16[512,2048]{1,0:T(8,128)(2,1)} %param.27) | copy-start | bytes 6291460
  7.2 3.8 copy-start.129
  7.2 3.8 copy-start.130
  7.2 4.5 copy-start.127
  7.2 5.1 copy-start.103
  7.2 5.1 copy-start.104
  7.2 174.3 %reduce-scatter.21.cloned.1.call-start = ((), (), s32[]{:S(2)}) async-start(), calls=%async_computation.14 | async-start | bytes 786432 | tf_op jit(solution)/shard_map/reduce_scatter | solution.py:221
  19.5 7.8 %copy-start.107 = (bf16[8,512]{1,0:T(8,128)(2,1)S(1)}, bf16[8,512]{1,0:T(8,128)(2,1)}, u32[]{:S(2)}) copy-start(bf16[8,512]{1,0:T(8,128)(2,1)} %param.31) | copy-start | bytes 24580
  19.5 7.9 %copy-start.42 = (bf16[2,2,128,512]{3,2,1,0:T(8,128)(2,1)S(1)}, bf16[2,2,128,512]{3,2,1,0:T(8,128)(2,1)}, u32[]{:S(2)}) copy-start(bf16[2,2,128,512]{3,2,1,0:T(8,128)(2,1)} %param.16) | copy-start | bytes 1572868
  27.3 3.0 copy-start.111
  27.3 3.0 copy-start.113
  34.6 22.8 %copy-start.59 = (bf16[2,128,512]{1,2,0:T(8,128)(2,1)}, bf16[2,128,512]{1,2,0:T(8,128)(2,1)S(1)}, u32[]{:S(2)}) copy-start(bf16[2,128,512]{1,2,0:T(8,128)(2,1)S(1)} %copy.91) | copy-start | bytes 786436
  43.2 8.2 %copy-start.47 = (bf16[2,256,512]{1,2,0:T(8,128)(2,1)}, bf16[2,256,512]{1,2,0:T(8,128)(2,1)S(1)}, u32[]{:S(2)}) copy-start(bf16[2,256,512]{1,2,0:T(8,128)(2,1)S(1)} %copy.100) | copy-start | bytes 1572868
  44.6 6.9 %copy-start.61 = (bf16[2,128,512]{1,2,0:T(8,128)(2,1)}, bf16[2,128,512]{1,2,0:T(8,128)(2,1)S(1)}, u32[]{:S(2)}) copy-start(bf16[2,128,512]{1,2,0:T(8,128)(2,1)S(1)} %copy.99) | copy-start | bytes 786436
  54.3 3.1 copy-start.99
  60.9 3.4 copy-start.128
  61.6 4.3 copy-start.101
  68.1 19.4 %copy-start.12 = (f32[2,128,512]{2,1,0:T(8,128)}, f32[2,128,512]{2,1,0:T(8,128)S(1)}, u32[]{:S(2)}) copy-start(f32[2,128,512]{2,1,0:T(8,128)S(1)} %get-tuple-element.134) | copy-start | bytes 1572868
  70.0 13.0 %copy-start.75 = (f32[2,128,2048]{2,1,0:T(8,128)}, f32[2,128,2048]{2,1,0:T(8,128)S(1)}, u32[]{:S(2)}) copy-start(f32[2,128,2048]{2,1,0:T(8,128)S(1)} %fusion.32) | copy-start | bytes 6291460
  71.0 14.7 %copy-start.73 = (f32[2,128,512]{2,1,0:T(8,128)}, f32[2,128,512]{2,1,0:T(8,128)S(1)}, u32[]{:S(2)}) copy-start(f32[2,128,512]{2,1,0:T(8,128)S(1)} %get-tuple-element.136) | copy-start | bytes 1572868
  74.4 13.1 %copy-start.14 = (f32[2,128,512]{2,1,0:T(8,128)}, f32[2,128,512]{2,1,0:T(8,128)S(1)}, u32[]{:S(2)}) copy-start(f32[2,128,512]{2,1,0:T(8,128)S(1)} %get-tuple-element.144) | copy-start | bytes 1572868
  75.5 3.9 copy-start.35
  76.5 5.6 %copy-start.45 = (f32[2,128,512]{2,1,0:T(8,128)}, f32[2,128,512]{2,1,0:T(8,128)S(1)}, u32[]{:S(2)}) copy-start(f32[2,128,512]{2,1,0:T(8,128)S(1)} %get-tuple-element.146) | copy-start | bytes 1572868
  77.3 8.4 %copy-start.119 = (f32[2,128]{1,0:T(2,128)}, f32[2,128]{1,0:T(2,128)S(1)}, u32[]{:S(2)}) copy-start(f32[2,128]{1,0:T(2,128)S(1)} %get-tuple-element.119) | copy-start | bytes 3076
  77.3 8.4 %copy-start.121 = (f32[2,128]{1,0:T(2,128)}, f32[2,128]{1,0:T(2,128)S(1)}, u32[]{:S(2)}) copy-start(f32[2,128]{1,0:T(2,128)S(1)} %get-tuple-element.120) | copy-start | bytes 3076
  77.4 4.7 copy-start.97
  79.3 6.4 %copy-start.131 = (f32[2,128]{1,0:T(2,128)}, f32[2,128]{1,0:T(2,128)S(1)}, u32[]{:S(2)}) copy-start(f32[2,128]{1,0:T(2,128)S(1)} %negate_multiply_fusion.5) | copy-start | bytes 3076
  87.6 5.4 %copy-start.9 = (f32[2,8,128,256]{3,2,1,0:T(8,128)S(1)}, f32[2,8,128,256]{3,2,1,0:T(8,128)}, u32[]{:S(2)}) copy-start(f32[2,8,128,256]{3,2,1,0:T(8,128)} %copy-done.8) | copy-start | bytes 6291460
  96.8 3.4 copy-start.118
  97.9 6.4 %copy-start.7 = (f32[2,8,128,256]{3,2,1,0:T(8,128)S(1)}, f32[2,8,128,256]{3,2,1,0:T(8,128)}, u32[]{:S(2)}) copy-start(f32[2,8,128,256]{3,2,1,0:T(8,128)} %copy-done.6) | copy-start | bytes 6291460
  100.1 82.5 %reduce-scatter.17.cloned.1.call-start = ((), (), s32[]{:S(2)}) async-start(), calls=%async_computation.12 | async-start | bytes 786432 | tf_op jit(solution)/shard_map/reduce_scatter | solution.py:221
  111.2 5.3 %copy-start.67 = (bf16[2,128,512]{1,2,0:T(8,128)(2,1)S(1)}, bf16[2,128,512]{1,2,0:T(8,128)(2,1)}, u32[]{:S(2)}) copy-start(bf16[2,128,512]{1,2,0:T(8,128)(2,1)} %copy.106) | copy-start | bytes 786436
  111.2 72.4 %reduce-scatter.23.cloned.1.call-start = ((), (), s32[]{:S(2)}) async-start(), calls=%async_computation.15 | async-start | bytes 786432 | tf_op jit(solution)/shard_map/reduce_scatter | solution.py:224
  116.4 68.2 %reduce-scatter.19.cloned.1.call-start = ((), (), s32[]{:S(2)}) async-start(), calls=%async_computation.13 | async-start | bytes 786432 | tf_op jit(solution)/shard_map/reduce_scatter | solution.py:224
  117.8 4.6 copy-start.20
  120.0 3.0 copy-start.25
  120.0 3.0 copy-start.27
  120.0 65.8 %reduce-scatter.15.cloned.1.call-start = ((), (), s32[]{:S(2)}) async-start(), calls=%async_computation.11 | async-start | bytes 786432 | tf_op jit(solution)/shard_map/reduce_scatter | solution.py:250
  124.9 5.4 %copy-start.5 = (f32[2,8,128,256]{3,2,1,0:T(8,128)S(1)}, f32[2,8,128,256]{3,2,1,0:T(8,128)}, u32[]{:S(2)}) copy-start(f32[2,8,128,256]{3,2,1,0:T(8,128)} %copy-done.4) | copy-start | bytes 6291460
  134.7 51.9 %reduce-scatter.13.cloned.1.call-start = ((), (), s32[]{:S(2)}) async-start(), calls=%async_computation.10 | async-start | bytes 786432 | tf_op jit(solution)/shard_map/reduce_scatter | solution.py:247
  138.5 3.4 copy-start.117
  139.6 6.3 %copy-start.3 = (f32[2,8,128,256]{3,2,1,0:T(8,128)S(1)}, f32[2,8,128,256]{3,2,1,0:T(8,128)}, u32[]{:S(2)}) copy-start(f32[2,8,128,256]{3,2,1,0:T(8,128)} %copy-done.2) | copy-start | bytes 6291460
  141.8 50.0 %reduce-scatter.11.cloned.1.call-start = ((), (), s32[]{:S(2)}) async-start(), calls=%async_computation.9 | async-start | bytes 786432 | tf_op jit(solution)/shard_map/reduce_scatter | solution.py:250
  150.4 42.2 %reduce-scatter.9.cloned.1.call-start = ((), (), s32[]{:S(2)}) async-start(), calls=%async_computation.8 | async-start | bytes 786432 | tf_op jit(solution)/shard_map/reduce_scatter | solution.py:247
  155.5 330.7 %all-reduce.4.cloned.1.call-start = ((), (), s32[]{:S(2)}) async-start(), calls=%async_computation.16 | async-start | bytes 33554432 | tf_op jit(solution)/shard_map/psum | solution.py:263
  156.6 2.9 copy-start.22
  156.7 2.9 copy-start.46
  160.8 3.1 copy-start.13
  160.8 3.1 copy-start.80
  163.9 2.8 copy-start.33
  163.9 2.8 copy-start.90
  169.5 3.3 copy-start.36
  169.5 3.3 copy-start.39
  169.5 3.3 copy-start.98
  169.5 3.3 copy-start.116
  172.9 5.9 %copy-start.10 = (f32[512,2048,1]{1,0,2:T(8,128)S(1)}, f32[512,2048,1]{1,0,2:T(8,128)}, u32[]{:S(2)}) copy-start(f32[512,2048,1]{1,0,2:T(8,128)} %fusion.147) | copy-start | bytes 12582916
  172.9 5.8 %copy-start.15 = (f32[2,128,512]{2,1,0:T(8,128)S(1)}, f32[2,128,512]{2,1,0:T(8,128)}, u32[]{:S(2)}) copy-start(f32[2,128,512]{2,1,0:T(8,128)} %copy-done.14) | copy-start | bytes 1572868
  172.9 5.8 %copy-start.78 = (bf16[2,128,2048]{2,1,0:T(8,128)(2,1)S(1)}, bf16[2,128,2048]{2,1,0:T(8,128)(2,1)}, u32[]{:S(2)}) copy-start(bf16[2,128,2048]{2,1,0:T(8,128)(2,1)} %copy-done.77) | copy-start | bytes 3145732
  200.6 46.8 %copy-start.11 = (bf16[512,1024]{1,0:T(8,128)(2,1)S(1)}, bf16[512,1024]{1,0:T(8,128)(2,1)}, u32[]{:S(2)}) copy-start(bf16[512,1024]{1,0:T(8,128)(2,1)} %param.25) | copy-start | bytes 3145732
  247.4 4.0 copy-start.95
  247.4 4.0 copy-start.96
  486.2 3.8 copy-start.94
  490.9 3.2 copy-start.91
  498.1 3.3 copy-start.1
  (79 other events, 124.0 us)
Sparse Core Ops, SparseCore 0:
  100.2 10.3 reduce-scatter.20
  113.0 9.1 reduce-scatter.16
  125.0 9.0 reduce-scatter.22
  136.3 9.0 reduce-scatter.18
  148.1 9.0 reduce-scatter.14
  159.9 9.1 reduce-scatter.12
  171.3 9.0 reduce-scatter.10
  183.4 9.1 reduce-scatter.8
  200.1 286.0 all-reduce.3
where the time goes:
time: 515 us; the launch traced here: 508 us
  waiting for transfers between devices  235 us (46%)
  matrix products  102 us (20%)
  local copies, waits for them, and re-layouts  73.4 us (14%)
  blocking collectives  63.2 us (12%)
  other arithmetic  17.5 us (3%)
  between operations  16 us (3%)
    psum x1, waiting for transfers between devices, local(): lax.psum((grad_totals[0], grad_totals[1], grad_totals[2], grad_totals[3],...  234 us
    psum x1, blocking collectives, local(): lax.psum((grad_totals[0], grad_totals[1], grad_totals[2], grad_totals[3],...  43.5 us
    dot_general x14, matrix products, weight_grad(): jnp.einsum('btd,bte->de', inputs, grads, preferred_element_type=jnp.float32)  29.7 us
    dot_general x14, matrix products, project_back(): jnp.einsum('bte,de->btd', grads, weight, preferred_element_type=jnp.float32)  23.1 us
    dynamic_slice x10, local copies, waits for them, and re-layouts, own_half(): lax.dynamic_slice_in_dim(whole_grad, seq_place * part_cols, part_cols, 1)  15.7 us
    dot_general x14, matrix products, project(): jnp.einsum('btd,de->bte', values, weight, preferred_element_type=jnp.floa...  14.9 us
    unnamed x271, local copies, waits for them, and re-layouts  14.2 us
  transfers between devices with their start and end apart: 9, of which 2 were waited for; matrix products, arithmetic and copies ran while one was open for 19% of the time, Pallas kernels for 0%

commit v1 on v0

v1 whole, which is shorter than its diff:
```python
import functools

import jax
import jax.numpy as jnp
from jax import lax
from jax.experimental import pallas as pl
from jax.experimental.pallas import tpu as pltpu
from jax.sharding import PartitionSpec as P

HEADS = 8
NORM_EPS = 1e-05
NEG_FILL = -1e30
BF = jnp.bfloat16
F32 = jnp.float32
MIB = 1 << 20
LANES = 1024


def mm(a, b):
    return lax.dot_general(a, b, (((1,), (0,)), ((), ())), preferred_element_type=F32)


def mm_bt(a, b):
    return lax.dot_general(a, b, (((1,), (1,)), ((), ())), preferred_element_type=F32)


def mm_at(a, b):
    return lax.dot_general(a, b, (((0,), (0,)), ((), ())), preferred_element_type=F32)


def norm_forward(values, gain, bias):
    center = values - jnp.mean(values, -1, keepdims=True)
    rstd = lax.rsqrt(jnp.mean(center * center, -1, keepdims=True) + NORM_EPS)
    xhat = center * rstd
    return xhat, rstd, xhat * gain + bias


def norm_backward(xhat, rstd, gain, upstream):
    scaled = upstream * gain
    first = jnp.mean(scaled, -1, keepdims=True)
    second = jnp.mean(scaled * xhat, -1, keepdims=True)
    grad = rstd * (scaled - first - xhat * second)
    return grad, jnp.sum(upstream * xhat, 0, keepdims=True), jnp.sum(upstream, 0, keepdims=True)


def lane_half(shape, half):
    lane = lax.broadcasted_iota(jnp.int32, shape, 1)
    return (lane < 64) if half == 0 else (lane >= 64)


def attend(q_ref, k_ref, v_ref, k_at, v_at, bias_ref, p_ref, out_ref, length):
    pairs = HEADS // 2

    def body(index, _):
        sentence = index // pairs
        pair = index - sentence * pairs
        rows = pl.ds(pl.multiple_of(sentence * length, length), length)
        lanes = pl.multiple_of(pair * 128, 128)
        queries = q_ref[rows, pl.ds(lanes, 128)]
        keys = k_ref[rows, pl.ds(pl.multiple_of(k_at + lanes, 128), 128)]
        values = v_ref[rows, pl.ds(pl.multiple_of(v_at + lanes, 128), 128)]
        bias = bias_ref[sentence]
        mixed = []
        for half in range(2):
            mine = lane_half(queries.shape, half)
            scores = mm_bt(jnp.where(mine, queries, jnp.zeros_like(queries)), keys) + bias
            top = jnp.max(scores, -1, keepdims=True)
            grown = jnp.exp(scores - top)
            probs = (grown * (1.0 / jnp.sum(grown, -1, keepdims=True))).astype(BF)
            p_ref[2 * index + half] = probs
            mixed.append(mm(probs, values))
        out_ref[rows, pl.ds(lanes, 128)] = jnp.where(
            lane_half(mixed[0].shape, 0), mixed[0], mixed[1]
        ).astype(BF)
        return 0

    lax.fori_loop(0, 2 * pairs, body, 0)


def attend_back(q_ref, k_ref, v_ref, k_at, v_at, p_ref, go_ref, gq_ref, gk_ref, gv_ref, gk_at, gv_at, length):
    pairs = HEADS // 2

    def body(index, _):
        sentence = index // pairs
        pair = index - sentence * pairs
        rows = pl.ds(pl.multiple_of(sentence * length, length), length)
        lanes = pl.multiple_of(pair * 128, 128)
        queries = q_ref[rows, pl.ds(lanes, 128)]
        keys = k_ref[rows, pl.ds(pl.multiple_of(k_at + lanes, 128), 128)]
        values = v_ref[rows, pl.ds(pl.multiple_of(v_at + lanes, 128), 128)]
        grads = go_ref[rows, pl.ds(lanes, 128)]
        gq, gk, gv = [], [], []
        for half in range(2):
            mine = lane_half(grads.shape, half)
            probs_low = p_ref[2 * index + half]
            probs = probs_low.astype(F32)
            grad_probs = mm_bt(jnp.where(mine, grads, jnp.zeros_like(grads)), values)
            row_dot = jnp.sum(probs * grad_probs, -1, keepdims=True)
            grad_scores = (probs * (grad_probs - row_dot)).astype(BF)
            gq.append(mm(grad_scores, keys))
            gk.append(mm_at(grad_scores, queries))
            gv.append(mm_at(probs_low, grads))
        first = lane_half(gq[0].shape, 0)
        gq_ref[rows, pl.ds(lanes, 128)] = (jnp.where(first, gq[0], gq[1]) * 0.125).astype(BF)
        gk_ref[rows, pl.ds(pl.multiple_of(gk_at + lanes, 128), 128)] = jnp.where(first, gk[0], gk[1]).astype(BF)
        gv_ref[rows, pl.ds(pl.multiple_of(gv_at + lanes, 128), 128)] = jnp.where(first, gv[0], gv[1]).astype(BF)
        return 0

    lax.fori_loop(0, 2 * pairs, body, 0)


def gather_rows(out_ref, place, own, other, length, change):
    half = length // 2
    for sentence in range(2):
        out_ref[pl.ds(pl.multiple_of(sentence * length + place * half, half), half), :] = change(own[sentence])
        out_ref[pl.ds(pl.multiple_of(sentence * length + (1 - place) * half, half), half), :] = change(other[sentence])


def part_rows(ref, place, own_ref, other_ref, length):
    half = length // 2
    for sentence in range(2):
        own_ref[sentence] = ref[pl.ds(pl.multiple_of(sentence * length + place * half, half), half), :]
        other_ref[sentence] = ref[pl.ds(pl.multiple_of(sentence * length + (1 - place) * half, half), half), :]


def forward_kernel(
    place_ref, tgt_ref, src_ref, pair_ref,
    dec_ref, dec2_ref, enc_ref, enc2_ref, og_ref, og2_ref,
    w_qkv, w_so, w_cq, w_ckv, w_co, w_fi, w_fo, gain_ref, nbias_ref, table_ref,
    out_own, out_oth, send_ref, keep_ref, gss_ref, dnorm_ref,
    elow, qkv, p_self, att, xhat1, rstd1, flow, encs, cq, ckv, p_cross, crossed,
    e_ref, bias_ref, fnorm, xhat2, rstd2, snorm, slow, hidden, slope, third, gff, ginner, og_s, outs, tr, trh,
):
    place = place_ref[0]
    length = 2 * dec_ref.shape[2]
    width = dec_ref.shape[3]
    inner = w_fi.shape[1]
    sents = range(2)
    rows_of = lambda s: pl.ds(s * length, length)
    gain = gain_ref[...].astype(F32)
    nbias = nbias_ref[...].astype(F32)
    picked = lax.broadcasted_iota(jnp.int32, table_ref.shape, 0) == pair_ref[place]
    row = jnp.sum(jnp.where(picked, table_ref[...].astype(F32), 0.0), 0, keepdims=True)

    gather_rows(e_ref, place, dec_ref[place], dec2_ref[place], length, lambda v: v.astype(F32) + row)
    gather_rows(encs, place, enc_ref[place], enc2_ref[place], length, lambda v: v)
    gather_rows(og_s, place, og_ref[place], og2_ref[place], length, lambda v: v)
    keys_at = lax.broadcasted_iota(jnp.int32, (length, length), 1)
    query_at = lax.broadcasted_iota(jnp.int32, (length, length), 0)
    for s in sents:
        bias_ref[s] = jnp.where((keys_at <= query_at) & (keys_at < tgt_ref[place, s]), 0.0, NEG_FILL)
    for s in sents:
        low = e_ref[rows_of(s), :].astype(BF)
        elow[rows_of(s), :] = low
        qkv[rows_of(s), 0:width] = (mm(low, w_qkv[:, 0:width]) * 0.125).astype(BF)
        qkv[rows_of(s), width : 3 * width] = mm(low, w_qkv[:, width : 3 * width]).astype(BF)
        ckv[rows_of(s), :] = mm(encs[rows_of(s), :], w_ckv[...]).astype(BF)
    attend(qkv, qkv, qkv, width, 2 * width, bias_ref, p_self, att, length)
    for s in sents:
        total = e_ref[rows_of(s), :] + mm(att[rows_of(s), :], w_so[...])
        xhat, rstd, normed = norm_forward(total, gain[0:1], nbias[0:1])
        xhat1[rows_of(s), :] = xhat
        rstd1[rows_of(s), :] = jnp.broadcast_to(rstd, (length, 128))
        fnorm[rows_of(s), :] = normed
        low = normed.astype(BF)
        flow[rows_of(s), :] = low
        cq[rows_of(s), :] = (mm(low, w_cq[...]).astype(BF).astype(F32) * 0.125).astype(BF)
    for s in sents:
        bias_ref[s] = jnp.where(keys_at < src_ref[place, s], 0.0, NEG_FILL)
    attend(cq, ckv, ckv, 0, width, bias_ref, p_cross, crossed, length)
    for s in sents:
        total = fnorm[rows_of(s), :] + mm(crossed[rows_of(s), :], w_co[...])
        xhat, rstd, normed = norm_forward(total, gain[1:2], nbias[1:2])
        xhat2[rows_of(s), :] = xhat
        rstd2[rows_of(s), :] = jnp.broadcast_to(rstd, (length, 128))
        snorm[rows_of(s), :] = normed
        slow[rows_of(s), :] = normed.astype(BF)
        third[rows_of(s), :] = normed
    step = 512

    def feed(index, _):
        cols = pl.ds(pl.multiple_of(index * step, step), step)
        for s in sents:
            v = mm(slow[rows_of(s), :], w_fi[:, cols])
            square = v * v
            bent = jnp.tanh(v * (0.7978845608028654 + (0.7978845608028654 * 0.044715) * square))
            half = 0.5 * (1.0 + bent)
            hid = (v * half).astype(BF)
            hidden[rows_of(s), cols] = hid
            slope[rows_of(s), cols] = (
                half
                + 0.5 * v * (1.0 - bent * bent) * (0.7978845608028654 + (3 * 0.7978845608028654 * 0.044715) * square)
            ).astype(BF)
            third[rows_of(s), :] += mm(hid, w_fo[cols, :])
        return 0

    lax.fori_loop(0, inner // step, feed, 0)
    gains_three = jnp.zeros((1, width), F32)
    biases_three = jnp.zeros((1, width), F32)
    for s in sents:
        xhat, rstd, normed = norm_forward(third[rows_of(s), :], gain[2:3], nbias[2:3])
        outs[rows_of(s), :] = normed.astype(BF)
        grad, dgain, dbias = norm_backward(xhat, rstd, gain[2:3], og_s[rows_of(s), :].astype(F32))
        gains_three += dgain
        biases_three += dbias
        third[rows_of(s), :] = grad
        gff[rows_of(s), :] = grad.astype(BF)
    part_rows(outs, place, out_own, out_oth, length)

    def feed_back(index, _):
        cols = pl.ds(pl.multiple_of(index * step, step), step)
        for s in sents:
            grad_hidden = mm_bt(gff[rows_of(s), :], w_fo[cols, :]).astype(BF)
            grad_inner = (grad_hidden.astype(F32) * slope[rows_of(s), cols].astype(F32)).astype(BF)
            ginner[rows_of(s), cols] = grad_inner
            third[rows_of(s), :] += mm_bt(grad_inner, w_fi[:, cols])
        trh[cols, :] = hidden[:, cols].T
        return 0

    lax.fori_loop(0, inner // step, feed_back, 0)
    tr[...] = slow[...].T
    half_in = inner // 2
    half_out = width // 2
    for which, ref in ((1 - place, send_ref), (place, keep_ref)):

        def block(index, _, which=which, ref=ref):
            cols = pl.ds(pl.multiple_of(which * half_in + index * 256, 256), 256)
            there = pl.ds(pl.multiple_of(index * 256, 256), 256)
            ref[0:width, there] = mm(tr[...], ginner[:, cols]).astype(BF)
            cols = pl.ds(pl.multiple_of(which * half_out, half_out), half_out)
            tall = pl.ds(pl.multiple_of(index * width, width), width)
            ref[width : 2 * width, there] = mm(trh[tall, :], gff[:, cols]).astype(BF)
            return 0

        lax.fori_loop(0, half_in // 256, block, 0)
    gains_two = jnp.zeros((1, width), F32)
    biases_two = jnp.zeros((1, width), F32)
    for s in sents:
        grad, dgain, dbias = norm_backward(xhat2[rows_of(s), :], rstd2[rows_of(s), 0:1], gain[1:2], third[rows_of(s), :])
        gains_two += dgain
        biases_two += dbias
        gss_ref[rows_of(s), :] = grad
    dnorm_ref[...] = jnp.zeros(dnorm_ref.shape, F32)
    dnorm_ref[1:2, :] = gains_two
    dnorm_ref[2:3, :] = gains_three
    dnorm_ref[4:5, :] = biases_two
    dnorm_ref[5:6, :] = biases_three


def cross_kernel(
    place_ref, gss_ref, dnorm_in, xhat1, rstd1, flow, encs, cq, ckv, p_cross, crossed, w_cq, w_ckv, w_co, gain_ref,
    genc_own, genc_oth, send_ref, keep_ref, gfs_ref, dnorm_ref,
    branch, gcrossed, gcq, gckv, genc, tr,
):
    place = place_ref[0]
    tokens, width = gss_ref.shape
    length = tokens // 2
    sents = range(2)
    rows_of = lambda s: pl.ds(s * length, length)
    gain = gain_ref[...].astype(F32)
    for s in sents:
        low = gss_ref[rows_of(s), :].astype(BF)
        branch[rows_of(s), :] = low
        gcrossed[rows_of(s), :] = mm_bt(low, w_co[...]).astype(BF)
    attend_back(cq, ckv, ckv, 0, width, p_cross, gcrossed, gcq, gckv, gckv, 0, width, length)
    gains_one = jnp.zeros((1, width), F32)
    biases_one = jnp.zeros((1, width), F32)
    for s in sents:
        genc[rows_of(s), :] = mm_bt(gckv[rows_of(s), :], w_ckv[...]).astype(BF)
        first = gss_ref[rows_of(s), :] + mm_bt(gcq[rows_of(s), :], w_cq[...])
        grad, dgain, dbias = norm_backward(xhat1[rows_of(s), :], rstd1[rows_of(s), 0:1], gain[0:1], first)
        gains_one += dgain
        biases_one += dbias
        gfs_ref[rows_of(s), :] = grad
    part_rows(genc, place, genc_own, genc_oth, length)
    dnorm_ref[...] = dnorm_in[...]
    dnorm_ref[0:1, :] = gains_one
    dnorm_ref[3:4, :] = biases_one
    half = width // 2
    for source, grads, at, cols in ((crossed, branch, 0, half), (flow, gcq, half, half), (encs, gckv, width, width)):
        tr[...] = source[...].T
        for which, ref in ((1 - place, send_ref), (place, keep_ref)):
            ref[:, at : at + cols] = mm(tr[...], grads[:, pl.ds(pl.multiple_of(which * cols, cols), cols)]).astype(BF)


def self_kernel(
    place_ref, pair_ref, gfs_ref, dnorm_in, elow, qkv, p_self, att, w_qkv, w_so,
    gin_own, gin_oth, send_ref, keep_ref,
    branch, gatt, gqkv, gin, tr, small,
):
    place = place_ref[0]
    tokens, width = gfs_ref.shape
    length = tokens // 2
    sents = range(2)
    rows_of = lambda s: pl.ds(s * length, length)
    for s in sents:
        low = gfs_ref[rows_of(s), :].astype(BF)
        branch[rows_of(s), :] = low
        gatt[rows_of(s), :] = mm_bt(low, w_so[...]).astype(BF)
    attend_back(qkv, qkv, qkv, width, 2 * width, p_self, gatt, gqkv, gqkv, gqkv, width, 2 * width, length)
    table_row = jnp.zeros((1, width), F32)
    for s in sents:
        start = gfs_ref[rows_of(s), :] + mm_bt(gqkv[rows_of(s), :], w_qkv[...])
        gin[rows_of(s), :] = start.astype(BF)
        table_row += jnp.sum(start, 0, keepdims=True)
    part_rows(gin, place, gin_own, gin_oth, length)
    small[0:8, :] = dnorm_in[...]
    picked = lax.broadcasted_iota(jnp.int32, (8, width), 0) == pair_ref[place]
    small[8:16, :] = jnp.where(picked, jnp.broadcast_to(table_row, (8, width)), 0.0)
    half = width // 2
    for which, ref in ((1 - place, send_ref), (place, keep_ref)):
        ref[width : width + 16, :] = jnp.zeros((16, ref.shape[1]), BF)
        ref[width : width + 16, 0:half] = small[:, pl.ds(pl.multiple_of(which * half, half), half)].astype(BF)
    for source, grads, at, cols in ((att, branch, 3 * half, half), (elow, gqkv, 0, 3 * half)):
        tr[...] = source[...].T
        for which, ref in ((1 - place, send_ref), (place, keep_ref)):
            ref[0:width, at : at + cols] = mm(tr[...], grads[:, pl.ds(pl.multiple_of(which * cols, half), cols)]).astype(BF)


def add_split_kernel(tail, bit_ref, a_ref, b_ref, send_ref, keep_ref):
    half = send_ref.shape[0] - tail
    bit = bit_ref[0]
    for which, ref in ((1 - bit, send_ref), (bit, keep_ref)):
        rows = pl.ds(pl.multiple_of(which * half, 16), half)
        ref[0:half, :] = (a_ref[rows, :].astype(F32) + b_ref[rows, :].astype(F32)).astype(BF)
        if tail:
            last = pl.ds(2 * half, tail)
            ref[half : half + tail, :] = (a_ref[last, :].astype(F32) + b_ref[last, :].astype(F32)).astype(BF)


def add_spread_kernel(tail, index_ref, a_ref, b_ref, *outs):
    rows = outs[0].shape[0] - tail
    for j, out in enumerate(outs):
        at = pl.ds(pl.multiple_of((index_ref[0] ^ j) * rows, 16), rows)
        out[0:rows, :] = (a_ref[at, :].astype(F32) + b_ref[at, :].astype(F32)).astype(BF)
        if tail:
            last = pl.ds(len(outs) * rows, tail)
            out[rows : rows + tail, :] = (a_ref[last, :].astype(F32) + b_ref[last, :].astype(F32)).astype(BF)


def add_all_kernel(*refs):
    total = refs[0][...].astype(F32)
    for ref in refs[1:-1]:
        total = total + ref[...].astype(F32)
    refs[-1][...] = total.astype(BF)


def join_kernel(index_ref, *refs):
    out = refs[-1]
    rows = refs[0].shape[0]
    for j, ref in enumerate(refs[:-1]):
        out[pl.ds(pl.multiple_of((index_ref[0] ^ j) * rows, 16), rows), :] = ref[...]


def unpack_kernel(unpack, index_ref, mine_ref, got_ref, *outs):
    @pl.when(index_ref[0] == 0)
    def _():
        unpack(mine_ref, got_ref, *outs)

    @pl.when(index_ref[0] != 0)
    def _():
        unpack(got_ref, mine_ref, *outs)


def unpack_ff(low_ref, high_ref, in_ref, out_ref):
    in_ref[...] = low_ref[...].astype(F32)
    width, cols = low_ref.shape[0], out_ref.shape[1]
    for j in range(out_ref.shape[0] // width):
        out_ref[j * width : (j + 1) * width, :] = high_ref[:, j * cols : (j + 1) * cols].astype(F32)


def unpack_columns(low_ref, high_ref, *outs):
    half, at = low_ref.shape[0], 0
    for out in outs:
        cols = pl.ds(at, out.shape[1])
        out[0:half, :] = low_ref[:, cols].astype(F32)
        out[half : 2 * half, :] = high_ref[:, cols].astype(F32)
        at += out.shape[1]


def smem():
    return pl.BlockSpec(memory_space=pltpu.SMEM)


def vmem():
    return pl.BlockSpec(memory_space=pltpu.VMEM)


def call(kernel, scalars, arrays, outs, scratch=(), limit=56, flops=0, name=None):
    moved = sum(a.size * a.dtype.itemsize for a in arrays)
    return pl.pallas_call(
        kernel,
        out_shape=tuple(jax.ShapeDtypeStruct(s, d) for s, d in outs),
        in_specs=[smem() for _ in scalars] + [vmem() for _ in arrays],
        out_specs=tuple(vmem() for _ in outs),
        scratch_shapes=[pltpu.VMEM(s, d) for s, d in scratch],
        compiler_params=pltpu.CompilerParams(vmem_limit_bytes=limit * MIB),
        cost_estimate=pl.CostEstimate(flops=flops, bytes_accessed=moved, transcendentals=0),
        name=name,
    )(*scalars, *arrays)


def local(
    dec_in, enc_out, out_grad, tgt_len, src_len, pair_id,
    self_qkv, self_out, cross_q, cross_kv, cross_out, ff_in, ff_out, norm_gain, norm_bias, lang_table,
):
    micro_count, sent_count, local_len, width = dec_in.shape
    seq_count = lax.axis_size("seq")
    dp_count = lax.axis_size("dp")
    place = lax.axis_index("seq")
    dp_place = lax.axis_index("dp")
    inner = ff_in.shape[1]
    length = local_len * seq_count
    tokens = sent_count * length
    half = width // 2
    place_arr = place.reshape(1)
    swap = [(0, 1), (1, 0)]

    dec2 = lax.ppermute(dec_in, "seq", swap)
    enc2 = lax.ppermute(enc_out, "seq", swap)
    og2 = lax.ppermute(out_grad, "seq", swap)

    rows = (sent_count, local_len, width)
    whole = (tokens, width)
    probs = (sent_count * HEADS, length, length)
    (
        out_own, out_oth, send_a, keep_a, gss, dnorm,
        elow, qkv, p_self, att, xhat1, rstd1, flow, encs, cq, ckv, p_cross, crossed,
    ) = call(
        forward_kernel,
        (place_arr, tgt_len, src_len, pair_id),
        (dec_in, dec2, enc_out, enc2, out_grad, og2, self_qkv, self_out, cross_q, cross_kv, cross_out, ff_in, ff_out,
         norm_gain, norm_bias, lang_table),
        [
            (rows, BF), (rows, BF), ((2 * width, LANES), BF), ((2 * width, LANES), BF), (whole, F32), ((8, width), F32),
            (whole, BF), ((tokens, 3 * width), BF), (probs, BF), (whole, BF), (whole, F32), ((tokens, 128), F32),
            (whole, BF), (whole, BF), (whole, BF), ((tokens, 2 * width), BF), (probs, BF), (whole, BF),
        ],
        [
            (whole, F32), ((sent_count, length, length), F32), (whole, F32), (whole, F32), ((tokens, 128), F32),
            (whole, F32), (whole, BF), ((tokens, inner), BF), ((tokens, inner), BF), (whole, F32), (whole, BF),
            ((tokens, inner), BF), (whole, BF), (whole, BF), ((width, tokens), BF), ((inner, tokens), BF),
        ],
        name="forward",
    )
    genc_own, genc_oth, send_b, keep_b, gfs, dnorm = call(
        cross_kernel,
        (place_arr,),
        (gss, dnorm, xhat1, rstd1, flow, encs, cq, ckv, p_cross, crossed, cross_q, cross_kv, cross_out, norm_gain),
        [(rows, BF), (rows, BF), ((width, LANES), BF), ((width, LANES), BF), (whole, F32), ((8, width), F32)],
        [(whole, BF), (whole, BF), (whole, BF), ((tokens, 2 * width), BF), (whole, BF), ((width, tokens), BF)],
        limit=40,
        name="cross_back",
    )
    gin_own, gin_oth, send_c, keep_c = call(
        self_kernel,
        (place_arr, pair_id),
        (gfs, dnorm, elow, qkv, p_self, att, self_qkv, self_out),
        [(rows, BF), (rows, BF), ((width + 16, LANES), BF), ((width + 16, LANES), BF)],
        [(whole, BF), (whole, BF), ((tokens, 3 * width), BF), (whole, BF), ((width, tokens), BF), ((16, width), F32)],
        limit=40,
        name="self_back",
    )

    def both(own, other):
        got = lax.ppermute(other, "seq", swap)
        return jnp.where(place == 0, jnp.stack([own, got]), jnp.stack([got, own]))

    output = both(out_own, out_oth)
    grad_encoder = both(genc_own, genc_oth)
    grad_input = both(gin_own, gin_oth)

    first_bit = jnp.where(place == 0, dp_place & 1, (dp_place >> 1) & 1).reshape(1)
    second_bit = jnp.where(place == 0, (dp_place >> 1) & 1, dp_place & 1).reshape(1)
    line_place = (dp_place >> 2).reshape(1)

    def flips(core_zero, core_one):
        return [(2 * d, 2 * (d ^ core_zero)) for d in range(dp_count)] + [
            (2 * d + 1, 2 * (d ^ core_one) + 1) for d in range(dp_count)
        ]

    def travel(array, core_zero, core_one):
        return lax.ppermute(array, ("dp", "seq"), flips(core_zero, core_one))

    def reduce_all(keep, send, outs, unpack, tail=0):
        rows, lanes = keep.shape
        body = rows - tail
        got = lax.ppermute(send, "seq", swap)
        if dp_count != 16:
            (total,) = call(add_all_kernel, (), (keep, got), [((rows, lanes), BF)], name="add_core")
            total = lax.psum(total, "dp")
            mine, other = total[: body // 2], total[body // 2 : body]
            last = total[body:]
            index = jnp.zeros_like(first_bit)
        else:
            shape = (body // 2 + tail, lanes)
            send, keep = call(functools.partial(add_split_kernel, tail), (first_bit,), (keep, got), [(shape, BF)] * 2, limit=16, name="add_core")
            got = travel(send, 1, 2)
            shape = (body // 4 + tail, lanes)
            send, keep = call(functools.partial(add_split_kernel, tail), (second_bit,), (keep, got), [(shape, BF)] * 2, limit=16, name="add_one")
            got = travel(send, 2, 1)
            shape = (body // 16 + tail, lanes)
            pieces = call(functools.partial(add_spread_kernel, tail), (line_place,), (keep, got), [(shape, BF)] * 4, limit=16, name="add_two")
            got = [travel(pieces[j], 4 * j, 4 * j) for j in (1, 2, 3)]
            (own,) = call(add_all_kernel, (), (pieces[0], *got), [(shape, BF)], limit=16, name="add_line")
            last = own[body // 16 :]
            own = own[: body // 16]
            got = [travel(own, 4 * j, 4 * j) for j in (1, 2, 3)]
            (mine,) = call(join_kernel, (line_place,), (own, *got), [((body // 4, lanes), BF)], limit=16, name="join_line")
            got = travel(mine, 2, 1)
            (mine,) = call(join_kernel, (second_bit,), (mine, got), [((body // 2, lanes), BF)], limit=16, name="join_two")
            other = travel(mine, 1, 2)
            index = first_bit
        return call(functools.partial(unpack_kernel, unpack), (index,), (mine, other), [(s, F32) for s in outs], limit=24, name="unpack"), last

    (g_ff_in, g_ff_out), _ = reduce_all(keep_a, send_a, [(width, inner // 2), (inner, half)], unpack_ff)
    (g_cross_out, g_cross_q, g_cross_kv), _ = reduce_all(keep_b, send_b, [(width, half), (width, half), (width, width)], unpack_columns)
    (g_qkv, g_self_out), last = reduce_all(keep_c, send_c, [(width, 3 * half), (width, half)], unpack_columns, tail=16)
    tot_s = last[:, :half].astype(F32)
    return (
        output,
        grad_input,
        grad_encoder,
        g_qkv,
        g_self_out,
        g_cross_q,
        g_cross_kv,
        g_cross_out,
        g_ff_in,
        g_ff_out,
        tot_s[0:3],
        tot_s[3:6],
        tot_s[8:16],
    )


def solution(mesh):
    acts = P(None, "dp", "seq", None)
    lens = P(None, "dp")
    cut = P(None, "seq")
    return jax.shard_map(
        local,
        mesh=mesh,
        in_specs=(acts, acts, acts, lens, lens) + (P(),) * 11,
        out_specs=(acts, acts, acts) + (cut,) * 10,
        check_vma=False,
    )
```

time: 515 us -> 209 us (0.41); the launches traced: 508 us -> 208 us
  waiting for transfers between devices: 235 us -> 55.5 us
  matrix products: 102 us -> 0 us
  Pallas kernels: 0 us -> 78.4 us
  blocking collectives: 63.2 us -> 0 us
  local copies, waits for them, and re-layouts: 73.4 us -> 17.9 us
  starting transfers between devices: 0.95 us -> 52.8 us
  between operations: 16 us -> 0.99 us
  other arithmetic: 17.5 us -> 2.61 us
    psum x1 -> x0, waiting for transfers between devices: 234 us -> none  [local(): lax.psum((grad_totals[0], grad_totals[1], grad_totals[2], grad_totals[3],...]
    dot_general x66 -> x0, matrix products: 102 us -> none  [the longest x14 29.7 us: weight_grad(): jnp.einsum('btd,bte->de', inputs, grads, preferred_element_type=jnp.float32)]
    pallas_call x0 -> x24, Pallas kernels: none -> 78.4 us  [call(): pl.pallas_call(kernel, out_shape=tuple((jax.ShapeDtypeStruct(s, d) for s,...]
    ppermute x0 -> x39, waiting for transfers between devices: none -> 55.5 us  [the longest x30 48.8 us: travel(): return lax.ppermute(array, ('dp', 'seq'), flips(core_zero, core_one))]
    ppermute x0 -> x39, starting transfers between devices: none -> 52.8 us  [the longest x30 50.7 us: travel(): return lax.ppermute(array, ('dp', 'seq'), flips(core_zero, core_one))]
    psum x1 -> x0, blocking collectives: 43.5 us -> none  [local(): lax.psum((grad_totals[0], grad_totals[1], grad_totals[2], grad_totals[3],...]
    convert_element_type x14 -> x0, local copies, waits for them, and re-layouts: 25.9 us -> none  [the longest x2 4.26 us: local(): grad_cross_keys_all.astype(jnp.bfloat16)]
    all_gather x8 -> x0, blocking collectives: 19.7 us -> none  [the longest x2 6.44 us: local(): lax.all_gather(values_local, 'seq', axis=1, tiled=True)]
  transfers between devices with their start and end apart: 9 -> 39, of which waited for: 2 -> 20; matrix products, arithmetic and copies ran while one was open for 19% -> 2% of each run, Pallas kernels for 0% -> 16%
where the time goes in v1:
time: 209 us; the launch traced here: 208 us
  Pallas kernels  78.4 us (38%)
  waiting for transfers between devices  55.5 us (27%)
  starting transfers between devices  52.8 us (25%)
  local copies, waits for them, and re-layouts  17.9 us (9%)
  other arithmetic  2.61 us (1%)
    pallas_call x24, Pallas kernels, call(): pl.pallas_call(kernel, out_shape=tuple((jax.ShapeDtypeStruct(s, d) for s,...  78.4 us
    ppermute x30, starting transfers between devices, travel(): return lax.ppermute(array, ('dp', 'seq'), flips(core_zero, core_one))  50.7 us
    ppermute x30, waiting for transfers between devices, travel(): return lax.ppermute(array, ('dp', 'seq'), flips(core_zero, core_one))  48.8 us
    unnamed x78, local copies, waits for them, and re-layouts  16.7 us
  transfers between devices with their start and end apart: 39, of which 20 were waited for; matrix products, arithmetic and copies ran while one was open for 2% of the time, Pallas kernels for 16%

profile of v1, /device:TPU:0, one launch (start us, length us, event | category | flops | bytes accessed | tf_op | source)
XLA Modules:
  0.0 208.3 jit_solution(8455507684493323726)
XLA Ops:
  1.7 1.2 collective-permute-done.dec2_ref
  5.2 42.0 %forward.1 = (bf16[2,128,512]{2,1,0:T(8,128)(2,1)}, bf16[2,128,512]{2,1,0:T(8,128)(2,1)}, bf16[1024,1024]{1,0:T(8,128)(2,1)}, bf16[1024,1024]{1,0:T(8,128)(2,1)}...) custom-call(s32[1]{0:T(128)} %bitcast.place_ref, ...), custom_call_target="tpu_custom_call" | custom-call | bytes 11548672 | tf_op jit(solution)/shard_map/forward/pallas_call | solution.py:391
  47.6 4.0 %collective-permute-done.28.b_ref = bf16[1024,1024]{1,0:T(8,128)(2,1)S(1)} collective-permute-done((bf16[1024,1024]{1,0:T(8,128)(2,1)}, bf16[1024,1024]{1,0:T(8,128)(2,1)S(1)}, u32[]{:S(2)}, u32[]{:S(2)}) %collective-permute-start.28) | collective-permute-done | bytes 2097184 | tf_op jit(solution)/shard_map/ppermute | solution.py:488
  51.6 1.6 copy-done.5
  53.3 1.4 add_core.5
  54.7 1.0 copy-done.12
  55.6 2.9 %collective-permute-start.29 = (bf16[512,1024]{1,0:T(8,128)(2,1)}, bf16[512,1024]{1,0:T(8,128)(2,1)}, u32[]{:S(2)}, u32[]{:S(2)}) collective-permute-start(bf16[512,1024]{1,0:T(8,128)(2,1)} %get-tuple-element.122), channel_id=1, source_target_pairs={{0,2},{2,0},{4,6},{6,4},{8,10},{10,8},{12,14},{14,12},{16,18},{18,... | collective-permute-start | bytes 3145736 | tf_op jit(solution)/shard_map/ppermute | solution.py:483
  58.5 1.2 copy-done.9
  59.8 1.2 copy-done.10
  61.0 1.2 copy-done.11
  62.2 1.0 copy-done.18
  63.2 1.0 copy-done.19
  64.3 1.0 copy-done.20
  65.3 1.0 copy-done.21
  66.4 0.9 copy-done.24
  67.4 11.1 %cross_back.1 = (bf16[2,128,512]{2,1,0:T(8,128)(2,1)S(1)}, bf16[2,128,512]{2,1,0:T(8,128)(2,1)S(1)}, bf16[512,1024]{1,0:T(8,128)(2,1)}, bf16[512,1024]{1,0:T(8,1...) custom-call(s32[1]{0:T(128)} %bitcast.place_ref, f32[512,512]{1,0:T(8,128)S(1)} %copy-done.9, ...), custom_call_target="tpu_custom_call" | custom-call | bytes 9718784 | tf_op jit(solution)/shard_map/cross_back/pallas_call | solution.py:391
  78.5 11.4 %self_back.1 = (bf16[2,128,512]{2,1,0:T(8,128)(2,1)S(1)}, bf16[2,128,512]{2,1,0:T(8,128)(2,1)S(1)}, bf16[528,1024]{1,0:T(8,128)(2,1)}, bf16[528,1024]{1,0:T(8,128)(2,1)S(1)}) custom-call(s32[1]{0:T(128)} %bitcast.place_ref, s32[2]{0:T(128)S(1)} %copy-done.29, f32[512,512]{1,0:T(8,128)S(1)} %get-tuple-element.84.gfs_ref, ...), custom_call_target="tpu_custom_call" | custom-call | bytes 7880704 | tf_op jit(solution)/shard_map/self_back/pallas_call | solution.py:391
  91.9 1.2 copy-done.13
  93.1 2.2 %add_one.5 = (bf16[256,1024]{1,0:T(8,128)(2,1)}, bf16[256,1024]{1,0:T(8,128)(2,1)S(1)}) custom-call(s32[1]{0:T(128)} %bitcast.8.bit_ref.index_ref, bf16[512,1024]{1,0:T(8,128)(2,1)S(1)} %copy-done.13, bf16[512,1024]{1,0:T(8,128)(2,1)} %collective-permute-done.29.b_ref), custom_call_target="tpu_custom_call" | custom-call | bytes 2097152 | tf_op jit(solution)/shard_map/add_one/pallas_call | solution.py:391
  96.1 1.5 collective-permute-start.30
  97.6 1.0 add_core.3
  99.2 2.2 %add_core.4 = (bf16[256,1024]{1,0:T(8,128)(2,1)}, bf16[256,1024]{1,0:T(8,128)(2,1)S(1)}) custom-call(s32[1]{0:T(128)} %bitcast.7.bit_ref.index_ref, bf16[512,1024]{1,0:T(8,128)(2,1)S(1)} %get-tuple-element.106.a_ref, bf16[512,1024]{1,0:T(8,128)(2,1)} %collective-permute-done.17.b_ref), custom_call_target="tpu_custom_call" | custom-call | bytes 2097152 | tf_op jit(solution)/shard_map/add_core/pallas_call | solution.py:391
  101.4 1.4 collective-permute-start.18
  102.8 7.3 %collective-permute-done.30.b_ref = bf16[256,1024]{1,0:T(8,128)(2,1)} collective-permute-done((bf16[256,1024]{1,0:T(8,128)(2,1)}, bf16[256,1024]{1,0:T(8,128)(2,1)}, u32[]{:S(2)}, u32[]{:S(2)}) %collective-permute-start.30) | collective-permute-done | bytes 524320 | tf_op jit(solution)/shard_map/ppermute | solution.py:483
  110.1 1.0 copy-done.23
  111.2 1.2 add_two.5
  112.3 1.6 collective-permute-start.31
  113.9 2.6 %collective-permute-start.32 = (bf16[64,1024]{1,0:T(8,128)(2,1)S(1)}, bf16[64,1024]{1,0:T(8,128)(2,1)S(1)}, u32[]{:S(2)}, u32[]{:S(2)}) collective-permute-start(bf16[64,1024]{1,0:T(8,128)(2,1)S(1)} %get-tuple-element.127), channel_id=1, source_target_pairs={{0,16},{2,18},{4,20},{6,22},{8,24},{10,26},{12,28},{14,30},{16,0},... | collective-permute-start | bytes 393224 | tf_op jit(solution)/shard_map/ppermute | solution.py:483
  116.8 1.9 collective-permute-done.31.refs_1_
  118.7 5.0 %collective-permute-done.32.refs_2_ = bf16[64,1024]{1,0:T(8,128)(2,1)S(1)} collective-permute-done((bf16[64,1024]{1,0:T(8,128)(2,1)S(1)}, bf16[64,1024]{1,0:T(8,128)(2,1)S(1)}, u32[]{:S(2)}, u32[]{:S(2)}) %collective-permute-start.32) | collective-permute-done | bytes 131104 | tf_op jit(solution)/shard_map/ppermute | solution.py:483
  123.8 2.0 collective-permute-start.34
  125.8 1.1 collective-permute-start.35
  127.0 1.4 collective-permute-start.36
  128.3 0.9 collective-permute-done.34.refs_1_
  129.3 7.4 %collective-permute-done.35.refs_2_ = bf16[64,1024]{1,0:T(8,128)(2,1)S(1)} collective-permute-done((bf16[64,1024]{1,0:T(8,128)(2,1)S(1)}, bf16[64,1024]{1,0:T(8,128)(2,1)S(1)}, u32[]{:S(2)}, u32[]{:S(2)}) %collective-permute-start.35) | collective-permute-done | bytes 131104 | tf_op jit(solution)/shard_map/ppermute | solution.py:483
  136.8 2.6 %collective-permute-start.37 = (bf16[256,1024]{1,0:T(8,128)(2,1)S(1)}, bf16[256,1024]{1,0:T(8,128)(2,1)S(1)}, u32[]{:S(2)}, u32[]{:S(2)}) collective-permute-start(bf16[256,1024]{1,0:T(8,128)(2,1)S(1)} %join_line.5.refs_0_), channel_id=1, source_target_pairs={{0,4},{2,6},{4,0},{6,2},{8,12},{10,14},{12,8},{14,10},{16,20},{18,... | collective-permute-start | bytes 1572872 | tf_op jit(solution)/shard_map/ppermute | solution.py:483
  139.8 2.1 collective-permute-start.8
  141.8 7.5 %collective-permute-done.19.b_ref = bf16[128,1024]{1,0:T(8,128)(2,1)S(1)} collective-permute-done((bf16[128,1024]{1,0:T(8,128)(2,1)S(1)}, bf16[128,1024]{1,0:T(8,128)(2,1)S(1)}, u32[]{:S(2)}, u32[]{:S(2)}) %collective-permute-start.19) | collective-permute-done | bytes 262176 | tf_op jit(solution)/shard_map/ppermute | solution.py:483
  149.4 2.0 collective-permute-start.20
  151.4 1.1 collective-permute-start.21
  152.7 2.0 collective-permute-start.9
  154.7 1.1 collective-permute-start.10
  155.7 1.4 collective-permute-start.22
  157.1 1.0 collective-permute-done.21.refs_2_
  158.1 3.7 %collective-permute-start.11 = (bf16[48,1024]{1,0:T(8,128)(2,1)S(1)}, bf16[48,1024]{1,0:T(8,128)(2,1)S(1)}, u32[]{:S(2)}, u32[]{:S(2)}) collective-permute-start(bf16[48,1024]{1,0:T(8,128)(2,1)S(1)} %get-tuple-element.103), channel_id=1, source_target_pairs={{0,24},{2,26},{4,28},{6,30},{8,16},{10,18},{12,20},{14,22},{16,8},... | collective-permute-start | bytes 294920 | tf_op jit(solution)/shard_map/ppermute | solution.py:483
  162.5 1.7 collective-permute-start.38
  164.3 5.5 %collective-permute-start.23 = (bf16[32,1024]{1,0:T(8,128)(2,1)S(1)}, bf16[32,1024]{1,0:T(8,128)(2,1)S(1)}, u32[]{:S(2)}, u32[]{:S(2)}) collective-permute-start(bf16[32,1024]{1,0:T(8,128)(2,1)S(1)} %add_line.4.refs_0_), channel_id=1, source_target_pairs={{0,8},{2,10},{4,12},{6,14},{8,0},{10,2},{12,4},{14,6},{16,24},{18,... | collective-permute-start | bytes 196616 | tf_op jit(solution)/shard_map/ppermute | solution.py:483
  170.2 2.0 collective-permute-start.25
  173.1 0.9 collective-permute-start.12
  174.0 1.2 collective-permute-done.24.refs_2_
  175.2 1.2 collective-permute-done.25.refs_3_
  176.4 1.3 collective-permute-start.13
  177.7 1.8 collective-permute-start.14
  179.6 3.3 %collective-permute-done.13.refs_2_ = bf16[32,1024]{1,0:T(8,128)(2,1)S(1)} collective-permute-done((bf16[32,1024]{1,0:T(8,128)(2,1)S(1)}, bf16[32,1024]{1,0:T(8,128)(2,1)S(1)}, u32[]{:S(2)}, u32[]{:S(2)}) %collective-permute-start.13) | collective-permute-done | bytes 65568 | tf_op jit(solution)/shard_map/ppermute | solution.py:483
  182.9 2.4 %collective-permute-start.26 = (bf16[128,1024]{1,0:T(8,128)(2,1)S(1)}, bf16[128,1024]{1,0:T(8,128)(2,1)S(1)}, u32[]{:S(2)}, u32[]{:S(2)}) collective-permute-start(bf16[128,1024]{1,0:T(8,128)(2,1)S(1)} %join_line.4.refs_0_), channel_id=1, source_target_pairs={{0,4},{2,6},{4,0},{6,2},{8,12},{10,14},{12,8},{14,10},{16,20},{18,... | collective-permute-start | bytes 786440 | tf_op jit(solution)/shard_map/ppermute | solution.py:483
  187.2 2.4 %collective-permute-done.26.refs_1_ = bf16[128,1024]{1,0:T(8,128)(2,1)S(1)} collective-permute-done((bf16[128,1024]{1,0:T(8,128)(2,1)S(1)}, bf16[128,1024]{1,0:T(8,128)(2,1)S(1)}, u32[]{:S(2)}, u32[]{:S(2)}) %collective-permute-start.26) | collective-permute-done | bytes 262176 | tf_op jit(solution)/shard_map/ppermute | solution.py:483
  189.6 1.4 collective-permute-start.27
  191.0 3.1 %collective-permute-done.15.refs_1_ = bf16[128,1024]{1,0:T(8,128)(2,1)S(1)} collective-permute-done((bf16[128,1024]{1,0:T(8,128)(2,1)S(1)}, bf16[128,1024]{1,0:T(8,128)(2,1)S(1)}, u32[]{:S(2)}, u32[]{:S(2)}) %collective-permute-start.15) | collective-permute-done | bytes 262176 | tf_op jit(solution)/shard_map/ppermute | solution.py:483
  194.2 1.7 collective-permute-start.16
  197.9 1.0 collective-permute-done.27.got_ref
  198.9 1.5 unpack.4
  200.4 4.2 %collective-permute-done.16.got_ref = bf16[256,1024]{1,0:T(8,128)(2,1)S(1)} collective-permute-done((bf16[256,1024]{1,0:T(8,128)(2,1)S(1)}, bf16[256,1024]{1,0:T(8,128)(2,1)S(1)}, u32[]{:S(2)}, u32[]{:S(2)}) %collective-permute-start.16) | collective-permute-done | bytes 524320 | tf_op jit(solution)/shard_map/ppermute | solution.py:483
  204.5 1.5 unpack.3
  206.0 2.3 %unpack.5 = (f32[512,1024]{1,0:T(8,128)}, f32[2048,256]{1,0:T(8,128)}) custom-call(s32[1]{0:T(128)} %bitcast.7.bit_ref.index_ref, bf16[512,1024]{1,0:T(8,128)(2,1)S(1)} %join_two.5.mine_ref, bf16[512,1024]{1,0:T(8,128)(2,1)S(1)} %collective-permute-done.38.got_ref), custom_call_target="tpu_custom_call" | custom-call | bytes 2097152 | tf_op jit(solution)/shard_map/unpack/pallas_call | solution.py:391
  (123 shorter events, 14.2 us)
Async XLA Ops:
  0.6 2.3 %collective-permute-start = (bf16[2,2,128,512]{3,2,1,0:T(8,128)(2,1)}, bf16[2,2,128,512]{3,2,1,0:T(8,128)(2,1)S(1)}, u32[]{:S(2)}, u32[]{:S(2)}) collective-permute-start(bf16[2,2,128,512]{3,2,1,0:T(8,128)(2,1)} %dec_ref.1), channel_id=1, source_target_pairs={{0,1},{1,0},{2,3},{3,2},{4,5},{5,4},{6,7},{7,6},{8,9},{9,8},{10,11... | collective-permute-start | bytes 1572872 | tf_op jit(solution)/shard_map/ppermute | solution.py:419
  1.2 2.5 %collective-permute-start.1 = (bf16[2,2,128,512]{3,2,1,0:T(8,128)(2,1)}, bf16[2,2,128,512]{3,2,1,0:T(8,128)(2,1)S(1)}, u32[]{:S(2)}, u32[]{:S(2)}) collective-permute-start(bf16[2,2,128,512]{3,2,1,0:T(8,128)(2,1)} %enc_ref.1), channel_id=1, source_target_pairs={{0,1},{1,0},{2,3},{3,2},{4,5},{5,4},{6,7},{7,6},{8,9},{9,8},{10,11... | collective-permute-start | bytes 1572872 | tf_op jit(solution)/shard_map/ppermute | solution.py:420
  1.2 3.2 %collective-permute-start.2 = (bf16[2,2,128,512]{3,2,1,0:T(8,128)(2,1)}, bf16[2,2,128,512]{3,2,1,0:T(8,128)(2,1)S(1)}, u32[]{:S(2)}, u32[]{:S(2)}) collective-permute-start(bf16[2,2,128,512]{3,2,1,0:T(8,128)(2,1)} %og_ref.1), channel_id=1, source_target_pairs={{0,1},{1,0},{2,3},{3,2},{4,5},{5,4},{6,7},{7,6},{8,9},{9,8},{10,11... | collective-permute-start | bytes 1572872 | tf_op jit(solution)/shard_map/ppermute | solution.py:421
  2.9 1.5 copy-start.34
  47.2 4.4 %collective-permute-start.28 = (bf16[1024,1024]{1,0:T(8,128)(2,1)}, bf16[1024,1024]{1,0:T(8,128)(2,1)S(1)}, u32[]{:S(2)}, u32[]{:S(2)}) collective-permute-start(bf16[1024,1024]{1,0:T(8,128)(2,1)} %get-tuple-element.120), channel_id=1, source_target_pairs={{0,1},{1,0},{2,3},{3,2},{4,5},{5,4},{6,7},{7,6},{8,9},{9,8},{10,11... | collective-permute-start | bytes 6291464 | tf_op jit(solution)/shard_map/ppermute | solution.py:488
  51.6 1.6 copy-start.5
  53.2 5.3 %copy-start.1 = (bf16[512,1024]{1,0:T(8,128)(2,1)S(1)}, bf16[512,1024]{1,0:T(8,128)(2,1)}, u32[]{:S(2)}) copy-start(bf16[512,1024]{1,0:T(8,128)(2,1)} %w_ckv.3) | copy-start | bytes 3145732
  53.2 5.3 %copy-start.2 = (bf16[512,512]{1,0:T(8,128)(2,1)S(1)}, bf16[512,512]{1,0:T(8,128)(2,1)}, u32[]{:S(2)}) copy-start(bf16[512,512]{1,0:T(8,128)(2,1)} %w_cq.3) | copy-start | bytes 1572868
  53.2 5.3 %copy-start.3 = (bf16[512,512]{1,0:T(8,128)(2,1)S(1)}, bf16[512,512]{1,0:T(8,128)(2,1)}, u32[]{:S(2)}) copy-start(bf16[512,512]{1,0:T(8,128)(2,1)} %w_co.3) | copy-start | bytes 1572868
  53.2 5.3 %copy-start.7 = (bf16[16,256,256]{2,1,0:T(8,128)(2,1)S(1)}, bf16[16,256,256]{2,1,0:T(8,128)(2,1)}, u32[]{:S(2)}) copy-start(bf16[16,256,256]{2,1,0:T(8,128)(2,1)} %get-tuple-element.82.p_cross) | copy-start | bytes 6291460
  53.2 5.3 %copy-start.27 = (bf16[3,512]{1,0:T(4,128)(2,1)S(1)}, bf16[3,512]{1,0:T(4,128)(2,1)}, u32[]{:S(2)}) copy-start(bf16[3,512]{1,0:T(4,128)(2,1)} %gain_ref.3) | copy-start | bytes 9220
  53.3 5.3 %copy-start.28 = (f32[8,512]{1,0:T(8,128)S(1)}, f32[8,512]{1,0:T(8,128)}, u32[]{:S(2)}) copy-start(f32[8,512]{1,0:T(8,128)} %get-tuple-element.75.dnorm_in) | copy-start | bytes 49156
  55.6 36.3 %collective-permute-start.29 = (bf16[512,1024]{1,0:T(8,128)(2,1)}, bf16[512,1024]{1,0:T(8,128)(2,1)}, u32[]{:S(2)}, u32[]{:S(2)}) collective-permute-start(bf16[512,1024]{1,0:T(8,128)(2,1)} %get-tuple-element.122), channel_id=1, source_target_pairs={{0,2},{2,0},{4,6},{6,4},{8,10},{10,8},{12,14},{14,12},{16,18},{18,... | collective-permute-start | bytes 3145736 | tf_op jit(solution)/shard_map/ppermute | solution.py:483
  58.5 1.2 copy-start.9
  67.3 11.2 %copy-start = (bf16[512,1536]{1,0:T(8,128)(2,1)S(1)}, bf16[512,1536]{1,0:T(8,128)(2,1)}, u32[]{:S(2)}) copy-start(bf16[512,1536]{1,0:T(8,128)(2,1)} %w_qkv.3) | copy-start | bytes 4718596
  67.3 11.2 %copy-start.4 = (bf16[512,512]{1,0:T(8,128)(2,1)S(1)}, bf16[512,512]{1,0:T(8,128)(2,1)}, u32[]{:S(2)}) copy-start(bf16[512,512]{1,0:T(8,128)(2,1)} %w_so.3) | copy-start | bytes 1572868
  67.3 11.2 %copy-start.6 = (bf16[16,256,256]{2,1,0:T(8,128)(2,1)S(1)}, bf16[16,256,256]{2,1,0:T(8,128)(2,1)}, u32[]{:S(2)}) copy-start(bf16[16,256,256]{2,1,0:T(8,128)(2,1)} %get-tuple-element.88.p_self) | copy-start | bytes 6291460
  67.3 11.2 %copy-start.8 = (bf16[512,1536]{1,0:T(8,128)(2,1)S(1)}, bf16[512,1536]{1,0:T(8,128)(2,1)}, u32[]{:S(2)}) copy-start(bf16[512,1536]{1,0:T(8,128)(2,1)} %get-tuple-element.87.qkv) | copy-start | bytes 4718596
  67.3 11.2 %copy-start.16 = (bf16[512,512]{1,0:T(8,128)(2,1)S(1)}, bf16[512,512]{1,0:T(8,128)(2,1)}, u32[]{:S(2)}) copy-start(bf16[512,512]{1,0:T(8,128)(2,1)} %get-tuple-element.86.elow) | copy-start | bytes 1572868
  67.3 11.2 %copy-start.17 = (bf16[512,512]{1,0:T(8,128)(2,1)S(1)}, bf16[512,512]{1,0:T(8,128)(2,1)}, u32[]{:S(2)}) copy-start(bf16[512,512]{1,0:T(8,128)(2,1)} %get-tuple-element.89.att) | copy-start | bytes 1572868
  67.4 11.2 %copy-start.29 = (s32[2]{0:T(128)S(1)}, s32[2]{0:T(128)}, u32[]{:S(2)}) copy-start(s32[2]{0:T(128)} %pair_ref.3) | copy-start | bytes 28
  78.5 11.5 %copy-start.30 = (bf16[2,128,512]{2,1,0:T(8,128)(2,1)}, bf16[2,128,512]{2,1,0:T(8,128)(2,1)S(1)}, u32[]{:S(2)}) copy-start(bf16[2,128,512]{2,1,0:T(8,128)(2,1)S(1)} %get-tuple-element.93) | copy-start | bytes 786436
  91.4 6.2 %collective-permute-start.6 = (bf16[528,1024]{1,0:T(8,128)(2,1)}, bf16[528,1024]{1,0:T(8,128)(2,1)S(1)}, u32[]{:S(2)}, u32[]{:S(2)}) collective-permute-start(bf16[528,1024]{1,0:T(8,128)(2,1)} %get-tuple-element.95), channel_id=1, source_target_pairs={{0,1},{1,0},{2,3},{3,2},{4,5},{5,4},{6,7},{7,6},{8,9},{9,8},{10,11... | collective-permute-start | bytes 3244040 | tf_op jit(solution)/shard_map/ppermute | solution.py:488
  91.4 7.8 %collective-permute-start.17 = (bf16[512,1024]{1,0:T(8,128)(2,1)}, bf16[512,1024]{1,0:T(8,128)(2,1)}, u32[]{:S(2)}, u32[]{:S(2)}) collective-permute-start(bf16[512,1024]{1,0:T(8,128)(2,1)} %get-tuple-element.107), channel_id=1, source_target_pairs={{0,1},{1,0},{2,3},{3,2},{4,5},{5,4},{6,7},{7,6},{8,9},{9,8},{10,11... | collective-permute-start | bytes 3145736 | tf_op jit(solution)/shard_map/ppermute | solution.py:488
  91.9 1.2 copy-start.13
  96.1 14.0 %collective-permute-start.30 = (bf16[256,1024]{1,0:T(8,128)(2,1)}, bf16[256,1024]{1,0:T(8,128)(2,1)}, u32[]{:S(2)}, u32[]{:S(2)}) collective-permute-start(bf16[256,1024]{1,0:T(8,128)(2,1)} %get-tuple-element.124), channel_id=1, source_target_pairs={{0,4},{2,6},{4,0},{6,2},{8,12},{10,14},{12,8},{14,10},{16,20},{18,... | collective-permute-start | bytes 1572872 | tf_op jit(solution)/shard_map/ppermute | solution.py:483
  98.6 2.8 %copy-start.14 = (bf16[272,1024]{1,0:T(8,128)(2,1)}, bf16[272,1024]{1,0:T(8,128)(2,1)S(1)}, u32[]{:S(2)}) copy-start(bf16[272,1024]{1,0:T(8,128)(2,1)S(1)} %get-tuple-element.96.a_ref) | copy-start | bytes 1671172
  98.6 41.0 %collective-permute-start.7 = (bf16[272,1024]{1,0:T(8,128)(2,1)}, bf16[272,1024]{1,0:T(8,128)(2,1)S(1)}, u32[]{:S(2)}, u32[]{:S(2)}) collective-permute-start(bf16[272,1024]{1,0:T(8,128)(2,1)} %get-tuple-element.97), channel_id=1, source_target_pairs={{0,2},{2,0},{4,6},{6,4},{8,10},{10,8},{12,14},{14,12},{16,18},{18,... | collective-permute-start | bytes 1671176 | tf_op jit(solution)/shard_map/ppermute | solution.py:483
  101.4 38.2 %copy-start.15 = (bf16[272,1024]{1,0:T(8,128)(2,1)S(1)}, bf16[272,1024]{1,0:T(8,128)(2,1)}, u32[]{:S(2)}) copy-start(bf16[272,1024]{1,0:T(8,128)(2,1)} %copy-done.14) | copy-start | bytes 1671172
  101.4 38.0 %collective-permute-start.18 = (bf16[256,1024]{1,0:T(8,128)(2,1)}, bf16[256,1024]{1,0:T(8,128)(2,1)S(1)}, u32[]{:S(2)}, u32[]{:S(2)}) collective-permute-start(bf16[256,1024]{1,0:T(8,128)(2,1)} %get-tuple-element.109), channel_id=1, source_target_pairs={{0,2},{2,0},{4,6},{6,4},{8,10},{10,8},{12,14},{14,12},{16,18},{18,... | collective-permute-start | bytes 1572872 | tf_op jit(solution)/shard_map/ppermute | solution.py:483
  112.3 6.4 %collective-permute-start.31 = (bf16[64,1024]{1,0:T(8,128)(2,1)S(1)}, bf16[64,1024]{1,0:T(8,128)(2,1)S(1)}, u32[]{:S(2)}, u32[]{:S(2)}) collective-permute-start(bf16[64,1024]{1,0:T(8,128)(2,1)S(1)} %get-tuple-element.126), channel_id=1, source_target_pairs={{0,8},{2,10},{4,12},{6,14},{8,0},{10,2},{12,4},{14,6},{16,24},{18,... | collective-permute-start | bytes 393224 | tf_op jit(solution)/shard_map/ppermute | solution.py:483
  113.9 9.8 %collective-permute-start.32 = (bf16[64,1024]{1,0:T(8,128)(2,1)S(1)}, bf16[64,1024]{1,0:T(8,128)(2,1)S(1)}, u32[]{:S(2)}, u32[]{:S(2)}) collective-permute-start(bf16[64,1024]{1,0:T(8,128)(2,1)S(1)} %get-tuple-element.127), channel_id=1, source_target_pairs={{0,16},{2,18},{4,20},{6,22},{8,24},{10,26},{12,28},{14,30},{16,0},... | collective-permute-start | bytes 393224 | tf_op jit(solution)/shard_map/ppermute | solution.py:483
  116.5 7.2 %collective-permute-start.33 = (bf16[64,1024]{1,0:T(8,128)(2,1)S(1)}, bf16[64,1024]{1,0:T(8,128)(2,1)S(1)}, u32[]{:S(2)}, u32[]{:S(2)}) collective-permute-start(bf16[64,1024]{1,0:T(8,128)(2,1)S(1)} %get-tuple-element.128), channel_id=1, source_target_pairs={{0,24},{2,26},{4,28},{6,30},{8,16},{10,18},{12,20},{14,22},{16,8},... | collective-permute-start | bytes 393224 | tf_op jit(solution)/shard_map/ppermute | solution.py:483
  123.8 34.3 %copy-start.38 = (bf16[2,128,512]{2,1,0:T(8,128)(2,1)S(1)}, bf16[2,128,512]{2,1,0:T(8,128)(2,1)}, u32[]{:S(2)}) copy-start(bf16[2,128,512]{2,1,0:T(8,128)(2,1)} %get-tuple-element.73) | copy-start | bytes 786436
  123.8 5.5 %collective-permute-start.34 = (bf16[64,1024]{1,0:T(8,128)(2,1)S(1)}, bf16[64,1024]{1,0:T(8,128)(2,1)S(1)}, u32[]{:S(2)}, u32[]{:S(2)}) collective-permute-start(bf16[64,1024]{1,0:T(8,128)(2,1)S(1)} %add_line.5.refs_0_), channel_id=1, source_target_pairs={{0,8},{2,10},{4,12},{6,14},{8,0},{10,2},{12,4},{14,6},{16,24},{18,... | collective-permute-start | bytes 393224 | tf_op jit(solution)/shard_map/ppermute | solution.py:483
  125.8 10.9 %collective-permute-start.35 = (bf16[64,1024]{1,0:T(8,128)(2,1)S(1)}, bf16[64,1024]{1,0:T(8,128)(2,1)S(1)}, u32[]{:S(2)}, u32[]{:S(2)}) collective-permute-start(bf16[64,1024]{1,0:T(8,128)(2,1)S(1)} %add_line.5.refs_0_), channel_id=1, source_target_pairs={{0,16},{2,18},{4,20},{6,22},{8,24},{10,26},{12,28},{14,30},{16,0},... | collective-permute-start | bytes 393224 | tf_op jit(solution)/shard_map/ppermute | solution.py:483
  127.0 9.8 %collective-permute-start.36 = (bf16[64,1024]{1,0:T(8,128)(2,1)S(1)}, bf16[64,1024]{1,0:T(8,128)(2,1)S(1)}, u32[]{:S(2)}, u32[]{:S(2)}) collective-permute-start(bf16[64,1024]{1,0:T(8,128)(2,1)S(1)} %add_line.5.refs_0_), channel_id=1, source_target_pairs={{0,24},{2,26},{4,28},{6,30},{8,16},{10,18},{12,20},{14,22},{16,8},... | collective-permute-start | bytes 393224 | tf_op jit(solution)/shard_map/ppermute | solution.py:483
  136.8 21.4 %collective-permute-start.37 = (bf16[256,1024]{1,0:T(8,128)(2,1)S(1)}, bf16[256,1024]{1,0:T(8,128)(2,1)S(1)}, u32[]{:S(2)}, u32[]{:S(2)}) collective-permute-start(bf16[256,1024]{1,0:T(8,128)(2,1)S(1)} %join_line.5.refs_0_), channel_id=1, source_target_pairs={{0,4},{2,6},{4,0},{6,2},{8,12},{10,14},{12,8},{14,10},{16,20},{18,... | collective-permute-start | bytes 1572872 | tf_op jit(solution)/shard_map/ppermute | solution.py:483
  139.5 9.8 %collective-permute-start.19 = (bf16[128,1024]{1,0:T(8,128)(2,1)S(1)}, bf16[128,1024]{1,0:T(8,128)(2,1)S(1)}, u32[]{:S(2)}, u32[]{:S(2)}) collective-permute-start(bf16[128,1024]{1,0:T(8,128)(2,1)S(1)} %get-tuple-element.111), channel_id=1, source_target_pairs={{0,4},{2,6},{4,0},{6,2},{8,12},{10,14},{12,8},{14,10},{16,20},{18,... | collective-permute-start | bytes 786440 | tf_op jit(solution)/shard_map/ppermute | solution.py:483
  139.8 35.5 %copy-start.33 = (bf16[2,128,512]{2,1,0:T(8,128)(2,1)S(1)}, bf16[2,128,512]{2,1,0:T(8,128)(2,1)}, u32[]{:S(2)}) copy-start(bf16[2,128,512]{2,1,0:T(8,128)(2,1)} %copy-done.32) | copy-start | bytes 786436
  139.8 12.8 %collective-permute-start.8 = (bf16[144,1024]{1,0:T(8,128)(2,1)S(1)}, bf16[144,1024]{1,0:T(8,128)(2,1)S(1)}, u32[]{:S(2)}, u32[]{:S(2)}) collective-permute-start(bf16[144,1024]{1,0:T(8,128)(2,1)S(1)} %get-tuple-element.99), channel_id=1, source_target_pairs={{0,4},{2,6},{4,0},{6,2},{8,12},{10,14},{12,8},{14,10},{16,20},{18,... | collective-permute-start | bytes 884744 | tf_op jit(solution)/shard_map/ppermute | solution.py:483
  149.4 6.3 %collective-permute-start.20 = (bf16[32,1024]{1,0:T(8,128)(2,1)S(1)}, bf16[32,1024]{1,0:T(8,128)(2,1)S(1)}, u32[]{:S(2)}, u32[]{:S(2)}) collective-permute-start(bf16[32,1024]{1,0:T(8,128)(2,1)S(1)} %get-tuple-element.113), channel_id=1, source_target_pairs={{0,8},{2,10},{4,12},{6,14},{8,0},{10,2},{12,4},{14,6},{16,24},{18,... | collective-permute-start | bytes 196616 | tf_op jit(solution)/shard_map/ppermute | solution.py:483
  151.4 6.7 %collective-permute-start.21 = (bf16[32,1024]{1,0:T(8,128)(2,1)S(1)}, bf16[32,1024]{1,0:T(8,128)(2,1)S(1)}, u32[]{:S(2)}, u32[]{:S(2)}) collective-permute-start(bf16[32,1024]{1,0:T(8,128)(2,1)S(1)} %get-tuple-element.114), channel_id=1, source_target_pairs={{0,16},{2,18},{4,20},{6,22},{8,24},{10,26},{12,28},{14,30},{16,0},... | collective-permute-start | bytes 196616 | tf_op jit(solution)/shard_map/ppermute | solution.py:483
  152.6 32.7 %copy-start.31 = (bf16[2,128,512]{2,1,0:T(8,128)(2,1)S(1)}, bf16[2,128,512]{2,1,0:T(8,128)(2,1)}, u32[]{:S(2)}) copy-start(bf16[2,128,512]{2,1,0:T(8,128)(2,1)} %copy-done.30) | copy-start | bytes 786436
  152.6 32.8 %copy-start.37 = (bf16[2,128,512]{2,1,0:T(8,128)(2,1)S(1)}, bf16[2,128,512]{2,1,0:T(8,128)(2,1)}, u32[]{:S(2)}) copy-start(bf16[2,128,512]{2,1,0:T(8,128)(2,1)} %get-tuple-element.72) | copy-start | bytes 786436
  152.7 11.6 %collective-permute-start.9 = (bf16[48,1024]{1,0:T(8,128)(2,1)S(1)}, bf16[48,1024]{1,0:T(8,128)(2,1)S(1)}, u32[]{:S(2)}, u32[]{:S(2)}) collective-permute-start(bf16[48,1024]{1,0:T(8,128)(2,1)S(1)} %get-tuple-element.101), channel_id=1, source_target_pairs={{0,8},{2,10},{4,12},{6,14},{8,0},{10,2},{12,4},{14,6},{16,24},{18,... | collective-permute-start | bytes 294920 | tf_op jit(solution)/shard_map/ppermute | solution.py:483
  154.7 15.1 %collective-permute-start.10 = (bf16[48,1024]{1,0:T(8,128)(2,1)S(1)}, bf16[48,1024]{1,0:T(8,128)(2,1)S(1)}, u32[]{:S(2)}, u32[]{:S(2)}) collective-permute-start(bf16[48,1024]{1,0:T(8,128)(2,1)S(1)} %get-tuple-element.102), channel_id=1, source_target_pairs={{0,16},{2,18},{4,20},{6,22},{8,24},{10,26},{12,28},{14,30},{16,0},... | collective-permute-start | bytes 294920 | tf_op jit(solution)/shard_map/ppermute | solution.py:483
  155.7 6.7 %collective-permute-start.22 = (bf16[32,1024]{1,0:T(8,128)(2,1)S(1)}, bf16[32,1024]{1,0:T(8,128)(2,1)S(1)}, u32[]{:S(2)}, u32[]{:S(2)}) collective-permute-start(bf16[32,1024]{1,0:T(8,128)(2,1)S(1)} %get-tuple-element.115), channel_id=1, source_target_pairs={{0,24},{2,26},{4,28},{6,30},{8,16},{10,18},{12,20},{14,22},{16,8},... | collective-permute-start | bytes 196616 | tf_op jit(solution)/shard_map/ppermute | solution.py:483
  158.1 27.3 %collective-permute-start.3 = (bf16[2,128,512]{2,1,0:T(8,128)(2,1)S(1)}, bf16[2,128,512]{2,1,0:T(8,128)(2,1)S(1)}, u32[]{:S(2)}, u32[]{:S(2)}) collective-permute-start(bf16[2,128,512]{2,1,0:T(8,128)(2,1)S(1)} %copy-done.38), channel_id=1, source_target_pairs={{0,1},{1,0},{2,3},{3,2},{4,5},{5,4},{6,7},{7,6},{8,9},{9,8},{10,11... | collective-permute-start | bytes 786440 | tf_op jit(solution)/shard_map/ppermute | solution.py:466
  158.1 28.2 %copy-start.26 = (bf16[2,128,512]{2,1,0:T(8,128)(2,1)S(1)}, bf16[2,128,512]{2,1,0:T(8,128)(2,1)}, u32[]{:S(2)}) copy-start(bf16[2,128,512]{2,1,0:T(8,128)(2,1)} %copy-done.25) | copy-start | bytes 786436
  158.1 12.1 %collective-permute-start.11 = (bf16[48,1024]{1,0:T(8,128)(2,1)S(1)}, bf16[48,1024]{1,0:T(8,128)(2,1)S(1)}, u32[]{:S(2)}, u32[]{:S(2)}) collective-permute-start(bf16[48,1024]{1,0:T(8,128)(2,1)S(1)} %get-tuple-element.103), channel_id=1, source_target_pairs={{0,24},{2,26},{4,28},{6,30},{8,16},{10,18},{12,20},{14,22},{16,8},... | collective-permute-start | bytes 294920 | tf_op jit(solution)/shard_map/ppermute | solution.py:483
  162.5 43.5 %collective-permute-start.38 = (bf16[512,1024]{1,0:T(8,128)(2,1)S(1)}, bf16[512,1024]{1,0:T(8,128)(2,1)S(1)}, u32[]{:S(2)}, u32[]{:S(2)}) collective-permute-start(bf16[512,1024]{1,0:T(8,128)(2,1)S(1)} %join_two.5.mine_ref), channel_id=1, source_target_pairs={{0,2},{2,0},{4,6},{6,4},{8,10},{10,8},{12,14},{14,12},{16,18},{18,... | collective-permute-start | bytes 3145736 | tf_op jit(solution)/shard_map/ppermute | solution.py:483
  164.3 8.8 %collective-permute-start.23 = (bf16[32,1024]{1,0:T(8,128)(2,1)S(1)}, bf16[32,1024]{1,0:T(8,128)(2,1)S(1)}, u32[]{:S(2)}, u32[]{:S(2)}) collective-permute-start(bf16[32,1024]{1,0:T(8,128)(2,1)S(1)} %add_line.4.refs_0_), channel_id=1, source_target_pairs={{0,8},{2,10},{4,12},{6,14},{8,0},{10,2},{12,4},{14,6},{16,24},{18,... | collective-permute-start | bytes 196616 | tf_op jit(solution)/shard_map/ppermute | solution.py:483
  169.7 5.5 %collective-permute-start.24 = (bf16[32,1024]{1,0:T(8,128)(2,1)S(1)}, bf16[32,1024]{1,0:T(8,128)(2,1)S(1)}, u32[]{:S(2)}, u32[]{:S(2)}) collective-permute-start(bf16[32,1024]{1,0:T(8,128)(2,1)S(1)} %add_line.4.refs_0_), channel_id=1, source_target_pairs={{0,16},{2,18},{4,20},{6,22},{8,24},{10,26},{12,28},{14,30},{16,0},... | collective-permute-start | bytes 196616 | tf_op jit(solution)/shard_map/ppermute | solution.py:483
  170.2 6.2 %collective-permute-start.25 = (bf16[32,1024]{1,0:T(8,128)(2,1)S(1)}, bf16[32,1024]{1,0:T(8,128)(2,1)S(1)}, u32[]{:S(2)}, u32[]{:S(2)}) collective-permute-start(bf16[32,1024]{1,0:T(8,128)(2,1)S(1)} %add_line.4.refs_0_), channel_id=1, source_target_pairs={{0,24},{2,26},{4,28},{6,30},{8,16},{10,18},{12,20},{14,22},{16,8},... | collective-permute-start | bytes 196616 | tf_op jit(solution)/shard_map/ppermute | solution.py:483
  173.1 4.6 %collective-permute-start.12 = (bf16[32,1024]{1,0:T(8,128)(2,1)S(1)}, bf16[32,1024]{1,0:T(8,128)(2,1)S(1)}, u32[]{:S(2)}, u32[]{:S(2)}) collective-permute-start(bf16[32,1024]{1,0:T(8,128)(2,1)S(1)} %slice.22.refs_0_), channel_id=1, source_target_pairs={{0,8},{2,10},{4,12},{6,14},{8,0},{10,2},{12,4},{14,6},{16,24},{18,... | collective-permute-start | bytes 196616 | tf_op jit(solution)/shard_map/ppermute | solution.py:483
  175.2 11.1 %collective-permute-start.4 = (bf16[2,128,512]{2,1,0:T(8,128)(2,1)S(1)}, bf16[2,128,512]{2,1,0:T(8,128)(2,1)S(1)}, u32[]{:S(2)}, u32[]{:S(2)}) collective-permute-start(bf16[2,128,512]{2,1,0:T(8,128)(2,1)S(1)} %copy-done.33), channel_id=1, source_target_pairs={{0,1},{1,0},{2,3},{3,2},{4,5},{5,4},{6,7},{7,6},{8,9},{9,8},{10,11... | collective-permute-start | bytes 786440 | tf_op jit(solution)/shard_map/ppermute | solution.py:466
  176.4 6.5 %collective-permute-start.13 = (bf16[32,1024]{1,0:T(8,128)(2,1)S(1)}, bf16[32,1024]{1,0:T(8,128)(2,1)S(1)}, u32[]{:S(2)}, u32[]{:S(2)}) collective-permute-start(bf16[32,1024]{1,0:T(8,128)(2,1)S(1)} %slice.22.refs_0_), channel_id=1, source_target_pairs={{0,16},{2,18},{4,20},{6,22},{8,24},{10,26},{12,28},{14,30},{16,0},... | collective-permute-start | bytes 196616 | tf_op jit(solution)/shard_map/ppermute | solution.py:483
  177.7 7.5 %collective-permute-start.14 = (bf16[32,1024]{1,0:T(8,128)(2,1)S(1)}, bf16[32,1024]{1,0:T(8,128)(2,1)S(1)}, u32[]{:S(2)}, u32[]{:S(2)}) collective-permute-start(bf16[32,1024]{1,0:T(8,128)(2,1)S(1)} %slice.22.refs_0_), channel_id=1, source_target_pairs={{0,24},{2,26},{4,28},{6,30},{8,16},{10,18},{12,20},{14,22},{16,8},... | collective-permute-start | bytes 196616 | tf_op jit(solution)/shard_map/ppermute | solution.py:483
  182.9 6.8 %collective-permute-start.26 = (bf16[128,1024]{1,0:T(8,128)(2,1)S(1)}, bf16[128,1024]{1,0:T(8,128)(2,1)S(1)}, u32[]{:S(2)}, u32[]{:S(2)}) collective-permute-start(bf16[128,1024]{1,0:T(8,128)(2,1)S(1)} %join_line.4.refs_0_), channel_id=1, source_target_pairs={{0,4},{2,6},{4,0},{6,2},{8,12},{10,14},{12,8},{14,10},{16,20},{18,... | collective-permute-start | bytes 786440 | tf_op jit(solution)/shard_map/ppermute | solution.py:483
  185.3 8.9 %collective-permute-start.15 = (bf16[128,1024]{1,0:T(8,128)(2,1)S(1)}, bf16[128,1024]{1,0:T(8,128)(2,1)S(1)}, u32[]{:S(2)}, u32[]{:S(2)}) collective-permute-start(bf16[128,1024]{1,0:T(8,128)(2,1)S(1)} %join_line.3.refs_0_), channel_id=1, source_target_pairs={{0,4},{2,6},{4,0},{6,2},{8,12},{10,14},{12,8},{14,10},{16,20},{18,... | collective-permute-start | bytes 786440 | tf_op jit(solution)/shard_map/ppermute | solution.py:483
  185.4 10.5 %collective-permute-start.5 = (bf16[2,128,512]{2,1,0:T(8,128)(2,1)S(1)}, bf16[2,128,512]{2,1,0:T(8,128)(2,1)S(1)}, u32[]{:S(2)}, u32[]{:S(2)}) collective-permute-start(bf16[2,128,512]{2,1,0:T(8,128)(2,1)S(1)} %copy-done.31), channel_id=1, source_target_pairs={{0,1},{1,0},{2,3},{3,2},{4,5},{5,4},{6,7},{7,6},{8,9},{9,8},{10,11... | collective-permute-start | bytes 786440 | tf_op jit(solution)/shard_map/ppermute | solution.py:466
  189.6 9.2 %collective-permute-start.27 = (bf16[256,1024]{1,0:T(8,128)(2,1)S(1)}, bf16[256,1024]{1,0:T(8,128)(2,1)S(1)}, u32[]{:S(2)}, u32[]{:S(2)}) collective-permute-start(bf16[256,1024]{1,0:T(8,128)(2,1)S(1)} %join_two.4.mine_ref), channel_id=1, source_target_pairs={{0,2},{2,0},{4,6},{6,4},{8,10},{10,8},{12,14},{14,12},{16,18},{18,... | collective-permute-start | bytes 1572872 | tf_op jit(solution)/shard_map/ppermute | solution.py:483
  194.2 10.3 %collective-permute-start.16 = (bf16[256,1024]{1,0:T(8,128)(2,1)S(1)}, bf16[256,1024]{1,0:T(8,128)(2,1)S(1)}, u32[]{:S(2)}, u32[]{:S(2)}) collective-permute-start(bf16[256,1024]{1,0:T(8,128)(2,1)S(1)} %join_two.3.mine_ref), channel_id=1, source_target_pairs={{0,2},{2,0},{4,6},{6,4},{8,10},{10,8},{12,14},{14,12},{16,18},{18,... | collective-permute-start | bytes 1572872 | tf_op jit(solution)/shard_map/ppermute | solution.py:483
  (14 other events, 13.4 us)

commit v2 on v1

v2 whole, which is shorter than its diff:
```python
import functools
import math

import jax
import jax.numpy as jnp
from jax import lax
from jax.experimental import pallas as pl
from jax.experimental.pallas import tpu as pltpu
from jax.sharding import PartitionSpec as P

HEADS = 8
NORM_EPS = 1e-05
NEG_FILL = -1e30
BF = jnp.bfloat16
F32 = jnp.float32
MIB = 1 << 20
ORDER = ('a', '', 'b', 'abcabcabcabcabcabcabcc')
ROUTES = (((1, 2), (2, 1), (4, 4), (8, 8)), ((1, 2), (2, 1), (4, 4), (8, 8)), ((1, 2), (2, 1), (4, 4), (8, 8)))
COST = {name: 100_000_000_000 for name in ("forward", "feed_keep", "cross", "cross_grads", "self", "self_grads")}
LANES = 1024


def mm(a, b):
    return lax.dot_general(a, b, (((1,), (0,)), ((), ())), preferred_element_type=F32)


def mm_bt(a, b):
    return lax.dot_general(a, b, (((1,), (1,)), ((), ())), preferred_element_type=F32)


def norm_forward(values, gain, bias):
    center = values - jnp.mean(values, -1, keepdims=True)
    rstd = lax.rsqrt(jnp.mean(center * center, -1, keepdims=True) + NORM_EPS)
    xhat = center * rstd
    return xhat, rstd, xhat * gain + bias


def norm_backward(xhat, rstd, gain, upstream):
    scaled = upstream * gain
    first = jnp.mean(scaled, -1, keepdims=True)
    second = jnp.mean(scaled * xhat, -1, keepdims=True)
    grad = rstd * (scaled - first - xhat * second)
    return grad, jnp.sum(upstream * xhat, 0, keepdims=True), jnp.sum(upstream, 0, keepdims=True)


def lane_half(shape, half):
    lane = lax.broadcasted_iota(jnp.int32, shape, 1)
    return (lane < 64) if half == 0 else (lane >= 64)


def weave(*lists):
    steps = [((i + 0.5) / len(some), k, step) for k, some in enumerate(lists) for i, step in enumerate(some)]
    for _, _, step in sorted(steps, key=lambda item: item[:2]):
        step()


def staged(count, *stages):
    held = {}

    def step(stage, item):
        def run():
            held[item] = stages[stage](item, held.get(item))

        return run

    return [
        step(k, t - k) for t in range(count + len(stages) - 1) for k in range(len(stages)) if 0 <= t - k < count
    ]


def attend_steps(sentence, length, q_ref, k_ref, v_ref, k_at, v_at, bias_ref, p_ref, rl_ref, out_ref, out_t):
    rows = pl.ds(sentence * length, length)

    def score(pair, _):
        queries = q_ref[rows, pair * 128 : pair * 128 + 128]
        keys = k_ref[rows, k_at + pair * 128 : k_at + pair * 128 + 128]
        zeros = jnp.zeros_like(queries)
        return [
            mm_bt(keys, jnp.where(lane_half(queries.shape, half), queries, zeros)) + bias_ref[sentence]
            for half in range(2)
        ]

    def soften(pair, scores):
        probs = []
        for half in range(2):
            top = jnp.max(scores[half], 0, keepdims=True)
            probs.append(jnp.exp(scores[half] - top).astype(BF))
            p_ref[sentence * HEADS + 2 * pair + half] = probs[half]
        return probs

    def mix(pair, probs):
        values_t = v_ref[rows, v_at + pair * 128 : v_at + pair * 128 + 128].T
        mixed = []
        for half in range(2):
            tall = jnp.concatenate([values_t[half * 64 : half * 64 + 64], jnp.ones((16, length), BF)], 0)
            both = mm(tall, probs[half])
            one_over = 1.0 / both[64:65]
            rl_ref[sentence * HEADS + 2 * pair + half] = one_over
            mixed.append(both[0:64] * one_over)
        joined = jnp.concatenate(mixed, 0).astype(BF)
        out_t[pair * 128 : pair * 128 + 128, rows] = joined
        out_ref[rows, pair * 128 : pair * 128 + 128] = joined.T

    return staged(HEADS // 2, score, soften, mix)


def attend_back_steps(
    sentence, length, q_ref, k_ref, v_ref, k_at, v_at, p_ref, rl_ref, out_t, go_t, gq_t, gk_t, gv_t, gk_at, gv_at
):
    rows = pl.ds(sentence * length, length)

    def start(pair, _):
        feats = slice(pair * 128, pair * 128 + 128)
        values = v_ref[rows, v_at + pair * 128 : v_at + pair * 128 + 128]
        mixed = out_t[feats, rows].astype(F32)
        grads = go_t[feats, rows].astype(F32)
        scaled, dots = [], []
        for half in range(2):
            part = slice(half * 64, half * 64 + 64)
            scaled.append((grads[part] * rl_ref[sentence * HEADS + 2 * pair + half]).astype(BF))
            dots.append(jnp.sum(mixed[part] * scaled[half].astype(F32), 0, keepdims=True))
        both = jnp.concatenate(scaled, 0)
        zeros = jnp.zeros_like(values)
        grad_probs = [mm(jnp.where(lane_half(values.shape, half), values, zeros), both) for half in range(2)]
        return scaled, dots, grad_probs

    def middle(pair, held):
        scaled, dots, grad_probs = held
        grad_scores = []
        for half in range(2):
            probs = p_ref[sentence * HEADS + 2 * pair + half].astype(F32)
            grad_scores.append((probs * (grad_probs[half] - dots[half])).astype(BF))
        return scaled, grad_scores

    def finish(pair, held):
        scaled, grad_scores = held
        queries_t = q_ref[rows, pair * 128 : pair * 128 + 128].T
        keys_t = k_ref[rows, k_at + pair * 128 : k_at + pair * 128 + 128].T
        gq, gk, gv = [], [], []
        for half in range(2):
            part = slice(half * 64, half * 64 + 64)
            gq.append(mm(keys_t[part], grad_scores[half]) * 0.125)
            gk.append(mm_bt(queries_t[part], grad_scores[half]))
            gv.append(mm_bt(scaled[half], p_ref[sentence * HEADS + 2 * pair + half]))
        for ref, at, grads in ((gq_t, 0, gq), (gk_t, gk_at, gk), (gv_t, gv_at, gv)):
            ref[at + pair * 128 : at + pair * 128 + 128, rows] = jnp.concatenate(grads, 0).astype(BF)

    return staged(HEADS // 2, start, middle, finish)


class Copies:
    def __init__(self, sems):
        self.sems, self.used, self.open = sems, 0, {}

    def start(self, name, source, target):
        copy = pltpu.make_async_copy(source, target, self.sems.at[self.used])
        self.used += 1
        copy.start()
        self.open.setdefault(name, []).append(copy)

    def wait(self, *names):
        for name in names or tuple(self.open):
            for copy in self.open.pop(name, ()):
                copy.wait()


def halves(place, length):
    half = length // 2
    return [
        [pl.ds(pl.multiple_of(sentence * length + which * half, half), half) for which in (place, 1 - place)]
        for sentence in range(2)
    ]


def feed_grads(which, ref, slow_t, ginner, gff_t, hidden):
    inner, width = hidden.shape[1], slow_t.shape[0]
    half_in, half_out = inner // 2, width // 2

    def give_in(index):
        def run():
            cols = pl.ds(pl.multiple_of(which * half_in + index * 256, 256), 256)
            ref[0:width, index * 256 : (index + 1) * 256] = mm(slow_t[...], ginner[:, cols]).astype(BF)

        return run

    def give_out(index):
        def run():
            feats = pl.ds(pl.multiple_of(which * half_out, half_out), half_out)
            low, at = width + (index // 2) * half_out, (index % 2) * 512
            ref[low : low + half_out, at : at + 512] = mm(
                gff_t[feats, :], hidden[:, index * 512 : (index + 1) * 512]
            ).astype(BF)

        return run

    return [give_out(i) for i in range(inner // 512)] + [give_in(i) for i in range(half_in // 256)]


def feed_keep_kernel(place_ref, gff_t, hidden, slow_t, ginner, keep_ref):
    weave(feed_grads(place_ref[0], keep_ref, slow_t, ginner, gff_t, hidden))


def forward_kernel(numbers_ref, *refs):
    (dec2_in, enc2_in, og2_in, dec_in, enc_in, og_in), refs = refs[:6], refs[6:]
    names = FORWARD_WEIGHTS
    weights_in, refs = refs[: len(names)], refs[len(names) :]
    kept = dict(zip(FORWARD_KEPT, refs))
    (out_own, out_oth, send_ref, gff_t, hidden, slow_t, ginner, gss, elow, qkv, p_self, rl_self, att_t, xhat1, rstd1,
     flow, encs, cq, ckv, p_cross, rl_cross, crossed_t, dnorm_ref) = refs[: len(FORWARD_KEPT) - len(PASSED_WEIGHTS)]
    refs = refs[len(FORWARD_KEPT) :]
    w = {name: kept["w_" + name] for name in PASSED_WEIGHTS}
    w.update(zip([name for name in names if name not in PASSED_WEIGHTS], refs))
    (dec_s, og_s, e_ref, bias_ref, att, fnorm, crossed, xhat2, rstd2, third, slow, slope, gff, outs, sems) = refs[
        len(names) - len(PASSED_WEIGHTS) :
    ]
    copies = Copies(sems)
    place = numbers_ref[0]
    tokens, width = e_ref.shape
    length = tokens // 2
    inner = ginner.shape[1]
    where = halves(place, length)
    for s in range(2):
        copies.start("dec", dec_in.at[place, s], dec_s.at[where[s][0]])
        copies.start("dec", dec2_in.at[place, s], dec_s.at[where[s][1]])
    for name, ref in zip(names[:4], weights_in[:4]):
        copies.start(name, ref, w[name])
    for s in range(2):
        copies.start("enc", enc_in.at[place, s], encs.at[where[s][0]])
        copies.start("enc", enc2_in.at[place, s], encs.at[where[s][1]])
    for name, ref in zip(names[4:], weights_in[4:]):
        copies.start(name, ref, w[name])
    for s in range(2):
        copies.start("og", og_in.at[place, s], og_s.at[where[s][0]])
        copies.start("og", og2_in.at[place, s], og_s.at[where[s][1]])

    rows = [slice(s * length, (s + 1) * length) for s in range(2)]
    keys_at = lax.broadcasted_iota(jnp.int32, (length, length), 0)
    query_at = lax.broadcasted_iota(jnp.int32, (length, length), 1)
    for s in range(2):
        bias_ref[s] = jnp.where((keys_at <= query_at) & (keys_at < numbers_ref[2 + s]), 0.0, NEG_FILL)
        bias_ref[2 + s] = jnp.where(keys_at < numbers_ref[4 + s], 0.0, NEG_FILL)

    def embed(s):
        def run():
            values = dec_s[rows[s]].astype(F32) + row
            e_ref[rows[s]] = values
            elow[rows[s]] = values.astype(BF)

        return run

    def pack(s, part):
        def run():
            cols = slice(part * width, (part + 1) * width)
            values = mm(elow[rows[s]], w["qkv"][:, cols])
            qkv[rows[s], cols] = (values * 0.125 if part == 0 else values).astype(BF)

        return run

    def pack_cross(s, part):
        def run():
            cols = slice(part * width, (part + 1) * width)
            ckv[rows[s], cols] = mm(encs[rows[s]], w["ckv"][:, cols]).astype(BF)

        return run

    held = {}

    def after_self(s):
        def project():
            held["first", s] = e_ref[rows[s]] + mm(att[rows[s]], w["so"][...])

        def norm():
            xhat, rstd, normed = norm_forward(held.pop(("first", s)), gain[0:1], nbias[0:1])
            xhat1[rows[s]] = xhat
            rstd1[rows[s]] = jnp.broadcast_to(rstd, (length, 128))
            fnorm[rows[s]] = normed
            flow[rows[s]] = normed.astype(BF)

        def query():
            cq[rows[s]] = (mm(flow[rows[s]], w["cq"][...]) * 0.125).astype(BF)

        return [project, norm, query]

    def after_cross(s):
        def project():
            held["second", s] = fnorm[rows[s]] + mm(crossed[rows[s]], w["co"][...])

        def norm():
            xhat, rstd, normed = norm_forward(held.pop(("second", s)), gain[1:2], nbias[1:2])
            xhat2[rows[s]] = xhat
            rstd2[rows[s]] = jnp.broadcast_to(rstd, (length, 128))
            third[rows[s]] = normed
            slow[rows[s]] = normed.astype(BF)

        def turn():
            slow_t[:, rows[s]] = slow[rows[s]].T

        return [project, norm, turn]

    step = 256

    def feed(s):
        def grow(index, _):
            return mm(slow[rows[s]], w["fi"][:, index * step : (index + 1) * step])

        def bend(index, v):
            cols = slice(index * step, (index + 1) * step)
            square = v * v
            bent = jnp.tanh(v * (0.7978845608028654 + (0.7978845608028654 * 0.044715) * square))
            half = 0.5 + 0.5 * bent
            hidden[rows[s], cols] = (v * half).astype(BF)
            rise = v * (0.7978845608028654 + (3 * 0.7978845608028654 * 0.044715) * square)
            slope[rows[s], cols] = (half + (0.5 - 0.5 * bent * bent) * rise).astype(BF)

        return staged(inner // step, grow, bend)

    gains = {}

    def after_feed(s):
        def shrink(part):
            def run():
                cols = slice(part * (width // 2), (part + 1) * (width // 2))
                third[rows[s], cols] += mm(hidden[rows[s]], w["fo"][:, cols])

            return run

        def norm():
            xhat, rstd, normed = norm_forward(third[rows[s]], gain[2:3], nbias[2:3])
            outs[rows[s]] = normed.astype(BF)
            grad, *gains[2, s] = norm_backward(xhat, rstd, gain[2:3], og_s[rows[s]].astype(F32))
            third[rows[s]] = grad
            gff[rows[s]] = grad.astype(BF)

        def turn():
            gff_t[:, rows[s]] = gff[rows[s]].T
            out_own[s] = outs[where[s][0], :]
            out_oth[s] = outs[where[s][1], :]

        return [shrink(0), shrink(1), norm, turn]

    def feed_back(s):
        def shrink(index, _):
            return mm_bt(gff[rows[s]], w["fo"][index * step : (index + 1) * step, :]).astype(BF)

        def bend(index, grad_hidden):
            cols = slice(index * step, (index + 1) * step)
            ginner[rows[s], cols] = (grad_hidden.astype(F32) * slope[rows[s], cols].astype(F32)).astype(BF)

        return staged(inner // step, shrink, bend)

    def after_feed_back(s):
        def shrink(part):
            def run():
                cols = slice(part * (width // 2), (part + 1) * (width // 2))
                third[rows[s], cols] += mm_bt(ginner[rows[s]], w["fi"][cols, :])

            return run

        def norm():
            gss[rows[s]], *gains[1, s] = norm_backward(xhat2[rows[s]], rstd2[rows[s], 0:1], gain[1:2], third[rows[s]])

        return [shrink(0), shrink(1), norm]

    copies.wait("table", "gain", "nbias", "dec", "qkv")
    gain = w["gain"][...].astype(F32)
    nbias = w["nbias"][...].astype(F32)
    picked = lax.broadcasted_iota(jnp.int32, w["table"].shape, 0) == numbers_ref[1]
    row = jnp.sum(jnp.where(picked, w["table"][...].astype(F32), 0.0), 0, keepdims=True)
    weave([embed(0)])
    weave([pack(0, part) for part in range(3)], [embed(1)])
    copies.wait("enc", "ckv")
    weave(
        attend_steps(0, length, qkv, qkv, qkv, width, 2 * width, bias_ref, p_self, rl_self, att, att_t),
        [pack(1, part) for part in range(3)] + [pack_cross(0, 0), pack_cross(0, 1)],
    )
    copies.wait("so", "cq", "co")
    weave(
        attend_steps(1, length, qkv, qkv, qkv, width, 2 * width, bias_ref, p_self, rl_self, att, att_t),
        after_self(0) + [pack_cross(1, 0), pack_cross(1, 1)],
    )
    cross_bias = bias_ref.at[2:4]
    weave(
        attend_steps(0, length, cq, ckv, ckv, 0, width, cross_bias, p_cross, rl_cross, crossed, crossed_t),
        after_self(1),
    )
    copies.wait("fi", "fo", "og")
    weave(
        attend_steps(1, length, cq, ckv, ckv, 0, width, cross_bias, p_cross, rl_cross, crossed, crossed_t),
        after_cross(0),
    )
    weave(feed(0), after_cross(1))
    weave(feed(1), after_feed(0))
    weave(feed_back(0), after_feed(1))
    weave(feed_back(1), after_feed_back(0))
    weave(feed_grads(1 - place, send_ref, slow_t, ginner, gff_t, hidden), after_feed_back(1))
    dnorm_ref[...] = jnp.zeros(dnorm_ref.shape, F32)
    for k in (1, 2):
        dnorm_ref[k : k + 1, :] = gains[k, 0][0] + gains[k, 1][0]
        dnorm_ref[3 + k : 4 + k, :] = gains[k, 0][1] + gains[k, 1][1]
    copies.wait()


FORWARD_WEIGHTS = ("table", "qkv", "gain", "nbias", "ckv", "so", "cq", "co", "fi", "fo")
PASSED_WEIGHTS = ("qkv", "gain", "ckv", "so", "cq", "co")
FORWARD_KEPT = (
    "out_own", "out_oth", "send_a", "gff_t", "hidden", "slow_t", "ginner", "gss", "elow", "qkv", "p_self", "rl_self",
    "att_t", "xhat1", "rstd1", "flow", "encs", "cq", "ckv", "p_cross", "rl_cross", "crossed_t", "dnorm",
) + tuple("w_" + name for name in PASSED_WEIGHTS)


def cross_kernel(
    gss, dnorm_in, w_gain, w_co, w_cq, ckv, cq, p_cross, rl_cross, crossed_t, xhat1, rstd1,
    branch, gq_t, gkv_t, gfs, dnorm_ref,
    go_t,
):
    tokens, width = gss.shape
    length = tokens // 2
    rows = [slice(s * length, (s + 1) * length) for s in range(2)]
    gain = w_gain[...].astype(F32)
    gains = {}

    def begin(s):
        def run():
            low = gss[rows[s]].astype(BF)
            branch[rows[s]] = low
            go_t[:, rows[s]] = mm_bt(w_co[...], low).astype(BF)

        return run

    def after(s):
        held = {}

        def query():
            held["first"] = gss[rows[s]] + mm_bt(gq_t[:, rows[s]].T, w_cq[...])

        def norm():
            gfs[rows[s]], *gains[s] = norm_backward(xhat1[rows[s]], rstd1[rows[s], 0:1], gain[0:1], held["first"])

        return [query, norm]

    def attention(s):
        return attend_back_steps(
            s, length, cq, ckv, ckv, 0, width, p_cross, rl_cross, crossed_t, go_t, gq_t, gkv_t, gkv_t, 0, width
        )

    begin(0)()
    weave(attention(0), [begin(1)])
    weave(attention(1), after(0))
    weave(after(1))
    dnorm_ref[...] = dnorm_in[...]
    dnorm_ref[0:1, :] = gains[0][0] + gains[1][0]
    dnorm_ref[3:4, :] = gains[0][1] + gains[1][1]


def give_tall(which, ref, mixed_t, branch):
    width = branch.shape[1]
    half = width // 2
    cols = pl.ds(pl.multiple_of(which * half, half), half)
    grads = mm(mixed_t[...], branch[:, cols]).astype(BF)
    ref[half:width, width : width + half] = grads[0:half]
    ref[half:width, width + half :] = grads[half:]


def cross_grads_kernel(
    place_ref, branch, gq_t, gkv_t, crossed_t, flow, encs, w_ckv, send_ref, keep_ref, genc_own, genc_oth, genc
):
    place = place_ref[0]
    tokens, width = branch.shape
    length = tokens // 2
    half = width // 2
    where = halves(place, length)

    def give(which, ref):
        def out():
            give_tall(which, ref, crossed_t, branch)

        def query():
            feats = pl.ds(pl.multiple_of(which * half, half), half)
            ref[0:half, width:] = mm(gq_t[feats, :], flow[...]).astype(BF)

        def pair():
            feats = pl.ds(pl.multiple_of(which * width, half), width)
            ref[:, 0:width] = mm(gkv_t[feats, :], encs[...]).astype(BF)

        return [out, query, pair]

    def encoder(s):
        def run():
            rows = slice(s * length, (s + 1) * length)
            genc[rows] = mm(w_ckv[...], gkv_t[:, rows]).astype(BF).T
            genc_own[s] = genc[where[s][0], :]
            genc_oth[s] = genc[where[s][1], :]

        return run

    weave(give(1 - place, send_ref) + give(place, keep_ref), [encoder(0), encoder(1)])


def self_kernel(gfs, w_so, qkv, p_self, rl_self, att_t, branch, gqkv_t, go_t):
    tokens, width = gfs.shape
    length = tokens // 2
    rows = [slice(s * length, (s + 1) * length) for s in range(2)]

    def begin(s):
        def run():
            low = gfs[rows[s]].astype(BF)
            branch[rows[s]] = low
            go_t[:, rows[s]] = mm_bt(w_so[...], low).astype(BF)

        return run

    def attention(s):
        return attend_back_steps(
            s, length, qkv, qkv, qkv, width, 2 * width, p_self, rl_self, att_t, go_t, gqkv_t, gqkv_t, gqkv_t,
            width, 2 * width,
        )

    begin(0)()
    weave(attention(0), [begin(1)])
    weave(attention(1))


def self_grads_kernel(
    numbers_ref, gfs, dnorm_in, branch, gqkv_t, att_t, elow, w_qkv,
    send_ref, keep_ref, gin_own, gin_oth,
    gin, small,
):
    place = numbers_ref[0]
    tokens, width = gfs.shape
    length = tokens // 2
    half = width // 2
    where = halves(place, length)
    sums, held = {}, {}

    def give(which, ref):
        def out():
            give_tall(which, ref, att_t, branch)

        def part(index):
            def run():
                feats = pl.ds(pl.multiple_of(which * 3 * half + index * half, half), half)
                low, at = ((0, 0), (half, 0), (0, width))[index]
                ref[low : low + half, at : at + width] = mm(gqkv_t[feats, :], elow[...]).astype(BF)

            return run

        return [out, part(0), part(1), part(2)]

    def back(s):
        rows = slice(s * length, (s + 1) * length)

        def start():
            held[s] = mm(w_qkv[...], gqkv_t[:, rows])

        def finish():
            total = gfs[rows] + held.pop(s).T
            gin[rows] = total.astype(BF)
            sums[s] = jnp.sum(total, 0, keepdims=True)
            gin_own[s] = gin[where[s][0], :]
            gin_oth[s] = gin[where[s][1], :]

        return [start, finish]

    weave(give(1 - place, send_ref) + give(place, keep_ref), back(0) + back(1))
    small[0:8, :] = dnorm_in[...]
    picked = lax.broadcasted_iota(jnp.int32, (8, width), 0) == numbers_ref[1]
    small[8:16, :] = jnp.where(picked, jnp.broadcast_to(sums[0] + sums[1], (8, width)), 0.0)
    for which, ref in ((1 - place, send_ref), (place, keep_ref)):
        ref[width : width + 16, :] = jnp.zeros((16, ref.shape[1]), BF)
        ref[width : width + 16, 0:half] = small[:, pl.ds(pl.multiple_of(which * half, half), half)].astype(BF)


def add_split_kernel(tail, bit_ref, a_ref, b_ref, send_ref, keep_ref):
    half = send_ref.shape[0] - tail
    bit = bit_ref[0]
    for which, ref in ((1 - bit, send_ref), (bit, keep_ref)):
        rows = pl.ds(pl.multiple_of(which * half, 16), half)
        ref[0:half, :] = (a_ref[rows, :].astype(F32) + b_ref[rows, :].astype(F32)).astype(BF)
        if tail:
            last = pl.ds(2 * half, tail)
            ref[half : half + tail, :] = (a_ref[last, :].astype(F32) + b_ref[last, :].astype(F32)).astype(BF)


def add_all_kernel(*refs):
    total = refs[0][...].astype(F32)
    for ref in refs[1:-1]:
        total = total + ref[...].astype(F32)
    refs[-1][...] = total.astype(BF)


def join_kernel(index_ref, *refs):
    out = refs[-1]
    rows = refs[0].shape[0]
    for j, ref in enumerate(refs[:-1]):
        out[pl.ds(pl.multiple_of((index_ref[0] ^ j) * rows, 16), rows), :] = ref[...]


def unpack_kernel(unpack, index_ref, mine_ref, got_ref, *outs):
    @pl.when(index_ref[0] == 0)
    def _():
        unpack(mine_ref, got_ref, *outs)

    @pl.when(index_ref[0] != 0)
    def _():
        unpack(got_ref, mine_ref, *outs)


def unpack_ff(low_ref, high_ref, in_ref, out_ref):
    in_ref[...] = low_ref[...].astype(F32)
    half = out_ref.shape[1]
    for j in range(2):
        tall = low_ref.shape[1]
        out_ref[j * tall : (j + 1) * tall, :] = high_ref[j * half : (j + 1) * half, :].T.astype(F32)


def unpack_tall(low_ref, high_ref, out_ref):
    half = out_ref.shape[1]
    width = 2 * half
    out_ref[0:half, :] = high_ref[:, width : width + half].astype(F32)
    out_ref[half:width, :] = high_ref[:, width + half :].astype(F32)


def unpack_cross(low_ref, high_ref, kv_ref, query_ref, out_ref):
    half, width = low_ref.shape[0], query_ref.shape[0]
    kv_ref[:, 0:half] = low_ref[:, 0:width].T.astype(F32)
    kv_ref[:, half:] = high_ref[:, 0:width].T.astype(F32)
    query_ref[...] = low_ref[:, width:].T.astype(F32)
    unpack_tall(low_ref, high_ref, out_ref)


def unpack_self(low_ref, high_ref, qkv_ref, out_ref):
    half, width = low_ref.shape[0], qkv_ref.shape[0]
    qkv_ref[:, 0:half] = low_ref[:, 0:width].T.astype(F32)
    qkv_ref[:, half:width] = high_ref[:, 0:width].T.astype(F32)
    qkv_ref[:, width:] = low_ref[:, width:].T.astype(F32)
    unpack_tall(low_ref, high_ref, out_ref)


def smem():
    return pl.BlockSpec(memory_space=pltpu.SMEM)


def vmem():
    return pl.BlockSpec(memory_space=pltpu.VMEM)


def call(kernel, scalars, arrays, outs, scratch=(), name=None, far=(), results=(), sems=0, after=()):
    held = [*results, *scratch]
    limit = sum(math.prod(s[:-2]) * -(-s[-2] // 16) * 16 * s[-1] * jnp.dtype(d).itemsize for s, d in held) + 4 * MIB
    taken = len(scalars) + len(arrays) + len(far)
    anywhere = pl.BlockSpec(memory_space=pl.ANY)

    def body(*refs):
        kernel(*refs[:taken], *refs[taken + len(after) :])

    return pl.pallas_call(
        body,
        out_shape=tuple(pltpu.VMEM(s, d) for s, d in outs) + tuple(jax.ShapeDtypeStruct(s, d) for s, d in results),
        in_specs=[smem() for _ in scalars]
        + [vmem() for _ in arrays]
        + [pl.BlockSpec(memory_space=pltpu.HBM) for _ in far]
        + [anywhere for _ in after],
        out_specs=tuple(vmem() for _ in (*outs, *results)),
        scratch_shapes=[pltpu.VMEM(s, d) for s, d in scratch] + ([pltpu.SemaphoreType.DMA((sems,))] if sems else []),
        compiler_params=pltpu.CompilerParams(vmem_limit_bytes=limit),
        cost_estimate=pl.CostEstimate(flops=COST.get(name, 1000), bytes_accessed=1000, transcendentals=0),
        name=name,
    )(
        *scalars,
        *(pltpu.with_memory_space_constraint(a, pltpu.VMEM) for a in arrays),
        *(pltpu.with_memory_space_constraint(a, pltpu.HBM) for a in far),
        *after,
    )


def local(
    dec_in, enc_out, out_grad, tgt_len, src_len, pair_id,
    self_qkv, self_out, cross_q, cross_kv, cross_out, ff_in, ff_out, norm_gain, norm_bias, lang_table,
):
    micro_count, sent_count, local_len, width = dec_in.shape
    seq_count = lax.axis_size("seq")
    dp_count = lax.axis_size("dp")
    place = lax.axis_index("seq")
    dp_place = lax.axis_index("dp")
    inner = ff_in.shape[1]
    length = local_len * seq_count
    tokens = sent_count * length
    half = width // 2
    mine = jnp.arange(micro_count) == place
    numbers = jnp.concatenate(
        [
            place.reshape(1),
            jnp.sum(jnp.where(mine, pair_id, 0)).reshape(1),
            jnp.sum(jnp.where(mine[:, None], tgt_len, 0), 0),
            jnp.sum(jnp.where(mine[:, None], src_len, 0), 0),
        ]
    ).astype(jnp.int32)
    swap = [(0, 1), (1, 0)]

    dec2 = lax.ppermute(dec_in, "seq", swap)
    enc2 = lax.ppermute(enc_out, "seq", swap)
    og2 = lax.ppermute(out_grad, "seq", swap)

    rows = (sent_count, local_len, width)
    whole = (tokens, width)
    probs = (sent_count * HEADS, length, length)
    sums = (sent_count * HEADS, 1, length)
    turned = (width, tokens)
    kinds = {
        "out_own": (rows, BF), "out_oth": (rows, BF), "send_a": ((2 * width, LANES), BF), "gff_t": (turned, BF),
        "hidden": ((tokens, inner), BF), "slow_t": (turned, BF), "ginner": ((tokens, inner), BF), "gss": (whole, F32),
        "elow": (whole, BF), "qkv": ((tokens, 3 * width), BF), "p_self": (probs, BF), "rl_self": (sums, F32),
        "att_t": (turned, BF), "xhat1": (whole, F32), "rstd1": ((tokens, 128), F32), "flow": (whole, BF),
        "encs": (whole, BF), "cq": (whole, BF), "ckv": ((tokens, 2 * width), BF), "p_cross": (probs, BF),
        "rl_cross": (sums, F32), "crossed_t": (turned, BF), "dnorm": ((8, width), F32),
    }
    params = {
        "qkv": self_qkv, "so": self_out, "cq": cross_q, "ckv": cross_kv, "co": cross_out, "fi": ff_in, "fo": ff_out,
        "gain": norm_gain, "nbias": norm_bias, "table": lang_table,
    }
    kinds.update({"w_" + name: (weight.shape, weight.dtype) for name, weight in params.items()})
    kept = call(
        forward_kernel,
        (numbers,),
        (dec2, enc2, og2),
        [kinds[name] for name in FORWARD_KEPT],
        [kinds["w_" + name] for name in FORWARD_WEIGHTS if name not in PASSED_WEIGHTS]
        + [
            (whole, BF), (whole, BF), (whole, F32), ((4, length, length), F32), (whole, BF), (whole, F32), (whole, BF),
            (whole, F32), ((tokens, 128), F32), (whole, F32), (whole, BF), ((tokens, inner), BF), (whole, BF), (whole, BF),
        ],
        name="forward",
        far=(dec_in, enc_out, out_grad, *(params[name] for name in FORWARD_WEIGHTS)),
        sems=32,
    )
    held = dict(zip(FORWARD_KEPT, kept))

    def of(*names):
        return [held[name] for name in names]

    def flips(core_zero, core_one):
        return [(2 * d, 2 * (d ^ core_zero)) for d in range(dp_count)] + [
            (2 * d + 1, 2 * (d ^ core_one) + 1) for d in range(dp_count)
        ]

    def travel(array, core_zero, core_one):
        return lax.ppermute(array, ("dp", "seq"), flips(core_zero, core_one))

    last = []

    def go_on(*groups):
        result = None
        for group in groups:
            result = next(group)
        return result

    def reduce_all(keep, send, outs, unpack, route, tail=0):
        def run(kernel, scalars, arrays, outs, name, results=()):
            got = call(kernel, scalars, arrays, outs, name=name, results=results, after=tuple(last))
            last[:] = [got[0]]
            return got

        rows, lanes = keep.shape
        body = rows - tail
        got = lax.ppermute(send, "seq", swap)
        if dp_count != 16:
            (total,) = run(add_all_kernel, (), (keep, got), [((rows, lanes), BF)], "add_core")
            total = lax.psum(total, "dp")
            mine, other, rest = total[: body // 2], total[body // 2 : body], total[body:]
            bit = jnp.zeros((1,), jnp.int32)
            for _ in range(2 * len(route)):
                yield
        else:
            bits = [
                (jnp.where(place == 0, dp_place & zero, dp_place & one) != 0).astype(jnp.int32).reshape(1)
                for zero, one in route
            ]
            held = body
            for bit, flip in zip(bits, route):
                held //= 2
                shape = (held + tail, lanes)
                send, keep = run(functools.partial(add_split_kernel, tail), (bit,), (keep, got), [(shape, BF)] * 2, "add_split")
                got = travel(send, *flip)
                yield
            (mine,) = run(add_all_kernel, (), (keep, got), [(shape, BF)], "add_last")
            mine, rest = mine[:held], mine[held:]
            for bit, flip in zip(bits[:0:-1], route[:0:-1]):
                other = travel(mine, *flip)
                yield
                held *= 2
                (mine,) = run(join_kernel, (bit,), (mine, other), [((held, lanes), BF)], "join")
            other = travel(mine, *route[0])
            bit = bits[0]
            yield
        unpacked = run(
            functools.partial(unpack_kernel, unpack), (bit,), (mine, other), [], "unpack", [(s, F32) for s in outs]
        )
        yield unpacked, rest

    groups = {}

    def go_through(letters):
        go_on(*(groups[letter] for letter in letters))

    (keep_a,) = call(
        feed_keep_kernel,
        (numbers,),
        of("gff_t", "hidden", "slow_t", "ginner"),
        [((2 * width, LANES), BF)],
        name="feed_keep",
    )
    groups["a"] = reduce_all(keep_a, held["send_a"], [(width, inner // 2), (inner, half)], unpack_ff, ROUTES[0])
    branch, gq_t, gkv_t, gfs, dnorm = call(
        cross_kernel,
        (),
        of("gss", "dnorm", "w_gain", "w_co", "w_cq", "ckv", "cq", "p_cross", "rl_cross", "crossed_t", "xhat1", "rstd1"),
        [(whole, BF), (turned, BF), ((2 * width, tokens), BF), (whole, F32), ((8, width), F32)],
        [(turned, BF)],
        name="cross",
        after=[keep_a],
    )
    go_through(ORDER[0])
    buffer = ((width, LANES), BF)
    send_b, keep_b, genc_own, genc_oth = call(
        cross_grads_kernel,
        (numbers,),
        [branch, gq_t, gkv_t, *of("crossed_t", "flow", "encs", "w_ckv")],
        [buffer, buffer, (rows, BF), (rows, BF)],
        [(whole, BF)],
        name="cross_grads",
        after=last,
    )
    groups["b"] = reduce_all(
        keep_b, send_b, [(width, width), (width, half), (width, half)], unpack_cross, ROUTES[1]
    )
    go_through(ORDER[1])
    branch, gqkv_t = call(
        self_kernel,
        (),
        [gfs, *of("w_so", "qkv", "p_self", "rl_self", "att_t")],
        [(whole, BF), ((3 * width, tokens), BF)],
        [(turned, BF)],
        name="self",
        after=last,
    )
    go_through(ORDER[2])
    buffer = ((width + 16, LANES), BF)
    send_c, keep_c, gin_own, gin_oth = call(
        self_grads_kernel,
        (numbers,),
        [gfs, dnorm, branch, gqkv_t, *of("att_t", "elow", "w_qkv")],
        [buffer, buffer, (rows, BF), (rows, BF)],
        [(whole, BF), ((16, width), F32)],
        name="self_grads",
        after=last,
    )
    groups["c"] = reduce_all(
        keep_c, send_c, [(width, 3 * half), (width, half)], unpack_self, ROUTES[2], tail=16
    )
    last[:] = [send_c]
    go_through(ORDER[3])
    (g_ff_in, g_ff_out), _ = go_on(groups["a"])
    (g_cross_kv, g_cross_q, g_cross_out), _ = go_on(groups["b"])
    (g_qkv, g_self_out), tot_s = go_on(groups["c"])
    tot_s = tot_s[:, :half].astype(F32)
    def both(own, other):
        got = lax.ppermute(other, "seq", swap)
        return jnp.where(place == 0, jnp.stack([own, got]), jnp.stack([got, own]))

    output = both(*of("out_own", "out_oth"))
    grad_encoder = both(genc_own, genc_oth)
    grad_input = both(gin_own, gin_oth)

    return (
        output,
        grad_input,
        grad_encoder,
        g_qkv,
        g_self_out,
        g_cross_q,
        g_cross_kv,
        g_cross_out,
        g_ff_in,
        g_ff_out,
        tot_s[0:3],
        tot_s[3:6],
        tot_s[8:16],
    )


def solution(mesh):
    acts = P(None, "dp", "seq", None)
    lens = P(None, "dp")
    cut = P(None, "seq")
    return jax.shard_map(
        local,
        mesh=mesh,
        in_specs=(acts, acts, acts, lens, lens) + (P(),) * 11,
        out_specs=(acts, acts, acts) + (cut,) * 10,
        check_vma=False,
    )
```

time: 209 us -> 148 us (0.71)
  Pallas kernels: 78.4 us -> 49.1 us
  starting transfers between devices: 52.8 us -> 33.4 us
  waiting for transfers between devices: 55.5 us -> 43.9 us
  local copies, waits for them, and re-layouts: 17.9 us -> 14.7 us
  other arithmetic: 2.61 us -> 5.4 us
    pallas_call x24 -> x33, Pallas kernels: 78.4 us -> 49.1 us  [call(): pl.pallas_call(body, out_shape=tuple((pltpu.VMEM(s, d) for s, d in outs))...]
    ppermute x30 -> x24, starting transfers between devices: 50.7 us -> 31.6 us  [travel(): return lax.ppermute(array, ('dp', 'seq'), flips(core_zero, core_one))]
    ppermute x30 -> x24, waiting for transfers between devices: 48.8 us -> 43.8 us  [travel(): return lax.ppermute(array, ('dp', 'seq'), flips(core_zero, core_one))]
    ppermute x3, waiting for transfers between devices: 4 us -> 0.01 us  [reduce_all(): got = lax.ppermute(send, 'seq', swap)]
    unnamed x78 -> x48, local copies, waits for them, and re-layouts: 16.7 us -> 13.5 us
  transfers between devices with their start and end apart: 39 -> 33, of which waited for: 20 -> 14; matrix products, arithmetic and copies ran while one was open for 2% -> 4% of each run, Pallas kernels for 16% -> 17%
where the time goes in v2:
time: 148 us; the launch traced here: 147 us
  Pallas kernels  49.1 us (33%)
  waiting for transfers between devices  43.9 us (30%)
  starting transfers between devices  33.4 us (23%)
  local copies, waits for them, and re-layouts  14.7 us (10%)
  other arithmetic  5.4 us (4%)
    pallas_call x33, Pallas kernels, call(): pl.pallas_call(body, out_shape=tuple((pltpu.VMEM(s, d) for s, d in outs))...  49.1 us
    ppermute x24, waiting for transfers between devices, travel(): return lax.ppermute(array, ('dp', 'seq'), flips(core_zero, core_one))  43.8 us
    ppermute x24, starting transfers between devices, travel(): return lax.ppermute(array, ('dp', 'seq'), flips(core_zero, core_one))  31.6 us
    unnamed x48, local copies, waits for them, and re-layouts  13.5 us
  transfers between devices with their start and end apart: 33, of which 14 were waited for; matrix products, arithmetic and copies ran while one was open for 4% of the time, Pallas kernels for 17%

profile of v2, /device:TPU:0, one launch (start us, length us, event | category | flops | bytes accessed | tf_op | source)
XLA Modules:
  0.0 147.5 jit_solution(16338724495901668211)
XLA Ops:
  1.7 1.3 select_reduce_fusion.2
  3.0 0.8 select_reduce_fusion.1
  3.8 0.7 pad_add_fusion.refs_0_
  4.5 19.3 %forward.1 = (bf16[2,128,512]{2,1,0:T(8,128)(2,1)S(1)}, bf16[2,128,512]{2,1,0:T(8,128)(2,1)S(1)}, bf16[1024,1024]{1,0:T(8,128)(2,1)}, bf16[512,512]{1,0:T(8,128)...) custom-call(s32[6]{0:T(128)S(1)} %pad_add_fusion.refs_0_, ...), custom_call_target="tpu_custom_call" | custom-call | flops 99999997952 | bytes 1000 | tf_op jit(solution)/shard_map/forward/pallas_call | solution.py:656
  24.0 1.8 %feed_keep.1.refs_12_.refs_1_ = bf16[1024,1024]{1,0:T(8,128)(2,1)S(1)} custom-call(s32[6]{0:T(128)S(1)} %pad_add_fusion.refs_0_, bf16[512,512]{1,0:T(8,128)(2,1)S(1)} %get-tuple-element.102.refs_1_, bf16[512,2048]{1,0:T(8,128)(2,1)S(1)} %get-tuple-element.103.refs_2_, bf16[512,512]{1,0:T(8,128)(2,1)S(1)} %get-tuple-element.104.refs_3_, ...), custom_call_target="tpu_custom_call" | custom-call | flops 99999997952 | bytes 1000 | tf_op jit(solution)/shard_map/feed_keep/pallas_call | solution.py:656
  25.9 3.5 %cross.1 = (bf16[512,512]{1,0:T(8,128)(2,1)S(1)}, bf16[512,512]{1,0:T(8,128)(2,1)S(1)}, bf16[1024,512]{1,0:T(8,128)(2,1)S(1)}, f32[512,512]{1,0:T(8,128)S(1)}, f32[8,512]{1,0:T(8,128)S(1)}) custom-call(f32[512,512]{1,0:T(8,128)S(1)} %get-tuple-element.90.refs_0_, f32[8,512]{1,0:T(8,128)S(1)} %get-tuple-element.91.refs_1_, ...), custom_call_target="tpu_custom_call" | custom-call | flops 99999997952 | bytes 1000 | tf_op jit(solution)/shard_map/cross/pallas_call | solution.py:656
  29.3 3.0 %add_split.12 = (bf16[512,1024]{1,0:T(8,128)(2,1)}, bf16[512,1024]{1,0:T(8,128)(2,1)S(1)}) custom-call(s32[1]{0:T(128)} %bitcast.4.refs_0_, bf16[1024,1024]{1,0:T(8,128)(2,1)S(1)} %feed_keep.1.refs_12_.refs_1_, bf16[1024,1024]{1,0:T(8,128)(2,1)} %collective-permute-done.4.refs_2_), custom_call_target="tpu_custom_call" | custom-call | flops 1000 | bytes 1000 | tf_op jit(solution)/shard_map/add_split/pallas_call | solution.py:656
  32.3 1.0 copy-done.2
  33.3 2.8 %collective-permute-start.10 = (bf16[512,1024]{1,0:T(8,128)(2,1)}, bf16[512,1024]{1,0:T(8,128)(2,1)}, u32[]{:S(2)}, u32[]{:S(2)}) collective-permute-start(bf16[512,1024]{1,0:T(8,128)(2,1)} %get-tuple-element.114.refs_6_.refs_8_.refs_3_), channel_id=1, source_target_pairs={{0,2},{2,0},{4,6},{6,4},{8,10},{10,8},{12,14},{14,12},{16,18},{18,... | collective-permute-start | bytes 3145736 | tf_op jit(solution)/shard_map/ppermute | solution.py:747
  36.1 2.4 %cross_grads.1 = (bf16[512,1024]{1,0:T(8,128)(2,1)S(1)}, bf16[512,1024]{1,0:T(8,128)(2,1)S(1)}, bf16[2,128,512]{2,1,0:T(8,128)(2,1)S(1)}, bf16[2,128,512]{2,1,0:T(8,128)(2,1)S(1)}) custom-call(s32[6]{0:T(128)S(1)} %pad_add_fusion.refs_0_, bf16[512,512]{1,0:T(8,128)(2,1)S(1)} %get-tuple-element.119.refs_1_, bf16[512,512]{1,0:T(8,128)(2,1)S(1)} %get-tuple-element.120.refs_2_, ...), custom_call_target="tpu_custom_call" | custom-call | flops 99999997952 | bytes 1000 | tf_op jit(solution)/shard_map/cross_grads/pallas_call | solution.py:656
  38.5 0.7 copy-done.10
  39.2 0.7 copy-done.20
  39.9 2.8 %self.1 = (bf16[512,512]{1,0:T(8,128)(2,1)S(1)}, bf16[1536,512]{1,0:T(8,128)(2,1)S(1)}) custom-call(f32[512,512]{1,0:T(8,128)S(1)} %get-tuple-element.106.refs_0_.refs_1_, bf16[512,512]{1,0:T(8,128)(2,1)S(1)} %get-tuple-element.108.refs_1_, bf16[512,1536]{1,0:T(8,128)(2,1)S(1)} %get-tuple-element.109.refs_2_, ...), custom_call_target="tpu_custom_call" | custom-call | flops 99999997952 | bytes 1000 | tf_op jit(solution)/shard_map/self/pallas_call | solution.py:656
  42.7 1.0 add_split.13
  43.7 0.8 copy-done.6
  44.5 2.9 %self_grads.1 = (bf16[528,1024]{1,0:T(8,128)(2,1)S(1)}, bf16[528,1024]{1,0:T(8,128)(2,1)S(1)}, bf16[2,128,512]{2,1,0:T(8,128)(2,1)S(1)}, bf16[2,128,512]{2,1,0:T(8,128)(2,1)S(1)}) custom-call(s32[6]{0:T(128)S(1)} %pad_add_fusion.refs_0_, f32[512,512]{1,0:T(8,128)S(1)} %get-tuple-element.106.refs_0_.refs_1_, f32[8,512]{1,0:T(8,128)S(1)} %get-tuple-element.107.refs_2_, ...), custom_call_target="tpu_custom_call" | custom-call | flops 99999997952 | bytes 1000 | tf_op jit(solution)/shard_map/self_grads/pallas_call | solution.py:656
  47.4 0.7 copy-done.12
  48.1 0.7 copy-done.22
  49.3 0.9 collective-permute-start.9
  50.2 1.2 copy-done.3
  51.5 2.2 %add_split.14 = (bf16[256,1024]{1,0:T(8,128)(2,1)}, bf16[256,1024]{1,0:T(8,128)(2,1)S(1)}) custom-call(s32[1]{0:T(128)} %bitcast.9.refs_0_, bf16[512,1024]{1,0:T(8,128)(2,1)S(1)} %copy-done.3, bf16[512,1024]{1,0:T(8,128)(2,1)} %collective-permute-done.10.refs_2_, bf16[528,1024]{1,0:T(8,128)(2,1)S(1)} %get-tuple-element.133.refs_3_), custom_call_target="tpu_custom_call" | custom-call | flops 1000 | bytes 1000 | tf_op jit(solution)/shard_map/add_split/pallas_call | solution.py:656
  53.7 1.1 collective-permute-start.13
  54.8 5.8 %collective-permute-done.9.refs_2_ = bf16[256,1024]{1,0:T(8,128)(2,1)} collective-permute-done((bf16[256,1024]{1,0:T(8,128)(2,1)}, bf16[256,1024]{1,0:T(8,128)(2,1)}, u32[]{:S(2)}, u32[]{:S(2)}) %collective-permute-start.9) | collective-permute-done | bytes 524320 | tf_op jit(solution)/shard_map/ppermute | solution.py:747
  60.6 1.8 %add_split.15 = (bf16[128,1024]{1,0:T(8,128)(2,1)}, bf16[128,1024]{1,0:T(8,128)(2,1)S(1)}) custom-call(s32[1]{0:T(128)} %bitcast.9.refs_0_, bf16[256,1024]{1,0:T(8,128)(2,1)S(1)} %copy-done.7, bf16[256,1024]{1,0:T(8,128)(2,1)} %collective-permute-done.9.refs_2_, bf16[256,1024]{1,0:T(8,128)(2,1)} %get-tuple-element.136.refs_3_), custom_call_target="tpu_custom_call" | custom-call | flops 1000 | bytes 1000 | tf_op jit(solution)/shard_map/add_split/pallas_call | solution.py:656
  62.4 0.7 copy-done.14
  63.4 0.8 copy-done.4
  64.2 1.3 collective-permute-start.11
  65.5 1.2 collective-permute-start.12
  66.7 1.0 copy-done.9
  67.8 1.2 add_split.17
  68.9 1.6 %collective-permute-start.16 = (bf16[128,1024]{1,0:T(8,128)(2,1)S(1)}, bf16[128,1024]{1,0:T(8,128)(2,1)S(1)}, u32[]{:S(2)}, u32[]{:S(2)}) collective-permute-start(bf16[128,1024]{1,0:T(8,128)(2,1)S(1)} %get-tuple-element.142.refs_3_), channel_id=1, source_target_pairs={{0,8},{2,10},{4,12},{6,14},{8,0},{10,2},{12,4},{14,6},{16,24},{18,... | collective-permute-start | bytes 786440 | tf_op jit(solution)/shard_map/ppermute | solution.py:747
  70.6 2.7 %collective-permute-done.12.refs_2_ = bf16[128,1024]{1,0:T(8,128)(2,1)S(1)} collective-permute-done((bf16[128,1024]{1,0:T(8,128)(2,1)}, bf16[128,1024]{1,0:T(8,128)(2,1)S(1)}, u32[]{:S(2)}, u32[]{:S(2)}) %collective-permute-start.12) | collective-permute-done | bytes 262176 | tf_op jit(solution)/shard_map/ppermute | solution.py:747
  73.2 0.9 copy-done.15
  75.5 1.7 %collective-permute-start.14 = (bf16[144,1024]{1,0:T(8,128)(2,1)S(1)}, bf16[144,1024]{1,0:T(8,128)(2,1)S(1)}, u32[]{:S(2)}, u32[]{:S(2)}) collective-permute-start(bf16[144,1024]{1,0:T(8,128)(2,1)S(1)} %get-tuple-element.145.refs_3_), channel_id=1, source_target_pairs={{0,4},{2,6},{4,0},{6,2},{8,12},{10,14},{12,8},{14,10},{16,20},{18,... | collective-permute-start | bytes 884744 | tf_op jit(solution)/shard_map/ppermute | solution.py:747
  77.3 1.6 %collective-permute-start.15 = (bf16[64,1024]{1,0:T(8,128)(2,1)}, bf16[64,1024]{1,0:T(8,128)(2,1)S(1)}, u32[]{:S(2)}, u32[]{:S(2)}) collective-permute-start(bf16[64,1024]{1,0:T(8,128)(2,1)} %get-tuple-element.143.refs_3_), channel_id=1, source_target_pairs={{0,8},{2,10},{4,12},{6,14},{8,0},{10,2},{12,4},{14,6},{16,24},{18,... | collective-permute-start | bytes 393224 | tf_op jit(solution)/shard_map/ppermute | solution.py:747
  78.9 2.7 %collective-permute-start.19 = (bf16[64,1024]{1,0:T(8,128)(2,1)S(1)}, bf16[64,1024]{1,0:T(8,128)(2,1)S(1)}, u32[]{:S(2)}, u32[]{:S(2)}) collective-permute-start(bf16[64,1024]{1,0:T(8,128)(2,1)S(1)} %get-tuple-element.148.refs_3_), channel_id=1, source_target_pairs={{0,16},{2,18},{4,20},{6,22},{8,24},{10,26},{12,28},{14,30},{16,0},... | collective-permute-start | bytes 393224 | tf_op jit(solution)/shard_map/ppermute | solution.py:747
  81.6 3.5 %collective-permute-done.15.refs_2_ = bf16[64,1024]{1,0:T(8,128)(2,1)S(1)} collective-permute-done((bf16[64,1024]{1,0:T(8,128)(2,1)}, bf16[64,1024]{1,0:T(8,128)(2,1)S(1)}, u32[]{:S(2)}, u32[]{:S(2)}) %collective-permute-start.15) | collective-permute-done | bytes 131104 | tf_op jit(solution)/shard_map/ppermute | solution.py:747
  85.1 0.9 copy-done.17
  86.4 2.9 %collective-permute-start.22 = (bf16[64,1024]{1,0:T(8,128)(2,1)S(1)}, bf16[64,1024]{1,0:T(8,128)(2,1)S(1)}, u32[]{:S(2)}, u32[]{:S(2)}) collective-permute-start(bf16[64,1024]{1,0:T(8,128)(2,1)S(1)} %add_last.3.refs_2_.refs_1_), channel_id=1, source_target_pairs={{0,16},{2,18},{4,20},{6,22},{8,24},{10,26},{12,28},{14,30},{16,0},... | collective-permute-start | bytes 393224 | tf_op jit(solution)/shard_map/ppermute | solution.py:747
  89.4 6.5 %collective-permute-done.18.refs_1_ = bf16[32,1024]{1,0:T(8,128)(2,1)S(1)} collective-permute-done((bf16[32,1024]{1,0:T(8,128)(2,1)S(1)}, bf16[32,1024]{1,0:T(8,128)(2,1)S(1)}, u32[]{:S(2)}, u32[]{:S(2)}) %collective-permute-start.18) | collective-permute-done | bytes 65568 | tf_op jit(solution)/shard_map/ppermute | solution.py:747
  96.2 2.8 %collective-permute-start.20 = (bf16[48,1024]{1,0:T(8,128)(2,1)S(1)}, bf16[48,1024]{1,0:T(8,128)(2,1)S(1)}, u32[]{:S(2)}, u32[]{:S(2)}) collective-permute-start(bf16[48,1024]{1,0:T(8,128)(2,1)S(1)} %get-tuple-element.155.refs_3_), channel_id=1, source_target_pairs={{0,16},{2,18},{4,20},{6,22},{8,24},{10,26},{12,28},{14,30},{16,0},... | collective-permute-start | bytes 294920 | tf_op jit(solution)/shard_map/ppermute | solution.py:747
  99.1 5.4 %collective-permute-done.21.refs_2_ = bf16[32,1024]{1,0:T(8,128)(2,1)S(1)} collective-permute-done((bf16[32,1024]{1,0:T(8,128)(2,1)S(1)}, bf16[32,1024]{1,0:T(8,128)(2,1)S(1)}, u32[]{:S(2)}, u32[]{:S(2)}) %collective-permute-start.21) | collective-permute-done | bytes 65568 | tf_op jit(solution)/shard_map/ppermute | solution.py:747
  104.6 1.7 %collective-permute-done.25.refs_2_ = bf16[128,1024]{1,0:T(8,128)(2,1)S(1)} collective-permute-done((bf16[128,1024]{1,0:T(8,128)(2,1)S(1)}, bf16[128,1024]{1,0:T(8,128)(2,1)S(1)}, u32[]{:S(2)}, u32[]{:S(2)}) %collective-permute-start.25) | collective-permute-done | bytes 262176 | tf_op jit(solution)/shard_map/ppermute | solution.py:747
  106.5 1.6 %collective-permute-start.24 = (bf16[64,1024]{1,0:T(8,128)(2,1)S(1)}, bf16[64,1024]{1,0:T(8,128)(2,1)S(1)}, u32[]{:S(2)}, u32[]{:S(2)}) collective-permute-start(bf16[64,1024]{1,0:T(8,128)(2,1)S(1)} %join.10.refs_2_.refs_1_), channel_id=1, source_target_pairs={{0,8},{2,10},{4,12},{6,14},{8,0},{10,2},{12,4},{14,6},{16,24},{18,... | collective-permute-start | bytes 393224 | tf_op jit(solution)/shard_map/ppermute | solution.py:747
  108.1 1.2 collective-permute-start.23
  109.3 2.2 %collective-permute-done.24.refs_2_ = bf16[64,1024]{1,0:T(8,128)(2,1)S(1)} collective-permute-done((bf16[64,1024]{1,0:T(8,128)(2,1)S(1)}, bf16[64,1024]{1,0:T(8,128)(2,1)S(1)}, u32[]{:S(2)}, u32[]{:S(2)}) %collective-permute-start.24) | collective-permute-done | bytes 131104 | tf_op jit(solution)/shard_map/ppermute | solution.py:747
  111.6 2.0 %collective-permute-start.27 = (bf16[128,1024]{1,0:T(8,128)(2,1)S(1)}, bf16[128,1024]{1,0:T(8,128)(2,1)S(1)}, u32[]{:S(2)}, u32[]{:S(2)}) collective-permute-start(bf16[128,1024]{1,0:T(8,128)(2,1)S(1)} %join.12.refs_3_.refs_1_), channel_id=1, source_target_pairs={{0,4},{2,6},{4,0},{6,2},{8,12},{10,14},{12,8},{14,10},{16,20},{18,... | collective-permute-start | bytes 786440 | tf_op jit(solution)/shard_map/ppermute | solution.py:747
  113.9 1.8 %collective-permute-done.28.refs_2_ = bf16[256,1024]{1,0:T(8,128)(2,1)S(1)} collective-permute-done((bf16[256,1024]{1,0:T(8,128)(2,1)S(1)}, bf16[256,1024]{1,0:T(8,128)(2,1)S(1)}, u32[]{:S(2)}, u32[]{:S(2)}) %collective-permute-start.28) | collective-permute-done | bytes 524320 | tf_op jit(solution)/shard_map/ppermute | solution.py:747
  115.8 1.8 %collective-permute-start.32 = (bf16[512,1024]{1,0:T(8,128)(2,1)S(1)}, bf16[512,1024]{1,0:T(8,128)(2,1)S(1)}, u32[]{:S(2)}, u32[]{:S(2)}) collective-permute-start(bf16[512,1024]{1,0:T(8,128)(2,1)S(1)} %join.14.refs_3_.refs_1_), channel_id=1, source_target_pairs={{0,2},{2,0},{4,6},{6,4},{8,10},{10,8},{12,14},{14,12},{16,18},{18,... | collective-permute-start | bytes 3145736 | tf_op jit(solution)/shard_map/ppermute | solution.py:747
  117.6 2.6 %collective-permute-done.27.refs_2_ = bf16[128,1024]{1,0:T(8,128)(2,1)S(1)} collective-permute-done((bf16[128,1024]{1,0:T(8,128)(2,1)S(1)}, bf16[128,1024]{1,0:T(8,128)(2,1)S(1)}, u32[]{:S(2)}, u32[]{:S(2)}) %collective-permute-start.27) | collective-permute-done | bytes 262176 | tf_op jit(solution)/shard_map/ppermute | solution.py:747
  120.3 2.2 %collective-permute-done.26.refs_2_ = bf16[64,1024]{1,0:T(8,128)(2,1)S(1)} collective-permute-done((bf16[64,1024]{1,0:T(8,128)(2,1)S(1)}, bf16[64,1024]{1,0:T(8,128)(2,1)S(1)}, u32[]{:S(2)}, u32[]{:S(2)}) %collective-permute-start.26) | collective-permute-done | bytes 131104 | tf_op jit(solution)/shard_map/ppermute | solution.py:747
  122.9 0.9 maximum_select_fusion
  123.8 0.9 maximum_select_fusion.2
  124.7 2.4 %collective-permute-start.31 = (bf16[256,1024]{1,0:T(8,128)(2,1)S(1)}, bf16[256,1024]{1,0:T(8,128)(2,1)S(1)}, u32[]{:S(2)}, u32[]{:S(2)}) collective-permute-start(bf16[256,1024]{1,0:T(8,128)(2,1)S(1)} %join.15.refs_3_.refs_1_), channel_id=1, source_target_pairs={{0,2},{2,0},{4,6},{6,4},{8,10},{10,8},{12,14},{14,12},{16,18},{18,... | collective-permute-start | bytes 1572872 | tf_op jit(solution)/shard_map/ppermute | solution.py:747
  127.1 4.8 %collective-permute-done.29.refs_2_ = bf16[128,1024]{1,0:T(8,128)(2,1)S(1)} collective-permute-done((bf16[128,1024]{1,0:T(8,128)(2,1)S(1)}, bf16[128,1024]{1,0:T(8,128)(2,1)S(1)}, u32[]{:S(2)}, u32[]{:S(2)}) %collective-permute-start.29) | collective-permute-done | bytes 262176 | tf_op jit(solution)/shard_map/ppermute | solution.py:747
  131.9 0.8 collective-permute-start.30
  132.6 0.9 maximum_select_fusion.1
  134.7 2.4 %unpack.3 = (f32[512,1024]{1,0:T(8,128)}, f32[2048,256]{1,0:T(8,128)}) custom-call(s32[1]{0:T(128)} %bitcast.4.refs_0_, bf16[512,1024]{1,0:T(8,128)(2,1)S(1)} %join.14.refs_3_.refs_1_, bf16[512,1024]{1,0:T(8,128)(2,1)S(1)} %collective-permute-done.32.refs_2_, bf16[256,1024]{1,0:T(8,128)(2,1)S(1)} %join.17.refs_3_.refs_1_), custom_call_target="tpu_custom_call" | custom-call | flops 1000 | bytes 1000 | tf_op jit(solution)/shard_map/unpack/pallas_call | solution.py:656
  137.2 1.9 %collective-permute-done.31.refs_2_ = bf16[256,1024]{1,0:T(8,128)(2,1)S(1)} collective-permute-done((bf16[256,1024]{1,0:T(8,128)(2,1)S(1)}, bf16[256,1024]{1,0:T(8,128)(2,1)S(1)}, u32[]{:S(2)}, u32[]{:S(2)}) %collective-permute-start.31) | collective-permute-done | bytes 524320 | tf_op jit(solution)/shard_map/ppermute | solution.py:747
  139.1 1.6 %copy-done = f32[512,1024]{1,0:T(8,128)S(1)} copy-done((f32[512,1024]{1,0:T(8,128)S(1)}, f32[512,1024]{1,0:T(8,128)}, u32[]{:S(2)}) %copy-start) | copy-done | bytes 2097176
  140.6 1.6 %unpack.4 = (f32[512,512]{1,0:T(8,128)}, f32[512,256]{1,0:T(8,128)}, f32[512,256]{1,0:T(8,128)}) custom-call(s32[1]{0:T(128)} %bitcast.4.refs_0_, bf16[256,1024]{1,0:T(8,128)(2,1)S(1)} %join.15.refs_3_.refs_1_, bf16[256,1024]{1,0:T(8,128)(2,1)S(1)} %collective-permute-done.31.refs_2_, f32[512,1024]{1,0:T(8,128)S(1)} %copy-done), custom_call_target="tpu_custom_call" | custom-call | flops 1000 | bytes 1000 | tf_op jit(solution)/shard_map/unpack/pallas_call | solution.py:656
  142.2 2.4 %collective-permute-done.30.refs_2_ = bf16[256,1024]{1,0:T(8,128)(2,1)S(1)} collective-permute-done((bf16[256,1024]{1,0:T(8,128)(2,1)S(1)}, bf16[256,1024]{1,0:T(8,128)(2,1)S(1)}, u32[]{:S(2)}, u32[]{:S(2)}) %collective-permute-start.30) | collective-permute-done | bytes 524320 | tf_op jit(solution)/shard_map/ppermute | solution.py:747
  144.7 1.2 copy-done.1
  145.9 1.6 %unpack.5 = (f32[512,768]{1,0:T(8,128)}, f32[512,256]{1,0:T(8,128)}) custom-call(s32[1]{0:T(128)} %bitcast.4.refs_0_, bf16[256,1024]{1,0:T(8,128)(2,1)S(1)} %join.17.refs_3_.refs_1_, bf16[256,1024]{1,0:T(8,128)(2,1)S(1)} %collective-permute-done.30.refs_2_, f32[512,512]{1,0:T(8,128)S(1)} %copy-done.1), custom_call_target="tpu_custom_call" | custom-call | flops 1000 | bytes 1000 | tf_op jit(solution)/shard_map/unpack/pallas_call | solution.py:656
  (94 shorter events, 6.8 us)
Async XLA Ops:
  0.6 3.8 %collective-permute-start = (bf16[2,2,128,512]{3,2,1,0:T(8,128)(2,1)}, bf16[2,2,128,512]{3,2,1,0:T(8,128)(2,1)S(1)}, u32[]{:S(2)}, u32[]{:S(2)}) collective-permute-start(bf16[2,2,128,512]{3,2,1,0:T(8,128)(2,1)} %refs_4_.1), channel_id=1, source_target_pairs={{0,1},{1,0},{2,3},{3,2},{4,5},{5,4},{6,7},{7,6},{8,9},{9,8},{10,11... | collective-permute-start | bytes 1572872 | tf_op jit(solution)/shard_map/ppermute | solution.py:700
  1.2 3.3 %collective-permute-start.1 = (bf16[2,2,128,512]{3,2,1,0:T(8,128)(2,1)}, bf16[2,2,128,512]{3,2,1,0:T(8,128)(2,1)S(1)}, u32[]{:S(2)}, u32[]{:S(2)}) collective-permute-start(bf16[2,2,128,512]{3,2,1,0:T(8,128)(2,1)} %refs_5_.1), channel_id=1, source_target_pairs={{0,1},{1,0},{2,3},{3,2},{4,5},{5,4},{6,7},{7,6},{8,9},{9,8},{10,11... | collective-permute-start | bytes 1572872 | tf_op jit(solution)/shard_map/ppermute | solution.py:701
  1.2 3.2 %collective-permute-start.2 = (bf16[2,2,128,512]{3,2,1,0:T(8,128)(2,1)}, bf16[2,2,128,512]{3,2,1,0:T(8,128)(2,1)S(1)}, u32[]{:S(2)}, u32[]{:S(2)}) collective-permute-start(bf16[2,2,128,512]{3,2,1,0:T(8,128)(2,1)} %refs_6_.1), channel_id=1, source_target_pairs={{0,1},{1,0},{2,3},{3,2},{4,5},{5,4},{6,7},{7,6},{8,9},{9,8},{10,11... | collective-permute-start | bytes 1572872 | tf_op jit(solution)/shard_map/ppermute | solution.py:702
  23.8 2.1 %copy-start.18 = (bf16[2,128,512]{2,1,0:T(8,128)(2,1)}, bf16[2,128,512]{2,1,0:T(8,128)(2,1)S(1)}, u32[]{:S(2)}) copy-start(bf16[2,128,512]{2,1,0:T(8,128)(2,1)S(1)} %get-tuple-element.89) | copy-start | bytes 786436
  23.8 5.5 %collective-permute-start.4 = (bf16[1024,1024]{1,0:T(8,128)(2,1)}, bf16[1024,1024]{1,0:T(8,128)(2,1)}, u32[]{:S(2)}, u32[]{:S(2)}) collective-permute-start(bf16[1024,1024]{1,0:T(8,128)(2,1)} %get-tuple-element.113), channel_id=1, source_target_pairs={{0,1},{1,0},{2,3},{3,2},{4,5},{5,4},{6,7},{7,6},{8,9},{9,8},{10,11... | collective-permute-start | bytes 6291464 | tf_op jit(solution)/shard_map/ppermute | solution.py:765
  32.3 1.0 copy-start.2
  33.3 17.0 %collective-permute-start.10 = (bf16[512,1024]{1,0:T(8,128)(2,1)}, bf16[512,1024]{1,0:T(8,128)(2,1)}, u32[]{:S(2)}, u32[]{:S(2)}) collective-permute-start(bf16[512,1024]{1,0:T(8,128)(2,1)} %get-tuple-element.114.refs_6_.refs_8_.refs_3_), channel_id=1, source_target_pairs={{0,2},{2,0},{4,6},{6,4},{8,10},{10,8},{12,14},{14,12},{16,18},{18,... | collective-permute-start | bytes 3145736 | tf_op jit(solution)/shard_map/ppermute | solution.py:747
  38.5 0.7 copy-start.10
  39.2 0.7 copy-start.20
  39.9 2.8 %collective-permute-start.5 = (bf16[512,1024]{1,0:T(8,128)(2,1)S(1)}, bf16[512,1024]{1,0:T(8,128)(2,1)S(1)}, u32[]{:S(2)}, u32[]{:S(2)}) collective-permute-start(bf16[512,1024]{1,0:T(8,128)(2,1)S(1)} %get-tuple-element.126), channel_id=1, source_target_pairs={{0,1},{1,0},{2,3},{3,2},{4,5},{5,4},{6,7},{7,6},{8,9},{9,8},{10,11... | collective-permute-start | bytes 3145736 | tf_op jit(solution)/shard_map/ppermute | solution.py:765
  43.7 0.8 copy-start.6
  47.4 0.7 copy-start.12
  48.1 0.7 copy-start.22
  48.8 14.3 %collective-permute-start.8 = (bf16[528,1024]{1,0:T(8,128)(2,1)S(1)}, bf16[528,1024]{1,0:T(8,128)(2,1)S(1)}, u32[]{:S(2)}, u32[]{:S(2)}) collective-permute-start(bf16[528,1024]{1,0:T(8,128)(2,1)S(1)} %get-tuple-element.133.refs_3_), channel_id=1, source_target_pairs={{0,1},{1,0},{2,3},{3,2},{4,5},{5,4},{6,7},{7,6},{8,9},{9,8},{10,11... | collective-permute-start | bytes 3244040 | tf_op jit(solution)/shard_map/ppermute | solution.py:765
  49.3 11.3 %collective-permute-start.9 = (bf16[256,1024]{1,0:T(8,128)(2,1)}, bf16[256,1024]{1,0:T(8,128)(2,1)}, u32[]{:S(2)}, u32[]{:S(2)}) collective-permute-start(bf16[256,1024]{1,0:T(8,128)(2,1)} %get-tuple-element.127.refs_8_), channel_id=1, source_target_pairs={{0,2},{2,0},{4,6},{6,4},{8,10},{10,8},{12,14},{14,12},{16,18},{18,... | collective-permute-start | bytes 1572872 | tf_op jit(solution)/shard_map/ppermute | solution.py:747
  50.2 1.2 copy-start.3
  51.5 9.2 %copy-start.7 = (bf16[256,1024]{1,0:T(8,128)(2,1)S(1)}, bf16[256,1024]{1,0:T(8,128)(2,1)}, u32[]{:S(2)}) copy-start(bf16[256,1024]{1,0:T(8,128)(2,1)} %copy-done.6) | copy-start | bytes 1572868
  53.7 9.7 %copy-start.8 = (bf16[256,1024]{1,0:T(8,128)(2,1)}, bf16[256,1024]{1,0:T(8,128)(2,1)S(1)}, u32[]{:S(2)}) copy-start(bf16[256,1024]{1,0:T(8,128)(2,1)S(1)} %get-tuple-element.141.refs_1_) | copy-start | bytes 1572868
  53.7 13.0 %collective-permute-start.13 = (bf16[256,1024]{1,0:T(8,128)(2,1)}, bf16[256,1024]{1,0:T(8,128)(2,1)}, u32[]{:S(2)}, u32[]{:S(2)}) collective-permute-start(bf16[256,1024]{1,0:T(8,128)(2,1)} %get-tuple-element.136.refs_3_), channel_id=1, source_target_pairs={{0,4},{2,6},{4,0},{6,2},{8,12},{10,14},{12,8},{14,10},{16,20},{18,... | collective-permute-start | bytes 1572872 | tf_op jit(solution)/shard_map/ppermute | solution.py:747
  62.4 0.7 copy-start.14
  63.4 0.8 copy-start.4
  64.2 10.7 %copy-start.5 = (bf16[272,1024]{1,0:T(8,128)(2,1)S(1)}, bf16[272,1024]{1,0:T(8,128)(2,1)}, u32[]{:S(2)}) copy-start(bf16[272,1024]{1,0:T(8,128)(2,1)} %copy-done.4) | copy-start | bytes 1671172
  64.2 10.7 %collective-permute-start.11 = (bf16[272,1024]{1,0:T(8,128)(2,1)S(1)}, bf16[272,1024]{1,0:T(8,128)(2,1)S(1)}, u32[]{:S(2)}, u32[]{:S(2)}) collective-permute-start(bf16[272,1024]{1,0:T(8,128)(2,1)S(1)} %get-tuple-element.139.refs_3_), channel_id=1, source_target_pairs={{0,2},{2,0},{4,6},{6,4},{8,10},{10,8},{12,14},{14,12},{16,18},{18,... | collective-permute-start | bytes 1671176 | tf_op jit(solution)/shard_map/ppermute | solution.py:747
  65.5 7.7 %collective-permute-start.12 = (bf16[128,1024]{1,0:T(8,128)(2,1)}, bf16[128,1024]{1,0:T(8,128)(2,1)S(1)}, u32[]{:S(2)}, u32[]{:S(2)}) collective-permute-start(bf16[128,1024]{1,0:T(8,128)(2,1)} %get-tuple-element.137.refs_3_), channel_id=1, source_target_pairs={{0,4},{2,6},{4,0},{6,2},{8,12},{10,14},{12,8},{14,10},{16,20},{18,... | collective-permute-start | bytes 786440 | tf_op jit(solution)/shard_map/ppermute | solution.py:747
  66.7 1.0 copy-start.9
  68.9 9.9 %collective-permute-start.16 = (bf16[128,1024]{1,0:T(8,128)(2,1)S(1)}, bf16[128,1024]{1,0:T(8,128)(2,1)S(1)}, u32[]{:S(2)}, u32[]{:S(2)}) collective-permute-start(bf16[128,1024]{1,0:T(8,128)(2,1)S(1)} %get-tuple-element.142.refs_3_), channel_id=1, source_target_pairs={{0,8},{2,10},{4,12},{6,14},{8,0},{10,2},{12,4},{14,6},{16,24},{18,... | collective-permute-start | bytes 786440 | tf_op jit(solution)/shard_map/ppermute | solution.py:747
  73.2 1.0 copy-start.15
  74.9 0.7 copy-start.16
  75.5 10.5 %collective-permute-start.14 = (bf16[144,1024]{1,0:T(8,128)(2,1)S(1)}, bf16[144,1024]{1,0:T(8,128)(2,1)S(1)}, u32[]{:S(2)}, u32[]{:S(2)}) collective-permute-start(bf16[144,1024]{1,0:T(8,128)(2,1)S(1)} %get-tuple-element.145.refs_3_), channel_id=1, source_target_pairs={{0,4},{2,6},{4,0},{6,2},{8,12},{10,14},{12,8},{14,10},{16,20},{18,... | collective-permute-start | bytes 884744 | tf_op jit(solution)/shard_map/ppermute | solution.py:747
  77.3 7.8 %collective-permute-start.15 = (bf16[64,1024]{1,0:T(8,128)(2,1)}, bf16[64,1024]{1,0:T(8,128)(2,1)S(1)}, u32[]{:S(2)}, u32[]{:S(2)}) collective-permute-start(bf16[64,1024]{1,0:T(8,128)(2,1)} %get-tuple-element.143.refs_3_), channel_id=1, source_target_pairs={{0,8},{2,10},{4,12},{6,14},{8,0},{10,2},{12,4},{14,6},{16,24},{18,... | collective-permute-start | bytes 393224 | tf_op jit(solution)/shard_map/ppermute | solution.py:747
  78.9 7.5 %collective-permute-start.19 = (bf16[64,1024]{1,0:T(8,128)(2,1)S(1)}, bf16[64,1024]{1,0:T(8,128)(2,1)S(1)}, u32[]{:S(2)}, u32[]{:S(2)}) collective-permute-start(bf16[64,1024]{1,0:T(8,128)(2,1)S(1)} %get-tuple-element.148.refs_3_), channel_id=1, source_target_pairs={{0,16},{2,18},{4,20},{6,22},{8,24},{10,26},{12,28},{14,30},{16,0},... | collective-permute-start | bytes 393224 | tf_op jit(solution)/shard_map/ppermute | solution.py:747
  85.1 0.9 copy-start.17
  86.1 9.8 %collective-permute-start.17 = (bf16[80,1024]{1,0:T(8,128)(2,1)S(1)}, bf16[80,1024]{1,0:T(8,128)(2,1)S(1)}, u32[]{:S(2)}, u32[]{:S(2)}) collective-permute-start(bf16[80,1024]{1,0:T(8,128)(2,1)S(1)} %get-tuple-element.151.refs_2_), channel_id=1, source_target_pairs={{0,8},{2,10},{4,12},{6,14},{8,0},{10,2},{12,4},{14,6},{16,24},{18,... | collective-permute-start | bytes 491528 | tf_op jit(solution)/shard_map/ppermute | solution.py:747
  86.4 9.6 %collective-permute-start.22 = (bf16[64,1024]{1,0:T(8,128)(2,1)S(1)}, bf16[64,1024]{1,0:T(8,128)(2,1)S(1)}, u32[]{:S(2)}, u32[]{:S(2)}) collective-permute-start(bf16[64,1024]{1,0:T(8,128)(2,1)S(1)} %add_last.3.refs_2_.refs_1_), channel_id=1, source_target_pairs={{0,16},{2,18},{4,20},{6,22},{8,24},{10,26},{12,28},{14,30},{16,0},... | collective-permute-start | bytes 393224 | tf_op jit(solution)/shard_map/ppermute | solution.py:747
  89.3 6.6 %collective-permute-start.18 = (bf16[32,1024]{1,0:T(8,128)(2,1)S(1)}, bf16[32,1024]{1,0:T(8,128)(2,1)S(1)}, u32[]{:S(2)}, u32[]{:S(2)}) collective-permute-start(bf16[32,1024]{1,0:T(8,128)(2,1)S(1)} %get-tuple-element.149.refs_3_), channel_id=1, source_target_pairs={{0,16},{2,18},{4,20},{6,22},{8,24},{10,26},{12,28},{14,30},{16,0},... | collective-permute-start | bytes 196616 | tf_op jit(solution)/shard_map/ppermute | solution.py:747
  96.0 17.6 %copy-start.19 = (bf16[2,128,512]{2,1,0:T(8,128)(2,1)S(1)}, bf16[2,128,512]{2,1,0:T(8,128)(2,1)}, u32[]{:S(2)}) copy-start(bf16[2,128,512]{2,1,0:T(8,128)(2,1)} %copy-done.18) | copy-start | bytes 786436
  96.1 10.3 %collective-permute-start.25 = (bf16[128,1024]{1,0:T(8,128)(2,1)S(1)}, bf16[128,1024]{1,0:T(8,128)(2,1)S(1)}, u32[]{:S(2)}, u32[]{:S(2)}) collective-permute-start(bf16[128,1024]{1,0:T(8,128)(2,1)S(1)} %join.9.refs_3_.refs_1_), channel_id=1, source_target_pairs={{0,8},{2,10},{4,12},{6,14},{8,0},{10,2},{12,4},{14,6},{16,24},{18,... | collective-permute-start | bytes 786440 | tf_op jit(solution)/shard_map/ppermute | solution.py:747
  96.2 8.4 %collective-permute-start.20 = (bf16[48,1024]{1,0:T(8,128)(2,1)S(1)}, bf16[48,1024]{1,0:T(8,128)(2,1)S(1)}, u32[]{:S(2)}, u32[]{:S(2)}) collective-permute-start(bf16[48,1024]{1,0:T(8,128)(2,1)S(1)} %get-tuple-element.155.refs_3_), channel_id=1, source_target_pairs={{0,16},{2,18},{4,20},{6,22},{8,24},{10,26},{12,28},{14,30},{16,0},... | collective-permute-start | bytes 294920 | tf_op jit(solution)/shard_map/ppermute | solution.py:747
  98.9 5.6 %collective-permute-start.21 = (bf16[32,1024]{1,0:T(8,128)(2,1)S(1)}, bf16[32,1024]{1,0:T(8,128)(2,1)S(1)}, u32[]{:S(2)}, u32[]{:S(2)}) collective-permute-start(bf16[32,1024]{1,0:T(8,128)(2,1)S(1)} %add_last.4.refs_3_.refs_1_), channel_id=1, source_target_pairs={{0,16},{2,18},{4,20},{6,22},{8,24},{10,26},{12,28},{14,30},{16,0},... | collective-permute-start | bytes 196616 | tf_op jit(solution)/shard_map/ppermute | solution.py:747
  106.4 11.1 %copy-start.21 = (bf16[2,128,512]{2,1,0:T(8,128)(2,1)S(1)}, bf16[2,128,512]{2,1,0:T(8,128)(2,1)}, u32[]{:S(2)}) copy-start(bf16[2,128,512]{2,1,0:T(8,128)(2,1)} %copy-done.20) | copy-start | bytes 786436
  106.4 9.2 %collective-permute-start.28 = (bf16[256,1024]{1,0:T(8,128)(2,1)S(1)}, bf16[256,1024]{1,0:T(8,128)(2,1)S(1)}, u32[]{:S(2)}, u32[]{:S(2)}) collective-permute-start(bf16[256,1024]{1,0:T(8,128)(2,1)S(1)} %join.11.refs_3_.refs_1_), channel_id=1, source_target_pairs={{0,4},{2,6},{4,0},{6,2},{8,12},{10,14},{12,8},{14,10},{16,20},{18,... | collective-permute-start | bytes 1572872 | tf_op jit(solution)/shard_map/ppermute | solution.py:747
  106.5 5.0 %collective-permute-start.24 = (bf16[64,1024]{1,0:T(8,128)(2,1)S(1)}, bf16[64,1024]{1,0:T(8,128)(2,1)S(1)}, u32[]{:S(2)}, u32[]{:S(2)}) collective-permute-start(bf16[64,1024]{1,0:T(8,128)(2,1)S(1)} %join.10.refs_2_.refs_1_), channel_id=1, source_target_pairs={{0,8},{2,10},{4,12},{6,14},{8,0},{10,2},{12,4},{14,6},{16,24},{18,... | collective-permute-start | bytes 393224 | tf_op jit(solution)/shard_map/ppermute | solution.py:747
  108.1 5.8 %collective-permute-start.23 = (bf16[32,1024]{1,0:T(8,128)(2,1)S(1)}, bf16[32,1024]{1,0:T(8,128)(2,1)S(1)}, u32[]{:S(2)}, u32[]{:S(2)}) collective-permute-start(bf16[32,1024]{1,0:T(8,128)(2,1)S(1)} %slice.22.refs_1_), channel_id=1, source_target_pairs={{0,16},{2,18},{4,20},{6,22},{8,24},{10,26},{12,28},{14,30},{16,0},... | collective-permute-start | bytes 196616 | tf_op jit(solution)/shard_map/ppermute | solution.py:747
  111.6 8.7 %collective-permute-start.27 = (bf16[128,1024]{1,0:T(8,128)(2,1)S(1)}, bf16[128,1024]{1,0:T(8,128)(2,1)S(1)}, u32[]{:S(2)}, u32[]{:S(2)}) collective-permute-start(bf16[128,1024]{1,0:T(8,128)(2,1)S(1)} %join.12.refs_3_.refs_1_), channel_id=1, source_target_pairs={{0,4},{2,6},{4,0},{6,2},{8,12},{10,14},{12,8},{14,10},{16,20},{18,... | collective-permute-start | bytes 786440 | tf_op jit(solution)/shard_map/ppermute | solution.py:747
  113.6 9.3 %collective-permute-start.3 = (bf16[2,128,512]{2,1,0:T(8,128)(2,1)S(1)}, bf16[2,128,512]{2,1,0:T(8,128)(2,1)S(1)}, u32[]{:S(2)}, u32[]{:S(2)}) collective-permute-start(bf16[2,128,512]{2,1,0:T(8,128)(2,1)S(1)} %copy-done.19), channel_id=1, source_target_pairs={{0,1},{1,0},{2,3},{3,2},{4,5},{5,4},{6,7},{7,6},{8,9},{9,8},{10,11... | collective-permute-start | bytes 786440 | tf_op jit(solution)/shard_map/ppermute | solution.py:867
  115.7 7.1 %copy-start.23 = (bf16[2,128,512]{2,1,0:T(8,128)(2,1)S(1)}, bf16[2,128,512]{2,1,0:T(8,128)(2,1)}, u32[]{:S(2)}) copy-start(bf16[2,128,512]{2,1,0:T(8,128)(2,1)} %copy-done.22) | copy-start | bytes 786436
  115.8 19.0 %collective-permute-start.32 = (bf16[512,1024]{1,0:T(8,128)(2,1)S(1)}, bf16[512,1024]{1,0:T(8,128)(2,1)S(1)}, u32[]{:S(2)}, u32[]{:S(2)}) collective-permute-start(bf16[512,1024]{1,0:T(8,128)(2,1)S(1)} %join.14.refs_3_.refs_1_), channel_id=1, source_target_pairs={{0,2},{2,0},{4,6},{6,4},{8,10},{10,8},{12,14},{14,12},{16,18},{18,... | collective-permute-start | bytes 3145736 | tf_op jit(solution)/shard_map/ppermute | solution.py:747
  117.5 5.0 %collective-permute-start.26 = (bf16[64,1024]{1,0:T(8,128)(2,1)S(1)}, bf16[64,1024]{1,0:T(8,128)(2,1)S(1)}, u32[]{:S(2)}, u32[]{:S(2)}) collective-permute-start(bf16[64,1024]{1,0:T(8,128)(2,1)S(1)} %join.13.refs_3_.refs_1_), channel_id=1, source_target_pairs={{0,8},{2,10},{4,12},{6,14},{8,0},{10,2},{12,4},{14,6},{16,24},{18,... | collective-permute-start | bytes 393224 | tf_op jit(solution)/shard_map/ppermute | solution.py:747
  117.5 6.2 %copy-start.11 = (bf16[2,128,512]{2,1,0:T(8,128)(2,1)S(1)}, bf16[2,128,512]{2,1,0:T(8,128)(2,1)}, u32[]{:S(2)}) copy-start(bf16[2,128,512]{2,1,0:T(8,128)(2,1)} %copy-done.10) | copy-start | bytes 786436
  117.5 6.2 %collective-permute-start.7 = (bf16[2,128,512]{2,1,0:T(8,128)(2,1)S(1)}, bf16[2,128,512]{2,1,0:T(8,128)(2,1)S(1)}, u32[]{:S(2)}, u32[]{:S(2)}) collective-permute-start(bf16[2,128,512]{2,1,0:T(8,128)(2,1)S(1)} %copy-done.21), channel_id=1, source_target_pairs={{0,1},{1,0},{2,3},{3,2},{4,5},{5,4},{6,7},{7,6},{8,9},{9,8},{10,11... | collective-permute-start | bytes 786440 | tf_op jit(solution)/shard_map/ppermute | solution.py:867
  120.3 12.4 %copy-start.13 = (bf16[2,128,512]{2,1,0:T(8,128)(2,1)S(1)}, bf16[2,128,512]{2,1,0:T(8,128)(2,1)}, u32[]{:S(2)}) copy-start(bf16[2,128,512]{2,1,0:T(8,128)(2,1)} %copy-done.12) | copy-start | bytes 786436
  122.5 9.3 %collective-permute-start.29 = (bf16[128,1024]{1,0:T(8,128)(2,1)S(1)}, bf16[128,1024]{1,0:T(8,128)(2,1)S(1)}, u32[]{:S(2)}, u32[]{:S(2)}) collective-permute-start(bf16[128,1024]{1,0:T(8,128)(2,1)S(1)} %join.16.refs_1_.refs_3_), channel_id=1, source_target_pairs={{0,4},{2,6},{4,0},{6,2},{8,12},{10,14},{12,8},{14,10},{16,20},{18,... | collective-permute-start | bytes 786440 | tf_op jit(solution)/shard_map/ppermute | solution.py:747
  122.9 9.7 %collective-permute-start.6 = (bf16[2,128,512]{2,1,0:T(8,128)(2,1)S(1)}, bf16[2,128,512]{2,1,0:T(8,128)(2,1)S(1)}, u32[]{:S(2)}, u32[]{:S(2)}) collective-permute-start(bf16[2,128,512]{2,1,0:T(8,128)(2,1)S(1)} %copy-done.23), channel_id=1, source_target_pairs={{0,1},{1,0},{2,3},{3,2},{4,5},{5,4},{6,7},{7,6},{8,9},{9,8},{10,11... | collective-permute-start | bytes 786440 | tf_op jit(solution)/shard_map/ppermute | solution.py:867
  124.7 14.4 %collective-permute-start.31 = (bf16[256,1024]{1,0:T(8,128)(2,1)S(1)}, bf16[256,1024]{1,0:T(8,128)(2,1)S(1)}, u32[]{:S(2)}, u32[]{:S(2)}) collective-permute-start(bf16[256,1024]{1,0:T(8,128)(2,1)S(1)} %join.15.refs_3_.refs_1_), channel_id=1, source_target_pairs={{0,2},{2,0},{4,6},{6,4},{8,10},{10,8},{12,14},{14,12},{16,18},{18,... | collective-permute-start | bytes 1572872 | tf_op jit(solution)/shard_map/ppermute | solution.py:747
  131.9 12.8 %collective-permute-start.30 = (bf16[256,1024]{1,0:T(8,128)(2,1)S(1)}, bf16[256,1024]{1,0:T(8,128)(2,1)S(1)}, u32[]{:S(2)}, u32[]{:S(2)}) collective-permute-start(bf16[256,1024]{1,0:T(8,128)(2,1)S(1)} %join.17.refs_3_.refs_1_), channel_id=1, source_target_pairs={{0,2},{2,0},{4,6},{6,4},{8,10},{10,8},{12,14},{14,12},{16,18},{18,... | collective-permute-start | bytes 1572872 | tf_op jit(solution)/shard_map/ppermute | solution.py:747
  139.1 1.6 %copy-start = (f32[512,1024]{1,0:T(8,128)S(1)}, f32[512,1024]{1,0:T(8,128)}, u32[]{:S(2)}) copy-start(f32[512,1024]{1,0:T(8,128)} %get-tuple-element.83.refs_3_) | copy-start | bytes 6291460
  144.7 1.2 copy-start.1

commit v3 on v2

--- a/solution.py
+++ b/solution.py
@@ -14,9 +14,16 @@
 BF = jnp.bfloat16
 F32 = jnp.float32
 MIB = 1 << 20
-ORDER = ('a', '', 'b', 'abcabcabcabcabcabcabcc')
-ROUTES = (((1, 2), (2, 1), (4, 4), (8, 8)), ((1, 2), (2, 1), (4, 4), (8, 8)), ((1, 2), (2, 1), (4, 4), (8, 8)))
-COST = {name: 100_000_000_000 for name in ("forward", "feed_keep", "cross", "cross_grads", "self", "self_grads")}
+ORDER = "XFfGSFxTfFsxFfsPxFsfxsFfxsFfxsFxfsxfFsxsf"
+PLANE_FIRST = ((1, 2), (2, 1), (4, 4), (8, 8))
+BETWEEN = ((1, 2), (4, 4), (2, 1), (8, 8))
+LINE_FIRST = ((4, 4), (1, 2), (2, 1), (8, 8))
+ROUTES = {"f": ((4, 4), (1, 2), (8, 8), (2, 1)), "F": PLANE_FIRST, "x": BETWEEN, "s": PLANE_FIRST}
+SMALL_COST = {"flops": 20_000_000_000, "bytes_accessed": 400_000_000}
+COST = {
+    name: {"flops": 100_000_000_000, "bytes_accessed": 1000}
+    for name in ("forward", "feed_keep", "cross", "cross_grads", "self", "self_grads")
+}
 LANES = 1024
 
 
@@ -172,22 +179,22 @@
     ]
 
 
-def feed_grads(which, ref, slow_t, ginner, gff_t, hidden):
+def feed_grads(which, in_ref, out_ref, slow_t, ginner, gff_t, hidden):
     inner, width = hidden.shape[1], slow_t.shape[0]
     half_in, half_out = inner // 2, width // 2
 
     def give_in(index):
         def run():
             cols = pl.ds(pl.multiple_of(which * half_in + index * 256, 256), 256)
-            ref[0:width, index * 256 : (index + 1) * 256] = mm(slow_t[...], ginner[:, cols]).astype(BF)
+            in_ref[:, index * 256 : (index + 1) * 256] = mm(slow_t[...], ginner[:, cols]).astype(BF)
 
         return run
 
     def give_out(index):
         def run():
             feats = pl.ds(pl.multiple_of(which * half_out, half_out), half_out)
-            low, at = width + (index // 2) * half_out, (index % 2) * 512
-            ref[low : low + half_out, at : at + 512] = mm(
+            low, at = (index // 2) * half_out, (index % 2) * 512
+            out_ref[low : low + half_out, at : at + 512] = mm(
                 gff_t[feats, :], hidden[:, index * 512 : (index + 1) * 512]
             ).astype(BF)
 
@@ -196,8 +203,8 @@
     return [give_out(i) for i in range(inner // 512)] + [give_in(i) for i in range(half_in // 256)]
 
 
-def feed_keep_kernel(place_ref, gff_t, hidden, slow_t, ginner, keep_ref):
-    weave(feed_grads(place_ref[0], keep_ref, slow_t, ginner, gff_t, hidden))
+def feed_keep_kernel(numbers_ref, gff_t, hidden, slow_t, ginner, in_ref, out_ref):
+    weave(feed_grads(numbers_ref[0], in_ref, out_ref, slow_t, ginner, gff_t, hidden))
 
 
 def forward_kernel(numbers_ref, *refs):
@@ -205,7 +212,7 @@
     names = FORWARD_WEIGHTS
     weights_in, refs = refs[: len(names)], refs[len(names) :]
     kept = dict(zip(FORWARD_KEPT, refs))
-    (out_own, out_oth, send_ref, gff_t, hidden, slow_t, ginner, gss, elow, qkv, p_self, rl_self, att_t, xhat1, rstd1,
+    (out_own, out_oth, send_in, send_out, gff_t, hidden, slow_t, ginner, gss, elow, qkv, p_self, rl_self, att_t, xhat1, rstd1,
      flow, encs, cq, ckv, p_cross, rl_cross, crossed_t, dnorm_ref) = refs[: len(FORWARD_KEPT) - len(PASSED_WEIGHTS)]
     refs = refs[len(FORWARD_KEPT) :]
     w = {name: kept["w_" + name] for name in PASSED_WEIGHTS}
@@ -334,7 +341,7 @@
         def turn():
             gff_t[:, rows[s]] = gff[rows[s]].T
             out_own[s] = outs[where[s][0], :]
-            out_oth[s] = outs[where[s][1], :]
+            out_oth[:, s * width : (s + 1) * width] = outs[where[s][1], :]
 
         return [shrink(0), shrink(1), norm, turn]
 
@@ -392,7 +399,7 @@
     weave(feed(1), after_feed(0))
     weave(feed_back(0), after_feed(1))
     weave(feed_back(1), after_feed_back(0))
-    weave(feed_grads(1 - place, send_ref, slow_t, ginner, gff_t, hidden), after_feed_back(1))
+    weave(feed_grads(1 - place, send_in, send_out, slow_t, ginner, gff_t, hidden), after_feed_back(1))
     dnorm_ref[...] = jnp.zeros(dnorm_ref.shape, F32)
     for k in (1, 2):
         dnorm_ref[k : k + 1, :] = gains[k, 0][0] + gains[k, 1][0]
@@ -403,7 +410,7 @@
 FORWARD_WEIGHTS = ("table", "qkv", "gain", "nbias", "ckv", "so", "cq", "co", "fi", "fo")
 PASSED_WEIGHTS = ("qkv", "gain", "ckv", "so", "cq", "co")
 FORWARD_KEPT = (
-    "out_own", "out_oth", "send_a", "gff_t", "hidden", "slow_t", "ginner", "gss", "elow", "qkv", "p_self", "rl_self",
+    "out_own", "out_oth", "send_in", "send_out", "gff_t", "hidden", "slow_t", "ginner", "gss", "elow", "qkv", "p_self", "rl_self",
     "att_t", "xhat1", "rstd1", "flow", "encs", "cq", "ckv", "p_cross", "rl_cross", "crossed_t", "dnorm",
 ) + tuple("w_" + name for name in PASSED_WEIGHTS)
 
@@ -462,9 +469,9 @@
 
 
 def cross_grads_kernel(
-    place_ref, branch, gq_t, gkv_t, crossed_t, flow, encs, w_ckv, send_ref, keep_ref, genc_own, genc_oth, genc
+    numbers_ref, branch, gq_t, gkv_t, crossed_t, flow, encs, w_ckv, out_oth, send_ref, keep_ref, genc_own, genc
 ):
-    place = place_ref[0]
+    place = numbers_ref[0]
     tokens, width = branch.shape
     length = tokens // 2
     half = width // 2
@@ -480,7 +487,7 @@
 
         def pair():
             feats = pl.ds(pl.multiple_of(which * width, half), width)
-            ref[:, 0:width] = mm(gkv_t[feats, :], encs[...]).astype(BF)
+            ref[0:width, 0:width] = mm(gkv_t[feats, :], encs[...]).astype(BF)
 
         return [out, query, pair]
 
@@ -489,11 +496,12 @@
             rows = slice(s * length, (s + 1) * length)
             genc[rows] = mm(w_ckv[...], gkv_t[:, rows]).astype(BF).T
             genc_own[s] = genc[where[s][0], :]
-            genc_oth[s] = genc[where[s][1], :]
+            send_ref[width : width + length // 2, s * width : (s + 1) * width] = genc[where[s][1], :]
 
         return run
 
     weave(give(1 - place, send_ref) + give(place, keep_ref), [encoder(0), encoder(1)])
+    send_ref[width + length // 2 :, :] = out_oth[...]
 
 
 def self_kernel(gfs, w_so, qkv, p_self, rl_self, att_t, branch, gqkv_t, go_t):
@@ -522,7 +530,7 @@
 
 def self_grads_kernel(
     numbers_ref, gfs, dnorm_in, branch, gqkv_t, att_t, elow, w_qkv,
-    send_ref, keep_ref, gin_own, gin_oth,
+    send_ref, keep_ref, gin_own,
     gin, small,
 ):
     place = numbers_ref[0]
@@ -557,7 +565,7 @@
             gin[rows] = total.astype(BF)
             sums[s] = jnp.sum(total, 0, keepdims=True)
             gin_own[s] = gin[where[s][0], :]
-            gin_oth[s] = gin[where[s][1], :]
+            send_ref[width + 16 :, s * width : (s + 1) * width] = gin[where[s][1], :]
 
         return [start, finish]
 
@@ -581,11 +589,12 @@
             ref[half : half + tail, :] = (a_ref[last, :].astype(F32) + b_ref[last, :].astype(F32)).astype(BF)
 
 
-def add_all_kernel(*refs):
-    total = refs[0][...].astype(F32)
-    for ref in refs[1:-1]:
-        total = total + ref[...].astype(F32)
-    refs[-1][...] = total.astype(BF)
+def add_kernel(tail, a_ref, b_ref, out_ref, *tail_refs):
+    rows = out_ref.shape[0]
+    out_ref[...] = (a_ref[0:rows, :].astype(F32) + b_ref[0:rows, :].astype(F32)).astype(BF)
+    if tail:
+        last = slice(rows, rows + tail)
+        tail_refs[0][...] = (a_ref[last, :].astype(F32) + b_ref[last, :].astype(F32)).astype(BF)
 
 
 def join_kernel(index_ref, *refs):
@@ -595,22 +604,30 @@
         out[pl.ds(pl.multiple_of((index_ref[0] ^ j) * rows, 16), rows), :] = ref[...]
 
 
-def unpack_kernel(unpack, index_ref, mine_ref, got_ref, *outs):
+def unpack_kernel(unpack, count, index_ref, mine_ref, got_ref, *refs):
+    rest = refs[: len(refs) - count - 1]
+    mark_ref, *outs = refs[len(rest) :]
+    mark_ref[...] = jnp.zeros(mark_ref.shape, F32)
+
     @pl.when(index_ref[0] == 0)
     def _():
-        unpack(mine_ref, got_ref, *outs)
+        unpack(mine_ref, got_ref, *rest, *outs)
 
     @pl.when(index_ref[0] != 0)
     def _():
-        unpack(got_ref, mine_ref, *outs)
-
-
-def unpack_ff(low_ref, high_ref, in_ref, out_ref):
-    in_ref[...] = low_ref[...].astype(F32)
-    half = out_ref.shape[1]
-    for j in range(2):
-        tall = low_ref.shape[1]
-        out_ref[j * tall : (j + 1) * tall, :] = high_ref[j * half : (j + 1) * half, :].T.astype(F32)
+        unpack(got_ref, mine_ref, *rest, *outs)
+
+
+def unpack_in(low_ref, high_ref, in_ref):
+    half = low_ref.shape[0]
+    in_ref[0:half, :] = low_ref[...].astype(F32)
+    in_ref[half:, :] = high_ref[...].astype(F32)
+
+
+def unpack_out(low_ref, high_ref, out_ref):
+    tall = low_ref.shape[1]
+    out_ref[0:tall, :] = low_ref[...].T.astype(F32)
+    out_ref[tall:, :] = high_ref[...].T.astype(F32)
 
 
 def unpack_tall(low_ref, high_ref, out_ref):
@@ -628,12 +645,27 @@
     unpack_tall(low_ref, high_ref, out_ref)
 
 
-def unpack_self(low_ref, high_ref, qkv_ref, out_ref):
+def unpack_self(low_ref, high_ref, small_ref, qkv_ref, out_ref, gain_ref, bias_ref, table_ref):
     half, width = low_ref.shape[0], qkv_ref.shape[0]
     qkv_ref[:, 0:half] = low_ref[:, 0:width].T.astype(F32)
     qkv_ref[:, half:width] = high_ref[:, 0:width].T.astype(F32)
     qkv_ref[:, width:] = low_ref[:, width:].T.astype(F32)
     unpack_tall(low_ref, high_ref, out_ref)
+    small = small_ref[:, 0 : gain_ref.shape[1]].astype(F32)
+    gain_ref[...] = small[0:3]
+    bias_ref[...] = small[3:6]
+    table_ref[...] = small[8:16]
+
+
+def place_kernel(numbers_ref, out_own, genc_own, gin_own, got_cross, got_self, *outs):
+    place = numbers_ref[0]
+    half, width = out_own.shape[1:]
+    first = width + 16
+    others = (got_cross, width + half), (got_cross, width), (got_self, first)
+    for own_ref, (got_ref, at), out_ref in zip((out_own, genc_own, gin_own), others, outs):
+        out_ref[place] = own_ref[...]
+        for sentence in range(2):
+            out_ref[1 - place, sentence] = got_ref[at : at + half, sentence * width : (sentence + 1) * width]
 
 
 def smem():
@@ -663,7 +695,7 @@
         out_specs=tuple(vmem() for _ in (*outs, *results)),
         scratch_shapes=[pltpu.VMEM(s, d) for s, d in scratch] + ([pltpu.SemaphoreType.DMA((sems,))] if sems else []),
         compiler_params=pltpu.CompilerParams(vmem_limit_bytes=limit),
-        cost_estimate=pl.CostEstimate(flops=COST.get(name, 1000), bytes_accessed=1000, transcendentals=0),
+        cost_estimate=pl.CostEstimate(**COST.get(name, SMALL_COST), transcendentals=0),
         name=name,
     )(
         *scalars,
@@ -706,8 +738,10 @@
     probs = (sent_count * HEADS, length, length)
     sums = (sent_count * HEADS, 1, length)
     turned = (width, tokens)
+    buffer = (width, LANES)
     kinds = {
-        "out_own": (rows, BF), "out_oth": (rows, BF), "send_a": ((2 * width, LANES), BF), "gff_t": (turned, BF),
+        "out_own": (rows, BF), "out_oth": ((local_len, LANES), BF), "send_in": (buffer, BF),
+        "send_out": (buffer, BF), "gff_t": (turned, BF),
         "hidden": ((tokens, inner), BF), "slow_t": (turned, BF), "ginner": ((tokens, inner), BF), "gss": (whole, F32),
         "elow": (whole, BF), "qkv": ((tokens, 3 * width), BF), "p_self": (probs, BF), "rl_self": (sums, F32),
         "att_t": (turned, BF), "xhat1": (whole, F32), "rstd1": ((tokens, 128), F32), "flow": (whole, BF),
@@ -748,13 +782,7 @@
 
     last = []
 
-    def go_on(*groups):
-        result = None
-        for group in groups:
-            result = next(group)
-        return result
-
-    def reduce_all(keep, send, outs, unpack, route, tail=0):
+    def reduce_all(keep, got, outs, unpack, route, tail=0):
         def run(kernel, scalars, arrays, outs, name, results=()):
             got = call(kernel, scalars, arrays, outs, name=name, results=results, after=tuple(last))
             last[:] = [got[0]]
@@ -762,11 +790,11 @@
 
         rows, lanes = keep.shape
         body = rows - tail
-        got = lax.ppermute(send, "seq", swap)
         if dp_count != 16:
-            (total,) = run(add_all_kernel, (), (keep, got), [((rows, lanes), BF)], "add_core")
+            (total,) = run(functools.partial(add_kernel, 0), (), (keep, got), [((rows, lanes), BF)], "add_core")
             total = lax.psum(total, "dp")
-            mine, other, rest = total[: body // 2], total[body // 2 : body], total[body:]
+            mine, other = total[: body // 2], total[body // 2 : body]
+            rest = (total[body:],) if tail else ()
             bit = jnp.zeros((1,), jnp.int32)
             for _ in range(2 * len(route)):
                 yield
@@ -782,8 +810,8 @@
                 send, keep = run(functools.partial(add_split_kernel, tail), (bit,), (keep, got), [(shape, BF)] * 2, "add_split")
                 got = travel(send, *flip)
                 yield
-            (mine,) = run(add_all_kernel, (), (keep, got), [(shape, BF)], "add_last")
-            mine, rest = mine[:held], mine[held:]
+            pieces = [((held, lanes), BF)] + ([((tail, lanes), BF)] if tail else [])
+            mine, *rest = run(functools.partial(add_kernel, tail), (), (keep, got), pieces, "add_last")
             for bit, flip in zip(bits[:0:-1], route[:0:-1]):
                 other = travel(mine, *flip)
                 yield
@@ -792,85 +820,116 @@
             other = travel(mine, *route[0])
             bit = bits[0]
             yield
-        unpacked = run(
-            functools.partial(unpack_kernel, unpack), (bit,), (mine, other), [], "unpack", [(s, F32) for s in outs]
+        _, *unpacked = run(
+            functools.partial(unpack_kernel, unpack, len(outs)),
+            (bit,),
+            (mine, other, *rest),
+            [((8, 128), F32)],
+            "unpack",
+            [(s, F32) for s in outs],
         )
-        yield unpacked, rest
-
-    groups = {}
-
-    def go_through(letters):
-        go_on(*(groups[letter] for letter in letters))
-
-    (keep_a,) = call(
+        yield unpacked
+
+    held["keep_in"], held["keep_out"] = call(
         feed_keep_kernel,
         (numbers,),
         of("gff_t", "hidden", "slow_t", "ginner"),
-        [((2 * width, LANES), BF)],
+        [(buffer, BF), (buffer, BF)],
         name="feed_keep",
     )
-    groups["a"] = reduce_all(keep_a, held["send_a"], [(width, inner // 2), (inner, half)], unpack_ff, ROUTES[0])
-    branch, gq_t, gkv_t, gfs, dnorm = call(
-        cross_kernel,
-        (),
-        of("gss", "dnorm", "w_gain", "w_co", "w_cq", "ckv", "cq", "p_cross", "rl_cross", "crossed_t", "xhat1", "rstd1"),
-        [(whole, BF), (turned, BF), ((2 * width, tokens), BF), (whole, F32), ((8, width), F32)],
-        [(turned, BF)],
-        name="cross",
-        after=[keep_a],
-    )
-    go_through(ORDER[0])
-    buffer = ((width, LANES), BF)
-    send_b, keep_b, genc_own, genc_oth = call(
-        cross_grads_kernel,
-        (numbers,),
-        [branch, gq_t, gkv_t, *of("crossed_t", "flow", "encs", "w_ckv")],
-        [buffer, buffer, (rows, BF), (rows, BF)],
-        [(whole, BF)],
-        name="cross_grads",
-        after=last,
-    )
-    groups["b"] = reduce_all(
-        keep_b, send_b, [(width, width), (width, half), (width, half)], unpack_cross, ROUTES[1]
-    )
-    go_through(ORDER[1])
-    branch, gqkv_t = call(
-        self_kernel,
-        (),
-        [gfs, *of("w_so", "qkv", "p_self", "rl_self", "att_t")],
-        [(whole, BF), ((3 * width, tokens), BF)],
-        [(turned, BF)],
-        name="self",
-        after=last,
-    )
-    go_through(ORDER[2])
-    buffer = ((width + 16, LANES), BF)
-    send_c, keep_c, gin_own, gin_oth = call(
-        self_grads_kernel,
-        (numbers,),
-        [gfs, dnorm, branch, gqkv_t, *of("att_t", "elow", "w_qkv")],
-        [buffer, buffer, (rows, BF), (rows, BF)],
-        [(whole, BF), ((16, width), F32)],
-        name="self_grads",
-        after=last,
-    )
-    groups["c"] = reduce_all(
-        keep_c, send_c, [(width, 3 * half), (width, half)], unpack_self, ROUTES[2], tail=16
-    )
-    last[:] = [send_c]
-    go_through(ORDER[3])
-    (g_ff_in, g_ff_out), _ = go_on(groups["a"])
-    (g_cross_kv, g_cross_q, g_cross_out), _ = go_on(groups["b"])
-    (g_qkv, g_self_out), tot_s = go_on(groups["c"])
-    tot_s = tot_s[:, :half].astype(F32)
-    def both(own, other):
-        got = lax.ppermute(other, "seq", swap)
-        return jnp.where(place == 0, jnp.stack([own, got]), jnp.stack([got, own]))
-
-    output = both(*of("out_own", "out_oth"))
-    grad_encoder = both(genc_own, genc_oth)
-    grad_input = both(gin_own, gin_oth)
-
+    last[:] = of("keep_in")
+
+    def store(names, arrays):
+        held.update(zip(names, arrays))
+        last[:] = [arrays[0]]
+
+    def cross_back():
+        store(
+            ("cross_branch", "gq_t", "gkv_t", "gfs", "dnorm"),
+            call(
+                cross_kernel,
+                (),
+                of("gss", "dnorm", "w_gain", "w_co", "w_cq", "ckv", "cq", "p_cross", "rl_cross", "crossed_t", "xhat1", "rstd1"),
+                [(whole, BF), (turned, BF), ((2 * width, tokens), BF), (whole, F32), ((8, width), F32)],
+                [(turned, BF)],
+                name="cross",
+                after=last,
+            ),
+        )
+
+    def cross_grads():
+        longer = (width + 2 * local_len, LANES)
+        send, keep, held["genc_own"] = call(
+            cross_grads_kernel,
+            (numbers,),
+            of("cross_branch", "gq_t", "gkv_t", "crossed_t", "flow", "encs", "w_ckv", "out_oth"),
+            [(longer, BF), (buffer, BF), (rows, BF)],
+            [(whole, BF)],
+            name="cross_grads",
+            after=last,
+        )
+        last[:] = [send]
+        held["got_cross"] = lax.ppermute(send, "seq", swap)
+        groups["x"] = reduce_all(
+            keep, held["got_cross"], [(width, width), (width, half), (width, half)], unpack_cross, ROUTES["x"]
+        )
+
+    def self_back():
+        store(
+            ("self_branch", "gqkv_t"),
+            call(
+                self_kernel,
+                (),
+                of("gfs", "w_so", "qkv", "p_self", "rl_self", "att_t"),
+                [(whole, BF), ((3 * width, tokens), BF)],
+                [(turned, BF)],
+                name="self",
+                after=last,
+            ),
+        )
+
+    def self_grads():
+        longer = (width + 16 + local_len, LANES)
+        send, keep, held["gin_own"] = call(
+            self_grads_kernel,
+            (numbers,),
+            of("gfs", "dnorm", "self_branch", "gqkv_t", "att_t", "elow", "w_qkv"),
+            [(longer, BF), ((width + 16, LANES), BF), (rows, BF)],
+            [(whole, BF), ((16, width), F32)],
+            name="self_grads",
+            after=last,
+        )
+        last[:] = [send]
+        held["got_self"] = lax.ppermute(send, "seq", swap)
+        results = [(width, 3 * half), (width, half), (3, half), (3, half), (8, half)]
+        groups["s"] = reduce_all(keep, held["got_self"], results, unpack_self, ROUTES["s"], tail=16)
+
+    def place_all():
+        held["placed"] = call(
+            place_kernel,
+            (numbers,),
+            of("out_own", "genc_own", "gin_own", "got_cross", "got_self"),
+            [],
+            name="place",
+            results=[(dec_in.shape, BF)] * 3,
+            after=last,
+        )
+
+    groups = {
+        "f": reduce_all(held["keep_in"], lax.ppermute(held["send_in"], "seq", swap), [(width, inner // 2)], unpack_in, ROUTES["f"]),
+        "F": reduce_all(held["keep_out"], lax.ppermute(held["send_out"], "seq", swap), [(inner, half)], unpack_out, ROUTES["F"]),
+    }
+    kernels = {"X": cross_back, "G": cross_grads, "S": self_back, "T": self_grads, "P": place_all}
+    sums = {}
+    for letter in ORDER:
+        if letter in kernels:
+            kernels[letter]()
+        else:
+            sums[letter] = next(groups[letter])
+    (g_ff_in,), (g_ff_out,) = sums["f"], sums["F"]
+    g_cross_kv, g_cross_q, g_cross_out = sums["x"]
+    g_qkv, g_self_out, g_gain, g_bias, g_table = sums["s"]
+    output, grad_encoder, grad_input = held["placed"]
     return (
         output,
         grad_input,
@@ -882,9 +941,9 @@
         g_cross_out,
         g_ff_in,
         g_ff_out,
-        tot_s[0:3],
-        tot_s[3:6],
-        tot_s[8:16],
+        g_gain,
+        g_bias,
+        g_table,
     )
 
 

time: 148 us -> 128 us (0.86)
  local copies, waits for them, and re-layouts: 14.7 us -> 0 us
  waiting for transfers between devices: 43.9 us -> 31.7 us
  starting transfers between devices: 33.4 us -> 42.1 us
  other arithmetic: 5.4 us -> 2.8 us
    unnamed x48 -> x0, local copies, waits for them, and re-layouts: 13.5 us -> none
    ppermute x24 -> x32, waiting for transfers between devices: 43.8 us -> 31.7 us  [travel(): return lax.ppermute(array, ('dp', 'seq'), flips(core_zero, core_one))]
    ppermute x24 -> x32, starting transfers between devices: 31.6 us -> 40.4 us  [travel(): return lax.ppermute(array, ('dp', 'seq'), flips(core_zero, core_one))]
    select_n x3 -> x0, other arithmetic: 2.6 us -> none  [both(): return jnp.where(place == 0, jnp.stack([own, got]), jnp.stack([got, own]))]
    pallas_call x33 -> x43, Pallas kernels: 49.1 us -> 50.4 us  [call(): pl.pallas_call(body, out_shape=tuple((pltpu.VMEM(s, d) for s, d in outs))...]
  transfers between devices with their start and end apart: 33 -> 39, of which waited for: 14 -> 13; matrix products, arithmetic and copies ran while one was open for 4% -> 2% of each run, Pallas kernels for 17% -> 23%
where the time goes in v3:
time: 128 us
  Pallas kernels  50.4 us (39%)
  starting transfers between devices  42.1 us (33%)
  waiting for transfers between devices  31.7 us (25%)
  other arithmetic  2.8 us (2%)
    pallas_call x43, Pallas kernels, call(): pl.pallas_call(body, out_shape=tuple((pltpu.VMEM(s, d) for s, d in outs))...  50.4 us
    ppermute x32, starting transfers between devices, travel(): return lax.ppermute(array, ('dp', 'seq'), flips(core_zero, core_one))  40.4 us
    ppermute x32, waiting for transfers between devices, travel(): return lax.ppermute(array, ('dp', 'seq'), flips(core_zero, core_one))  31.7 us
  transfers between devices with their start and end apart: 39, of which 13 were waited for; matrix products, arithmetic and copies ran while one was open for 2% of the time, Pallas kernels for 23%

profile of v3, /device:TPU:0, one launch (start us, length us, event | category | flops | bytes accessed | tf_op | source)
XLA Modules:
  0.0 127.9 jit_solution(5028601657365017222)
XLA Ops:
  0.6 0.5 collective-permute-start
  1.2 0.4 collective-permute-start.2
  1.7 1.3 %select_reduce_fusion.2 = s32[]{:T(128)} fusion(s32[2]{0:T(128)} %param.21, s32[]{:T(128)} %axis_index.22), kind=kLoop, calls=%fused_computation.3 | loop fusion | flops 5 | bytes 16 | tf_op jit(solution)/shard_map/reduce_sum | solution.py:725
  3.0 0.8 select_reduce_fusion.1
  3.8 0.7 pad_add_fusion.refs_0_
  4.5 19.0 %forward.1 = (bf16[2,128,512]{2,1,0:T(8,128)(2,1)S(1)}, bf16[128,1024]{1,0:T(8,128)(2,1)S(1)}, bf16[512,1024]{1,0:T(8,128)(2,1)}, bf16[512,1024]{1,0:T(8,128)(2,...) custom-call(s32[6]{0:T(128)S(1)} %pad_add_fusion.refs_0_, ...), custom_call_target="tpu_custom_call" | custom-call | flops 99999997952 | bytes 1000 | tf_op jit(solution)/shard_map/forward/pallas_call | solution.py:688
  23.7 0.3 collective-permute-start.3
  24.0 1.8 %feed_keep.1 = (bf16[512,1024]{1,0:T(8,128)(2,1)S(1)}, bf16[512,1024]{1,0:T(8,128)(2,1)S(1)}) custom-call(s32[6]{0:T(128)S(1)} %pad_add_fusion.refs_0_, bf16[512,512]{1,0:T(8,128)(2,1)S(1)} %get-tuple-element.121.refs_1_, bf16[512,2048]{1,0:T(8,128)(2,1)S(1)} %get-tuple-element.122.refs_2_, bf16[512,512]{1,0:T(8,128)(2,1)S(1)} %get-tuple-element.123.refs_3_, ...), custom_call_target="tpu_custom_call" | custom-call | flops 99999997952 | bytes 1000 | tf_op jit(solution)/shard_map/feed_keep/pallas_call | solution.py:688
  25.8 3.5 %cross.1 = (bf16[512,512]{1,0:T(8,128)(2,1)S(1)}, bf16[512,512]{1,0:T(8,128)(2,1)S(1)}, bf16[1024,512]{1,0:T(8,128)(2,1)S(1)}, f32[512,512]{1,0:T(8,128)S(1)}, f32[8,512]{1,0:T(8,128)S(1)}) custom-call(f32[512,512]{1,0:T(8,128)S(1)} %get-tuple-element.109.refs_0_, f32[8,512]{1,0:T(8,128)S(1)} %get-tuple-element.110.refs_1_, ...), custom_call_target="tpu_custom_call" | custom-call | flops 99999997952 | bytes 1000 | tf_op jit(solution)/shard_map/cross/pallas_call | solution.py:688
  29.3 2.2 %add_split.16 = (bf16[256,1024]{1,0:T(8,128)(2,1)}, bf16[256,1024]{1,0:T(8,128)(2,1)S(1)}) custom-call(s32[1]{0:T(128)} %bitcast.3.refs_0_, bf16[512,1024]{1,0:T(8,128)(2,1)S(1)} %get-tuple-element.134.refs_1_, bf16[512,1024]{1,0:T(8,128)(2,1)} %collective-permute-done.4.refs_2_, bf16[512,512]{1,0:T(8,128)(2,1)S(1)} %get-tuple-element.126.refs_3_.refs_1_), custom_call_target="tpu_custom_call" | custom-call | flops 20000000000 | bytes 400000000 | tf_op jit(solution)/shard_map/add_split/pallas_call | solution.py:688
  31.5 2.7 %collective-permute-start.6 = (bf16[256,1024]{1,0:T(8,128)(2,1)}, bf16[256,1024]{1,0:T(8,128)(2,1)}, u32[]{:S(2)}, u32[]{:S(2)}) collective-permute-start(bf16[256,1024]{1,0:T(8,128)(2,1)} %get-tuple-element.136.refs_3_), channel_id=1, source_target_pairs={{0,2},{2,0},{4,6},{6,4},{8,10},{10,8},{12,14},{14,12},{16,18},{18,... | collective-permute-start | bytes 1572872 | tf_op jit(solution)/shard_map/ppermute | solution.py:781
  34.2 2.2 %add_split.17 = (bf16[256,1024]{1,0:T(8,128)(2,1)}, bf16[256,1024]{1,0:T(8,128)(2,1)S(1)}) custom-call(s32[1]{0:T(128)} %bitcast.2.refs_0_, bf16[512,1024]{1,0:T(8,128)(2,1)S(1)} %get-tuple-element.125.refs_12_.refs_1_, bf16[512,1024]{1,0:T(8,128)(2,1)} %collective-permute-done.3.refs_2_, bf16[256,1024]{1,0:T(8,128)(2,1)} %get-tuple-element.136.refs_3_), custom_call_target="tpu_custom_call" | custom-call | flops 20000000000 | bytes 400000000 | tf_op jit(solution)/shard_map/add_split/pallas_call | solution.py:688
  36.4 1.6 %collective-permute-start.9 = (bf16[256,1024]{1,0:T(8,128)(2,1)}, bf16[256,1024]{1,0:T(8,128)(2,1)}, u32[]{:S(2)}, u32[]{:S(2)}) collective-permute-start(bf16[256,1024]{1,0:T(8,128)(2,1)} %get-tuple-element.137.refs_9_), channel_id=1, source_target_pairs={{0,8},{2,10},{4,12},{6,14},{8,0},{10,2},{12,4},{14,6},{16,24},{18,... | collective-permute-start | bytes 1572872 | tf_op jit(solution)/shard_map/ppermute | solution.py:781
  37.9 2.4 %cross_grads.1 = (bf16[768,1024]{1,0:T(8,128)(2,1)S(1)}, bf16[512,1024]{1,0:T(8,128)(2,1)S(1)}, bf16[2,128,512]{2,1,0:T(8,128)(2,1)S(1)}) custom-call(s32[6]{0:T(128)S(1)} %pad_add_fusion.refs_0_, bf16[512,512]{1,0:T(8,128)(2,1)S(1)} %get-tuple-element.126.refs_3_.refs_1_, bf16[512,512]{1,0:T(8,128)(2,1)S(1)} %get-tuple-element.127.refs_2_, ...), custom_call_target="tpu_custom_call" | custom-call | flops 99999997952 | bytes 1000 | tf_op jit(solution)/shard_map/cross_grads/pallas_call | solution.py:688
  40.4 2.8 %self.1 = (bf16[512,512]{1,0:T(8,128)(2,1)S(1)}, bf16[1536,512]{1,0:T(8,128)(2,1)S(1)}) custom-call(f32[512,512]{1,0:T(8,128)S(1)} %get-tuple-element.139.refs_0_.refs_1_, bf16[512,512]{1,0:T(8,128)(2,1)S(1)} %get-tuple-element.141.refs_1_, bf16[512,1536]{1,0:T(8,128)(2,1)S(1)} %get-tuple-element.142.refs_2_, ...), custom_call_target="tpu_custom_call" | custom-call | flops 99999997952 | bytes 1000 | tf_op jit(solution)/shard_map/self/pallas_call | solution.py:688
  43.2 1.2 add_split.18
  44.4 1.6 %collective-permute-start.8 = (bf16[128,1024]{1,0:T(8,128)(2,1)S(1)}, bf16[128,1024]{1,0:T(8,128)(2,1)S(1)}, u32[]{:S(2)}, u32[]{:S(2)}) collective-permute-start(bf16[128,1024]{1,0:T(8,128)(2,1)S(1)} %get-tuple-element.153.refs_3_), channel_id=1, source_target_pairs={{0,4},{2,6},{4,0},{6,2},{8,12},{10,14},{12,8},{14,10},{16,20},{18,... | collective-permute-start | bytes 786440 | tf_op jit(solution)/shard_map/ppermute | solution.py:781
  46.0 1.0 add_split.19
  47.0 0.5 collective-permute-start.13
  47.5 2.9 %self_grads.1 = (bf16[656,1024]{1,0:T(8,128)(2,1)S(1)}, bf16[528,1024]{1,0:T(8,128)(2,1)S(1)}, bf16[2,128,512]{2,1,0:T(8,128)(2,1)S(1)}) custom-call(s32[6]{0:T(128)S(1)} %pad_add_fusion.refs_0_, f32[512,512]{1,0:T(8,128)S(1)} %get-tuple-element.139.refs_0_.refs_1_, f32[8,512]{1,0:T(8,128)S(1)} %get-tuple-element.140.refs_2_, ...), custom_call_target="tpu_custom_call" | custom-call | flops 99999997952 | bytes 1000 | tf_op jit(solution)/shard_map/self_grads/pallas_call | solution.py:688
  50.6 1.2 add_split.20
  51.7 1.4 %collective-permute-start.11 = (bf16[128,1024]{1,0:T(8,128)(2,1)S(1)}, bf16[128,1024]{1,0:T(8,128)(2,1)S(1)}, u32[]{:S(2)}, u32[]{:S(2)}) collective-permute-start(bf16[128,1024]{1,0:T(8,128)(2,1)S(1)} %get-tuple-element.160.refs_3_), channel_id=1, source_target_pairs={{0,2},{2,0},{4,6},{6,4},{8,10},{10,8},{12,14},{14,12},{16,18},{18,... | collective-permute-start | bytes 786440 | tf_op jit(solution)/shard_map/ppermute | solution.py:781
  53.3 1.6 %collective-permute-start.12 = (bf16[64,1024]{1,0:T(8,128)(2,1)S(1)}, bf16[64,1024]{1,0:T(8,128)(2,1)S(1)}, u32[]{:S(2)}, u32[]{:S(2)}) collective-permute-start(bf16[64,1024]{1,0:T(8,128)(2,1)S(1)} %get-tuple-element.161.refs_3_), channel_id=1, source_target_pairs={{0,8},{2,10},{4,12},{6,14},{8,0},{10,2},{12,4},{14,6},{16,24},{18,... | collective-permute-start | bytes 393224 | tf_op jit(solution)/shard_map/ppermute | solution.py:781
  54.9 0.3 add_split.22
  55.1 0.8 collective-permute-start.10
  55.9 0.6 collective-permute-done.13.refs_2_
  56.5 1.2 add_split.23
  57.6 0.6 collective-permute-start.16
  58.2 0.5 collective-permute-done.12.refs_2_
  58.7 2.7 %collective-permute-start.15 = (bf16[32,1024]{1,0:T(8,128)(2,1)S(1)}, bf16[32,1024]{1,0:T(8,128)(2,1)S(1)}, u32[]{:S(2)}, u32[]{:S(2)}) collective-permute-start(bf16[32,1024]{1,0:T(8,128)(2,1)S(1)} %get-tuple-element.168.refs_3_), channel_id=1, source_target_pairs={{0,16},{2,18},{4,20},{6,22},{8,24},{10,26},{12,28},{14,30},{16,0},... | collective-permute-start | bytes 196616 | tf_op jit(solution)/shard_map/ppermute | solution.py:781
  61.4 0.4 collective-permute-start.19
  61.9 3.3 %collective-permute-done.10.refs_2_ = bf16[272,1024]{1,0:T(8,128)(2,1)S(1)} collective-permute-done((bf16[272,1024]{1,0:T(8,128)(2,1)S(1)}, bf16[272,1024]{1,0:T(8,128)(2,1)S(1)}, u32[]{:S(2)}, u32[]{:S(2)}) %collective-permute-start.10) | collective-permute-done | bytes 557088 | tf_op jit(solution)/shard_map/ppermute | solution.py:781
  65.3 1.2 collective-permute-start.14
  66.5 3.7 %collective-permute-done.16.refs_2_ = bf16[128,1024]{1,0:T(8,128)(2,1)S(1)} collective-permute-done((bf16[128,1024]{1,0:T(8,128)(2,1)S(1)}, bf16[128,1024]{1,0:T(8,128)(2,1)S(1)}, u32[]{:S(2)}, u32[]{:S(2)}) %collective-permute-start.16) | collective-permute-done | bytes 262176 | tf_op jit(solution)/shard_map/ppermute | solution.py:781
  70.3 1.6 %collective-permute-start.18 = (bf16[64,1024]{1,0:T(8,128)(2,1)S(1)}, bf16[64,1024]{1,0:T(8,128)(2,1)S(1)}, u32[]{:S(2)}, u32[]{:S(2)}) collective-permute-start(bf16[64,1024]{1,0:T(8,128)(2,1)S(1)} %get-tuple-element.177.refs_2_), channel_id=1, source_target_pairs={{0,4},{2,6},{4,0},{6,2},{8,12},{10,14},{12,8},{14,10},{16,20},{18,... | collective-permute-start | bytes 393224 | tf_op jit(solution)/shard_map/ppermute | solution.py:781
  72.0 1.8 %place.1 = (bf16[2,2,128,512]{3,2,1,0:T(8,128)(2,1)}, bf16[2,2,128,512]{3,2,1,0:T(8,128)(2,1)}, bf16[2,2,128,512]{3,2,1,0:T(8,128)(2,1)}) custom-call(s32[6]{0:T(128)S(1)} %pad_add_fusion.refs_0_, bf16[2,128,512]{2,1,0:T(8,128)(2,1)S(1)} %get-tuple-element.108.refs_1_, bf16[2,128,512]{2,1,0:T(8,128)(2,1)S(1)} %get-tuple-element.138.refs_2_, ...), custom_call_target="tpu_custom_call" | custom-call | flops 20000000000 | bytes 400000000 | tf_op jit(solution)/shard_map/place/pallas_call | solution.py:688
  73.9 2.1 %collective-permute-start.17 = (bf16[80,1024]{1,0:T(8,128)(2,1)S(1)}, bf16[80,1024]{1,0:T(8,128)(2,1)S(1)}, u32[]{:S(2)}, u32[]{:S(2)}) collective-permute-start(bf16[80,1024]{1,0:T(8,128)(2,1)S(1)} %get-tuple-element.179.refs_3_), channel_id=1, source_target_pairs={{0,8},{2,10},{4,12},{6,14},{8,0},{10,2},{12,4},{14,6},{16,24},{18,... | collective-permute-start | bytes 491528 | tf_op jit(solution)/shard_map/ppermute | solution.py:781
  76.0 0.6 collective-permute-start.22
  76.6 1.0 collective-permute-start.21
  77.6 3.1 %collective-permute-done.17.refs_2_ = bf16[80,1024]{1,0:T(8,128)(2,1)S(1)} collective-permute-done((bf16[80,1024]{1,0:T(8,128)(2,1)S(1)}, bf16[80,1024]{1,0:T(8,128)(2,1)S(1)}, u32[]{:S(2)}, u32[]{:S(2)}) %collective-permute-start.17) | collective-permute-done | bytes 163872 | tf_op jit(solution)/shard_map/ppermute | solution.py:781
  80.7 2.0 %collective-permute-start.20 = (bf16[48,1024]{1,0:T(8,128)(2,1)S(1)}, bf16[48,1024]{1,0:T(8,128)(2,1)S(1)}, u32[]{:S(2)}, u32[]{:S(2)}) collective-permute-start(bf16[48,1024]{1,0:T(8,128)(2,1)S(1)} %get-tuple-element.185.refs_3_), channel_id=1, source_target_pairs={{0,16},{2,18},{4,20},{6,22},{8,24},{10,26},{12,28},{14,30},{16,0},... | collective-permute-start | bytes 294920 | tf_op jit(solution)/shard_map/ppermute | solution.py:781
  82.8 1.0 collective-permute-start.27
  83.8 1.5 %collective-permute-start.26 = (bf16[32,1024]{1,0:T(8,128)(2,1)S(1)}, bf16[32,1024]{1,0:T(8,128)(2,1)S(1)}, u32[]{:S(2)}, u32[]{:S(2)}) collective-permute-start(bf16[32,1024]{1,0:T(8,128)(2,1)S(1)} %add_last.5.refs_2_.refs_1_), channel_id=1, source_target_pairs={{0,4},{2,6},{4,0},{6,2},{8,12},{10,14},{12,8},{14,10},{16,20},{18,... | collective-permute-start | bytes 196616 | tf_op jit(solution)/shard_map/ppermute | solution.py:781
  85.3 1.5 %collective-permute-start.25 = (bf16[32,1024]{1,0:T(8,128)(2,1)S(1)}, bf16[32,1024]{1,0:T(8,128)(2,1)S(1)}, u32[]{:S(2)}, u32[]{:S(2)}) collective-permute-start(bf16[32,1024]{1,0:T(8,128)(2,1)S(1)} %add_last.6.refs_2_.refs_1_), channel_id=1, source_target_pairs={{0,16},{2,18},{4,20},{6,22},{8,24},{10,26},{12,28},{14,30},{16,0},... | collective-permute-start | bytes 196616 | tf_op jit(solution)/shard_map/ppermute | solution.py:781
  86.8 2.8 %collective-permute-done.20.refs_1_ = bf16[48,1024]{1,0:T(8,128)(2,1)S(1)} collective-permute-done((bf16[48,1024]{1,0:T(8,128)(2,1)S(1)}, bf16[48,1024]{1,0:T(8,128)(2,1)S(1)}, u32[]{:S(2)}, u32[]{:S(2)}) %collective-permute-start.20) | collective-permute-done | bytes 98336 | tf_op jit(solution)/shard_map/ppermute | solution.py:781
  89.8 1.2 collective-permute-start.31
  90.9 2.8 %collective-permute-start.29 = (bf16[64,1024]{1,0:T(8,128)(2,1)S(1)}, bf16[64,1024]{1,0:T(8,128)(2,1)S(1)}, u32[]{:S(2)}, u32[]{:S(2)}) collective-permute-start(bf16[64,1024]{1,0:T(8,128)(2,1)S(1)} %join.14.refs_3_.refs_1_), channel_id=1, source_target_pairs={{0,16},{2,18},{4,20},{6,22},{8,24},{10,26},{12,28},{14,30},{16,0},... | collective-permute-start | bytes 393224 | tf_op jit(solution)/shard_map/ppermute | solution.py:781
  93.7 1.2 collective-permute-start.30
  94.9 1.5 %collective-permute-done.24.refs_2_ = bf16[32,1024]{1,0:T(8,128)(2,1)S(1)} collective-permute-done((bf16[32,1024]{1,0:T(8,128)(2,1)S(1)}, bf16[32,1024]{1,0:T(8,128)(2,1)S(1)}, u32[]{:S(2)}, u32[]{:S(2)}) %collective-permute-start.24) | collective-permute-done | bytes 65568 | tf_op jit(solution)/shard_map/ppermute | solution.py:781
  96.6 2.6 %collective-permute-done.30.refs_2_ = bf16[64,1024]{1,0:T(8,128)(2,1)S(1)} collective-permute-done((bf16[64,1024]{1,0:T(8,128)(2,1)S(1)}, bf16[64,1024]{1,0:T(8,128)(2,1)S(1)}, u32[]{:S(2)}, u32[]{:S(2)}) %collective-permute-start.30) | collective-permute-done | bytes 131104 | tf_op jit(solution)/shard_map/ppermute | solution.py:781
  99.3 2.0 %collective-permute-start.35 = (bf16[128,1024]{1,0:T(8,128)(2,1)S(1)}, bf16[128,1024]{1,0:T(8,128)(2,1)S(1)}, u32[]{:S(2)}, u32[]{:S(2)}) collective-permute-start(bf16[128,1024]{1,0:T(8,128)(2,1)S(1)} %join.18.refs_3_.refs_1_), channel_id=1, source_target_pairs={{0,8},{2,10},{4,12},{6,14},{8,0},{10,2},{12,4},{14,6},{16,24},{18,... | collective-permute-start | bytes 786440 | tf_op jit(solution)/shard_map/ppermute | solution.py:781
  101.4 1.7 %collective-permute-start.34 = (bf16[128,1024]{1,0:T(8,128)(2,1)S(1)}, bf16[128,1024]{1,0:T(8,128)(2,1)S(1)}, u32[]{:S(2)}, u32[]{:S(2)}) collective-permute-start(bf16[128,1024]{1,0:T(8,128)(2,1)S(1)} %join.19.refs_3_.refs_1_), channel_id=1, source_target_pairs={{0,2},{2,0},{4,6},{6,4},{8,10},{10,8},{12,14},{14,12},{16,18},{18,... | collective-permute-start | bytes 786440 | tf_op jit(solution)/shard_map/ppermute | solution.py:781
  103.1 1.4 %collective-permute-start.32 = (bf16[128,1024]{1,0:T(8,128)(2,1)S(1)}, bf16[128,1024]{1,0:T(8,128)(2,1)S(1)}, u32[]{:S(2)}, u32[]{:S(2)}) collective-permute-start(bf16[128,1024]{1,0:T(8,128)(2,1)S(1)} %join.20.refs_3_.refs_1_), channel_id=1, source_target_pairs={{0,4},{2,6},{4,0},{6,2},{8,12},{10,14},{12,8},{14,10},{16,20},{18,... | collective-permute-start | bytes 786440 | tf_op jit(solution)/shard_map/ppermute | solution.py:781
  104.4 2.4 %collective-permute-done.35.refs_2_ = bf16[128,1024]{1,0:T(8,128)(2,1)S(1)} collective-permute-done((bf16[128,1024]{1,0:T(8,128)(2,1)S(1)}, bf16[128,1024]{1,0:T(8,128)(2,1)S(1)}, u32[]{:S(2)}, u32[]{:S(2)}) %collective-permute-start.35) | collective-permute-done | bytes 262176 | tf_op jit(solution)/shard_map/ppermute | solution.py:781
  106.9 0.5 collective-permute-start.37
  107.4 4.0 %collective-permute-done.34.refs_2_ = bf16[128,1024]{1,0:T(8,128)(2,1)S(1)} collective-permute-done((bf16[128,1024]{1,0:T(8,128)(2,1)S(1)}, bf16[128,1024]{1,0:T(8,128)(2,1)S(1)}, u32[]{:S(2)}, u32[]{:S(2)}) %collective-permute-start.34) | collective-permute-done | bytes 262176 | tf_op jit(solution)/shard_map/ppermute | solution.py:781
  111.5 2.4 %collective-permute-start.38 = (bf16[256,1024]{1,0:T(8,128)(2,1)S(1)}, bf16[256,1024]{1,0:T(8,128)(2,1)S(1)}, u32[]{:S(2)}, u32[]{:S(2)}) collective-permute-start(bf16[256,1024]{1,0:T(8,128)(2,1)S(1)} %join.22.refs_3_.refs_1_), channel_id=1, source_target_pairs={{0,8},{2,10},{4,12},{6,14},{8,0},{10,2},{12,4},{14,6},{16,24},{18,... | collective-permute-start | bytes 1572872 | tf_op jit(solution)/shard_map/ppermute | solution.py:781
  113.9 1.6 %unpack.4 = (f32[8,128]{1,0:T(8,128)S(1)}, f32[2048,256]{1,0:T(8,128)}) custom-call(s32[1]{0:T(128)} %bitcast.3.refs_0_, bf16[256,1024]{1,0:T(8,128)(2,1)S(1)} %join.17.refs_3_.refs_1_, bf16[256,1024]{1,0:T(8,128)(2,1)S(1)} %collective-permute-done.33.refs_2_, bf16[256,1024]{1,0:T(8,128)(2,1)S(1)} %join.22.refs_3_.refs_1_), custom_call_target="tpu_custom_call" | custom-call | flops 20000000000 | bytes 400000000 | tf_op jit(solution)/shard_map/unpack/pallas_call | solution.py:688
  115.6 0.7 collective-permute-start.36
  116.3 0.7 collective-permute-done.37.refs_2_
  117.1 1.6 %unpack.5 = (f32[8,128]{1,0:T(8,128)S(1)}, f32[512,512]{1,0:T(8,128)}, f32[512,256]{1,0:T(8,128)}, f32[512,256]{1,0:T(8,128)}) custom-call(s32[1]{0:T(128)} %bitcast.3.refs_0_, bf16[256,1024]{1,0:T(8,128)(2,1)S(1)} %join.21.refs_3_.refs_1_, bf16[256,1024]{1,0:T(8,128)(2,1)S(1)} %collective-permute-done.37.refs_2_, bf16[256,1024]{1,0:T(8,128)(2,1)S(1)} %join.23.refs_3_.refs_1_), custom_call_target="tpu_custom_call" | custom-call | flops 20000000000 | bytes 400000000 | tf_op jit(solution)/shard_map/unpack/pallas_call | solution.py:688
  118.7 6.2 %collective-permute-done.36.refs_2_ = bf16[256,1024]{1,0:T(8,128)(2,1)S(1)} collective-permute-done((bf16[256,1024]{1,0:T(8,128)(2,1)S(1)}, bf16[256,1024]{1,0:T(8,128)(2,1)S(1)}, u32[]{:S(2)}, u32[]{:S(2)}) %collective-permute-start.36) | collective-permute-done | bytes 524320 | tf_op jit(solution)/shard_map/ppermute | solution.py:781
  124.9 1.6 %unpack.6 = (f32[8,128]{1,0:T(8,128)S(1)}, f32[512,768]{1,0:T(8,128)}, f32[512,256]{1,0:T(8,128)}, f32[3,256]{1,0:T(4,128)}, f32[3,256]{1,0:T(4,128)}, /*index=5*/f32[8,256]{1,0:T(8,128)}) custom-call(s32[1]{0:T(128)} %bitcast.3.refs_0_, bf16[256,1024]{1,0:T(8,128)(2,1)S(1)} %join.23.refs_3_.refs_1_, bf16[256,1024]{1,0:T(8,128)(2,1)S(1)} %collective-permute-done.36.refs_2_, ...), custom_call_target="tpu_custom_call" | custom-call | flops 20000000000 | bytes 400000000 | tf_op jit(solution)/shard_map/unpack/pallas_call | solution.py:688
  126.5 1.5 %unpack.7 = (f32[8,128]{1,0:T(8,128)}, f32[512,1024]{1,0:T(8,128)}) custom-call(s32[1]{0:T(128)} %bitcast.2.refs_0_, bf16[256,1024]{1,0:T(8,128)(2,1)S(1)} %join.22.refs_3_.refs_1_, bf16[256,1024]{1,0:T(8,128)(2,1)S(1)} %collective-permute-done.38.refs_2_, f32[8,128]{1,0:T(8,128)S(1)} %get-tuple-element.197.refs_3_), custom_call_target="tpu_custom_call" | custom-call | flops 20000000000 | bytes 400000000 | tf_op jit(solution)/shard_map/unpack/pallas_call | solution.py:688
  (61 shorter events, 1.8 us)
Async XLA Ops:
  0.6 3.8 %collective-permute-start = (bf16[2,2,128,512]{3,2,1,0:T(8,128)(2,1)}, bf16[2,2,128,512]{3,2,1,0:T(8,128)(2,1)S(1)}, u32[]{:S(2)}, u32[]{:S(2)}) collective-permute-start(bf16[2,2,128,512]{3,2,1,0:T(8,128)(2,1)} %refs_4_.1), channel_id=1, source_target_pairs={{0,1},{1,0},{2,3},{3,2},{4,5},{5,4},{6,7},{7,6},{8,9},{9,8},{10,11... | collective-permute-start | bytes 1572872 | tf_op jit(solution)/shard_map/ppermute | solution.py:732
  1.2 3.3 %collective-permute-start.1 = (bf16[2,2,128,512]{3,2,1,0:T(8,128)(2,1)}, bf16[2,2,128,512]{3,2,1,0:T(8,128)(2,1)S(1)}, u32[]{:S(2)}, u32[]{:S(2)}) collective-permute-start(bf16[2,2,128,512]{3,2,1,0:T(8,128)(2,1)} %refs_5_.1), channel_id=1, source_target_pairs={{0,1},{1,0},{2,3},{3,2},{4,5},{5,4},{6,7},{7,6},{8,9},{9,8},{10,11... | collective-permute-start | bytes 1572872 | tf_op jit(solution)/shard_map/ppermute | solution.py:733
  1.2 3.2 %collective-permute-start.2 = (bf16[2,2,128,512]{3,2,1,0:T(8,128)(2,1)}, bf16[2,2,128,512]{3,2,1,0:T(8,128)(2,1)S(1)}, u32[]{:S(2)}, u32[]{:S(2)}) collective-permute-start(bf16[2,2,128,512]{3,2,1,0:T(8,128)(2,1)} %refs_6_.1), channel_id=1, source_target_pairs={{0,1},{1,0},{2,3},{3,2},{4,5},{5,4},{6,7},{7,6},{8,9},{9,8},{10,11... | collective-permute-start | bytes 1572872 | tf_op jit(solution)/shard_map/ppermute | solution.py:734
  23.5 5.8 %collective-permute-start.4 = (bf16[512,1024]{1,0:T(8,128)(2,1)}, bf16[512,1024]{1,0:T(8,128)(2,1)}, u32[]{:S(2)}, u32[]{:S(2)}) collective-permute-start(bf16[512,1024]{1,0:T(8,128)(2,1)} %get-tuple-element.135), channel_id=1, source_target_pairs={{0,1},{1,0},{2,3},{3,2},{4,5},{5,4},{6,7},{7,6},{8,9},{9,8},{10,11... | collective-permute-start | bytes 3145736 | tf_op jit(solution)/shard_map/ppermute | solution.py:920
  23.7 10.5 %collective-permute-start.3 = (bf16[512,1024]{1,0:T(8,128)(2,1)}, bf16[512,1024]{1,0:T(8,128)(2,1)}, u32[]{:S(2)}, u32[]{:S(2)}) collective-permute-start(bf16[512,1024]{1,0:T(8,128)(2,1)} %get-tuple-element.133), channel_id=1, source_target_pairs={{0,1},{1,0},{2,3},{3,2},{4,5},{5,4},{6,7},{7,6},{8,9},{9,8},{10,11... | collective-permute-start | bytes 3145736 | tf_op jit(solution)/shard_map/ppermute | solution.py:919
  31.5 11.7 %collective-permute-start.6 = (bf16[256,1024]{1,0:T(8,128)(2,1)}, bf16[256,1024]{1,0:T(8,128)(2,1)}, u32[]{:S(2)}, u32[]{:S(2)}) collective-permute-start(bf16[256,1024]{1,0:T(8,128)(2,1)} %get-tuple-element.136.refs_3_), channel_id=1, source_target_pairs={{0,2},{2,0},{4,6},{6,4},{8,10},{10,8},{12,14},{14,12},{16,18},{18,... | collective-permute-start | bytes 1572872 | tf_op jit(solution)/shard_map/ppermute | solution.py:781
  36.4 14.2 %collective-permute-start.9 = (bf16[256,1024]{1,0:T(8,128)(2,1)}, bf16[256,1024]{1,0:T(8,128)(2,1)}, u32[]{:S(2)}, u32[]{:S(2)}) collective-permute-start(bf16[256,1024]{1,0:T(8,128)(2,1)} %get-tuple-element.137.refs_9_), channel_id=1, source_target_pairs={{0,8},{2,10},{4,12},{6,14},{8,0},{10,2},{12,4},{14,6},{16,24},{18,... | collective-permute-start | bytes 1572872 | tf_op jit(solution)/shard_map/ppermute | solution.py:781
  40.3 5.7 %collective-permute-start.5 = (bf16[768,1024]{1,0:T(8,128)(2,1)S(1)}, bf16[768,1024]{1,0:T(8,128)(2,1)S(1)}, u32[]{:S(2)}, u32[]{:S(2)}) collective-permute-start(bf16[768,1024]{1,0:T(8,128)(2,1)S(1)} %get-tuple-element.146.refs_6_), channel_id=1, source_target_pairs={{0,1},{1,0},{2,3},{3,2},{4,5},{5,4},{6,7},{7,6},{8,9},{9,8},{10,11... | collective-permute-start | bytes 4718600 | tf_op jit(solution)/shard_map/ppermute | solution.py:872
  44.4 8.8 %collective-permute-start.8 = (bf16[128,1024]{1,0:T(8,128)(2,1)S(1)}, bf16[128,1024]{1,0:T(8,128)(2,1)S(1)}, u32[]{:S(2)}, u32[]{:S(2)}) collective-permute-start(bf16[128,1024]{1,0:T(8,128)(2,1)S(1)} %get-tuple-element.153.refs_3_), channel_id=1, source_target_pairs={{0,4},{2,6},{4,0},{6,2},{8,12},{10,14},{12,8},{14,10},{16,20},{18,... | collective-permute-start | bytes 786440 | tf_op jit(solution)/shard_map/ppermute | solution.py:781
  47.0 9.5 %collective-permute-start.13 = (bf16[256,1024]{1,0:T(8,128)(2,1)}, bf16[256,1024]{1,0:T(8,128)(2,1)}, u32[]{:S(2)}, u32[]{:S(2)}) collective-permute-start(bf16[256,1024]{1,0:T(8,128)(2,1)} %get-tuple-element.154.refs_8_), channel_id=1, source_target_pairs={{0,2},{2,0},{4,6},{6,4},{8,10},{10,8},{12,14},{14,12},{16,18},{18,... | collective-permute-start | bytes 1572872 | tf_op jit(solution)/shard_map/ppermute | solution.py:781
  50.4 4.5 %collective-permute-start.7 = (bf16[656,1024]{1,0:T(8,128)(2,1)S(1)}, bf16[656,1024]{1,0:T(8,128)(2,1)S(1)}, u32[]{:S(2)}, u32[]{:S(2)}) collective-permute-start(bf16[656,1024]{1,0:T(8,128)(2,1)S(1)} %get-tuple-element.156.refs_3_), channel_id=1, source_target_pairs={{0,1},{1,0},{2,3},{3,2},{4,5},{5,4},{6,7},{7,6},{8,9},{9,8},{10,11... | collective-permute-start | bytes 4030472 | tf_op jit(solution)/shard_map/ppermute | solution.py:903
  51.7 9.6 %collective-permute-start.11 = (bf16[128,1024]{1,0:T(8,128)(2,1)S(1)}, bf16[128,1024]{1,0:T(8,128)(2,1)S(1)}, u32[]{:S(2)}, u32[]{:S(2)}) collective-permute-start(bf16[128,1024]{1,0:T(8,128)(2,1)S(1)} %get-tuple-element.160.refs_3_), channel_id=1, source_target_pairs={{0,2},{2,0},{4,6},{6,4},{8,10},{10,8},{12,14},{14,12},{16,18},{18,... | collective-permute-start | bytes 786440 | tf_op jit(solution)/shard_map/ppermute | solution.py:781
  53.3 5.4 %collective-permute-start.12 = (bf16[64,1024]{1,0:T(8,128)(2,1)S(1)}, bf16[64,1024]{1,0:T(8,128)(2,1)S(1)}, u32[]{:S(2)}, u32[]{:S(2)}) collective-permute-start(bf16[64,1024]{1,0:T(8,128)(2,1)S(1)} %get-tuple-element.161.refs_3_), channel_id=1, source_target_pairs={{0,8},{2,10},{4,12},{6,14},{8,0},{10,2},{12,4},{14,6},{16,24},{18,... | collective-permute-start | bytes 393224 | tf_op jit(solution)/shard_map/ppermute | solution.py:781
  55.1 10.0 %collective-permute-start.10 = (bf16[272,1024]{1,0:T(8,128)(2,1)S(1)}, bf16[272,1024]{1,0:T(8,128)(2,1)S(1)}, u32[]{:S(2)}, u32[]{:S(2)}) collective-permute-start(bf16[272,1024]{1,0:T(8,128)(2,1)S(1)} %get-tuple-element.163.refs_3_), channel_id=1, source_target_pairs={{0,2},{2,0},{4,6},{6,4},{8,10},{10,8},{12,14},{14,12},{16,18},{18,... | collective-permute-start | bytes 1671176 | tf_op jit(solution)/shard_map/ppermute | solution.py:781
  57.6 12.6 %collective-permute-start.16 = (bf16[128,1024]{1,0:T(8,128)(2,1)S(1)}, bf16[128,1024]{1,0:T(8,128)(2,1)S(1)}, u32[]{:S(2)}, u32[]{:S(2)}) collective-permute-start(bf16[128,1024]{1,0:T(8,128)(2,1)S(1)} %get-tuple-element.167.refs_3_), channel_id=1, source_target_pairs={{0,8},{2,10},{4,12},{6,14},{8,0},{10,2},{12,4},{14,6},{16,24},{18,... | collective-permute-start | bytes 786440 | tf_op jit(solution)/shard_map/ppermute | solution.py:781
  58.7 13.2 %collective-permute-start.15 = (bf16[32,1024]{1,0:T(8,128)(2,1)S(1)}, bf16[32,1024]{1,0:T(8,128)(2,1)S(1)}, u32[]{:S(2)}, u32[]{:S(2)}) collective-permute-start(bf16[32,1024]{1,0:T(8,128)(2,1)S(1)} %get-tuple-element.168.refs_3_), channel_id=1, source_target_pairs={{0,16},{2,18},{4,20},{6,22},{8,24},{10,26},{12,28},{14,30},{16,0},... | collective-permute-start | bytes 196616 | tf_op jit(solution)/shard_map/ppermute | solution.py:781
  61.4 14.5 %collective-permute-start.19 = (bf16[64,1024]{1,0:T(8,128)(2,1)S(1)}, bf16[64,1024]{1,0:T(8,128)(2,1)S(1)}, u32[]{:S(2)}, u32[]{:S(2)}) collective-permute-start(bf16[64,1024]{1,0:T(8,128)(2,1)S(1)} %get-tuple-element.169.refs_3_), channel_id=1, source_target_pairs={{0,16},{2,18},{4,20},{6,22},{8,24},{10,26},{12,28},{14,30},{16,0},... | collective-permute-start | bytes 393224 | tf_op jit(solution)/shard_map/ppermute | solution.py:781
  65.3 8.5 %collective-permute-start.14 = (bf16[144,1024]{1,0:T(8,128)(2,1)S(1)}, bf16[144,1024]{1,0:T(8,128)(2,1)S(1)}, u32[]{:S(2)}, u32[]{:S(2)}) collective-permute-start(bf16[144,1024]{1,0:T(8,128)(2,1)S(1)} %get-tuple-element.170.refs_6_.refs_3_), channel_id=1, source_target_pairs={{0,4},{2,6},{4,0},{6,2},{8,12},{10,14},{12,8},{14,10},{16,20},{18,... | collective-permute-start | bytes 884744 | tf_op jit(solution)/shard_map/ppermute | solution.py:781
  70.3 6.3 %collective-permute-start.18 = (bf16[64,1024]{1,0:T(8,128)(2,1)S(1)}, bf16[64,1024]{1,0:T(8,128)(2,1)S(1)}, u32[]{:S(2)}, u32[]{:S(2)}) collective-permute-start(bf16[64,1024]{1,0:T(8,128)(2,1)S(1)} %get-tuple-element.177.refs_2_), channel_id=1, source_target_pairs={{0,4},{2,6},{4,0},{6,2},{8,12},{10,14},{12,8},{14,10},{16,20},{18,... | collective-permute-start | bytes 393224 | tf_op jit(solution)/shard_map/ppermute | solution.py:781
  71.9 10.8 %collective-permute-start.23 = (bf16[32,1024]{1,0:T(8,128)(2,1)S(1)}, bf16[32,1024]{1,0:T(8,128)(2,1)S(1)}, u32[]{:S(2)}, u32[]{:S(2)}) collective-permute-start(bf16[32,1024]{1,0:T(8,128)(2,1)S(1)} %add_last.4.refs_3_.refs_1_), channel_id=1, source_target_pairs={{0,16},{2,18},{4,20},{6,22},{8,24},{10,26},{12,28},{14,30},{16,0},... | collective-permute-start | bytes 196616 | tf_op jit(solution)/shard_map/ppermute | solution.py:781
  73.9 6.8 %collective-permute-start.17 = (bf16[80,1024]{1,0:T(8,128)(2,1)S(1)}, bf16[80,1024]{1,0:T(8,128)(2,1)S(1)}, u32[]{:S(2)}, u32[]{:S(2)}) collective-permute-start(bf16[80,1024]{1,0:T(8,128)(2,1)S(1)} %get-tuple-element.179.refs_3_), channel_id=1, source_target_pairs={{0,8},{2,10},{4,12},{6,14},{8,0},{10,2},{12,4},{14,6},{16,24},{18,... | collective-permute-start | bytes 491528 | tf_op jit(solution)/shard_map/ppermute | solution.py:781
  76.0 7.7 %collective-permute-start.22 = (bf16[32,1024]{1,0:T(8,128)(2,1)S(1)}, bf16[32,1024]{1,0:T(8,128)(2,1)S(1)}, u32[]{:S(2)}, u32[]{:S(2)}) collective-permute-start(bf16[32,1024]{1,0:T(8,128)(2,1)S(1)} %get-tuple-element.182.refs_3_), channel_id=1, source_target_pairs={{0,4},{2,6},{4,0},{6,2},{8,12},{10,14},{12,8},{14,10},{16,20},{18,... | collective-permute-start | bytes 196616 | tf_op jit(solution)/shard_map/ppermute | solution.py:781
  76.6 8.6 %collective-permute-start.21 = (bf16[32,1024]{1,0:T(8,128)(2,1)S(1)}, bf16[32,1024]{1,0:T(8,128)(2,1)S(1)}, u32[]{:S(2)}, u32[]{:S(2)}) collective-permute-start(bf16[32,1024]{1,0:T(8,128)(2,1)S(1)} %get-tuple-element.183.refs_3_), channel_id=1, source_target_pairs={{0,16},{2,18},{4,20},{6,22},{8,24},{10,26},{12,28},{14,30},{16,0},... | collective-permute-start | bytes 196616 | tf_op jit(solution)/shard_map/ppermute | solution.py:781
  80.7 8.9 %collective-permute-start.20 = (bf16[48,1024]{1,0:T(8,128)(2,1)S(1)}, bf16[48,1024]{1,0:T(8,128)(2,1)S(1)}, u32[]{:S(2)}, u32[]{:S(2)}) collective-permute-start(bf16[48,1024]{1,0:T(8,128)(2,1)S(1)} %get-tuple-element.185.refs_3_), channel_id=1, source_target_pairs={{0,16},{2,18},{4,20},{6,22},{8,24},{10,26},{12,28},{14,30},{16,0},... | collective-permute-start | bytes 294920 | tf_op jit(solution)/shard_map/ppermute | solution.py:781
  82.8 7.0 %collective-permute-start.27 = (bf16[64,1024]{1,0:T(8,128)(2,1)S(1)}, bf16[64,1024]{1,0:T(8,128)(2,1)S(1)}, u32[]{:S(2)}, u32[]{:S(2)}) collective-permute-start(bf16[64,1024]{1,0:T(8,128)(2,1)S(1)} %join.12.refs_2_.refs_1_), channel_id=1, source_target_pairs={{0,8},{2,10},{4,12},{6,14},{8,0},{10,2},{12,4},{14,6},{16,24},{18,... | collective-permute-start | bytes 393224 | tf_op jit(solution)/shard_map/ppermute | solution.py:781
  83.8 7.2 %collective-permute-start.26 = (bf16[32,1024]{1,0:T(8,128)(2,1)S(1)}, bf16[32,1024]{1,0:T(8,128)(2,1)S(1)}, u32[]{:S(2)}, u32[]{:S(2)}) collective-permute-start(bf16[32,1024]{1,0:T(8,128)(2,1)S(1)} %add_last.5.refs_2_.refs_1_), channel_id=1, source_target_pairs={{0,4},{2,6},{4,0},{6,2},{8,12},{10,14},{12,8},{14,10},{16,20},{18,... | collective-permute-start | bytes 196616 | tf_op jit(solution)/shard_map/ppermute | solution.py:781
  85.3 8.4 %collective-permute-start.25 = (bf16[32,1024]{1,0:T(8,128)(2,1)S(1)}, bf16[32,1024]{1,0:T(8,128)(2,1)S(1)}, u32[]{:S(2)}, u32[]{:S(2)}) collective-permute-start(bf16[32,1024]{1,0:T(8,128)(2,1)S(1)} %add_last.6.refs_2_.refs_1_), channel_id=1, source_target_pairs={{0,16},{2,18},{4,20},{6,22},{8,24},{10,26},{12,28},{14,30},{16,0},... | collective-permute-start | bytes 196616 | tf_op jit(solution)/shard_map/ppermute | solution.py:781
  89.6 6.8 %collective-permute-start.24 = (bf16[32,1024]{1,0:T(8,128)(2,1)S(1)}, bf16[32,1024]{1,0:T(8,128)(2,1)S(1)}, u32[]{:S(2)}, u32[]{:S(2)}) collective-permute-start(bf16[32,1024]{1,0:T(8,128)(2,1)S(1)} %get-tuple-element.188.refs_3_.refs_1_), channel_id=1, source_target_pairs={{0,16},{2,18},{4,20},{6,22},{8,24},{10,26},{12,28},{14,30},{16,0},... | collective-permute-start | bytes 196616 | tf_op jit(solution)/shard_map/ppermute | solution.py:781
  89.8 6.8 %collective-permute-start.31 = (bf16[128,1024]{1,0:T(8,128)(2,1)S(1)}, bf16[128,1024]{1,0:T(8,128)(2,1)S(1)}, u32[]{:S(2)}, u32[]{:S(2)}) collective-permute-start(bf16[128,1024]{1,0:T(8,128)(2,1)S(1)} %join.13.refs_3_.refs_1_), channel_id=1, source_target_pairs={{0,4},{2,6},{4,0},{6,2},{8,12},{10,14},{12,8},{14,10},{16,20},{18,... | collective-permute-start | bytes 786440 | tf_op jit(solution)/shard_map/ppermute | solution.py:781
  90.9 10.4 %collective-permute-start.29 = (bf16[64,1024]{1,0:T(8,128)(2,1)S(1)}, bf16[64,1024]{1,0:T(8,128)(2,1)S(1)}, u32[]{:S(2)}, u32[]{:S(2)}) collective-permute-start(bf16[64,1024]{1,0:T(8,128)(2,1)S(1)} %join.14.refs_3_.refs_1_), channel_id=1, source_target_pairs={{0,16},{2,18},{4,20},{6,22},{8,24},{10,26},{12,28},{14,30},{16,0},... | collective-permute-start | bytes 393224 | tf_op jit(solution)/shard_map/ppermute | solution.py:781
  93.7 5.6 %collective-permute-start.30 = (bf16[64,1024]{1,0:T(8,128)(2,1)S(1)}, bf16[64,1024]{1,0:T(8,128)(2,1)S(1)}, u32[]{:S(2)}, u32[]{:S(2)}) collective-permute-start(bf16[64,1024]{1,0:T(8,128)(2,1)S(1)} %join.15.refs_3_.refs_1_), channel_id=1, source_target_pairs={{0,4},{2,6},{4,0},{6,2},{8,12},{10,14},{12,8},{14,10},{16,20},{18,... | collective-permute-start | bytes 393224 | tf_op jit(solution)/shard_map/ppermute | solution.py:781
  96.4 6.6 %collective-permute-start.28 = (bf16[64,1024]{1,0:T(8,128)(2,1)S(1)}, bf16[64,1024]{1,0:T(8,128)(2,1)S(1)}, u32[]{:S(2)}, u32[]{:S(2)}) collective-permute-start(bf16[64,1024]{1,0:T(8,128)(2,1)S(1)} %join.16.refs_3_.refs_1_), channel_id=1, source_target_pairs={{0,8},{2,10},{4,12},{6,14},{8,0},{10,2},{12,4},{14,6},{16,24},{18,... | collective-permute-start | bytes 393224 | tf_op jit(solution)/shard_map/ppermute | solution.py:781
  96.6 17.3 %collective-permute-start.33 = (bf16[256,1024]{1,0:T(8,128)(2,1)S(1)}, bf16[256,1024]{1,0:T(8,128)(2,1)S(1)}, u32[]{:S(2)}, u32[]{:S(2)}) collective-permute-start(bf16[256,1024]{1,0:T(8,128)(2,1)S(1)} %join.17.refs_3_.refs_1_), channel_id=1, source_target_pairs={{0,2},{2,0},{4,6},{6,4},{8,10},{10,8},{12,14},{14,12},{16,18},{18,... | collective-permute-start | bytes 1572872 | tf_op jit(solution)/shard_map/ppermute | solution.py:781
  99.3 7.5 %collective-permute-start.35 = (bf16[128,1024]{1,0:T(8,128)(2,1)S(1)}, bf16[128,1024]{1,0:T(8,128)(2,1)S(1)}, u32[]{:S(2)}, u32[]{:S(2)}) collective-permute-start(bf16[128,1024]{1,0:T(8,128)(2,1)S(1)} %join.18.refs_3_.refs_1_), channel_id=1, source_target_pairs={{0,8},{2,10},{4,12},{6,14},{8,0},{10,2},{12,4},{14,6},{16,24},{18,... | collective-permute-start | bytes 786440 | tf_op jit(solution)/shard_map/ppermute | solution.py:781
  101.4 10.1 %collective-permute-start.34 = (bf16[128,1024]{1,0:T(8,128)(2,1)S(1)}, bf16[128,1024]{1,0:T(8,128)(2,1)S(1)}, u32[]{:S(2)}, u32[]{:S(2)}) collective-permute-start(bf16[128,1024]{1,0:T(8,128)(2,1)S(1)} %join.19.refs_3_.refs_1_), channel_id=1, source_target_pairs={{0,2},{2,0},{4,6},{6,4},{8,10},{10,8},{12,14},{14,12},{16,18},{18,... | collective-permute-start | bytes 786440 | tf_op jit(solution)/shard_map/ppermute | solution.py:781
  103.1 12.5 %collective-permute-start.32 = (bf16[128,1024]{1,0:T(8,128)(2,1)S(1)}, bf16[128,1024]{1,0:T(8,128)(2,1)S(1)}, u32[]{:S(2)}, u32[]{:S(2)}) collective-permute-start(bf16[128,1024]{1,0:T(8,128)(2,1)S(1)} %join.20.refs_3_.refs_1_), channel_id=1, source_target_pairs={{0,4},{2,6},{4,0},{6,2},{8,12},{10,14},{12,8},{14,10},{16,20},{18,... | collective-permute-start | bytes 786440 | tf_op jit(solution)/shard_map/ppermute | solution.py:781
  106.9 10.2 %collective-permute-start.37 = (bf16[256,1024]{1,0:T(8,128)(2,1)S(1)}, bf16[256,1024]{1,0:T(8,128)(2,1)S(1)}, u32[]{:S(2)}, u32[]{:S(2)}) collective-permute-start(bf16[256,1024]{1,0:T(8,128)(2,1)S(1)} %join.21.refs_3_.refs_1_), channel_id=1, source_target_pairs={{0,2},{2,0},{4,6},{6,4},{8,10},{10,8},{12,14},{14,12},{16,18},{18,... | collective-permute-start | bytes 1572872 | tf_op jit(solution)/shard_map/ppermute | solution.py:781
  111.5 15.0 %collective-permute-start.38 = (bf16[256,1024]{1,0:T(8,128)(2,1)S(1)}, bf16[256,1024]{1,0:T(8,128)(2,1)S(1)}, u32[]{:S(2)}, u32[]{:S(2)}) collective-permute-start(bf16[256,1024]{1,0:T(8,128)(2,1)S(1)} %join.22.refs_3_.refs_1_), channel_id=1, source_target_pairs={{0,8},{2,10},{4,12},{6,14},{8,0},{10,2},{12,4},{14,6},{16,24},{18,... | collective-permute-start | bytes 1572872 | tf_op jit(solution)/shard_map/ppermute | solution.py:781
  115.6 9.2 %collective-permute-start.36 = (bf16[256,1024]{1,0:T(8,128)(2,1)S(1)}, bf16[256,1024]{1,0:T(8,128)(2,1)S(1)}, u32[]{:S(2)}, u32[]{:S(2)}) collective-permute-start(bf16[256,1024]{1,0:T(8,128)(2,1)S(1)} %join.23.refs_3_.refs_1_), channel_id=1, source_target_pairs={{0,2},{2,0},{4,6},{6,4},{8,10},{10,8},{12,14},{14,12},{16,18},{18,... | collective-permute-start | bytes 1572872 | tf_op jit(solution)/shard_map/ppermute | solution.py:781

commit v4 on v3

--- a/solution.py
+++ b/solution.py
@@ -1,5 +1,7 @@
 import functools
 import math
+from types import SimpleNamespace
+from typing import Any, NamedTuple
 
 import jax
 import jax.numpy as jnp
@@ -14,11 +16,11 @@
 BF = jnp.bfloat16
 F32 = jnp.float32
 MIB = 1 << 20
-ORDER = "XFfGSFxTfFsxFfsPxFsfxsFfxsFfxsFxfsxfFsxsf"
+ORDER = "XfFGSfxTFfsxfFsFxsxfFsFfPxsxfsFxsfxFs"
 PLANE_FIRST = ((1, 2), (2, 1), (4, 4), (8, 8))
 BETWEEN = ((1, 2), (4, 4), (2, 1), (8, 8))
 LINE_FIRST = ((4, 4), (1, 2), (2, 1), (8, 8))
-ROUTES = {"f": ((4, 4), (1, 2), (8, 8), (2, 1)), "F": PLANE_FIRST, "x": BETWEEN, "s": PLANE_FIRST}
+ROUTES = {"f": PLANE_FIRST, "F": LINE_FIRST, "x": BETWEEN, "s": PLANE_FIRST}
 SMALL_COST = {"flops": 20_000_000_000, "bytes_accessed": 400_000_000}
 COST = {
     name: {"flops": 100_000_000_000, "bytes_accessed": 1000}
@@ -207,38 +209,82 @@
     weave(feed_grads(numbers_ref[0], in_ref, out_ref, slow_t, ginner, gff_t, hidden))
 
 
+class Weights(NamedTuple):
+    table: Any
+    qkv: Any
+    gain: Any
+    nbias: Any
+    ckv: Any
+    so: Any
+    cq: Any
+    co: Any
+    fi: Any
+    fo: Any
+
+
+class Kept(NamedTuple):
+    out_own: Any
+    out_oth: Any
+    send_in: Any
+    send_out: Any
+    gff_t: Any
+    hidden: Any
+    slow_t: Any
+    ginner: Any
+    gss: Any
+    elow: Any
+    qkv: Any
+    p_self: Any
+    rl_self: Any
+    att_t: Any
+    xhat1: Any
+    rstd1: Any
+    flow: Any
+    encs: Any
+    cq: Any
+    ckv: Any
+    p_cross: Any
+    rl_cross: Any
+    crossed_t: Any
+    dnorm: Any
+    w_qkv: Any
+    w_gain: Any
+    w_ckv: Any
+    w_so: Any
+    w_cq: Any
+    w_co: Any
+
+
 def forward_kernel(numbers_ref, *refs):
     (dec2_in, enc2_in, og2_in, dec_in, enc_in, og_in), refs = refs[:6], refs[6:]
-    names = FORWARD_WEIGHTS
-    weights_in, refs = refs[: len(names)], refs[len(names) :]
-    kept = dict(zip(FORWARD_KEPT, refs))
-    (out_own, out_oth, send_in, send_out, gff_t, hidden, slow_t, ginner, gss, elow, qkv, p_self, rl_self, att_t, xhat1, rstd1,
-     flow, encs, cq, ckv, p_cross, rl_cross, crossed_t, dnorm_ref) = refs[: len(FORWARD_KEPT) - len(PASSED_WEIGHTS)]
-    refs = refs[len(FORWARD_KEPT) :]
-    w = {name: kept["w_" + name] for name in PASSED_WEIGHTS}
-    w.update(zip([name for name in names if name not in PASSED_WEIGHTS], refs))
-    (dec_s, og_s, e_ref, bias_ref, att, fnorm, crossed, xhat2, rstd2, third, slow, slope, gff, outs, sems) = refs[
-        len(names) - len(PASSED_WEIGHTS) :
-    ]
+    weights_in, refs = Weights(*refs[: len(Weights._fields)]), refs[len(Weights._fields) :]
+    kept, refs = Kept(*refs[: len(Kept._fields)]), refs[len(Kept._fields) :]
+    (out_own, out_oth, send_in, send_out, gff_t, hidden, slow_t, ginner, gss, elow, qkv, p_self, rl_self, att_t, xhat1,
+     rstd1, flow, encs, cq, ckv, p_cross, rl_cross, crossed_t, dnorm_ref) = kept[:24]
+    w = Weights(*refs[:1], kept.w_qkv, kept.w_gain, refs[1], kept.w_ckv, kept.w_so, kept.w_cq, kept.w_co, *refs[2:4])
+    (dec_s, og_s, bias_ref, att, xhat2, rstd2, third, slow, slope, gff, outs, sems) = refs[4:]
+    crossed = att
+    at = Weights(*range(len(Weights._fields)))
+    dec, enc, og = (-1, -2, -3)
     copies = Copies(sems)
     place = numbers_ref[0]
-    tokens, width = e_ref.shape
+    tokens, width = dec_s.shape
     length = tokens // 2
     inner = ginner.shape[1]
     where = halves(place, length)
     for s in range(2):
-        copies.start("dec", dec_in.at[place, s], dec_s.at[where[s][0]])
-        copies.start("dec", dec2_in.at[place, s], dec_s.at[where[s][1]])
-    for name, ref in zip(names[:4], weights_in[:4]):
-        copies.start(name, ref, w[name])
+        copies.start(dec, dec_in.at[place, s], dec_s.at[where[s][0]])
+        copies.start(dec, dec2_in.at[place, s], dec_s.at[where[s][1]])
+    for key in at[:4]:
+        copies.start(key, weights_in[key], w[key])
     for s in range(2):
-        copies.start("enc", enc_in.at[place, s], encs.at[where[s][0]])
-        copies.start("enc", enc2_in.at[place, s], encs.at[where[s][1]])
-    for name, ref in zip(names[4:], weights_in[4:]):
-        copies.start(name, ref, w[name])
+        copies.start(enc, enc_in.at[place, s], encs.at[where[s][0]])
+        copies.start(enc, enc2_in.at[place, s], encs.at[where[s][1]])
+    for key in at[4:]:
+        copies.start(key, weights_in[key], w[key])
     for s in range(2):
-        copies.start("og", og_in.at[place, s], og_s.at[where[s][0]])
-        copies.start("og", og2_in.at[place, s], og_s.at[where[s][1]])
+        copies.start(og, og_in.at[place, s], og_s.at[where[s][0]])
+        copies.start(og, og2_in.at[place, s], og_s.at[where[s][1]])
 
     rows = [slice(s * length, (s + 1) * length) for s in range(2)]
     keys_at = lax.broadcasted_iota(jnp.int32, (length, length), 0)
@@ -249,16 +295,14 @@
 
     def embed(s):
         def run():
-            values = dec_s[rows[s]].astype(F32) + row
-            e_ref[rows[s]] = values
-            elow[rows[s]] = values.astype(BF)
+            elow[rows[s]] = (dec_s[rows[s]].astype(F32) + row).astype(BF)
 
         return run
 
     def pack(s, part):
         def run():
             cols = slice(part * width, (part + 1) * width)
-            values = mm(elow[rows[s]], w["qkv"][:, cols])
+            values = mm(elow[rows[s]], w.qkv[:, cols])
             qkv[rows[s], cols] = (values * 0.125 if part == 0 else values).astype(BF)
 
         return run
@@ -266,7 +310,7 @@
     def pack_cross(s, part):
         def run():
             cols = slice(part * width, (part + 1) * width)
-            ckv[rows[s], cols] = mm(encs[rows[s]], w["ckv"][:, cols]).astype(BF)
+            ckv[rows[s], cols] = mm(encs[rows[s]], w.ckv[:, cols]).astype(BF)
 
         return run
 
@@ -274,26 +318,25 @@
 
     def after_self(s):
         def project():
-            held["first", s] = e_ref[rows[s]] + mm(att[rows[s]], w["so"][...])
+            held[0, s] = dec_s[rows[s]].astype(F32) + row + mm(att[rows[s]], w.so[...])
 
         def norm():
-            xhat, rstd, normed = norm_forward(held.pop(("first", s)), gain[0:1], nbias[0:1])
+            xhat, rstd, normed = norm_forward(held.pop((0, s)), gain[0:1], nbias[0:1])
             xhat1[rows[s]] = xhat
             rstd1[rows[s]] = jnp.broadcast_to(rstd, (length, 128))
-            fnorm[rows[s]] = normed
             flow[rows[s]] = normed.astype(BF)
 
         def query():
-            cq[rows[s]] = (mm(flow[rows[s]], w["cq"][...]) * 0.125).astype(BF)
+            cq[rows[s]] = (mm(flow[rows[s]], w.cq[...]) * 0.125).astype(BF)
 
         return [project, norm, query]
 
     def after_cross(s):
         def project():
-            held["second", s] = fnorm[rows[s]] + mm(crossed[rows[s]], w["co"][...])
+            held[1, s] = xhat1[rows[s]] * gain[0:1] + nbias[0:1] + mm(crossed[rows[s]], w.co[...])
 
         def norm():
-            xhat, rstd, normed = norm_forward(held.pop(("second", s)), gain[1:2], nbias[1:2])
+            xhat, rstd, normed = norm_forward(held.pop((1, s)), gain[1:2], nbias[1:2])
             xhat2[rows[s]] = xhat
             rstd2[rows[s]] = jnp.broadcast_to(rstd, (length, 128))
             third[rows[s]] = normed
@@ -308,7 +351,7 @@
 
     def feed(s):
         def grow(index, _):
-            return mm(slow[rows[s]], w["fi"][:, index * step : (index + 1) * step])
+            return mm(slow[rows[s]], w.fi[:, index * step : (index + 1) * step])
 
         def bend(index, v):
             cols = slice(index * step, (index + 1) * step)
@@ -327,7 +370,7 @@
         def shrink(part):
             def run():
                 cols = slice(part * (width // 2), (part + 1) * (width // 2))
-                third[rows[s], cols] += mm(hidden[rows[s]], w["fo"][:, cols])
+                third[rows[s], cols] += mm(hidden[rows[s]], w.fo[:, cols])
 
             return run
 
@@ -347,7 +390,7 @@
 
     def feed_back(s):
         def shrink(index, _):
-            return mm_bt(gff[rows[s]], w["fo"][index * step : (index + 1) * step, :]).astype(BF)
+            return mm_bt(gff[rows[s]], w.fo[index * step : (index + 1) * step, :]).astype(BF)
 
         def bend(index, grad_hidden):
             cols = slice(index * step, (index + 1) * step)
@@ -359,7 +402,7 @@
         def shrink(part):
             def run():
                 cols = slice(part * (width // 2), (part + 1) * (width // 2))
-                third[rows[s], cols] += mm_bt(ginner[rows[s]], w["fi"][cols, :])
+                third[rows[s], cols] += mm_bt(ginner[rows[s]], w.fi[cols, :])
 
             return run
 
@@ -368,19 +411,19 @@
 
         return [shrink(0), shrink(1), norm]
 
-    copies.wait("table", "gain", "nbias", "dec", "qkv")
-    gain = w["gain"][...].astype(F32)
-    nbias = w["nbias"][...].astype(F32)
-    picked = lax.broadcasted_iota(jnp.int32, w["table"].shape, 0) == numbers_ref[1]
-    row = jnp.sum(jnp.where(picked, w["table"][...].astype(F32), 0.0), 0, keepdims=True)
+    copies.wait(at.table, at.gain, at.nbias, dec, at.qkv)
+    gain = w.gain[...].astype(F32)
+    nbias = w.nbias[...].astype(F32)
+    picked = lax.broadcasted_iota(jnp.int32, w.table.shape, 0) == numbers_ref[1]
+    row = jnp.sum(jnp.where(picked, w.table[...].astype(F32), 0.0), 0, keepdims=True)
     weave([embed(0)])
     weave([pack(0, part) for part in range(3)], [embed(1)])
-    copies.wait("enc", "ckv")
+    copies.wait(enc, at.ckv)
     weave(
         attend_steps(0, length, qkv, qkv, qkv, width, 2 * width, bias_ref, p_self, rl_self, att, att_t),
         [pack(1, part) for part in range(3)] + [pack_cross(0, 0), pack_cross(0, 1)],
     )
-    copies.wait("so", "cq", "co")
+    copies.wait(at.so, at.cq, at.co)
     weave(
         attend_steps(1, length, qkv, qkv, qkv, width, 2 * width, bias_ref, p_self, rl_self, att, att_t),
         after_self(0) + [pack_cross(1, 0), pack_cross(1, 1)],
@@ -390,7 +433,7 @@
         attend_steps(0, length, cq, ckv, ckv, 0, width, cross_bias, p_cross, rl_cross, crossed, crossed_t),
         after_self(1),
     )
-    copies.wait("fi", "fo", "og")
+    copies.wait(at.fi, at.fo, og)
     weave(
         attend_steps(1, length, cq, ckv, ckv, 0, width, cross_bias, p_cross, rl_cross, crossed, crossed_t),
         after_cross(0),
@@ -407,14 +450,6 @@
     copies.wait()
 
 
-FORWARD_WEIGHTS = ("table", "qkv", "gain", "nbias", "ckv", "so", "cq", "co", "fi", "fo")
-PASSED_WEIGHTS = ("qkv", "gain", "ckv", "so", "cq", "co")
-FORWARD_KEPT = (
-    "out_own", "out_oth", "send_in", "send_out", "gff_t", "hidden", "slow_t", "ginner", "gss", "elow", "qkv", "p_self", "rl_self",
-    "att_t", "xhat1", "rstd1", "flow", "encs", "cq", "ckv", "p_cross", "rl_cross", "crossed_t", "dnorm",
-) + tuple("w_" + name for name in PASSED_WEIGHTS)
-
-
 def cross_kernel(
     gss, dnorm_in, w_gain, w_co, w_cq, ckv, cq, p_cross, rl_cross, crossed_t, xhat1, rstd1,
     branch, gq_t, gkv_t, gfs, dnorm_ref,
@@ -438,10 +473,10 @@
         held = {}
 
         def query():
-            held["first"] = gss[rows[s]] + mm_bt(gq_t[:, rows[s]].T, w_cq[...])
+            held[0] = gss[rows[s]] + mm_bt(gq_t[:, rows[s]].T, w_cq[...])
 
         def norm():
-            gfs[rows[s]], *gains[s] = norm_backward(xhat1[rows[s]], rstd1[rows[s], 0:1], gain[0:1], held["first"])
+            gfs[rows[s]], *gains[s] = norm_backward(xhat1[rows[s]], rstd1[rows[s], 0:1], gain[0:1], held[0])
 
         return [query, norm]
 
@@ -678,7 +713,7 @@
 
 def call(kernel, scalars, arrays, outs, scratch=(), name=None, far=(), results=(), sems=0, after=()):
     held = [*results, *scratch]
-    limit = sum(math.prod(s[:-2]) * -(-s[-2] // 16) * 16 * s[-1] * jnp.dtype(d).itemsize for s, d in held) + 4 * MIB
+    limit = sum(math.prod(s[:-2]) * -(-s[-2] // 16) * 16 * s[-1] * jnp.dtype(d).itemsize for s, d in held) + 6 * MIB
     taken = len(scalars) + len(arrays) + len(far)
     anywhere = pl.BlockSpec(memory_space=pl.ANY)
 
@@ -739,38 +774,57 @@
     sums = (sent_count * HEADS, 1, length)
     turned = (width, tokens)
     buffer = (width, LANES)
-    kinds = {
-        "out_own": (rows, BF), "out_oth": ((local_len, LANES), BF), "send_in": (buffer, BF),
-        "send_out": (buffer, BF), "gff_t": (turned, BF),
-        "hidden": ((tokens, inner), BF), "slow_t": (turned, BF), "ginner": ((tokens, inner), BF), "gss": (whole, F32),
-        "elow": (whole, BF), "qkv": ((tokens, 3 * width), BF), "p_self": (probs, BF), "rl_self": (sums, F32),
-        "att_t": (turned, BF), "xhat1": (whole, F32), "rstd1": ((tokens, 128), F32), "flow": (whole, BF),
-        "encs": (whole, BF), "cq": (whole, BF), "ckv": ((tokens, 2 * width), BF), "p_cross": (probs, BF),
-        "rl_cross": (sums, F32), "crossed_t": (turned, BF), "dnorm": ((8, width), F32),
-    }
-    params = {
-        "qkv": self_qkv, "so": self_out, "cq": cross_q, "ckv": cross_kv, "co": cross_out, "fi": ff_in, "fo": ff_out,
-        "gain": norm_gain, "nbias": norm_bias, "table": lang_table,
-    }
-    kinds.update({"w_" + name: (weight.shape, weight.dtype) for name, weight in params.items()})
+    like = lambda a: (a.shape, a.dtype)
+    params = Weights(
+        lang_table, self_qkv, norm_gain, norm_bias, cross_kv, self_out, cross_q, cross_out, ff_in, ff_out
+    )
+    kinds = Kept(
+        out_own=(rows, BF),
+        out_oth=((local_len, LANES), BF),
+        send_in=(buffer, BF),
+        send_out=(buffer, BF),
+        gff_t=(turned, BF),
+        hidden=((tokens, inner), BF),
+        slow_t=(turned, BF),
+        ginner=((tokens, inner), BF),
+        gss=(whole, F32),
+        elow=(whole, BF),
+        qkv=((tokens, 3 * width), BF),
+        p_self=(probs, BF),
+        rl_self=(sums, F32),
+        att_t=(turned, BF),
+        xhat1=(whole, F32),
+        rstd1=((tokens, 128), F32),
+        flow=(whole, BF),
+        encs=(whole, BF),
+        cq=(whole, BF),
+        ckv=((tokens, 2 * width), BF),
+        p_cross=(probs, BF),
+        rl_cross=(sums, F32),
+        crossed_t=(turned, BF),
+        dnorm=((8, width), F32),
+        w_qkv=like(self_qkv),
+        w_gain=like(norm_gain),
+        w_ckv=like(cross_kv),
+        w_so=like(self_out),
+        w_cq=like(cross_q),
+        w_co=like(cross_out),
+    )
     kept = call(
         forward_kernel,
         (numbers,),
         (dec2, enc2, og2),
-        [kinds[name] for name in FORWARD_KEPT],
-        [kinds["w_" + name] for name in FORWARD_WEIGHTS if name not in PASSED_WEIGHTS]
+        list(kinds),
+        [like(lang_table), like(norm_bias), like(ff_in), like(ff_out)]
         + [
-            (whole, BF), (whole, BF), (whole, F32), ((4, length, length), F32), (whole, BF), (whole, F32), (whole, BF),
-            (whole, F32), ((tokens, 128), F32), (whole, F32), (whole, BF), ((tokens, inner), BF), (whole, BF), (whole, BF),
+            (whole, BF), (whole, BF), ((4, length, length), F32), (whole, BF), (whole, F32), ((tokens, 128), F32),
+            (whole, F32), (whole, BF), ((tokens, inner), BF), (whole, BF), (whole, BF),
         ],
         name="forward",
-        far=(dec_in, enc_out, out_grad, *(params[name] for name in FORWARD_WEIGHTS)),
+        far=(dec_in, enc_out, out_grad, *params),
         sems=32,
     )
-    held = dict(zip(FORWARD_KEPT, kept))
-
-    def of(*names):
-        return [held[name] for name in names]
+    held = SimpleNamespace(**Kept(*kept)._asdict())
 
     def flips(core_zero, core_one):
         return [(2 * d, 2 * (d ^ core_zero)) for d in range(dp_count)] + [
@@ -796,7 +850,7 @@
             mine, other = total[: body // 2], total[body // 2 : body]
             rest = (total[body:],) if tail else ()
             bit = jnp.zeros((1,), jnp.int32)
-            for _ in range(2 * len(route)):
+            for _ in range(2 * len(route) - 1):
                 yield
         else:
             bits = [
@@ -804,15 +858,18 @@
                 for zero, one in route
             ]
             held = body
-            for bit, flip in zip(bits, route):
+            for bit, flip in zip(bits, route[:-1]):
                 held //= 2
                 shape = (held + tail, lanes)
                 send, keep = run(functools.partial(add_split_kernel, tail), (bit,), (keep, got), [(shape, BF)] * 2, "add_split")
                 got = travel(send, *flip)
                 yield
+            (keep,) = run(functools.partial(add_kernel, 0), (), (keep, got), [(shape, BF)], "add_all")
+            got = travel(keep, *route[-1])
+            yield
             pieces = [((held, lanes), BF)] + ([((tail, lanes), BF)] if tail else [])
             mine, *rest = run(functools.partial(add_kernel, tail), (), (keep, got), pieces, "add_last")
-            for bit, flip in zip(bits[:0:-1], route[:0:-1]):
+            for bit, flip in zip(bits[1:-1][::-1], route[1:-1][::-1]):
                 other = travel(mine, *flip)
                 yield
                 held *= 2
@@ -830,85 +887,81 @@
         )
         yield unpacked
 
-    held["keep_in"], held["keep_out"] = call(
+    held.keep_in, held.keep_out = call(
         feed_keep_kernel,
         (numbers,),
-        of("gff_t", "hidden", "slow_t", "ginner"),
+        [held.gff_t, held.hidden, held.slow_t, held.ginner],
         [(buffer, BF), (buffer, BF)],
         name="feed_keep",
     )
-    last[:] = of("keep_in")
-
-    def store(names, arrays):
-        held.update(zip(names, arrays))
-        last[:] = [arrays[0]]
+    last[:] = [held.keep_in]
 
     def cross_back():
-        store(
-            ("cross_branch", "gq_t", "gkv_t", "gfs", "dnorm"),
+        held.cross_branch, held.gq_t, held.gkv_t, held.gfs, held.dnorm = (
             call(
                 cross_kernel,
                 (),
-                of("gss", "dnorm", "w_gain", "w_co", "w_cq", "ckv", "cq", "p_cross", "rl_cross", "crossed_t", "xhat1", "rstd1"),
+                [held.gss, held.dnorm, held.w_gain, held.w_co, held.w_cq, held.ckv, held.cq, held.p_cross, held.rl_cross, held.crossed_t, held.xhat1, held.rstd1],
                 [(whole, BF), (turned, BF), ((2 * width, tokens), BF), (whole, F32), ((8, width), F32)],
                 [(turned, BF)],
                 name="cross",
                 after=last,
-            ),
+            )
         )
+        last[:] = [held.gfs]
 
     def cross_grads():
         longer = (width + 2 * local_len, LANES)
-        send, keep, held["genc_own"] = call(
+        send, keep, held.genc_own = call(
             cross_grads_kernel,
             (numbers,),
-            of("cross_branch", "gq_t", "gkv_t", "crossed_t", "flow", "encs", "w_ckv", "out_oth"),
+            [held.cross_branch, held.gq_t, held.gkv_t, held.crossed_t, held.flow, held.encs, held.w_ckv, held.out_oth],
             [(longer, BF), (buffer, BF), (rows, BF)],
             [(whole, BF)],
             name="cross_grads",
             after=last,
         )
         last[:] = [send]
-        held["got_cross"] = lax.ppermute(send, "seq", swap)
+        held.got_cross = lax.ppermute(send, "seq", swap)
         groups["x"] = reduce_all(
-            keep, held["got_cross"], [(width, width), (width, half), (width, half)], unpack_cross, ROUTES["x"]
+            keep, held.got_cross, [(width, width), (width, half), (width, half)], unpack_cross, ROUTES["x"]
         )
 
     def self_back():
-        store(
-            ("self_branch", "gqkv_t"),
+        held.self_branch, held.gqkv_t = (
             call(
                 self_kernel,
                 (),
-                of("gfs", "w_so", "qkv", "p_self", "rl_self", "att_t"),
+                [held.gfs, held.w_so, held.qkv, held.p_self, held.rl_self, held.att_t],
                 [(whole, BF), ((3 * width, tokens), BF)],
                 [(turned, BF)],
                 name="self",
                 after=last,
-            ),
+            )
         )
+        last[:] = [held.self_branch]
 
     def self_grads():
         longer = (width + 16 + local_len, LANES)
-        send, keep, held["gin_own"] = call(
+        send, keep, held.gin_own = call(
             self_grads_kernel,
             (numbers,),
-            of("gfs", "dnorm", "self_branch", "gqkv_t", "att_t", "elow", "w_qkv"),
+            [held.gfs, held.dnorm, held.self_branch, held.gqkv_t, held.att_t, held.elow, held.w_qkv],
             [(longer, BF), ((width + 16, LANES), BF), (rows, BF)],
             [(whole, BF), ((16, width), F32)],
             name="self_grads",
             after=last,
         )
         last[:] = [send]
-        held["got_self"] = lax.ppermute(send, "seq", swap)
+        held.got_self = lax.ppermute(send, "seq", swap)
         results = [(width, 3 * half), (width, half), (3, half), (3, half), (8, half)]
-        groups["s"] = reduce_all(keep, held["got_self"], results, unpack_self, ROUTES["s"], tail=16)
+        groups["s"] = reduce_all(keep, held.got_self, results, unpack_self, ROUTES["s"], tail=16)
 
     def place_all():
-        held["placed"] = call(
+        held.placed = call(
             place_kernel,
             (numbers,),
-            of("out_own", "genc_own", "gin_own", "got_cross", "got_self"),
+            [held.out_own, held.genc_own, held.gin_own, held.got_cross, held.got_self],
             [],
             name="place",
             results=[(dec_in.shape, BF)] * 3,
@@ -916,8 +969,8 @@
         )
 
     groups = {
-        "f": reduce_all(held["keep_in"], lax.ppermute(held["send_in"], "seq", swap), [(width, inner // 2)], unpack_in, ROUTES["f"]),
-        "F": reduce_all(held["keep_out"], lax.ppermute(held["send_out"], "seq", swap), [(inner, half)], unpack_out, ROUTES["F"]),
+        "f": reduce_all(held.keep_in, lax.ppermute(held.send_in, "seq", swap), [(width, inner // 2)], unpack_in, ROUTES["f"]),
+        "F": reduce_all(held.keep_out, lax.ppermute(held.send_out, "seq", swap), [(inner, half)], unpack_out, ROUTES["F"]),
     }
     kernels = {"X": cross_back, "G": cross_grads, "S": self_back, "T": self_grads, "P": place_all}
     sums = {}
@@ -929,7 +982,7 @@
     (g_ff_in,), (g_ff_out,) = sums["f"], sums["F"]
     g_cross_kv, g_cross_q, g_cross_out = sums["x"]
     g_qkv, g_self_out, g_gain, g_bias, g_table = sums["s"]
-    output, grad_encoder, grad_input = held["placed"]
+    output, grad_encoder, grad_input = held.placed
     return (
         output,
         grad_input,

time: 128 us -> 122 us (0.953)
  starting transfers between devices: 42.1 us -> 36.2 us
  waiting for transfers between devices: 31.7 us -> 30.1 us
    ppermute x32 -> x28, starting transfers between devices: 40.4 us -> 34.4 us  [travel(): return lax.ppermute(array, ('dp', 'seq'), flips(core_zero, core_one))]
    ppermute x32 -> x28, waiting for transfers between devices: 31.7 us -> 30.1 us  [travel(): return lax.ppermute(array, ('dp', 'seq'), flips(core_zero, core_one))]
    pallas_call x43 -> x39, Pallas kernels: 50.4 us -> 50.5 us  [call(): pl.pallas_call(body, out_shape=tuple((pltpu.VMEM(s, d) for s, d in outs))...]
  transfers between devices with their start and end apart: 39 -> 35, of which waited for: 13 -> 14; matrix products, arithmetic and copies ran while one was open for 2% -> 2% of each run, Pallas kernels for 23% -> 25%
where the time goes in v4:
time: 122 us; the launch traced here: 121 us
  Pallas kernels  50.5 us (41%)
  starting transfers between devices  36.2 us (30%)
  waiting for transfers between devices  30.1 us (25%)
  other arithmetic  2.8 us (2%)
    pallas_call x39, Pallas kernels, call(): pl.pallas_call(body, out_shape=tuple((pltpu.VMEM(s, d) for s, d in outs))...  50.5 us
    ppermute x28, starting transfers between devices, travel(): return lax.ppermute(array, ('dp', 'seq'), flips(core_zero, core_one))  34.4 us
    ppermute x28, waiting for transfers between devices, travel(): return lax.ppermute(array, ('dp', 'seq'), flips(core_zero, core_one))  30.1 us
  transfers between devices with their start and end apart: 35, of which 14 were waited for; matrix products, arithmetic and copies ran while one was open for 2% of the time, Pallas kernels for 25%

profile of v4, /device:TPU:0, one launch (start us, length us, event | category | flops | bytes accessed | tf_op | source)
XLA Modules:
  0.0 121.2 jit_solution(8520499697569824078)
XLA Ops:
  0.6 0.5 collective-permute-start
  1.2 0.4 collective-permute-start.2
  1.7 1.3 %select_reduce_fusion.2 = s32[]{:T(128)} fusion(s32[2]{0:T(128)} %param.21, s32[]{:T(128)} %axis_index.22), kind=kLoop, calls=%fused_computation.3 | loop fusion | flops 5 | bytes 16 | tf_op jit(solution)/shard_map/reduce_sum | solution.py:760
  3.0 0.8 select_reduce_fusion.1
  3.8 0.7 pad_add_fusion.refs_0_
  4.5 19.1 %forward.1 = (bf16[2,128,512]{2,1,0:T(8,128)(2,1)S(1)}, bf16[128,1024]{1,0:T(8,128)(2,1)S(1)}, bf16[512,1024]{1,0:T(8,128)(2,1)}, bf16[512,1024]{1,0:T(8,128)(2,...) custom-call(s32[6]{0:T(128)S(1)} %pad_add_fusion.refs_0_, ...), custom_call_target="tpu_custom_call" | custom-call | flops 99999997952 | bytes 1000 | tf_op jit(solution)/shard_map/forward/pallas_call | solution.py:723
  23.6 0.2 collective-permute-start.4
  23.8 0.3 collective-permute-start.3
  24.1 1.8 %feed_keep.1 = (bf16[512,1024]{1,0:T(8,128)(2,1)S(1)}, bf16[512,1024]{1,0:T(8,128)(2,1)S(1)}) custom-call(s32[6]{0:T(128)S(1)} %pad_add_fusion.refs_0_, bf16[512,512]{1,0:T(8,128)(2,1)S(1)} %get-tuple-element.113.refs_1_, bf16[512,2048]{1,0:T(8,128)(2,1)S(1)} %get-tuple-element.114.refs_2_, bf16[512,512]{1,0:T(8,128)(2,1)S(1)} %get-tuple-element.115.refs_3_, ...), custom_call_target="tpu_custom_call" | custom-call | flops 99999997952 | bytes 1000 | tf_op jit(solution)/shard_map/feed_keep/pallas_call | solution.py:723
  25.9 3.4 %cross.1 = (bf16[512,512]{1,0:T(8,128)(2,1)S(1)}, bf16[512,512]{1,0:T(8,128)(2,1)S(1)}, bf16[1024,512]{1,0:T(8,128)(2,1)S(1)}, f32[512,512]{1,0:T(8,128)S(1)}, f32[8,512]{1,0:T(8,128)S(1)}) custom-call(f32[512,512]{1,0:T(8,128)S(1)} %get-tuple-element.101.refs_0_, f32[8,512]{1,0:T(8,128)S(1)} %get-tuple-element.102.refs_1_, ...), custom_call_target="tpu_custom_call" | custom-call | flops 99999997952 | bytes 1000 | tf_op jit(solution)/shard_map/cross/pallas_call | solution.py:723
  29.4 2.2 %add_split.12 = (bf16[256,1024]{1,0:T(8,128)(2,1)}, bf16[256,1024]{1,0:T(8,128)(2,1)S(1)}) custom-call(s32[1]{0:T(128)} %bitcast.3.refs_0_, bf16[512,1024]{1,0:T(8,128)(2,1)S(1)} %get-tuple-element.117.refs_12_.refs_1_, bf16[512,1024]{1,0:T(8,128)(2,1)} %collective-permute-done.4.refs_2_, f32[512,512]{1,0:T(8,128)S(1)} %get-tuple-element.128.refs_3_.refs_0_.refs_1_), custom_call_target="tpu_custom_call" | custom-call | flops 20000000000 | bytes 400000000 | tf_op jit(solution)/shard_map/add_split/pallas_call | solution.py:723
  31.6 2.7 %collective-permute-start.6 = (bf16[256,1024]{1,0:T(8,128)(2,1)}, bf16[256,1024]{1,0:T(8,128)(2,1)}, u32[]{:S(2)}, u32[]{:S(2)}) collective-permute-start(bf16[256,1024]{1,0:T(8,128)(2,1)} %get-tuple-element.129.refs_3_), channel_id=1, source_target_pairs={{0,2},{2,0},{4,6},{6,4},{8,10},{10,8},{12,14},{14,12},{16,18},{18,... | collective-permute-start | bytes 1572872 | tf_op jit(solution)/shard_map/ppermute | solution.py:835
  34.3 2.2 %add_split.13 = (bf16[256,1024]{1,0:T(8,128)(2,1)}, bf16[256,1024]{1,0:T(8,128)(2,1)S(1)}) custom-call(s32[1]{0:T(128)} %bitcast.2.refs_0_, bf16[512,1024]{1,0:T(8,128)(2,1)S(1)} %get-tuple-element.125.refs_1_, bf16[512,1024]{1,0:T(8,128)(2,1)} %collective-permute-done.3.refs_2_, bf16[256,1024]{1,0:T(8,128)(2,1)} %get-tuple-element.129.refs_3_), custom_call_target="tpu_custom_call" | custom-call | flops 20000000000 | bytes 400000000 | tf_op jit(solution)/shard_map/add_split/pallas_call | solution.py:723
  36.4 1.6 %collective-permute-start.9 = (bf16[256,1024]{1,0:T(8,128)(2,1)}, bf16[256,1024]{1,0:T(8,128)(2,1)}, u32[]{:S(2)}, u32[]{:S(2)}) collective-permute-start(bf16[256,1024]{1,0:T(8,128)(2,1)} %get-tuple-element.130.refs_9_), channel_id=1, source_target_pairs={{0,8},{2,10},{4,12},{6,14},{8,0},{10,2},{12,4},{14,6},{16,24},{18,... | collective-permute-start | bytes 1572872 | tf_op jit(solution)/shard_map/ppermute | solution.py:835
  38.0 2.4 %cross_grads.1 = (bf16[768,1024]{1,0:T(8,128)(2,1)S(1)}, bf16[512,1024]{1,0:T(8,128)(2,1)S(1)}, bf16[2,128,512]{2,1,0:T(8,128)(2,1)S(1)}) custom-call(s32[6]{0:T(128)S(1)} %pad_add_fusion.refs_0_, bf16[512,512]{1,0:T(8,128)(2,1)S(1)} %get-tuple-element.118.refs_1_, bf16[512,512]{1,0:T(8,128)(2,1)S(1)} %get-tuple-element.119.refs_2_, ...), custom_call_target="tpu_custom_call" | custom-call | flops 99999997952 | bytes 1000 | tf_op jit(solution)/shard_map/cross_grads/pallas_call | solution.py:723
  40.5 2.8 %self.1 = (bf16[512,512]{1,0:T(8,128)(2,1)S(1)}, bf16[1536,512]{1,0:T(8,128)(2,1)S(1)}) custom-call(f32[512,512]{1,0:T(8,128)S(1)} %get-tuple-element.128.refs_3_.refs_0_.refs_1_, bf16[512,512]{1,0:T(8,128)(2,1)S(1)} %get-tuple-element.133.refs_1_, bf16[512,1536]{1,0:T(8,128)(2,1)S(1)} %get-tuple-element.134.refs_2_, ...), custom_call_target="tpu_custom_call" | custom-call | flops 99999997952 | bytes 1000 | tf_op jit(solution)/shard_map/self/pallas_call | solution.py:723
  43.3 1.2 add_split.14
  44.5 1.6 %collective-permute-start.8 = (bf16[128,1024]{1,0:T(8,128)(2,1)S(1)}, bf16[128,1024]{1,0:T(8,128)(2,1)S(1)}, u32[]{:S(2)}, u32[]{:S(2)}) collective-permute-start(bf16[128,1024]{1,0:T(8,128)(2,1)S(1)} %get-tuple-element.145.refs_3_), channel_id=1, source_target_pairs={{0,4},{2,6},{4,0},{6,2},{8,12},{10,14},{12,8},{14,10},{16,20},{18,... | collective-permute-start | bytes 786440 | tf_op jit(solution)/shard_map/ppermute | solution.py:835
  46.1 1.0 add_split.15
  47.1 0.5 collective-permute-start.11
  47.6 2.9 %self_grads.1 = (bf16[656,1024]{1,0:T(8,128)(2,1)S(1)}, bf16[528,1024]{1,0:T(8,128)(2,1)S(1)}, bf16[2,128,512]{2,1,0:T(8,128)(2,1)S(1)}) custom-call(s32[6]{0:T(128)S(1)} %pad_add_fusion.refs_0_, f32[512,512]{1,0:T(8,128)S(1)} %get-tuple-element.128.refs_3_.refs_0_.refs_1_, f32[8,512]{1,0:T(8,128)S(1)} %get-tuple-element.132.refs_2_, ...), custom_call_target="tpu_custom_call" | custom-call | flops 99999997952 | bytes 1000 | tf_op jit(solution)/shard_map/self_grads/pallas_call | solution.py:723
  50.6 1.2 add_split.16
  51.8 1.5 %collective-permute-start.14 = (bf16[128,1024]{1,0:T(8,128)(2,1)S(1)}, bf16[128,1024]{1,0:T(8,128)(2,1)S(1)}, u32[]{:S(2)}, u32[]{:S(2)}) collective-permute-start(bf16[128,1024]{1,0:T(8,128)(2,1)S(1)} %get-tuple-element.151.refs_3_), channel_id=1, source_target_pairs={{0,2},{2,0},{4,6},{6,4},{8,10},{10,8},{12,14},{14,12},{16,18},{18,... | collective-permute-start | bytes 786440 | tf_op jit(solution)/shard_map/ppermute | solution.py:835
  53.4 1.6 %collective-permute-start.10 = (bf16[64,1024]{1,0:T(8,128)(2,1)S(1)}, bf16[64,1024]{1,0:T(8,128)(2,1)S(1)}, u32[]{:S(2)}, u32[]{:S(2)}) collective-permute-start(bf16[64,1024]{1,0:T(8,128)(2,1)S(1)} %get-tuple-element.153.refs_3_), channel_id=1, source_target_pairs={{0,8},{2,10},{4,12},{6,14},{8,0},{10,2},{12,4},{14,6},{16,24},{18,... | collective-permute-start | bytes 393224 | tf_op jit(solution)/shard_map/ppermute | solution.py:835
  55.0 0.3 add_split.18
  55.2 0.8 copy-done
  56.0 0.7 collective-permute-start.16
  56.7 1.2 add_split.19
  57.8 0.5 collective-permute-start.13
  58.4 0.4 collective-permute-done.10.refs_1_
  58.8 2.7 %collective-permute-start.12 = (bf16[64,1024]{1,0:T(8,128)(2,1)S(1)}, bf16[64,1024]{1,0:T(8,128)(2,1)S(1)}, u32[]{:S(2)}, u32[]{:S(2)}) collective-permute-start(bf16[64,1024]{1,0:T(8,128)(2,1)S(1)} %add_all.4.refs_3_.refs_0_), channel_id=1, source_target_pairs={{0,16},{2,18},{4,20},{6,22},{8,24},{10,26},{12,28},{14,30},{16,0},... | collective-permute-start | bytes 393224 | tf_op jit(solution)/shard_map/ppermute | solution.py:835
  61.5 0.8 collective-permute-start.15
  62.4 4.6 %collective-permute-done.16.refs_2_ = bf16[272,1024]{1,0:T(8,128)(2,1)S(1)} collective-permute-done((bf16[272,1024]{1,0:T(8,128)(2,1)S(1)}, bf16[272,1024]{1,0:T(8,128)(2,1)S(1)}, u32[]{:S(2)}, u32[]{:S(2)}) %collective-permute-start.16) | collective-permute-done | bytes 557088 | tf_op jit(solution)/shard_map/ppermute | solution.py:835
  67.1 0.9 collective-permute-start.18
  68.0 2.6 %collective-permute-start.20 = (bf16[64,1024]{1,0:T(8,128)(2,1)S(1)}, bf16[64,1024]{1,0:T(8,128)(2,1)S(1)}, u32[]{:S(2)}, u32[]{:S(2)}) collective-permute-start(bf16[64,1024]{1,0:T(8,128)(2,1)S(1)} %add_all.5.refs_3_.refs_0_), channel_id=1, source_target_pairs={{0,16},{2,18},{4,20},{6,22},{8,24},{10,26},{12,28},{14,30},{16,0},... | collective-permute-start | bytes 393224 | tf_op jit(solution)/shard_map/ppermute | solution.py:835
  70.7 1.3 %collective-permute-start.17 = (bf16[64,1024]{1,0:T(8,128)(2,1)S(1)}, bf16[64,1024]{1,0:T(8,128)(2,1)S(1)}, u32[]{:S(2)}, u32[]{:S(2)}) collective-permute-start(bf16[64,1024]{1,0:T(8,128)(2,1)S(1)} %get-tuple-element.165.refs_3_), channel_id=1, source_target_pairs={{0,4},{2,6},{4,0},{6,2},{8,12},{10,14},{12,8},{14,10},{16,20},{18,... | collective-permute-start | bytes 393224 | tf_op jit(solution)/shard_map/ppermute | solution.py:835
  72.0 1.9 %collective-permute-done.18.refs_2_ = bf16[144,1024]{1,0:T(8,128)(2,1)S(1)} collective-permute-done((bf16[144,1024]{1,0:T(8,128)(2,1)S(1)}, bf16[144,1024]{1,0:T(8,128)(2,1)S(1)}, u32[]{:S(2)}, u32[]{:S(2)}) %collective-permute-start.18) | collective-permute-done | bytes 294944 | tf_op jit(solution)/shard_map/ppermute | solution.py:835
  74.0 0.4 collective-permute-start.22
  74.3 1.4 %collective-permute-done.17.refs_1_ = bf16[64,1024]{1,0:T(8,128)(2,1)S(1)} collective-permute-done((bf16[64,1024]{1,0:T(8,128)(2,1)S(1)}, bf16[64,1024]{1,0:T(8,128)(2,1)S(1)}, u32[]{:S(2)}, u32[]{:S(2)}) %collective-permute-start.17) | collective-permute-done | bytes 131104 | tf_op jit(solution)/shard_map/ppermute | solution.py:835
  75.8 2.2 %collective-permute-start.24 = (bf16[64,1024]{1,0:T(8,128)(2,1)S(1)}, bf16[64,1024]{1,0:T(8,128)(2,1)S(1)}, u32[]{:S(2)}, u32[]{:S(2)}) collective-permute-start(bf16[64,1024]{1,0:T(8,128)(2,1)S(1)} %add_all.6.refs_2_.refs_0_), channel_id=1, source_target_pairs={{0,16},{2,18},{4,20},{6,22},{8,24},{10,26},{12,28},{14,30},{16,0},... | collective-permute-start | bytes 393224 | tf_op jit(solution)/shard_map/ppermute | solution.py:835
  78.0 0.8 collective-permute-start.19
  78.9 0.9 collective-permute-start.21
  79.8 4.2 %collective-permute-done.22.refs_1_ = bf16[80,1024]{1,0:T(8,128)(2,1)S(1)} collective-permute-done((bf16[80,1024]{1,0:T(8,128)(2,1)S(1)}, bf16[80,1024]{1,0:T(8,128)(2,1)S(1)}, u32[]{:S(2)}, u32[]{:S(2)}) %collective-permute-start.22) | collective-permute-done | bytes 163872 | tf_op jit(solution)/shard_map/ppermute | solution.py:835
  84.3 0.6 collective-permute-start.30
  84.9 2.0 %collective-permute-done.19.refs_2_ = bf16[64,1024]{1,0:T(8,128)(2,1)S(1)} collective-permute-done((bf16[64,1024]{1,0:T(8,128)(2,1)S(1)}, bf16[64,1024]{1,0:T(8,128)(2,1)S(1)}, u32[]{:S(2)}, u32[]{:S(2)}) %collective-permute-start.19) | collective-permute-done | bytes 131104 | tf_op jit(solution)/shard_map/ppermute | solution.py:835
  87.0 0.4 collective-permute-start.26
  87.3 1.8 %collective-permute-start.27 = (bf16[64,1024]{1,0:T(8,128)(2,1)S(1)}, bf16[64,1024]{1,0:T(8,128)(2,1)S(1)}, u32[]{:S(2)}, u32[]{:S(2)}) collective-permute-start(bf16[64,1024]{1,0:T(8,128)(2,1)S(1)} %add_last.6.refs_2_.refs_1_), channel_id=1, source_target_pairs={{0,4},{2,6},{4,0},{6,2},{8,12},{10,14},{12,8},{14,10},{16,20},{18,... | collective-permute-start | bytes 393224 | tf_op jit(solution)/shard_map/ppermute | solution.py:835
  89.2 1.8 %place.1 = (bf16[2,2,128,512]{3,2,1,0:T(8,128)(2,1)}, bf16[2,2,128,512]{3,2,1,0:T(8,128)(2,1)}, bf16[2,2,128,512]{3,2,1,0:T(8,128)(2,1)}) custom-call(s32[6]{0:T(128)S(1)} %pad_add_fusion.refs_0_, bf16[2,128,512]{2,1,0:T(8,128)(2,1)S(1)} %get-tuple-element.100.refs_1_, bf16[2,128,512]{2,1,0:T(8,128)(2,1)S(1)} %get-tuple-element.131.refs_2_, ...), custom_call_target="tpu_custom_call" | custom-call | flops 20000000000 | bytes 400000000 | tf_op jit(solution)/shard_map/place/pallas_call | solution.py:723
  90.9 1.8 %collective-permute-done.23.refs_1_ = bf16[80,1024]{1,0:T(8,128)(2,1)S(1)} collective-permute-done((bf16[80,1024]{1,0:T(8,128)(2,1)S(1)}, bf16[80,1024]{1,0:T(8,128)(2,1)S(1)}, u32[]{:S(2)}, u32[]{:S(2)}) %collective-permute-start.23) | collective-permute-done | bytes 163872 | tf_op jit(solution)/shard_map/ppermute | solution.py:835
  92.8 2.0 %collective-permute-done.27.refs_2_ = bf16[64,1024]{1,0:T(8,128)(2,1)S(1)} collective-permute-done((bf16[64,1024]{1,0:T(8,128)(2,1)S(1)}, bf16[64,1024]{1,0:T(8,128)(2,1)S(1)}, u32[]{:S(2)}, u32[]{:S(2)}) %collective-permute-start.27) | collective-permute-done | bytes 131104 | tf_op jit(solution)/shard_map/ppermute | solution.py:835
  94.8 1.5 %collective-permute-start.29 = (bf16[128,1024]{1,0:T(8,128)(2,1)S(1)}, bf16[128,1024]{1,0:T(8,128)(2,1)S(1)}, u32[]{:S(2)}, u32[]{:S(2)}) collective-permute-start(bf16[128,1024]{1,0:T(8,128)(2,1)S(1)} %join.10.refs_3_.refs_1_), channel_id=1, source_target_pairs={{0,8},{2,10},{4,12},{6,14},{8,0},{10,2},{12,4},{14,6},{16,24},{18,... | collective-permute-start | bytes 786440 | tf_op jit(solution)/shard_map/ppermute | solution.py:835
  96.3 1.0 collective-permute-start.34
  97.3 0.4 collective-permute-done.25.refs_2_
  97.8 2.0 %collective-permute-start.28 = (bf16[128,1024]{1,0:T(8,128)(2,1)S(1)}, bf16[128,1024]{1,0:T(8,128)(2,1)S(1)}, u32[]{:S(2)}, u32[]{:S(2)}) collective-permute-start(bf16[128,1024]{1,0:T(8,128)(2,1)S(1)} %join.12.refs_3_.refs_1_), channel_id=1, source_target_pairs={{0,4},{2,6},{4,0},{6,2},{8,12},{10,14},{12,8},{14,10},{16,20},{18,... | collective-permute-start | bytes 786440 | tf_op jit(solution)/shard_map/ppermute | solution.py:835
  99.9 3.9 %collective-permute-done.29.refs_2_ = bf16[128,1024]{1,0:T(8,128)(2,1)S(1)} collective-permute-done((bf16[128,1024]{1,0:T(8,128)(2,1)S(1)}, bf16[128,1024]{1,0:T(8,128)(2,1)S(1)}, u32[]{:S(2)}, u32[]{:S(2)}) %collective-permute-start.29) | collective-permute-done | bytes 262176 | tf_op jit(solution)/shard_map/ppermute | solution.py:835
  103.8 1.1 collective-permute-start.33
  104.9 2.2 %collective-permute-done.28.refs_2_ = bf16[128,1024]{1,0:T(8,128)(2,1)S(1)} collective-permute-done((bf16[128,1024]{1,0:T(8,128)(2,1)S(1)}, bf16[128,1024]{1,0:T(8,128)(2,1)S(1)}, u32[]{:S(2)}, u32[]{:S(2)}) %collective-permute-start.28) | collective-permute-done | bytes 262176 | tf_op jit(solution)/shard_map/ppermute | solution.py:835
  107.1 2.6 %collective-permute-start.31 = (bf16[256,1024]{1,0:T(8,128)(2,1)S(1)}, bf16[256,1024]{1,0:T(8,128)(2,1)S(1)}, u32[]{:S(2)}, u32[]{:S(2)}) collective-permute-start(bf16[256,1024]{1,0:T(8,128)(2,1)S(1)} %join.15.refs_3_.refs_1_), channel_id=1, source_target_pairs={{0,2},{2,0},{4,6},{6,4},{8,10},{10,8},{12,14},{14,12},{16,18},{18,... | collective-permute-start | bytes 1572872 | tf_op jit(solution)/shard_map/ppermute | solution.py:835
  109.7 1.5 %unpack.4 = (f32[8,128]{1,0:T(8,128)S(1)}, f32[512,1024]{1,0:T(8,128)}) custom-call(s32[1]{0:T(128)} %bitcast.3.refs_0_, bf16[256,1024]{1,0:T(8,128)(2,1)S(1)} %join.11.refs_3_.refs_1_, bf16[256,1024]{1,0:T(8,128)(2,1)S(1)} %collective-permute-done.34.refs_2_, bf16[256,1024]{1,0:T(8,128)(2,1)S(1)} %join.15.refs_3_.refs_1_), custom_call_target="tpu_custom_call" | custom-call | flops 20000000000 | bytes 400000000 | tf_op jit(solution)/shard_map/unpack/pallas_call | solution.py:723
  111.2 2.8 %collective-permute-done.33.refs_2_ = bf16[256,1024]{1,0:T(8,128)(2,1)S(1)} collective-permute-done((bf16[256,1024]{1,0:T(8,128)(2,1)S(1)}, bf16[256,1024]{1,0:T(8,128)(2,1)S(1)}, u32[]{:S(2)}, u32[]{:S(2)}) %collective-permute-start.33) | collective-permute-done | bytes 524320 | tf_op jit(solution)/shard_map/ppermute | solution.py:835
  114.0 1.6 %unpack.5 = (f32[8,128]{1,0:T(8,128)S(1)}, f32[512,512]{1,0:T(8,128)}, f32[512,256]{1,0:T(8,128)}, f32[512,256]{1,0:T(8,128)}) custom-call(s32[1]{0:T(128)} %bitcast.3.refs_0_, bf16[256,1024]{1,0:T(8,128)(2,1)S(1)} %join.14.refs_3_.refs_1_, bf16[256,1024]{1,0:T(8,128)(2,1)S(1)} %collective-permute-done.33.refs_2_, f32[8,128]{1,0:T(8,128)S(1)} %get-tuple-element.174.refs_3_), custom_call_target="tpu_custom_call" | custom-call | flops 20000000000 | bytes 400000000 | tf_op jit(solution)/shard_map/unpack/pallas_call | solution.py:723
  115.6 1.6 %unpack.6 = (f32[8,128]{1,0:T(8,128)S(1)}, f32[2048,256]{1,0:T(8,128)}) custom-call(s32[1]{0:T(128)} %bitcast.2.refs_0_, bf16[256,1024]{1,0:T(8,128)(2,1)S(1)} %join.13.refs_3_.refs_1_, bf16[256,1024]{1,0:T(8,128)(2,1)S(1)} %collective-permute-done.32.refs_2_, f32[8,128]{1,0:T(8,128)S(1)} %get-tuple-element.175.refs_3_), custom_call_target="tpu_custom_call" | custom-call | flops 20000000000 | bytes 400000000 | tf_op jit(solution)/shard_map/unpack/pallas_call | solution.py:723
  117.3 2.4 %collective-permute-done.31.refs_2_ = bf16[256,1024]{1,0:T(8,128)(2,1)S(1)} collective-permute-done((bf16[256,1024]{1,0:T(8,128)(2,1)S(1)}, bf16[256,1024]{1,0:T(8,128)(2,1)S(1)}, u32[]{:S(2)}, u32[]{:S(2)}) %collective-permute-start.31) | collective-permute-done | bytes 524320 | tf_op jit(solution)/shard_map/ppermute | solution.py:835
  119.6 1.6 %unpack.7 = (f32[8,128]{1,0:T(8,128)}, f32[512,768]{1,0:T(8,128)}, f32[512,256]{1,0:T(8,128)}, f32[3,256]{1,0:T(4,128)}, f32[3,256]{1,0:T(4,128)}, /*index=5*/f32[8,256]{1,0:T(8,128)}) custom-call(s32[1]{0:T(128)} %bitcast.3.refs_0_, bf16[256,1024]{1,0:T(8,128)(2,1)S(1)} %join.15.refs_3_.refs_1_, bf16[256,1024]{1,0:T(8,128)(2,1)S(1)} %collective-permute-done.31.refs_2_, ...), custom_call_target="tpu_custom_call" | custom-call | flops 20000000000 | bytes 400000000 | tf_op jit(solution)/shard_map/unpack/pallas_call | solution.py:723
  (53 shorter events, 1.7 us)
Async XLA Ops:
  0.6 3.8 %collective-permute-start = (bf16[2,2,128,512]{3,2,1,0:T(8,128)(2,1)}, bf16[2,2,128,512]{3,2,1,0:T(8,128)(2,1)S(1)}, u32[]{:S(2)}, u32[]{:S(2)}) collective-permute-start(bf16[2,2,128,512]{3,2,1,0:T(8,128)(2,1)} %refs_4_.1), channel_id=1, source_target_pairs={{0,1},{1,0},{2,3},{3,2},{4,5},{5,4},{6,7},{7,6},{8,9},{9,8},{10,11... | collective-permute-start | bytes 1572872 | tf_op jit(solution)/shard_map/ppermute | solution.py:767
  1.2 3.3 %collective-permute-start.1 = (bf16[2,2,128,512]{3,2,1,0:T(8,128)(2,1)}, bf16[2,2,128,512]{3,2,1,0:T(8,128)(2,1)S(1)}, u32[]{:S(2)}, u32[]{:S(2)}) collective-permute-start(bf16[2,2,128,512]{3,2,1,0:T(8,128)(2,1)} %refs_5_.1), channel_id=1, source_target_pairs={{0,1},{1,0},{2,3},{3,2},{4,5},{5,4},{6,7},{7,6},{8,9},{9,8},{10,11... | collective-permute-start | bytes 1572872 | tf_op jit(solution)/shard_map/ppermute | solution.py:768
  1.2 3.2 %collective-permute-start.2 = (bf16[2,2,128,512]{3,2,1,0:T(8,128)(2,1)}, bf16[2,2,128,512]{3,2,1,0:T(8,128)(2,1)S(1)}, u32[]{:S(2)}, u32[]{:S(2)}) collective-permute-start(bf16[2,2,128,512]{3,2,1,0:T(8,128)(2,1)} %refs_6_.1), channel_id=1, source_target_pairs={{0,1},{1,0},{2,3},{3,2},{4,5},{5,4},{6,7},{7,6},{8,9},{9,8},{10,11... | collective-permute-start | bytes 1572872 | tf_op jit(solution)/shard_map/ppermute | solution.py:769
  23.6 5.8 %collective-permute-start.4 = (bf16[512,1024]{1,0:T(8,128)(2,1)}, bf16[512,1024]{1,0:T(8,128)(2,1)}, u32[]{:S(2)}, u32[]{:S(2)}) collective-permute-start(bf16[512,1024]{1,0:T(8,128)(2,1)} %get-tuple-element.127), channel_id=1, source_target_pairs={{0,1},{1,0},{2,3},{3,2},{4,5},{5,4},{6,7},{7,6},{8,9},{9,8},{10,11... | collective-permute-start | bytes 3145736 | tf_op jit(solution)/shard_map/ppermute | solution.py:972
  23.8 10.5 %collective-permute-start.3 = (bf16[512,1024]{1,0:T(8,128)(2,1)}, bf16[512,1024]{1,0:T(8,128)(2,1)}, u32[]{:S(2)}, u32[]{:S(2)}) collective-permute-start(bf16[512,1024]{1,0:T(8,128)(2,1)} %get-tuple-element.126), channel_id=1, source_target_pairs={{0,1},{1,0},{2,3},{3,2},{4,5},{5,4},{6,7},{7,6},{8,9},{9,8},{10,11... | collective-permute-start | bytes 3145736 | tf_op jit(solution)/shard_map/ppermute | solution.py:973
  31.6 11.7 %collective-permute-start.6 = (bf16[256,1024]{1,0:T(8,128)(2,1)}, bf16[256,1024]{1,0:T(8,128)(2,1)}, u32[]{:S(2)}, u32[]{:S(2)}) collective-permute-start(bf16[256,1024]{1,0:T(8,128)(2,1)} %get-tuple-element.129.refs_3_), channel_id=1, source_target_pairs={{0,2},{2,0},{4,6},{6,4},{8,10},{10,8},{12,14},{14,12},{16,18},{18,... | collective-permute-start | bytes 1572872 | tf_op jit(solution)/shard_map/ppermute | solution.py:835
  36.4 14.2 %collective-permute-start.9 = (bf16[256,1024]{1,0:T(8,128)(2,1)}, bf16[256,1024]{1,0:T(8,128)(2,1)}, u32[]{:S(2)}, u32[]{:S(2)}) collective-permute-start(bf16[256,1024]{1,0:T(8,128)(2,1)} %get-tuple-element.130.refs_9_), channel_id=1, source_target_pairs={{0,8},{2,10},{4,12},{6,14},{8,0},{10,2},{12,4},{14,6},{16,24},{18,... | collective-permute-start | bytes 1572872 | tf_op jit(solution)/shard_map/ppermute | solution.py:835
  40.5 5.7 %collective-permute-start.5 = (bf16[768,1024]{1,0:T(8,128)(2,1)S(1)}, bf16[768,1024]{1,0:T(8,128)(2,1)S(1)}, u32[]{:S(2)}, u32[]{:S(2)}) collective-permute-start(bf16[768,1024]{1,0:T(8,128)(2,1)S(1)} %get-tuple-element.138.refs_6_), channel_id=1, source_target_pairs={{0,1},{1,0},{2,3},{3,2},{4,5},{5,4},{6,7},{7,6},{8,9},{9,8},{10,11... | collective-permute-start | bytes 4718600 | tf_op jit(solution)/shard_map/ppermute | solution.py:925
  44.5 8.8 %collective-permute-start.8 = (bf16[128,1024]{1,0:T(8,128)(2,1)S(1)}, bf16[128,1024]{1,0:T(8,128)(2,1)S(1)}, u32[]{:S(2)}, u32[]{:S(2)}) collective-permute-start(bf16[128,1024]{1,0:T(8,128)(2,1)S(1)} %get-tuple-element.145.refs_3_), channel_id=1, source_target_pairs={{0,4},{2,6},{4,0},{6,2},{8,12},{10,14},{12,8},{14,10},{16,20},{18,... | collective-permute-start | bytes 786440 | tf_op jit(solution)/shard_map/ppermute | solution.py:835
  47.1 9.6 %collective-permute-start.11 = (bf16[256,1024]{1,0:T(8,128)(2,1)}, bf16[256,1024]{1,0:T(8,128)(2,1)}, u32[]{:S(2)}, u32[]{:S(2)}) collective-permute-start(bf16[256,1024]{1,0:T(8,128)(2,1)} %get-tuple-element.146.refs_8_), channel_id=1, source_target_pairs={{0,2},{2,0},{4,6},{6,4},{8,10},{10,8},{12,14},{14,12},{16,18},{18,... | collective-permute-start | bytes 1572872 | tf_op jit(solution)/shard_map/ppermute | solution.py:835
  50.5 4.5 %collective-permute-start.7 = (bf16[656,1024]{1,0:T(8,128)(2,1)S(1)}, bf16[656,1024]{1,0:T(8,128)(2,1)S(1)}, u32[]{:S(2)}, u32[]{:S(2)}) collective-permute-start(bf16[656,1024]{1,0:T(8,128)(2,1)S(1)} %get-tuple-element.148.refs_3_), channel_id=1, source_target_pairs={{0,1},{1,0},{2,3},{3,2},{4,5},{5,4},{6,7},{7,6},{8,9},{9,8},{10,11... | collective-permute-start | bytes 4030472 | tf_op jit(solution)/shard_map/ppermute | solution.py:956
  51.8 9.6 %collective-permute-start.14 = (bf16[128,1024]{1,0:T(8,128)(2,1)S(1)}, bf16[128,1024]{1,0:T(8,128)(2,1)S(1)}, u32[]{:S(2)}, u32[]{:S(2)}) collective-permute-start(bf16[128,1024]{1,0:T(8,128)(2,1)S(1)} %get-tuple-element.151.refs_3_), channel_id=1, source_target_pairs={{0,2},{2,0},{4,6},{6,4},{8,10},{10,8},{12,14},{14,12},{16,18},{18,... | collective-permute-start | bytes 786440 | tf_op jit(solution)/shard_map/ppermute | solution.py:835
  53.4 5.4 %collective-permute-start.10 = (bf16[64,1024]{1,0:T(8,128)(2,1)S(1)}, bf16[64,1024]{1,0:T(8,128)(2,1)S(1)}, u32[]{:S(2)}, u32[]{:S(2)}) collective-permute-start(bf16[64,1024]{1,0:T(8,128)(2,1)S(1)} %get-tuple-element.153.refs_3_), channel_id=1, source_target_pairs={{0,8},{2,10},{4,12},{6,14},{8,0},{10,2},{12,4},{14,6},{16,24},{18,... | collective-permute-start | bytes 393224 | tf_op jit(solution)/shard_map/ppermute | solution.py:835
  55.0 1.1 copy-start
  56.0 10.9 %collective-permute-start.16 = (bf16[272,1024]{1,0:T(8,128)(2,1)S(1)}, bf16[272,1024]{1,0:T(8,128)(2,1)S(1)}, u32[]{:S(2)}, u32[]{:S(2)}) collective-permute-start(bf16[272,1024]{1,0:T(8,128)(2,1)S(1)} %get-tuple-element.156.refs_3_), channel_id=1, source_target_pairs={{0,2},{2,0},{4,6},{6,4},{8,10},{10,8},{12,14},{14,12},{16,18},{18,... | collective-permute-start | bytes 1671176 | tf_op jit(solution)/shard_map/ppermute | solution.py:835
  57.8 12.8 %collective-permute-start.13 = (bf16[128,1024]{1,0:T(8,128)(2,1)S(1)}, bf16[128,1024]{1,0:T(8,128)(2,1)S(1)}, u32[]{:S(2)}, u32[]{:S(2)}) collective-permute-start(bf16[128,1024]{1,0:T(8,128)(2,1)S(1)} %get-tuple-element.157.refs_2_), channel_id=1, source_target_pairs={{0,8},{2,10},{4,12},{6,14},{8,0},{10,2},{12,4},{14,6},{16,24},{18,... | collective-permute-start | bytes 786440 | tf_op jit(solution)/shard_map/ppermute | solution.py:835
  58.8 19.2 %collective-permute-start.12 = (bf16[64,1024]{1,0:T(8,128)(2,1)S(1)}, bf16[64,1024]{1,0:T(8,128)(2,1)S(1)}, u32[]{:S(2)}, u32[]{:S(2)}) collective-permute-start(bf16[64,1024]{1,0:T(8,128)(2,1)S(1)} %add_all.4.refs_3_.refs_0_), channel_id=1, source_target_pairs={{0,16},{2,18},{4,20},{6,22},{8,24},{10,26},{12,28},{14,30},{16,0},... | collective-permute-start | bytes 393224 | tf_op jit(solution)/shard_map/ppermute | solution.py:835
  61.5 6.5 %collective-permute-start.15 = (bf16[64,1024]{1,0:T(8,128)(2,1)S(1)}, bf16[64,1024]{1,0:T(8,128)(2,1)S(1)}, u32[]{:S(2)}, u32[]{:S(2)}) collective-permute-start(bf16[64,1024]{1,0:T(8,128)(2,1)S(1)} %get-tuple-element.161.refs_3_), channel_id=1, source_target_pairs={{0,4},{2,6},{4,0},{6,2},{8,12},{10,14},{12,8},{14,10},{16,20},{18,... | collective-permute-start | bytes 393224 | tf_op jit(solution)/shard_map/ppermute | solution.py:835
  67.1 6.8 %collective-permute-start.18 = (bf16[144,1024]{1,0:T(8,128)(2,1)S(1)}, bf16[144,1024]{1,0:T(8,128)(2,1)S(1)}, u32[]{:S(2)}, u32[]{:S(2)}) collective-permute-start(bf16[144,1024]{1,0:T(8,128)(2,1)S(1)} %get-tuple-element.163.refs_2_), channel_id=1, source_target_pairs={{0,4},{2,6},{4,0},{6,2},{8,12},{10,14},{12,8},{14,10},{16,20},{18,... | collective-permute-start | bytes 884744 | tf_op jit(solution)/shard_map/ppermute | solution.py:835
  68.0 10.8 %collective-permute-start.20 = (bf16[64,1024]{1,0:T(8,128)(2,1)S(1)}, bf16[64,1024]{1,0:T(8,128)(2,1)S(1)}, u32[]{:S(2)}, u32[]{:S(2)}) collective-permute-start(bf16[64,1024]{1,0:T(8,128)(2,1)S(1)} %add_all.5.refs_3_.refs_0_), channel_id=1, source_target_pairs={{0,16},{2,18},{4,20},{6,22},{8,24},{10,26},{12,28},{14,30},{16,0},... | collective-permute-start | bytes 393224 | tf_op jit(solution)/shard_map/ppermute | solution.py:835
  70.7 5.0 %collective-permute-start.17 = (bf16[64,1024]{1,0:T(8,128)(2,1)S(1)}, bf16[64,1024]{1,0:T(8,128)(2,1)S(1)}, u32[]{:S(2)}, u32[]{:S(2)}) collective-permute-start(bf16[64,1024]{1,0:T(8,128)(2,1)S(1)} %get-tuple-element.165.refs_3_), channel_id=1, source_target_pairs={{0,4},{2,6},{4,0},{6,2},{8,12},{10,14},{12,8},{14,10},{16,20},{18,... | collective-permute-start | bytes 393224 | tf_op jit(solution)/shard_map/ppermute | solution.py:835
  74.0 10.0 %collective-permute-start.22 = (bf16[80,1024]{1,0:T(8,128)(2,1)S(1)}, bf16[80,1024]{1,0:T(8,128)(2,1)S(1)}, u32[]{:S(2)}, u32[]{:S(2)}) collective-permute-start(bf16[80,1024]{1,0:T(8,128)(2,1)S(1)} %get-tuple-element.167.refs_2_), channel_id=1, source_target_pairs={{0,8},{2,10},{4,12},{6,14},{8,0},{10,2},{12,4},{14,6},{16,24},{18,... | collective-permute-start | bytes 491528 | tf_op jit(solution)/shard_map/ppermute | solution.py:835
  75.8 11.5 %collective-permute-start.24 = (bf16[64,1024]{1,0:T(8,128)(2,1)S(1)}, bf16[64,1024]{1,0:T(8,128)(2,1)S(1)}, u32[]{:S(2)}, u32[]{:S(2)}) collective-permute-start(bf16[64,1024]{1,0:T(8,128)(2,1)S(1)} %add_all.6.refs_2_.refs_0_), channel_id=1, source_target_pairs={{0,16},{2,18},{4,20},{6,22},{8,24},{10,26},{12,28},{14,30},{16,0},... | collective-permute-start | bytes 393224 | tf_op jit(solution)/shard_map/ppermute | solution.py:835
  78.0 8.9 %collective-permute-start.19 = (bf16[64,1024]{1,0:T(8,128)(2,1)S(1)}, bf16[64,1024]{1,0:T(8,128)(2,1)S(1)}, u32[]{:S(2)}, u32[]{:S(2)}) collective-permute-start(bf16[64,1024]{1,0:T(8,128)(2,1)S(1)} %add_last.4.refs_2_.refs_1_), channel_id=1, source_target_pairs={{0,8},{2,10},{4,12},{6,14},{8,0},{10,2},{12,4},{14,6},{16,24},{18,... | collective-permute-start | bytes 393224 | tf_op jit(solution)/shard_map/ppermute | solution.py:835
  78.9 5.4 %collective-permute-start.21 = (bf16[64,1024]{1,0:T(8,128)(2,1)S(1)}, bf16[64,1024]{1,0:T(8,128)(2,1)S(1)}, u32[]{:S(2)}, u32[]{:S(2)}) collective-permute-start(bf16[64,1024]{1,0:T(8,128)(2,1)S(1)} %add_last.5.refs_2_.refs_1_), channel_id=1, source_target_pairs={{0,4},{2,6},{4,0},{6,2},{8,12},{10,14},{12,8},{14,10},{16,20},{18,... | collective-permute-start | bytes 393224 | tf_op jit(solution)/shard_map/ppermute | solution.py:835
  84.0 8.7 %collective-permute-start.23 = (bf16[80,1024]{1,0:T(8,128)(2,1)S(1)}, bf16[80,1024]{1,0:T(8,128)(2,1)S(1)}, u32[]{:S(2)}, u32[]{:S(2)}) collective-permute-start(bf16[80,1024]{1,0:T(8,128)(2,1)S(1)} %add_all.7.refs_3_.refs_0_), channel_id=1, source_target_pairs={{0,16},{2,18},{4,20},{6,22},{8,24},{10,26},{12,28},{14,30},{16,0},... | collective-permute-start | bytes 491528 | tf_op jit(solution)/shard_map/ppermute | solution.py:835
  84.3 15.5 %collective-permute-start.30 = (bf16[128,1024]{1,0:T(8,128)(2,1)S(1)}, bf16[128,1024]{1,0:T(8,128)(2,1)S(1)}, u32[]{:S(2)}, u32[]{:S(2)}) collective-permute-start(bf16[128,1024]{1,0:T(8,128)(2,1)S(1)} %join.8.refs_3_.refs_1_), channel_id=1, source_target_pairs={{0,2},{2,0},{4,6},{6,4},{8,10},{10,8},{12,14},{14,12},{16,18},{18,... | collective-permute-start | bytes 786440 | tf_op jit(solution)/shard_map/ppermute | solution.py:835
  86.9 2.2 %copy-start.1 = (bf16[656,1024]{1,0:T(8,128)(2,1)S(1)}, bf16[656,1024]{1,0:T(8,128)(2,1)}, u32[]{:S(2)}) copy-start(bf16[656,1024]{1,0:T(8,128)(2,1)} %copy-done) | copy-start | bytes 4030468
  87.0 9.3 %collective-permute-start.26 = (bf16[128,1024]{1,0:T(8,128)(2,1)S(1)}, bf16[128,1024]{1,0:T(8,128)(2,1)S(1)}, u32[]{:S(2)}, u32[]{:S(2)}) collective-permute-start(bf16[128,1024]{1,0:T(8,128)(2,1)S(1)} %join.9.refs_6_.refs_2_.refs_1_), channel_id=1, source_target_pairs={{0,4},{2,6},{4,0},{6,2},{8,12},{10,14},{12,8},{14,10},{16,20},{18,... | collective-permute-start | bytes 786440 | tf_op jit(solution)/shard_map/ppermute | solution.py:835
  87.3 7.5 %collective-permute-start.27 = (bf16[64,1024]{1,0:T(8,128)(2,1)S(1)}, bf16[64,1024]{1,0:T(8,128)(2,1)S(1)}, u32[]{:S(2)}, u32[]{:S(2)}) collective-permute-start(bf16[64,1024]{1,0:T(8,128)(2,1)S(1)} %add_last.6.refs_2_.refs_1_), channel_id=1, source_target_pairs={{0,4},{2,6},{4,0},{6,2},{8,12},{10,14},{12,8},{14,10},{16,20},{18,... | collective-permute-start | bytes 393224 | tf_op jit(solution)/shard_map/ppermute | solution.py:835
  92.7 5.0 %collective-permute-start.25 = (bf16[64,1024]{1,0:T(8,128)(2,1)S(1)}, bf16[64,1024]{1,0:T(8,128)(2,1)S(1)}, u32[]{:S(2)}, u32[]{:S(2)}) collective-permute-start(bf16[64,1024]{1,0:T(8,128)(2,1)S(1)} %get-tuple-element.172.refs_3_.refs_1_), channel_id=1, source_target_pairs={{0,8},{2,10},{4,12},{6,14},{8,0},{10,2},{12,4},{14,6},{16,24},{18,... | collective-permute-start | bytes 393224 | tf_op jit(solution)/shard_map/ppermute | solution.py:835
  94.8 8.9 %collective-permute-start.29 = (bf16[128,1024]{1,0:T(8,128)(2,1)S(1)}, bf16[128,1024]{1,0:T(8,128)(2,1)S(1)}, u32[]{:S(2)}, u32[]{:S(2)}) collective-permute-start(bf16[128,1024]{1,0:T(8,128)(2,1)S(1)} %join.10.refs_3_.refs_1_), channel_id=1, source_target_pairs={{0,8},{2,10},{4,12},{6,14},{8,0},{10,2},{12,4},{14,6},{16,24},{18,... | collective-permute-start | bytes 786440 | tf_op jit(solution)/shard_map/ppermute | solution.py:835
  96.3 13.4 %collective-permute-start.34 = (bf16[256,1024]{1,0:T(8,128)(2,1)S(1)}, bf16[256,1024]{1,0:T(8,128)(2,1)S(1)}, u32[]{:S(2)}, u32[]{:S(2)}) collective-permute-start(bf16[256,1024]{1,0:T(8,128)(2,1)S(1)} %join.11.refs_3_.refs_1_), channel_id=1, source_target_pairs={{0,2},{2,0},{4,6},{6,4},{8,10},{10,8},{12,14},{14,12},{16,18},{18,... | collective-permute-start | bytes 1572872 | tf_op jit(solution)/shard_map/ppermute | solution.py:835
  97.8 9.2 %collective-permute-start.28 = (bf16[128,1024]{1,0:T(8,128)(2,1)S(1)}, bf16[128,1024]{1,0:T(8,128)(2,1)S(1)}, u32[]{:S(2)}, u32[]{:S(2)}) collective-permute-start(bf16[128,1024]{1,0:T(8,128)(2,1)S(1)} %join.12.refs_3_.refs_1_), channel_id=1, source_target_pairs={{0,4},{2,6},{4,0},{6,2},{8,12},{10,14},{12,8},{14,10},{16,20},{18,... | collective-permute-start | bytes 786440 | tf_op jit(solution)/shard_map/ppermute | solution.py:835
  99.8 15.8 %collective-permute-start.32 = (bf16[256,1024]{1,0:T(8,128)(2,1)S(1)}, bf16[256,1024]{1,0:T(8,128)(2,1)S(1)}, u32[]{:S(2)}, u32[]{:S(2)}) collective-permute-start(bf16[256,1024]{1,0:T(8,128)(2,1)S(1)} %join.13.refs_3_.refs_1_), channel_id=1, source_target_pairs={{0,8},{2,10},{4,12},{6,14},{8,0},{10,2},{12,4},{14,6},{16,24},{18,... | collective-permute-start | bytes 1572872 | tf_op jit(solution)/shard_map/ppermute | solution.py:835
  103.8 10.2 %collective-permute-start.33 = (bf16[256,1024]{1,0:T(8,128)(2,1)S(1)}, bf16[256,1024]{1,0:T(8,128)(2,1)S(1)}, u32[]{:S(2)}, u32[]{:S(2)}) collective-permute-start(bf16[256,1024]{1,0:T(8,128)(2,1)S(1)} %join.14.refs_3_.refs_1_), channel_id=1, source_target_pairs={{0,2},{2,0},{4,6},{6,4},{8,10},{10,8},{12,14},{14,12},{16,18},{18,... | collective-permute-start | bytes 1572872 | tf_op jit(solution)/shard_map/ppermute | solution.py:835
  107.1 12.6 %collective-permute-start.31 = (bf16[256,1024]{1,0:T(8,128)(2,1)S(1)}, bf16[256,1024]{1,0:T(8,128)(2,1)S(1)}, u32[]{:S(2)}, u32[]{:S(2)}) collective-permute-start(bf16[256,1024]{1,0:T(8,128)(2,1)S(1)} %join.15.refs_3_.refs_1_), channel_id=1, source_target_pairs={{0,2},{2,0},{4,6},{6,4},{8,10},{10,8},{12,14},{14,12},{16,18},{18,... | collective-permute-start | bytes 1572872 | tf_op jit(solution)/shard_map/ppermute | solution.py:835

commit v5 on v4

--- a/solution.py
+++ b/solution.py
@@ -16,15 +16,15 @@
 BF = jnp.bfloat16
 F32 = jnp.float32
 MIB = 1 << 20
-ORDER = "XfFGSfxTFfsxfFsFxsxfFsFfPxsxfsFxsfxFs"
+ORDER = "JFKfXGSfxTFfsxfFsFxsxfsPFfxFsxfsFxfsxFs"
 PLANE_FIRST = ((1, 2), (2, 1), (4, 4), (8, 8))
 BETWEEN = ((1, 2), (4, 4), (2, 1), (8, 8))
 LINE_FIRST = ((4, 4), (1, 2), (2, 1), (8, 8))
-ROUTES = {"f": PLANE_FIRST, "F": LINE_FIRST, "x": BETWEEN, "s": PLANE_FIRST}
+ROUTES = {"f": BETWEEN, "F": LINE_FIRST, "x": BETWEEN, "s": PLANE_FIRST}
 SMALL_COST = {"flops": 20_000_000_000, "bytes_accessed": 400_000_000}
 COST = {
     name: {"flops": 100_000_000_000, "bytes_accessed": 1000}
-    for name in ("forward", "feed_keep", "cross", "cross_grads", "self", "self_grads")
+    for name in ("forward", "feed_back", "feed_keep", "cross", "cross_grads", "self", "self_grads")
 }
 LANES = 1024
 
@@ -181,32 +181,62 @@
     ]
 
 
-def feed_grads(which, in_ref, out_ref, slow_t, ginner, gff_t, hidden):
-    inner, width = hidden.shape[1], slow_t.shape[0]
-    half_in, half_out = inner // 2, width // 2
-
-    def give_in(index):
+def give_out_steps(which, ref, gff_t, hidden):
+    half = gff_t.shape[0] // 2
+
+    def give(index):
         def run():
-            cols = pl.ds(pl.multiple_of(which * half_in + index * 256, 256), 256)
-            in_ref[:, index * 256 : (index + 1) * 256] = mm(slow_t[...], ginner[:, cols]).astype(BF)
-
-        return run
-
-    def give_out(index):
-        def run():
-            feats = pl.ds(pl.multiple_of(which * half_out, half_out), half_out)
-            low, at = (index // 2) * half_out, (index % 2) * 512
-            out_ref[low : low + half_out, at : at + 512] = mm(
+            feats = pl.ds(pl.multiple_of(which * half, half), half)
+            low, at = (index // 2) * half, (index % 2) * 512
+            ref[low : low + half, at : at + 512] = mm(
                 gff_t[feats, :], hidden[:, index * 512 : (index + 1) * 512]
             ).astype(BF)
 
         return run
 
-    return [give_out(i) for i in range(inner // 512)] + [give_in(i) for i in range(half_in // 256)]
-
-
-def feed_keep_kernel(numbers_ref, gff_t, hidden, slow_t, ginner, in_ref, out_ref):
-    weave(feed_grads(numbers_ref[0], in_ref, out_ref, slow_t, ginner, gff_t, hidden))
+    return [give(index) for index in range(hidden.shape[1] // 512)]
+
+
+def give_in_steps(which, ref, slow_t, ginner):
+    length, inner = ginner[0].shape
+    half = inner // 2
+
+    def give(index):
+        def run():
+            cols = pl.ds(pl.multiple_of(which * half + index * 256, 256), 256)
+            total = mm(slow_t[:, 0:length], ginner[0][:, cols]) + mm(slow_t[:, length:], ginner[1][:, cols])
+            ref[:, index * 256 : (index + 1) * 256] = total.astype(BF)
+
+        return run
+
+    return [give(index) for index in range(half // 256)]
+
+
+def feed_back_steps(gff, w_fo, slope, ginner):
+    step = 256
+
+    def shrink(index, _):
+        return mm_bt(gff[...], w_fo[index * step : (index + 1) * step, :]).astype(BF)
+
+    def bend(index, grad_hidden):
+        cols = slice(index * step, (index + 1) * step)
+        ginner[:, cols] = (grad_hidden.astype(F32) * slope[:, cols].astype(F32)).astype(BF)
+
+    return staged(ginner.shape[1] // step, shrink, bend)
+
+
+def feed_kernel(numbers_ref, gff, w_fo, slope, slow_t, gff_t, hidden, ginner_first, send_in, keep_out, ginner_last):
+    place = numbers_ref[0]
+    length = ginner_last.shape[0]
+    weave(
+        feed_back_steps(gff.at[length:], w_fo, slope.at[length:], ginner_last),
+        give_out_steps(place, keep_out, gff_t, hidden),
+    )
+    weave(give_in_steps(1 - place, send_in, slow_t, (ginner_first, ginner_last)))
+
+
+def feed_keep_kernel(numbers_ref, slow_t, ginner_first, ginner_last, keep_in):
+    weave(give_in_steps(numbers_ref[0], keep_in, slow_t, (ginner_first, ginner_last)))
 
 
 class Weights(NamedTuple):
@@ -225,13 +255,16 @@
 class Kept(NamedTuple):
     out_own: Any
     out_oth: Any
-    send_in: Any
     send_out: Any
+    gff: Any
     gff_t: Any
     hidden: Any
+    slope: Any
     slow_t: Any
     ginner: Any
-    gss: Any
+    third: Any
+    xhat2: Any
+    rstd2: Any
     elow: Any
     qkv: Any
     p_self: Any
@@ -253,16 +286,18 @@
     w_so: Any
     w_cq: Any
     w_co: Any
+    w_fi: Any
+    w_fo: Any
 
 
 def forward_kernel(numbers_ref, *refs):
     (dec2_in, enc2_in, og2_in, dec_in, enc_in, og_in), refs = refs[:6], refs[6:]
     weights_in, refs = Weights(*refs[: len(Weights._fields)]), refs[len(Weights._fields) :]
     kept, refs = Kept(*refs[: len(Kept._fields)]), refs[len(Kept._fields) :]
-    (out_own, out_oth, send_in, send_out, gff_t, hidden, slow_t, ginner, gss, elow, qkv, p_self, rl_self, att_t, xhat1,
-     rstd1, flow, encs, cq, ckv, p_cross, rl_cross, crossed_t, dnorm_ref) = kept[:24]
-    w = Weights(*refs[:1], kept.w_qkv, kept.w_gain, refs[1], kept.w_ckv, kept.w_so, kept.w_cq, kept.w_co, *refs[2:4])
-    (dec_s, og_s, bias_ref, att, xhat2, rstd2, third, slow, slope, gff, outs, sems) = refs[4:]
+    (out_own, out_oth, send_out, gff, gff_t, hidden, slope, slow_t, ginner, third, xhat2, rstd2, elow, qkv, p_self,
+     rl_self, att_t, xhat1, rstd1, flow, encs, cq, ckv, p_cross, rl_cross, crossed_t, dnorm_ref) = kept[:27]
+    w = Weights(refs[0], kept.w_qkv, kept.w_gain, refs[1], *kept[29:])
+    (dec_s, og_s, bias_ref, att, slow, outs, sems) = refs[2:]
     crossed = att
     at = Weights(*range(len(Weights._fields)))
     dec, enc, og = (-1, -2, -3)
@@ -270,7 +305,7 @@
     place = numbers_ref[0]
     tokens, width = dec_s.shape
     length = tokens // 2
-    inner = ginner.shape[1]
+    inner = hidden.shape[1]
     where = halves(place, length)
     for s in range(2):
         copies.start(dec, dec_in.at[place, s], dec_s.at[where[s][0]])
@@ -387,29 +422,6 @@
             out_oth[:, s * width : (s + 1) * width] = outs[where[s][1], :]
 
         return [shrink(0), shrink(1), norm, turn]
-
-    def feed_back(s):
-        def shrink(index, _):
-            return mm_bt(gff[rows[s]], w.fo[index * step : (index + 1) * step, :]).astype(BF)
-
-        def bend(index, grad_hidden):
-            cols = slice(index * step, (index + 1) * step)
-            ginner[rows[s], cols] = (grad_hidden.astype(F32) * slope[rows[s], cols].astype(F32)).astype(BF)
-
-        return staged(inner // step, shrink, bend)
-
-    def after_feed_back(s):
-        def shrink(part):
-            def run():
-                cols = slice(part * (width // 2), (part + 1) * (width // 2))
-                third[rows[s], cols] += mm_bt(ginner[rows[s]], w.fi[cols, :])
-
-            return run
-
-        def norm():
-            gss[rows[s]], *gains[1, s] = norm_backward(xhat2[rows[s]], rstd2[rows[s], 0:1], gain[1:2], third[rows[s]])
-
-        return [shrink(0), shrink(1), norm]
 
     copies.wait(at.table, at.gain, at.nbias, dec, at.qkv)
     gain = w.gain[...].astype(F32)
@@ -440,26 +452,41 @@
     )
     weave(feed(0), after_cross(1))
     weave(feed(1), after_feed(0))
-    weave(feed_back(0), after_feed(1))
-    weave(feed_back(1), after_feed_back(0))
-    weave(feed_grads(1 - place, send_in, send_out, slow_t, ginner, gff_t, hidden), after_feed_back(1))
+    weave(feed_back_steps(gff.at[0:length], w.fo, slope.at[0:length], ginner), after_feed(1))
+    weave(give_out_steps(1 - place, send_out, gff_t, hidden))
     dnorm_ref[...] = jnp.zeros(dnorm_ref.shape, F32)
-    for k in (1, 2):
-        dnorm_ref[k : k + 1, :] = gains[k, 0][0] + gains[k, 1][0]
-        dnorm_ref[3 + k : 4 + k, :] = gains[k, 0][1] + gains[k, 1][1]
+    dnorm_ref[2:3, :] = gains[2, 0][0] + gains[2, 1][0]
+    dnorm_ref[5:6, :] = gains[2, 0][1] + gains[2, 1][1]
     copies.wait()
 
 
 def cross_kernel(
-    gss, dnorm_in, w_gain, w_co, w_cq, ckv, cq, p_cross, rl_cross, crossed_t, xhat1, rstd1,
+    third, ginner_first, ginner_last, w_fi, xhat2, rstd2, dnorm_in, w_gain, w_co, w_cq, ckv, cq, p_cross, rl_cross, crossed_t, xhat1, rstd1,
     branch, gq_t, gkv_t, gfs, dnorm_ref,
-    go_t,
+    go_t, gss,
 ):
     tokens, width = gss.shape
     length = tokens // 2
     rows = [slice(s * length, (s + 1) * length) for s in range(2)]
     gain = w_gain[...].astype(F32)
-    gains = {}
+    gains, seconds = {}, {}
+    ginner = (ginner_first, ginner_last)
+
+    def before(s):
+        held = []
+
+        def shrink(part):
+            def run():
+                cols = slice(part * (width // 2), (part + 1) * (width // 2))
+                held.append(third[rows[s], cols] + mm_bt(ginner[s][...], w_fi[cols, :]))
+
+            return run
+
+        def norm():
+            upstream = jnp.concatenate(held, 1)
+            gss[rows[s]], *seconds[s] = norm_backward(xhat2[rows[s]], rstd2[rows[s], 0:1], gain[1:2], upstream)
+
+        return [shrink(0), shrink(1), norm, begin(s)]
 
     def begin(s):
         def run():
@@ -485,13 +512,14 @@
             s, length, cq, ckv, ckv, 0, width, p_cross, rl_cross, crossed_t, go_t, gq_t, gkv_t, gkv_t, 0, width
         )
 
-    begin(0)()
-    weave(attention(0), [begin(1)])
+    weave(before(0))
+    weave(attention(0), before(1))
     weave(attention(1), after(0))
     weave(after(1))
     dnorm_ref[...] = dnorm_in[...]
-    dnorm_ref[0:1, :] = gains[0][0] + gains[1][0]
-    dnorm_ref[3:4, :] = gains[0][1] + gains[1][1]
+    for k, sums in enumerate((gains, seconds)):
+        dnorm_ref[k : k + 1, :] = sums[0][0] + sums[1][0]
+        dnorm_ref[3 + k : 4 + k, :] = sums[0][1] + sums[1][1]
 
 
 def give_tall(which, ref, mixed_t, branch):
@@ -781,13 +809,16 @@
     kinds = Kept(
         out_own=(rows, BF),
         out_oth=((local_len, LANES), BF),
-        send_in=(buffer, BF),
         send_out=(buffer, BF),
+        gff=(whole, BF),
         gff_t=(turned, BF),
         hidden=((tokens, inner), BF),
+        slope=((tokens, inner), BF),
         slow_t=(turned, BF),
-        ginner=((tokens, inner), BF),
-        gss=(whole, F32),
+        ginner=((length, inner), BF),
+        third=(whole, F32),
+        xhat2=(whole, F32),
+        rstd2=((tokens, 128), F32),
         elow=(whole, BF),
         qkv=((tokens, 3 * width), BF),
         p_self=(probs, BF),
@@ -809,16 +840,17 @@
         w_so=like(self_out),
         w_cq=like(cross_q),
         w_co=like(cross_out),
+        w_fi=like(ff_in),
+        w_fo=like(ff_out),
     )
     kept = call(
         forward_kernel,
         (numbers,),
         (dec2, enc2, og2),
         list(kinds),
-        [like(lang_table), like(norm_bias), like(ff_in), like(ff_out)]
-        + [
-            (whole, BF), (whole, BF), ((4, length, length), F32), (whole, BF), (whole, F32), ((tokens, 128), F32),
-            (whole, F32), (whole, BF), ((tokens, inner), BF), (whole, BF), (whole, BF),
+        [
+            like(lang_table), like(norm_bias), (whole, BF), (whole, BF), ((4, length, length), F32), (whole, BF),
+            (whole, BF), (whole, BF),
         ],
         name="forward",
         far=(dec_in, enc_out, out_grad, *params),
@@ -887,23 +919,45 @@
         )
         yield unpacked
 
-    held.keep_in, held.keep_out = call(
-        feed_keep_kernel,
-        (numbers,),
-        [held.gff_t, held.hidden, held.slow_t, held.ginner],
-        [(buffer, BF), (buffer, BF)],
-        name="feed_keep",
-    )
-    last[:] = [held.keep_in]
+    last[:] = [held.dnorm]
+
+    def feed_back():
+        send, held.keep_out, held.ginner_last = call(
+            feed_kernel,
+            (numbers,),
+            [held.gff, held.w_fo, held.slope, held.slow_t, held.gff_t, held.hidden, held.ginner],
+            [(buffer, BF), (buffer, BF), ((length, inner), BF)],
+            name="feed_back",
+            after=last,
+        )
+        last[:] = [send]
+        held.got_in = lax.ppermute(send, "seq", swap)
+        groups["F"] = reduce_all(held.keep_out, held.got_out, [(inner, half)], unpack_out, ROUTES["F"])
+
+    def feed_keep():
+        (keep,) = call(
+            feed_keep_kernel,
+            (numbers,),
+            [held.slow_t, held.ginner, held.ginner_last],
+            [(buffer, BF)],
+            name="feed_keep",
+            after=last,
+        )
+        last[:] = [keep]
+        groups["f"] = reduce_all(keep, held.got_in, [(width, inner // 2)], unpack_in, ROUTES["f"])
 
     def cross_back():
         held.cross_branch, held.gq_t, held.gkv_t, held.gfs, held.dnorm = (
             call(
                 cross_kernel,
                 (),
-                [held.gss, held.dnorm, held.w_gain, held.w_co, held.w_cq, held.ckv, held.cq, held.p_cross, held.rl_cross, held.crossed_t, held.xhat1, held.rstd1],
+                [
+                    held.third, held.ginner, held.ginner_last, held.w_fi, held.xhat2, held.rstd2, held.dnorm, held.w_gain,
+                    held.w_co, held.w_cq, held.ckv, held.cq, held.p_cross, held.rl_cross, held.crossed_t, held.xhat1,
+                    held.rstd1,
+                ],
                 [(whole, BF), (turned, BF), ((2 * width, tokens), BF), (whole, F32), ((8, width), F32)],
-                [(turned, BF)],
+                [(turned, BF), (whole, F32)],
                 name="cross",
                 after=last,
             )
@@ -968,11 +1022,9 @@
             after=last,
         )
 
-    groups = {
-        "f": reduce_all(held.keep_in, lax.ppermute(held.send_in, "seq", swap), [(width, inner // 2)], unpack_in, ROUTES["f"]),
-        "F": reduce_all(held.keep_out, lax.ppermute(held.send_out, "seq", swap), [(inner, half)], unpack_out, ROUTES["F"]),
-    }
-    kernels = {"X": cross_back, "G": cross_grads, "S": self_back, "T": self_grads, "P": place_all}
+    groups = {}
+    held.got_out = lax.ppermute(held.send_out, "seq", swap)
+    kernels = {"J": feed_back, "K": feed_keep, "X": cross_back, "G": cross_grads, "S": self_back, "T": self_grads, "P": place_all}
     sums = {}
     for letter in ORDER:
         if letter in kernels:

time: 122 us -> 118 us (0.967)
  waiting for transfers between devices: 30.1 us -> 22 us
  starting transfers between devices: 36.2 us -> 42.8 us
  Pallas kernels: 50.5 us -> 48.6 us
    ppermute x28, waiting for transfers between devices: 30.1 us -> 22 us  [travel(): return lax.ppermute(array, ('dp', 'seq'), flips(core_zero, core_one))]
    ppermute x28, starting transfers between devices: 34.4 us -> 40.8 us  [travel(): return lax.ppermute(array, ('dp', 'seq'), flips(core_zero, core_one))]
    pallas_call x39 -> x40, Pallas kernels: 50.5 us -> 48.6 us  [call(): pl.pallas_call(body, out_shape=tuple((pltpu.VMEM(s, d) for s, d in outs))...]
  transfers between devices with their start and end apart: 35 -> 35, of which waited for: 14 -> 11; matrix products, arithmetic and copies ran while one was open for 2% -> 2% of each run, Pallas kernels for 25% -> 26%
where the time goes in v5:
time: 118 us
  Pallas kernels  48.6 us (41%)
  starting transfers between devices  42.8 us (36%)
  waiting for transfers between devices  22 us (19%)
  other arithmetic  2.8 us (2%)
    pallas_call x40, Pallas kernels, call(): pl.pallas_call(body, out_shape=tuple((pltpu.VMEM(s, d) for s, d in outs))...  48.6 us
    ppermute x28, starting transfers between devices, travel(): return lax.ppermute(array, ('dp', 'seq'), flips(core_zero, core_one))  40.8 us
    ppermute x28, waiting for transfers between devices, travel(): return lax.ppermute(array, ('dp', 'seq'), flips(core_zero, core_one))  22 us
  transfers between devices with their start and end apart: 35, of which 11 were waited for; matrix products, arithmetic and copies ran while one was open for 2% of the time, Pallas kernels for 26%

profile of v5, /device:TPU:0, one launch (start us, length us, event | category | flops | bytes accessed | tf_op | source)
XLA Modules:
  0.0 117.9 jit_solution(9987492468875823824)
XLA Ops:
  0.6 0.5 collective-permute-start
  1.2 0.4 collective-permute-start.2
  1.7 1.3 %select_reduce_fusion.2 = s32[]{:T(128)} fusion(s32[2]{0:T(128)} %param.21, s32[]{:T(128)} %axis_index.22), kind=kLoop, calls=%fused_computation.3 | loop fusion | flops 5 | bytes 16 | tf_op jit(solution)/shard_map/reduce_sum | solution.py:788
  3.0 0.8 select_reduce_fusion.1
  3.8 0.7 pad_add_fusion.refs_0_
  4.5 15.8 %forward.1 = (bf16[2,128,512]{2,1,0:T(8,128)(2,1)S(1)}, bf16[128,1024]{1,0:T(8,128)(2,1)S(1)}, bf16[512,1024]{1,0:T(8,128)(2,1)S(1)}, bf16[512,512]{1,0:T(8,128)...) custom-call(s32[6]{0:T(128)S(1)} %pad_add_fusion.refs_0_, ...), custom_call_target="tpu_custom_call" | custom-call | flops 99999997952 | bytes 1000 | tf_op jit(solution)/shard_map/forward/pallas_call | solution.py:751
  20.6 2.7 %feed_back.1 = (bf16[512,1024]{1,0:T(8,128)(2,1)S(1)}, bf16[512,1024]{1,0:T(8,128)(2,1)S(1)}, bf16[256,2048]{1,0:T(8,128)(2,1)S(1)}) custom-call(s32[6]{0:T(128)S(1)} %pad_add_fusion.refs_0_, bf16[512,512]{1,0:T(8,128)(2,1)S(1)} %get-tuple-element.109.refs_1_, bf16[2048,512]{1,0:T(8,128)(2,1)S(1)} %get-tuple-element.110.refs_2_, ...), custom_call_target="tpu_custom_call" | custom-call | flops 99999997952 | bytes 1000 | tf_op jit(solution)/shard_map/feed_back/pallas_call | solution.py:751
  23.2 0.4 collective-permute-start.4
  23.6 1.0 add_split.12
  24.6 2.7 %collective-permute-start.9 = (bf16[256,1024]{1,0:T(8,128)(2,1)}, bf16[256,1024]{1,0:T(8,128)(2,1)}, u32[]{:S(2)}, u32[]{:S(2)}) collective-permute-start(bf16[256,1024]{1,0:T(8,128)(2,1)} %get-tuple-element.133.refs_4_), channel_id=1, source_target_pairs={{0,8},{2,10},{4,12},{6,14},{8,0},{10,2},{12,4},{14,6},{16,24},{18,... | collective-permute-start | bytes 1572872 | tf_op jit(solution)/shard_map/ppermute | solution.py:867
  27.3 1.3 %feed_keep.1.refs_1_.refs_3_ = bf16[512,1024]{1,0:T(8,128)(2,1)S(1)} custom-call(s32[6]{0:T(128)S(1)} %pad_add_fusion.refs_0_, bf16[512,512]{1,0:T(8,128)(2,1)S(1)} %get-tuple-element.112.refs_4_.refs_1_, bf16[256,2048]{1,0:T(8,128)(2,1)S(1)} %get-tuple-element.108.refs_7_.refs_2_.refs_1_, bf16[256,2048]{1,0:T(8,128)(2,1)S(1)} %get-tuple-element.116.refs_3_.refs_2_, ...), custom_call_target="tpu_custom_call" | custom-call | flops 99999997952 | bytes 1000 | tf_op jit(solution)/shard_map/feed_keep/pallas_call | solution.py:751
  28.6 1.0 add_split.13
  29.6 1.5 %collective-permute-start.6 = (bf16[256,1024]{1,0:T(8,128)(2,1)}, bf16[256,1024]{1,0:T(8,128)(2,1)}, u32[]{:S(2)}, u32[]{:S(2)}) collective-permute-start(bf16[256,1024]{1,0:T(8,128)(2,1)} %get-tuple-element.134.refs_17_), channel_id=1, source_target_pairs={{0,2},{2,0},{4,6},{6,4},{8,10},{10,8},{12,14},{14,12},{16,18},{18,... | collective-permute-start | bytes 1572872 | tf_op jit(solution)/shard_map/ppermute | solution.py:867
  31.1 5.1 %cross.1 = (bf16[512,512]{1,0:T(8,128)(2,1)S(1)}, bf16[512,512]{1,0:T(8,128)(2,1)S(1)}, bf16[1024,512]{1,0:T(8,128)(2,1)S(1)}, f32[512,512]{1,0:T(8,128)S(1)}, f32[8,512]{1,0:T(8,128)S(1)}) custom-call(f32[512,512]{1,0:T(8,128)S(1)} %get-tuple-element.107.refs_0_, bf16[256,2048]{1,0:T(8,128)(2,1)S(1)} %get-tuple-element.108.refs_7_.refs_2_.refs_1_, ...), custom_call_target="tpu_custom_call" | custom-call | flops 99999997952 | bytes 1000 | tf_op jit(solution)/shard_map/cross/pallas_call | solution.py:751
  36.2 2.4 %cross_grads.1 = (bf16[768,1024]{1,0:T(8,128)(2,1)S(1)}, bf16[512,1024]{1,0:T(8,128)(2,1)S(1)}, bf16[2,128,512]{2,1,0:T(8,128)(2,1)S(1)}) custom-call(s32[6]{0:T(128)S(1)} %pad_add_fusion.refs_0_, bf16[512,512]{1,0:T(8,128)(2,1)S(1)} %get-tuple-element.135.refs_1_, bf16[512,512]{1,0:T(8,128)(2,1)S(1)} %get-tuple-element.136.refs_2_, ...), custom_call_target="tpu_custom_call" | custom-call | flops 99999997952 | bytes 1000 | tf_op jit(solution)/shard_map/cross_grads/pallas_call | solution.py:751
  38.7 2.8 %self.1 = (bf16[512,512]{1,0:T(8,128)(2,1)S(1)}, bf16[1536,512]{1,0:T(8,128)(2,1)S(1)}) custom-call(f32[512,512]{1,0:T(8,128)S(1)} %get-tuple-element.142.refs_9_.refs_0_.refs_1_, bf16[512,512]{1,0:T(8,128)(2,1)S(1)} %get-tuple-element.145.refs_1_, bf16[512,1536]{1,0:T(8,128)(2,1)S(1)} %get-tuple-element.146.refs_2_, ...), custom_call_target="tpu_custom_call" | custom-call | flops 99999997952 | bytes 1000 | tf_op jit(solution)/shard_map/self/pallas_call | solution.py:751
  41.6 1.2 add_split.14
  42.7 0.5 collective-permute-start.8
  43.3 1.0 add_split.15
  44.2 1.3 %collective-permute-start.13 = (bf16[256,1024]{1,0:T(8,128)(2,1)}, bf16[256,1024]{1,0:T(8,128)(2,1)}, u32[]{:S(2)}, u32[]{:S(2)}) collective-permute-start(bf16[256,1024]{1,0:T(8,128)(2,1)} %get-tuple-element.158.refs_8_), channel_id=1, source_target_pairs={{0,2},{2,0},{4,6},{6,4},{8,10},{10,8},{12,14},{14,12},{16,18},{18,... | collective-permute-start | bytes 1572872 | tf_op jit(solution)/shard_map/ppermute | solution.py:867
  45.5 2.9 %self_grads.1 = (bf16[656,1024]{1,0:T(8,128)(2,1)S(1)}, bf16[528,1024]{1,0:T(8,128)(2,1)S(1)}, bf16[2,128,512]{2,1,0:T(8,128)(2,1)S(1)}) custom-call(s32[6]{0:T(128)S(1)} %pad_add_fusion.refs_0_, f32[512,512]{1,0:T(8,128)S(1)} %get-tuple-element.142.refs_9_.refs_0_.refs_1_, f32[8,512]{1,0:T(8,128)S(1)} %get-tuple-element.144.refs_2_, ...), custom_call_target="tpu_custom_call" | custom-call | flops 99999997952 | bytes 1000 | tf_op jit(solution)/shard_map/self_grads/pallas_call | solution.py:751
  48.6 1.2 add_split.16
  49.8 0.7 collective-permute-start.11
  50.5 1.0 collective-permute-done.8.refs_2_
  51.6 1.6 %collective-permute-start.12 = (bf16[64,1024]{1,0:T(8,128)(2,1)S(1)}, bf16[64,1024]{1,0:T(8,128)(2,1)S(1)}, u32[]{:S(2)}, u32[]{:S(2)}) collective-permute-start(bf16[64,1024]{1,0:T(8,128)(2,1)S(1)} %get-tuple-element.165.refs_3_), channel_id=1, source_target_pairs={{0,4},{2,6},{4,0},{6,2},{8,12},{10,14},{12,8},{14,10},{16,20},{18,... | collective-permute-start | bytes 393224 | tf_op jit(solution)/shard_map/ppermute | solution.py:867
  53.4 0.8 copy-done
  54.2 0.5 collective-permute-start.10
  54.8 1.2 add_split.19
  55.9 0.7 collective-permute-start.15
  56.6 1.4 %collective-permute-done.12.refs_1_ = bf16[64,1024]{1,0:T(8,128)(2,1)S(1)} collective-permute-done((bf16[64,1024]{1,0:T(8,128)(2,1)S(1)}, bf16[64,1024]{1,0:T(8,128)(2,1)S(1)}, u32[]{:S(2)}, u32[]{:S(2)}) %collective-permute-start.12) | collective-permute-done | bytes 131104 | tf_op jit(solution)/shard_map/ppermute | solution.py:867
  58.1 2.7 %collective-permute-start.18 = (bf16[64,1024]{1,0:T(8,128)(2,1)S(1)}, bf16[64,1024]{1,0:T(8,128)(2,1)S(1)}, u32[]{:S(2)}, u32[]{:S(2)}) collective-permute-start(bf16[64,1024]{1,0:T(8,128)(2,1)S(1)} %add_all.4.refs_3_.refs_0_), channel_id=1, source_target_pairs={{0,16},{2,18},{4,20},{6,22},{8,24},{10,26},{12,28},{14,30},{16,0},... | collective-permute-start | bytes 393224 | tf_op jit(solution)/shard_map/ppermute | solution.py:867
  60.8 1.6 %collective-permute-start.16 = (bf16[64,1024]{1,0:T(8,128)(2,1)S(1)}, bf16[64,1024]{1,0:T(8,128)(2,1)S(1)}, u32[]{:S(2)}, u32[]{:S(2)}) collective-permute-start(bf16[64,1024]{1,0:T(8,128)(2,1)S(1)} %get-tuple-element.172.refs_3_), channel_id=1, source_target_pairs={{0,4},{2,6},{4,0},{6,2},{8,12},{10,14},{12,8},{14,10},{16,20},{18,... | collective-permute-start | bytes 393224 | tf_op jit(solution)/shard_map/ppermute | solution.py:867
  62.4 2.8 %collective-permute-done.10.refs_2_ = bf16[272,1024]{1,0:T(8,128)(2,1)S(1)} collective-permute-done((bf16[272,1024]{1,0:T(8,128)(2,1)S(1)}, bf16[272,1024]{1,0:T(8,128)(2,1)S(1)}, u32[]{:S(2)}, u32[]{:S(2)}) %collective-permute-start.10) | collective-permute-done | bytes 557088 | tf_op jit(solution)/shard_map/ppermute | solution.py:867
  65.3 1.6 %collective-permute-start.14 = (bf16[144,1024]{1,0:T(8,128)(2,1)S(1)}, bf16[144,1024]{1,0:T(8,128)(2,1)S(1)}, u32[]{:S(2)}, u32[]{:S(2)}) collective-permute-start(bf16[144,1024]{1,0:T(8,128)(2,1)S(1)} %get-tuple-element.174.refs_2_), channel_id=1, source_target_pairs={{0,4},{2,6},{4,0},{6,2},{8,12},{10,14},{12,8},{14,10},{16,20},{18,... | collective-permute-start | bytes 884744 | tf_op jit(solution)/shard_map/ppermute | solution.py:867
  67.0 2.6 %collective-permute-start.21 = (bf16[64,1024]{1,0:T(8,128)(2,1)S(1)}, bf16[64,1024]{1,0:T(8,128)(2,1)S(1)}, u32[]{:S(2)}, u32[]{:S(2)}) collective-permute-start(bf16[64,1024]{1,0:T(8,128)(2,1)S(1)} %add_all.5.refs_3_.refs_0_), channel_id=1, source_target_pairs={{0,16},{2,18},{4,20},{6,22},{8,24},{10,26},{12,28},{14,30},{16,0},... | collective-permute-start | bytes 393224 | tf_op jit(solution)/shard_map/ppermute | solution.py:867
  69.7 0.6 collective-permute-start.19
  70.3 1.9 %collective-permute-done.14.refs_2_ = bf16[144,1024]{1,0:T(8,128)(2,1)S(1)} collective-permute-done((bf16[144,1024]{1,0:T(8,128)(2,1)S(1)}, bf16[144,1024]{1,0:T(8,128)(2,1)S(1)}, u32[]{:S(2)}, u32[]{:S(2)}) %collective-permute-start.14) | collective-permute-done | bytes 294944 | tf_op jit(solution)/shard_map/ppermute | solution.py:867
  72.2 1.6 %collective-permute-start.17 = (bf16[80,1024]{1,0:T(8,128)(2,1)S(1)}, bf16[80,1024]{1,0:T(8,128)(2,1)S(1)}, u32[]{:S(2)}, u32[]{:S(2)}) collective-permute-start(bf16[80,1024]{1,0:T(8,128)(2,1)S(1)} %get-tuple-element.179.refs_2_), channel_id=1, source_target_pairs={{0,8},{2,10},{4,12},{6,14},{8,0},{10,2},{12,4},{14,6},{16,24},{18,... | collective-permute-start | bytes 491528 | tf_op jit(solution)/shard_map/ppermute | solution.py:867
  73.8 0.9 collective-permute-done.19.refs_1_
  74.8 1.8 %collective-permute-start.23 = (bf16[64,1024]{1,0:T(8,128)(2,1)S(1)}, bf16[64,1024]{1,0:T(8,128)(2,1)S(1)}, u32[]{:S(2)}, u32[]{:S(2)}) collective-permute-start(bf16[64,1024]{1,0:T(8,128)(2,1)S(1)} %add_all.6.refs_2_.refs_0_), channel_id=1, source_target_pairs={{0,16},{2,18},{4,20},{6,22},{8,24},{10,26},{12,28},{14,30},{16,0},... | collective-permute-start | bytes 393224 | tf_op jit(solution)/shard_map/ppermute | solution.py:867
  76.6 1.6 %collective-permute-start.24 = (bf16[64,1024]{1,0:T(8,128)(2,1)S(1)}, bf16[64,1024]{1,0:T(8,128)(2,1)S(1)}, u32[]{:S(2)}, u32[]{:S(2)}) collective-permute-start(bf16[64,1024]{1,0:T(8,128)(2,1)S(1)} %add_last.4.refs_2_.refs_1_), channel_id=1, source_target_pairs={{0,4},{2,6},{4,0},{6,2},{8,12},{10,14},{12,8},{14,10},{16,20},{18,... | collective-permute-start | bytes 393224 | tf_op jit(solution)/shard_map/ppermute | solution.py:867
  78.2 2.2 %collective-permute-done.17.refs_1_ = bf16[80,1024]{1,0:T(8,128)(2,1)S(1)} collective-permute-done((bf16[80,1024]{1,0:T(8,128)(2,1)S(1)}, bf16[80,1024]{1,0:T(8,128)(2,1)S(1)}, u32[]{:S(2)}, u32[]{:S(2)}) %collective-permute-start.17) | collective-permute-done | bytes 163872 | tf_op jit(solution)/shard_map/ppermute | solution.py:867
  80.4 0.8 collective-permute-start.20
  81.2 1.4 %collective-permute-start.22 = (bf16[64,1024]{1,0:T(8,128)(2,1)S(1)}, bf16[64,1024]{1,0:T(8,128)(2,1)S(1)}, u32[]{:S(2)}, u32[]{:S(2)}) collective-permute-start(bf16[64,1024]{1,0:T(8,128)(2,1)S(1)} %add_last.5.refs_3_.refs_1_), channel_id=1, source_target_pairs={{0,4},{2,6},{4,0},{6,2},{8,12},{10,14},{12,8},{14,10},{16,20},{18,... | collective-permute-start | bytes 393224 | tf_op jit(solution)/shard_map/ppermute | solution.py:867
  82.7 2.6 %collective-permute-start.26 = (bf16[128,1024]{1,0:T(8,128)(2,1)S(1)}, bf16[128,1024]{1,0:T(8,128)(2,1)S(1)}, u32[]{:S(2)}, u32[]{:S(2)}) collective-permute-start(bf16[128,1024]{1,0:T(8,128)(2,1)S(1)} %join.8.refs_2_.refs_1_), channel_id=1, source_target_pairs={{0,8},{2,10},{4,12},{6,14},{8,0},{10,2},{12,4},{14,6},{16,24},{18,... | collective-permute-start | bytes 786440 | tf_op jit(solution)/shard_map/ppermute | solution.py:867
  85.3 1.0 collective-permute-start.27
  86.3 1.8 %place.1 = (bf16[2,2,128,512]{3,2,1,0:T(8,128)(2,1)}, bf16[2,2,128,512]{3,2,1,0:T(8,128)(2,1)}, bf16[2,2,128,512]{3,2,1,0:T(8,128)(2,1)}) custom-call(s32[6]{0:T(128)S(1)} %pad_add_fusion.refs_0_, bf16[2,128,512]{2,1,0:T(8,128)(2,1)S(1)} %get-tuple-element.106.refs_1_, bf16[2,128,512]{2,1,0:T(8,128)(2,1)S(1)} %get-tuple-element.143.refs_2_, ...), custom_call_target="tpu_custom_call" | custom-call | flops 20000000000 | bytes 400000000 | tf_op jit(solution)/shard_map/place/pallas_call | solution.py:751
  88.1 1.2 collective-permute-start.31
  89.3 1.9 %collective-permute-start.25 = (bf16[64,1024]{1,0:T(8,128)(2,1)S(1)}, bf16[64,1024]{1,0:T(8,128)(2,1)S(1)}, u32[]{:S(2)}, u32[]{:S(2)}) collective-permute-start(bf16[64,1024]{1,0:T(8,128)(2,1)S(1)} %get-tuple-element.184.refs_3_.refs_1_), channel_id=1, source_target_pairs={{0,8},{2,10},{4,12},{6,14},{8,0},{10,2},{12,4},{14,6},{16,24},{18,... | collective-permute-start | bytes 393224 | tf_op jit(solution)/shard_map/ppermute | solution.py:867
  91.2 1.9 %collective-permute-start.30 = (bf16[128,1024]{1,0:T(8,128)(2,1)S(1)}, bf16[128,1024]{1,0:T(8,128)(2,1)S(1)}, u32[]{:S(2)}, u32[]{:S(2)}) collective-permute-start(bf16[128,1024]{1,0:T(8,128)(2,1)S(1)} %join.10.refs_3_.refs_1_), channel_id=1, source_target_pairs={{0,8},{2,10},{4,12},{6,14},{8,0},{10,2},{12,4},{14,6},{16,24},{18,... | collective-permute-start | bytes 786440 | tf_op jit(solution)/shard_map/ppermute | solution.py:867
  93.2 0.8 collective-permute-start.29
  94.0 1.8 %collective-permute-done.25.refs_2_ = bf16[64,1024]{1,0:T(8,128)(2,1)S(1)} collective-permute-done((bf16[64,1024]{1,0:T(8,128)(2,1)S(1)}, bf16[64,1024]{1,0:T(8,128)(2,1)S(1)}, u32[]{:S(2)}, u32[]{:S(2)}) %collective-permute-start.25) | collective-permute-done | bytes 131104 | tf_op jit(solution)/shard_map/ppermute | solution.py:867
  95.8 1.6 %collective-permute-start.28 = (bf16[128,1024]{1,0:T(8,128)(2,1)S(1)}, bf16[128,1024]{1,0:T(8,128)(2,1)S(1)}, u32[]{:S(2)}, u32[]{:S(2)}) collective-permute-start(bf16[128,1024]{1,0:T(8,128)(2,1)S(1)} %join.12.refs_3_.refs_1_), channel_id=1, source_target_pairs={{0,4},{2,6},{4,0},{6,2},{8,12},{10,14},{12,8},{14,10},{16,20},{18,... | collective-permute-start | bytes 786440 | tf_op jit(solution)/shard_map/ppermute | solution.py:867
  97.5 1.6 %collective-permute-start.33 = (bf16[256,1024]{1,0:T(8,128)(2,1)S(1)}, bf16[256,1024]{1,0:T(8,128)(2,1)S(1)}, u32[]{:S(2)}, u32[]{:S(2)}) collective-permute-start(bf16[256,1024]{1,0:T(8,128)(2,1)S(1)} %join.13.refs_3_.refs_1_), channel_id=1, source_target_pairs={{0,8},{2,10},{4,12},{6,14},{8,0},{10,2},{12,4},{14,6},{16,24},{18,... | collective-permute-start | bytes 1572872 | tf_op jit(solution)/shard_map/ppermute | solution.py:867
  99.0 2.4 %collective-permute-done.30.refs_2_ = bf16[128,1024]{1,0:T(8,128)(2,1)S(1)} collective-permute-done((bf16[128,1024]{1,0:T(8,128)(2,1)S(1)}, bf16[128,1024]{1,0:T(8,128)(2,1)S(1)}, u32[]{:S(2)}, u32[]{:S(2)}) %collective-permute-start.30) | collective-permute-done | bytes 262176 | tf_op jit(solution)/shard_map/ppermute | solution.py:867
  101.5 1.1 collective-permute-start.34
  102.6 0.5 collective-permute-done.29.refs_2_
  103.1 1.5 %unpack.4 = (f32[8,128]{1,0:T(8,128)S(1)}, f32[512,1024]{1,0:T(8,128)}) custom-call(s32[1]{0:T(128)} %bitcast.2.refs_0_, bf16[256,1024]{1,0:T(8,128)(2,1)S(1)} %join.11.refs_3_.refs_1_, bf16[256,1024]{1,0:T(8,128)(2,1)S(1)} %collective-permute-done.29.refs_2_, bf16[256,1024]{1,0:T(8,128)(2,1)S(1)} %join.14.refs_3_.refs_1_), custom_call_target="tpu_custom_call" | custom-call | flops 20000000000 | bytes 400000000 | tf_op jit(solution)/shard_map/unpack/pallas_call | solution.py:751
  104.6 1.4 %collective-permute-start.32 = (bf16[256,1024]{1,0:T(8,128)(2,1)S(1)}, bf16[256,1024]{1,0:T(8,128)(2,1)S(1)}, u32[]{:S(2)}, u32[]{:S(2)}) collective-permute-start(bf16[256,1024]{1,0:T(8,128)(2,1)S(1)} %join.15.refs_3_.refs_1_), channel_id=1, source_target_pairs={{0,2},{2,0},{4,6},{6,4},{8,10},{10,8},{12,14},{14,12},{16,18},{18,... | collective-permute-start | bytes 1572872 | tf_op jit(solution)/shard_map/ppermute | solution.py:867
  106.0 4.7 %collective-permute-done.34.refs_2_ = bf16[256,1024]{1,0:T(8,128)(2,1)S(1)} collective-permute-done((bf16[256,1024]{1,0:T(8,128)(2,1)S(1)}, bf16[256,1024]{1,0:T(8,128)(2,1)S(1)}, u32[]{:S(2)}, u32[]{:S(2)}) %collective-permute-start.34) | collective-permute-done | bytes 524320 | tf_op jit(solution)/shard_map/ppermute | solution.py:867
  110.7 1.6 %unpack.5 = (f32[8,128]{1,0:T(8,128)S(1)}, f32[512,512]{1,0:T(8,128)}, f32[512,256]{1,0:T(8,128)}, f32[512,256]{1,0:T(8,128)}) custom-call(s32[1]{0:T(128)} %bitcast.2.refs_0_, bf16[256,1024]{1,0:T(8,128)(2,1)S(1)} %join.14.refs_3_.refs_1_, bf16[256,1024]{1,0:T(8,128)(2,1)S(1)} %collective-permute-done.34.refs_2_, bf16[256,1024]{1,0:T(8,128)(2,1)S(1)} %join.15.refs_3_.refs_1_), custom_call_target="tpu_custom_call" | custom-call | flops 20000000000 | bytes 400000000 | tf_op jit(solution)/shard_map/unpack/pallas_call | solution.py:751
  112.3 1.6 %unpack.6 = (f32[8,128]{1,0:T(8,128)S(1)}, f32[2048,256]{1,0:T(8,128)}) custom-call(s32[1]{0:T(128)} %bitcast.3.refs_0_, bf16[256,1024]{1,0:T(8,128)(2,1)S(1)} %join.13.refs_3_.refs_1_, bf16[256,1024]{1,0:T(8,128)(2,1)S(1)} %collective-permute-done.33.refs_2_, f32[8,128]{1,0:T(8,128)S(1)} %get-tuple-element.187.refs_3_), custom_call_target="tpu_custom_call" | custom-call | flops 20000000000 | bytes 400000000 | tf_op jit(solution)/shard_map/unpack/pallas_call | solution.py:751
  114.0 2.4 %collective-permute-done.32.refs_2_ = bf16[256,1024]{1,0:T(8,128)(2,1)S(1)} collective-permute-done((bf16[256,1024]{1,0:T(8,128)(2,1)S(1)}, bf16[256,1024]{1,0:T(8,128)(2,1)S(1)}, u32[]{:S(2)}, u32[]{:S(2)}) %collective-permute-start.32) | collective-permute-done | bytes 524320 | tf_op jit(solution)/shard_map/ppermute | solution.py:867
  116.3 1.6 %unpack.7 = (f32[8,128]{1,0:T(8,128)}, f32[512,768]{1,0:T(8,128)}, f32[512,256]{1,0:T(8,128)}, f32[3,256]{1,0:T(4,128)}, f32[3,256]{1,0:T(4,128)}, /*index=5*/f32[8,256]{1,0:T(8,128)}) custom-call(s32[1]{0:T(128)} %bitcast.2.refs_0_, bf16[256,1024]{1,0:T(8,128)(2,1)S(1)} %join.15.refs_3_.refs_1_, bf16[256,1024]{1,0:T(8,128)(2,1)S(1)} %collective-permute-done.32.refs_2_, ...), custom_call_target="tpu_custom_call" | custom-call | flops 20000000000 | bytes 400000000 | tf_op jit(solution)/shard_map/unpack/pallas_call | solution.py:751
  (54 shorter events, 1.9 us)
Async XLA Ops:
  0.6 3.8 %collective-permute-start = (bf16[2,2,128,512]{3,2,1,0:T(8,128)(2,1)}, bf16[2,2,128,512]{3,2,1,0:T(8,128)(2,1)S(1)}, u32[]{:S(2)}, u32[]{:S(2)}) collective-permute-start(bf16[2,2,128,512]{3,2,1,0:T(8,128)(2,1)} %refs_4_.1), channel_id=1, source_target_pairs={{0,1},{1,0},{2,3},{3,2},{4,5},{5,4},{6,7},{7,6},{8,9},{9,8},{10,11... | collective-permute-start | bytes 1572872 | tf_op jit(solution)/shard_map/ppermute | solution.py:795
  1.2 3.3 %collective-permute-start.1 = (bf16[2,2,128,512]{3,2,1,0:T(8,128)(2,1)}, bf16[2,2,128,512]{3,2,1,0:T(8,128)(2,1)S(1)}, u32[]{:S(2)}, u32[]{:S(2)}) collective-permute-start(bf16[2,2,128,512]{3,2,1,0:T(8,128)(2,1)} %refs_5_.1), channel_id=1, source_target_pairs={{0,1},{1,0},{2,3},{3,2},{4,5},{5,4},{6,7},{7,6},{8,9},{9,8},{10,11... | collective-permute-start | bytes 1572872 | tf_op jit(solution)/shard_map/ppermute | solution.py:796
  1.2 3.2 %collective-permute-start.2 = (bf16[2,2,128,512]{3,2,1,0:T(8,128)(2,1)}, bf16[2,2,128,512]{3,2,1,0:T(8,128)(2,1)S(1)}, u32[]{:S(2)}, u32[]{:S(2)}) collective-permute-start(bf16[2,2,128,512]{3,2,1,0:T(8,128)(2,1)} %refs_6_.1), channel_id=1, source_target_pairs={{0,1},{1,0},{2,3},{3,2},{4,5},{5,4},{6,7},{7,6},{8,9},{9,8},{10,11... | collective-permute-start | bytes 1572872 | tf_op jit(solution)/shard_map/ppermute | solution.py:797
  20.3 3.3 %collective-permute-start.3 = (bf16[512,1024]{1,0:T(8,128)(2,1)S(1)}, bf16[512,1024]{1,0:T(8,128)(2,1)S(1)}, u32[]{:S(2)}, u32[]{:S(2)}) collective-permute-start(bf16[512,1024]{1,0:T(8,128)(2,1)S(1)} %get-tuple-element.131), channel_id=1, source_target_pairs={{0,1},{1,0},{2,3},{3,2},{4,5},{5,4},{6,7},{7,6},{8,9},{9,8},{10,11... | collective-permute-start | bytes 3145736 | tf_op jit(solution)/shard_map/ppermute | solution.py:1026
  23.2 5.4 %collective-permute-start.4 = (bf16[512,1024]{1,0:T(8,128)(2,1)S(1)}, bf16[512,1024]{1,0:T(8,128)(2,1)S(1)}, u32[]{:S(2)}, u32[]{:S(2)}) collective-permute-start(bf16[512,1024]{1,0:T(8,128)(2,1)S(1)} %get-tuple-element.132.refs_3_), channel_id=1, source_target_pairs={{0,1},{1,0},{2,3},{3,2},{4,5},{5,4},{6,7},{7,6},{8,9},{9,8},{10,11... | collective-permute-start | bytes 3145736 | tf_op jit(solution)/shard_map/ppermute | solution.py:934
  24.6 24.0 %collective-permute-start.9 = (bf16[256,1024]{1,0:T(8,128)(2,1)}, bf16[256,1024]{1,0:T(8,128)(2,1)}, u32[]{:S(2)}, u32[]{:S(2)}) collective-permute-start(bf16[256,1024]{1,0:T(8,128)(2,1)} %get-tuple-element.133.refs_4_), channel_id=1, source_target_pairs={{0,8},{2,10},{4,12},{6,14},{8,0},{10,2},{12,4},{14,6},{16,24},{18,... | collective-permute-start | bytes 1572872 | tf_op jit(solution)/shard_map/ppermute | solution.py:867
  29.6 12.0 %collective-permute-start.6 = (bf16[256,1024]{1,0:T(8,128)(2,1)}, bf16[256,1024]{1,0:T(8,128)(2,1)}, u32[]{:S(2)}, u32[]{:S(2)}) collective-permute-start(bf16[256,1024]{1,0:T(8,128)(2,1)} %get-tuple-element.134.refs_17_), channel_id=1, source_target_pairs={{0,2},{2,0},{4,6},{6,4},{8,10},{10,8},{12,14},{14,12},{16,18},{18,... | collective-permute-start | bytes 1572872 | tf_op jit(solution)/shard_map/ppermute | solution.py:867
  38.7 4.6 %collective-permute-start.5 = (bf16[768,1024]{1,0:T(8,128)(2,1)S(1)}, bf16[768,1024]{1,0:T(8,128)(2,1)S(1)}, u32[]{:S(2)}, u32[]{:S(2)}) collective-permute-start(bf16[768,1024]{1,0:T(8,128)(2,1)S(1)} %get-tuple-element.150.refs_6_), channel_id=1, source_target_pairs={{0,1},{1,0},{2,3},{3,2},{4,5},{5,4},{6,7},{7,6},{8,9},{9,8},{10,11... | collective-permute-start | bytes 4718600 | tf_op jit(solution)/shard_map/ppermute | solution.py:979
  42.7 8.8 %collective-permute-start.8 = (bf16[128,1024]{1,0:T(8,128)(2,1)S(1)}, bf16[128,1024]{1,0:T(8,128)(2,1)S(1)}, u32[]{:S(2)}, u32[]{:S(2)}) collective-permute-start(bf16[128,1024]{1,0:T(8,128)(2,1)S(1)} %get-tuple-element.157.refs_3_), channel_id=1, source_target_pairs={{0,8},{2,10},{4,12},{6,14},{8,0},{10,2},{12,4},{14,6},{16,24},{18,... | collective-permute-start | bytes 786440 | tf_op jit(solution)/shard_map/ppermute | solution.py:867
  44.2 10.5 %collective-permute-start.13 = (bf16[256,1024]{1,0:T(8,128)(2,1)}, bf16[256,1024]{1,0:T(8,128)(2,1)}, u32[]{:S(2)}, u32[]{:S(2)}) collective-permute-start(bf16[256,1024]{1,0:T(8,128)(2,1)} %get-tuple-element.158.refs_8_), channel_id=1, source_target_pairs={{0,2},{2,0},{4,6},{6,4},{8,10},{10,8},{12,14},{14,12},{16,18},{18,... | collective-permute-start | bytes 1572872 | tf_op jit(solution)/shard_map/ppermute | solution.py:867
  48.4 4.8 %collective-permute-start.7 = (bf16[656,1024]{1,0:T(8,128)(2,1)S(1)}, bf16[656,1024]{1,0:T(8,128)(2,1)S(1)}, u32[]{:S(2)}, u32[]{:S(2)}) collective-permute-start(bf16[656,1024]{1,0:T(8,128)(2,1)S(1)} %get-tuple-element.160.refs_3_), channel_id=1, source_target_pairs={{0,1},{1,0},{2,3},{3,2},{4,5},{5,4},{6,7},{7,6},{8,9},{9,8},{10,11... | collective-permute-start | bytes 4030472 | tf_op jit(solution)/shard_map/ppermute | solution.py:1010
  49.8 11.0 %collective-permute-start.11 = (bf16[128,1024]{1,0:T(8,128)(2,1)S(1)}, bf16[128,1024]{1,0:T(8,128)(2,1)S(1)}, u32[]{:S(2)}, u32[]{:S(2)}) collective-permute-start(bf16[128,1024]{1,0:T(8,128)(2,1)S(1)} %get-tuple-element.164.refs_3_), channel_id=1, source_target_pairs={{0,2},{2,0},{4,6},{6,4},{8,10},{10,8},{12,14},{14,12},{16,18},{18,... | collective-permute-start | bytes 786440 | tf_op jit(solution)/shard_map/ppermute | solution.py:867
  51.6 6.5 %collective-permute-start.12 = (bf16[64,1024]{1,0:T(8,128)(2,1)S(1)}, bf16[64,1024]{1,0:T(8,128)(2,1)S(1)}, u32[]{:S(2)}, u32[]{:S(2)}) collective-permute-start(bf16[64,1024]{1,0:T(8,128)(2,1)S(1)} %get-tuple-element.165.refs_3_), channel_id=1, source_target_pairs={{0,4},{2,6},{4,0},{6,2},{8,12},{10,14},{12,8},{14,10},{16,20},{18,... | collective-permute-start | bytes 393224 | tf_op jit(solution)/shard_map/ppermute | solution.py:867
  53.2 1.1 copy-start
  54.2 10.9 %collective-permute-start.10 = (bf16[272,1024]{1,0:T(8,128)(2,1)S(1)}, bf16[272,1024]{1,0:T(8,128)(2,1)S(1)}, u32[]{:S(2)}, u32[]{:S(2)}) collective-permute-start(bf16[272,1024]{1,0:T(8,128)(2,1)S(1)} %get-tuple-element.167.refs_3_), channel_id=1, source_target_pairs={{0,2},{2,0},{4,6},{6,4},{8,10},{10,8},{12,14},{14,12},{16,18},{18,... | collective-permute-start | bytes 1671176 | tf_op jit(solution)/shard_map/ppermute | solution.py:867
  55.9 13.7 %collective-permute-start.15 = (bf16[128,1024]{1,0:T(8,128)(2,1)S(1)}, bf16[128,1024]{1,0:T(8,128)(2,1)S(1)}, u32[]{:S(2)}, u32[]{:S(2)}) collective-permute-start(bf16[128,1024]{1,0:T(8,128)(2,1)S(1)} %get-tuple-element.171.refs_2_), channel_id=1, source_target_pairs={{0,8},{2,10},{4,12},{6,14},{8,0},{10,2},{12,4},{14,6},{16,24},{18,... | collective-permute-start | bytes 786440 | tf_op jit(solution)/shard_map/ppermute | solution.py:867
  58.1 18.4 %collective-permute-start.18 = (bf16[64,1024]{1,0:T(8,128)(2,1)S(1)}, bf16[64,1024]{1,0:T(8,128)(2,1)S(1)}, u32[]{:S(2)}, u32[]{:S(2)}) collective-permute-start(bf16[64,1024]{1,0:T(8,128)(2,1)S(1)} %add_all.4.refs_3_.refs_0_), channel_id=1, source_target_pairs={{0,16},{2,18},{4,20},{6,22},{8,24},{10,26},{12,28},{14,30},{16,0},... | collective-permute-start | bytes 393224 | tf_op jit(solution)/shard_map/ppermute | solution.py:867
  60.8 6.1 %collective-permute-start.16 = (bf16[64,1024]{1,0:T(8,128)(2,1)S(1)}, bf16[64,1024]{1,0:T(8,128)(2,1)S(1)}, u32[]{:S(2)}, u32[]{:S(2)}) collective-permute-start(bf16[64,1024]{1,0:T(8,128)(2,1)S(1)} %get-tuple-element.172.refs_3_), channel_id=1, source_target_pairs={{0,4},{2,6},{4,0},{6,2},{8,12},{10,14},{12,8},{14,10},{16,20},{18,... | collective-permute-start | bytes 393224 | tf_op jit(solution)/shard_map/ppermute | solution.py:867
  65.3 6.8 %collective-permute-start.14 = (bf16[144,1024]{1,0:T(8,128)(2,1)S(1)}, bf16[144,1024]{1,0:T(8,128)(2,1)S(1)}, u32[]{:S(2)}, u32[]{:S(2)}) collective-permute-start(bf16[144,1024]{1,0:T(8,128)(2,1)S(1)} %get-tuple-element.174.refs_2_), channel_id=1, source_target_pairs={{0,4},{2,6},{4,0},{6,2},{8,12},{10,14},{12,8},{14,10},{16,20},{18,... | collective-permute-start | bytes 884744 | tf_op jit(solution)/shard_map/ppermute | solution.py:867
  67.0 14.2 %collective-permute-start.21 = (bf16[64,1024]{1,0:T(8,128)(2,1)S(1)}, bf16[64,1024]{1,0:T(8,128)(2,1)S(1)}, u32[]{:S(2)}, u32[]{:S(2)}) collective-permute-start(bf16[64,1024]{1,0:T(8,128)(2,1)S(1)} %add_all.5.refs_3_.refs_0_), channel_id=1, source_target_pairs={{0,16},{2,18},{4,20},{6,22},{8,24},{10,26},{12,28},{14,30},{16,0},... | collective-permute-start | bytes 393224 | tf_op jit(solution)/shard_map/ppermute | solution.py:867
  69.7 5.0 %collective-permute-start.19 = (bf16[64,1024]{1,0:T(8,128)(2,1)S(1)}, bf16[64,1024]{1,0:T(8,128)(2,1)S(1)}, u32[]{:S(2)}, u32[]{:S(2)}) collective-permute-start(bf16[64,1024]{1,0:T(8,128)(2,1)S(1)} %get-tuple-element.177.refs_3_), channel_id=1, source_target_pairs={{0,4},{2,6},{4,0},{6,2},{8,12},{10,14},{12,8},{14,10},{16,20},{18,... | collective-permute-start | bytes 393224 | tf_op jit(solution)/shard_map/ppermute | solution.py:867
  72.2 8.1 %collective-permute-start.17 = (bf16[80,1024]{1,0:T(8,128)(2,1)S(1)}, bf16[80,1024]{1,0:T(8,128)(2,1)S(1)}, u32[]{:S(2)}, u32[]{:S(2)}) collective-permute-start(bf16[80,1024]{1,0:T(8,128)(2,1)S(1)} %get-tuple-element.179.refs_2_), channel_id=1, source_target_pairs={{0,8},{2,10},{4,12},{6,14},{8,0},{10,2},{12,4},{14,6},{16,24},{18,... | collective-permute-start | bytes 491528 | tf_op jit(solution)/shard_map/ppermute | solution.py:867
  74.8 10.5 %collective-permute-start.23 = (bf16[64,1024]{1,0:T(8,128)(2,1)S(1)}, bf16[64,1024]{1,0:T(8,128)(2,1)S(1)}, u32[]{:S(2)}, u32[]{:S(2)}) collective-permute-start(bf16[64,1024]{1,0:T(8,128)(2,1)S(1)} %add_all.6.refs_2_.refs_0_), channel_id=1, source_target_pairs={{0,16},{2,18},{4,20},{6,22},{8,24},{10,26},{12,28},{14,30},{16,0},... | collective-permute-start | bytes 393224 | tf_op jit(solution)/shard_map/ppermute | solution.py:867
  76.6 6.1 %collective-permute-start.24 = (bf16[64,1024]{1,0:T(8,128)(2,1)S(1)}, bf16[64,1024]{1,0:T(8,128)(2,1)S(1)}, u32[]{:S(2)}, u32[]{:S(2)}) collective-permute-start(bf16[64,1024]{1,0:T(8,128)(2,1)S(1)} %add_last.4.refs_2_.refs_1_), channel_id=1, source_target_pairs={{0,4},{2,6},{4,0},{6,2},{8,12},{10,14},{12,8},{14,10},{16,20},{18,... | collective-permute-start | bytes 393224 | tf_op jit(solution)/shard_map/ppermute | solution.py:867
  80.4 8.9 %collective-permute-start.20 = (bf16[80,1024]{1,0:T(8,128)(2,1)S(1)}, bf16[80,1024]{1,0:T(8,128)(2,1)S(1)}, u32[]{:S(2)}, u32[]{:S(2)}) collective-permute-start(bf16[80,1024]{1,0:T(8,128)(2,1)S(1)} %add_all.7.refs_6_.refs_2_.refs_0_), channel_id=1, source_target_pairs={{0,16},{2,18},{4,20},{6,22},{8,24},{10,26},{12,28},{14,30},{16,0},... | collective-permute-start | bytes 491528 | tf_op jit(solution)/shard_map/ppermute | solution.py:867
  81.2 6.9 %collective-permute-start.22 = (bf16[64,1024]{1,0:T(8,128)(2,1)S(1)}, bf16[64,1024]{1,0:T(8,128)(2,1)S(1)}, u32[]{:S(2)}, u32[]{:S(2)}) collective-permute-start(bf16[64,1024]{1,0:T(8,128)(2,1)S(1)} %add_last.5.refs_3_.refs_1_), channel_id=1, source_target_pairs={{0,4},{2,6},{4,0},{6,2},{8,12},{10,14},{12,8},{14,10},{16,20},{18,... | collective-permute-start | bytes 393224 | tf_op jit(solution)/shard_map/ppermute | solution.py:867
  82.7 3.6 %copy-start.1 = (bf16[656,1024]{1,0:T(8,128)(2,1)S(1)}, bf16[656,1024]{1,0:T(8,128)(2,1)}, u32[]{:S(2)}) copy-start(bf16[656,1024]{1,0:T(8,128)(2,1)} %copy-done) | copy-start | bytes 4030468
  82.7 10.4 %collective-permute-start.26 = (bf16[128,1024]{1,0:T(8,128)(2,1)S(1)}, bf16[128,1024]{1,0:T(8,128)(2,1)S(1)}, u32[]{:S(2)}, u32[]{:S(2)}) collective-permute-start(bf16[128,1024]{1,0:T(8,128)(2,1)S(1)} %join.8.refs_2_.refs_1_), channel_id=1, source_target_pairs={{0,8},{2,10},{4,12},{6,14},{8,0},{10,2},{12,4},{14,6},{16,24},{18,... | collective-permute-start | bytes 786440 | tf_op jit(solution)/shard_map/ppermute | solution.py:867
  85.3 5.9 %collective-permute-start.27 = (bf16[64,1024]{1,0:T(8,128)(2,1)S(1)}, bf16[64,1024]{1,0:T(8,128)(2,1)S(1)}, u32[]{:S(2)}, u32[]{:S(2)}) collective-permute-start(bf16[64,1024]{1,0:T(8,128)(2,1)S(1)} %add_last.6.refs_3_.refs_1_), channel_id=1, source_target_pairs={{0,4},{2,6},{4,0},{6,2},{8,12},{10,14},{12,8},{14,10},{16,20},{18,... | collective-permute-start | bytes 393224 | tf_op jit(solution)/shard_map/ppermute | solution.py:867
  88.1 9.3 %collective-permute-start.31 = (bf16[128,1024]{1,0:T(8,128)(2,1)S(1)}, bf16[128,1024]{1,0:T(8,128)(2,1)S(1)}, u32[]{:S(2)}, u32[]{:S(2)}) collective-permute-start(bf16[128,1024]{1,0:T(8,128)(2,1)S(1)} %join.9.refs_2_.refs_1_), channel_id=1, source_target_pairs={{0,2},{2,0},{4,6},{6,4},{8,10},{10,8},{12,14},{14,12},{16,18},{18,... | collective-permute-start | bytes 786440 | tf_op jit(solution)/shard_map/ppermute | solution.py:867
  89.3 6.5 %collective-permute-start.25 = (bf16[64,1024]{1,0:T(8,128)(2,1)S(1)}, bf16[64,1024]{1,0:T(8,128)(2,1)S(1)}, u32[]{:S(2)}, u32[]{:S(2)}) collective-permute-start(bf16[64,1024]{1,0:T(8,128)(2,1)S(1)} %get-tuple-element.184.refs_3_.refs_1_), channel_id=1, source_target_pairs={{0,8},{2,10},{4,12},{6,14},{8,0},{10,2},{12,4},{14,6},{16,24},{18,... | collective-permute-start | bytes 393224 | tf_op jit(solution)/shard_map/ppermute | solution.py:867
  91.2 10.2 %collective-permute-start.30 = (bf16[128,1024]{1,0:T(8,128)(2,1)S(1)}, bf16[128,1024]{1,0:T(8,128)(2,1)S(1)}, u32[]{:S(2)}, u32[]{:S(2)}) collective-permute-start(bf16[128,1024]{1,0:T(8,128)(2,1)S(1)} %join.10.refs_3_.refs_1_), channel_id=1, source_target_pairs={{0,8},{2,10},{4,12},{6,14},{8,0},{10,2},{12,4},{14,6},{16,24},{18,... | collective-permute-start | bytes 786440 | tf_op jit(solution)/shard_map/ppermute | solution.py:867
  93.2 9.9 %collective-permute-start.29 = (bf16[256,1024]{1,0:T(8,128)(2,1)S(1)}, bf16[256,1024]{1,0:T(8,128)(2,1)S(1)}, u32[]{:S(2)}, u32[]{:S(2)}) collective-permute-start(bf16[256,1024]{1,0:T(8,128)(2,1)S(1)} %join.11.refs_3_.refs_1_), channel_id=1, source_target_pairs={{0,2},{2,0},{4,6},{6,4},{8,10},{10,8},{12,14},{14,12},{16,18},{18,... | collective-permute-start | bytes 1572872 | tf_op jit(solution)/shard_map/ppermute | solution.py:867
  95.8 8.7 %collective-permute-start.28 = (bf16[128,1024]{1,0:T(8,128)(2,1)S(1)}, bf16[128,1024]{1,0:T(8,128)(2,1)S(1)}, u32[]{:S(2)}, u32[]{:S(2)}) collective-permute-start(bf16[128,1024]{1,0:T(8,128)(2,1)S(1)} %join.12.refs_3_.refs_1_), channel_id=1, source_target_pairs={{0,4},{2,6},{4,0},{6,2},{8,12},{10,14},{12,8},{14,10},{16,20},{18,... | collective-permute-start | bytes 786440 | tf_op jit(solution)/shard_map/ppermute | solution.py:867
  97.5 14.9 %collective-permute-start.33 = (bf16[256,1024]{1,0:T(8,128)(2,1)S(1)}, bf16[256,1024]{1,0:T(8,128)(2,1)S(1)}, u32[]{:S(2)}, u32[]{:S(2)}) collective-permute-start(bf16[256,1024]{1,0:T(8,128)(2,1)S(1)} %join.13.refs_3_.refs_1_), channel_id=1, source_target_pairs={{0,8},{2,10},{4,12},{6,14},{8,0},{10,2},{12,4},{14,6},{16,24},{18,... | collective-permute-start | bytes 1572872 | tf_op jit(solution)/shard_map/ppermute | solution.py:867
  101.5 9.2 %collective-permute-start.34 = (bf16[256,1024]{1,0:T(8,128)(2,1)S(1)}, bf16[256,1024]{1,0:T(8,128)(2,1)S(1)}, u32[]{:S(2)}, u32[]{:S(2)}) collective-permute-start(bf16[256,1024]{1,0:T(8,128)(2,1)S(1)} %join.14.refs_3_.refs_1_), channel_id=1, source_target_pairs={{0,2},{2,0},{4,6},{6,4},{8,10},{10,8},{12,14},{14,12},{16,18},{18,... | collective-permute-start | bytes 1572872 | tf_op jit(solution)/shard_map/ppermute | solution.py:867
  104.6 11.7 %collective-permute-start.32 = (bf16[256,1024]{1,0:T(8,128)(2,1)S(1)}, bf16[256,1024]{1,0:T(8,128)(2,1)S(1)}, u32[]{:S(2)}, u32[]{:S(2)}) collective-permute-start(bf16[256,1024]{1,0:T(8,128)(2,1)S(1)} %join.15.refs_3_.refs_1_), channel_id=1, source_target_pairs={{0,2},{2,0},{4,6},{6,4},{8,10},{10,8},{12,14},{14,12},{16,18},{18,... | collective-permute-start | bytes 1572872 | tf_op jit(solution)/shard_map/ppermute | solution.py:867

commit v6 on v5

--- a/solution.py
+++ b/solution.py
@@ -225,8 +225,8 @@
     return staged(ginner.shape[1] // step, shrink, bend)
 
 
-def feed_kernel(numbers_ref, gff, w_fo, slope, slow_t, gff_t, hidden, ginner_first, send_in, keep_out, ginner_last):
-    place = numbers_ref[0]
+def feed_kernel(gff, w_fo, slope, slow_t, gff_t, hidden, ginner_first, send_in, keep_out, ginner_last):
+    place = lax.axis_index("seq")
     length = ginner_last.shape[0]
     weave(
         feed_back_steps(gff.at[length:], w_fo, slope.at[length:], ginner_last),
@@ -235,8 +235,8 @@
     weave(give_in_steps(1 - place, send_in, slow_t, (ginner_first, ginner_last)))
 
 
-def feed_keep_kernel(numbers_ref, slow_t, ginner_first, ginner_last, keep_in):
-    weave(give_in_steps(numbers_ref[0], keep_in, slow_t, (ginner_first, ginner_last)))
+def feed_keep_kernel(slow_t, ginner_first, ginner_last, keep_in):
+    weave(give_in_steps(lax.axis_index("seq"), keep_in, slow_t, (ginner_first, ginner_last)))
 
 
 class Weights(NamedTuple):
@@ -302,20 +302,20 @@
     at = Weights(*range(len(Weights._fields)))
     dec, enc, og = (-1, -2, -3)
     copies = Copies(sems)
-    place = numbers_ref[0]
+    place = lax.axis_index("seq")
     tokens, width = dec_s.shape
     length = tokens // 2
     inner = hidden.shape[1]
     where = halves(place, length)
+    copies.start(at.table, weights_in.table, w.table)
     for s in range(2):
         copies.start(dec, dec_in.at[place, s], dec_s.at[where[s][0]])
-        copies.start(dec, dec2_in.at[place, s], dec_s.at[where[s][1]])
-    for key in at[:4]:
-        copies.start(key, weights_in[key], w[key])
+    parts = [slice(part * width, (part + 1) * width) for part in range(3)]
+    for part in parts:
+        copies.start((at.qkv, part.start), weights_in.qkv.at[:, part], w.qkv.at[:, part])
     for s in range(2):
         copies.start(enc, enc_in.at[place, s], encs.at[where[s][0]])
-        copies.start(enc, enc2_in.at[place, s], encs.at[where[s][1]])
-    for key in at[4:]:
+    for key in (at.ckv, at.so, at.gain, at.nbias, *at[6:]):
         copies.start(key, weights_in[key], w[key])
     for s in range(2):
         copies.start(og, og_in.at[place, s], og_s.at[where[s][0]])
@@ -325,27 +325,31 @@
     keys_at = lax.broadcasted_iota(jnp.int32, (length, length), 0)
     query_at = lax.broadcasted_iota(jnp.int32, (length, length), 1)
     for s in range(2):
-        bias_ref[s] = jnp.where((keys_at <= query_at) & (keys_at < numbers_ref[2 + s]), 0.0, NEG_FILL)
-        bias_ref[2 + s] = jnp.where(keys_at < numbers_ref[4 + s], 0.0, NEG_FILL)
+        bias_ref[s] = jnp.where((keys_at <= query_at) & (keys_at < numbers_ref[place, s]), 0.0, NEG_FILL)
+        bias_ref[2 + s] = jnp.where(keys_at < numbers_ref[place, 2 + s], 0.0, NEG_FILL)
 
     def embed(s):
         def run():
+            dec_s[where[s][1], :] = dec2_in[place, s]
             elow[rows[s]] = (dec_s[rows[s]].astype(F32) + row).astype(BF)
+            encs[where[s][1], :] = enc2_in[place, s]
 
         return run
 
     def pack(s, part):
         def run():
-            cols = slice(part * width, (part + 1) * width)
-            values = mm(elow[rows[s]], w.qkv[:, cols])
-            qkv[rows[s], cols] = (values * 0.125 if part == 0 else values).astype(BF)
+            if s == 0:
+                copies.wait((at.qkv, parts[part].start))
+            values = mm(elow[rows[s]], w.qkv[:, parts[part]])
+            qkv[rows[s], parts[part]] = (values * 0.125 if part == 0 else values).astype(BF)
 
         return run
 
     def pack_cross(s, part):
         def run():
-            cols = slice(part * width, (part + 1) * width)
-            ckv[rows[s], cols] = mm(encs[rows[s]], w.ckv[:, cols]).astype(BF)
+            if s == 0 and part == 0:
+                copies.wait(enc, at.ckv)
+            ckv[rows[s], parts[part]] = mm(encs[rows[s]], w.ckv[:, parts[part]]).astype(BF)
 
         return run
 
@@ -423,19 +427,18 @@
 
         return [shrink(0), shrink(1), norm, turn]
 
-    copies.wait(at.table, at.gain, at.nbias, dec, at.qkv)
-    gain = w.gain[...].astype(F32)
-    nbias = w.nbias[...].astype(F32)
-    picked = lax.broadcasted_iota(jnp.int32, w.table.shape, 0) == numbers_ref[1]
+    copies.wait(at.table, dec)
+    picked = lax.broadcasted_iota(jnp.int32, w.table.shape, 0) == numbers_ref[place, 4]
     row = jnp.sum(jnp.where(picked, w.table[...].astype(F32), 0.0), 0, keepdims=True)
     weave([embed(0)])
     weave([pack(0, part) for part in range(3)], [embed(1)])
-    copies.wait(enc, at.ckv)
     weave(
         attend_steps(0, length, qkv, qkv, qkv, width, 2 * width, bias_ref, p_self, rl_self, att, att_t),
         [pack(1, part) for part in range(3)] + [pack_cross(0, 0), pack_cross(0, 1)],
     )
-    copies.wait(at.so, at.cq, at.co)
+    copies.wait(at.so, at.cq, at.co, at.gain, at.nbias)
+    gain = w.gain[...].astype(F32)
+    nbias = w.nbias[...].astype(F32)
     weave(
         attend_steps(1, length, qkv, qkv, qkv, width, 2 * width, bias_ref, p_self, rl_self, att, att_t),
         after_self(0) + [pack_cross(1, 0), pack_cross(1, 1)],
@@ -532,9 +535,9 @@
 
 
 def cross_grads_kernel(
-    numbers_ref, branch, gq_t, gkv_t, crossed_t, flow, encs, w_ckv, out_oth, send_ref, keep_ref, genc_own, genc
+    branch, gq_t, gkv_t, crossed_t, flow, encs, w_ckv, out_oth, send_ref, keep_ref, genc_own, genc
 ):
-    place = numbers_ref[0]
+    place = lax.axis_index("seq")
     tokens, width = branch.shape
     length = tokens // 2
     half = width // 2
@@ -596,7 +599,7 @@
     send_ref, keep_ref, gin_own,
     gin, small,
 ):
-    place = numbers_ref[0]
+    place = lax.axis_index("seq")
     tokens, width = gfs.shape
     length = tokens // 2
     half = width // 2
@@ -634,7 +637,7 @@
 
     weave(give(1 - place, send_ref) + give(place, keep_ref), back(0) + back(1))
     small[0:8, :] = dnorm_in[...]
-    picked = lax.broadcasted_iota(jnp.int32, (8, width), 0) == numbers_ref[1]
+    picked = lax.broadcasted_iota(jnp.int32, (8, width), 0) == numbers_ref[place, 4]
     small[8:16, :] = jnp.where(picked, jnp.broadcast_to(sums[0] + sums[1], (8, width)), 0.0)
     for which, ref in ((1 - place, send_ref), (place, keep_ref)):
         ref[width : width + 16, :] = jnp.zeros((16, ref.shape[1]), BF)
@@ -720,8 +723,8 @@
     table_ref[...] = small[8:16]
 
 
-def place_kernel(numbers_ref, out_own, genc_own, gin_own, got_cross, got_self, *outs):
-    place = numbers_ref[0]
+def place_kernel(out_own, genc_own, gin_own, got_cross, got_self, *outs):
+    place = lax.axis_index("seq")
     half, width = out_own.shape[1:]
     first = width + 16
     others = (got_cross, width + half), (got_cross, width), (got_self, first)
@@ -781,15 +784,8 @@
     length = local_len * seq_count
     tokens = sent_count * length
     half = width // 2
-    mine = jnp.arange(micro_count) == place
-    numbers = jnp.concatenate(
-        [
-            place.reshape(1),
-            jnp.sum(jnp.where(mine, pair_id, 0)).reshape(1),
-            jnp.sum(jnp.where(mine[:, None], tgt_len, 0), 0),
-            jnp.sum(jnp.where(mine[:, None], src_len, 0), 0),
-        ]
-    ).astype(jnp.int32)
+    pairs = lax.broadcast_in_dim(pair_id, (micro_count, 1), (0,))
+    numbers = jnp.concatenate([tgt_len, src_len, pairs], 1).astype(jnp.int32)
     swap = [(0, 1), (1, 0)]
 
     dec2 = lax.ppermute(dec_in, "seq", swap)
@@ -924,7 +920,7 @@
     def feed_back():
         send, held.keep_out, held.ginner_last = call(
             feed_kernel,
-            (numbers,),
+            (),
             [held.gff, held.w_fo, held.slope, held.slow_t, held.gff_t, held.hidden, held.ginner],
             [(buffer, BF), (buffer, BF), ((length, inner), BF)],
             name="feed_back",
@@ -937,7 +933,7 @@
     def feed_keep():
         (keep,) = call(
             feed_keep_kernel,
-            (numbers,),
+            (),
             [held.slow_t, held.ginner, held.ginner_last],
             [(buffer, BF)],
             name="feed_keep",
@@ -968,7 +964,7 @@
         longer = (width + 2 * local_len, LANES)
         send, keep, held.genc_own = call(
             cross_grads_kernel,
-            (numbers,),
+            (),
             [held.cross_branch, held.gq_t, held.gkv_t, held.crossed_t, held.flow, held.encs, held.w_ckv, held.out_oth],
             [(longer, BF), (buffer, BF), (rows, BF)],
             [(whole, BF)],
@@ -1014,7 +1010,7 @@
     def place_all():
         held.placed = call(
             place_kernel,
-            (numbers,),
+            (),
             [held.out_own, held.genc_own, held.gin_own, held.got_cross, held.got_self],
             [],
             name="place",

time: 118 us -> 117 us (level)
  waiting for transfers between devices: 22 us -> 29.1 us
  starting transfers between devices: 42.8 us -> 38.7 us
  Pallas kernels: 48.6 us -> 46.2 us
  other arithmetic: 2.8 us -> 0.77 us
    ppermute x28, waiting for transfers between devices: 22 us -> 27.8 us  [travel(): return lax.ppermute(array, ('dp', 'seq'), flips(core_zero, core_one))]
    ppermute x28, starting transfers between devices: 40.8 us -> 36.9 us  [travel(): return lax.ppermute(array, ('dp', 'seq'), flips(core_zero, core_one))]
    pallas_call x40, Pallas kernels: 48.6 us -> 46.2 us  [call(): pl.pallas_call(body, out_shape=tuple((pltpu.VMEM(s, d) for s, d in outs))...]
    reduce_sum x2 -> x0, other arithmetic: 2.07 us -> none  [the longest x1 1.29 us: local(): jnp.sum(jnp.where(mine, pair_id, 0)).reshape(1)]
  transfers between devices with their start and end apart: 35 -> 35, of which waited for: 11 -> 16; matrix products, arithmetic and copies ran while one was open for 2% -> 1% of each run, Pallas kernels for 26% -> 25%
where the time goes in v6:
time: 117 us
  Pallas kernels  46.2 us (39%)
  starting transfers between devices  38.7 us (33%)
  waiting for transfers between devices  29.1 us (25%)
  local copies, waits for them, and re-layouts  1.56 us (1%)
    pallas_call x40, Pallas kernels, call(): pl.pallas_call(body, out_shape=tuple((pltpu.VMEM(s, d) for s, d in outs))...  46.2 us
    ppermute x28, starting transfers between devices, travel(): return lax.ppermute(array, ('dp', 'seq'), flips(core_zero, core_one))  36.9 us
    ppermute x28, waiting for transfers between devices, travel(): return lax.ppermute(array, ('dp', 'seq'), flips(core_zero, core_one))  27.8 us
  transfers between devices with their start and end apart: 35, of which 16 were waited for; matrix products, arithmetic and copies ran while one was open for 1% of the time, Pallas kernels for 25%

profile of v6, /device:TPU:0, one launch (start us, length us, event | category | flops | bytes accessed | tf_op | source)
XLA Modules:
  0.0 117.2 jit_solution(10892986863037009606)
XLA Ops:
  0.6 0.5 collective-permute-start
  1.7 0.7 copy.29
  2.4 0.8 pad_add_fusion.refs_0_
  3.2 0.5 collective-permute-done.1.refs_2_
  3.7 0.7 collective-permute-done.2.refs_3_
  4.4 15.5 %forward.1 = (bf16[2,128,512]{2,1,0:T(8,128)(2,1)S(1)}, bf16[128,1024]{1,0:T(8,128)(2,1)S(1)}, bf16[512,1024]{1,0:T(8,128)(2,1)S(1)}, bf16[512,512]{1,0:T(8,128)...) custom-call(s32[2,5]{1,0:T(2,128)S(1)} %pad_add_fusion.refs_0_, ...), custom_call_target="tpu_custom_call" | custom-call | flops 99999997952 | bytes 1000 | tf_op jit(solution)/shard_map/forward/pallas_call | solution.py:754
  19.9 0.5 collective-permute-start.3
  20.4 2.1 %feed_back.1 = (bf16[512,1024]{1,0:T(8,128)(2,1)S(1)}, bf16[512,1024]{1,0:T(8,128)(2,1)S(1)}, bf16[256,2048]{1,0:T(8,128)(2,1)S(1)}) custom-call(bf16[512,512]{1,0:T(8,128)(2,1)S(1)} %get-tuple-element.109.refs_0_, bf16[2048,512]{1,0:T(8,128)(2,1)S(1)} %get-tuple-element.110.refs_1_, bf16[512,2048]{1,0:T(8,128)(2,1)S(1)} %get-tuple-element.111.refs_2_, ...), custom_call_target="tpu_custom_call" | custom-call | flops 99999997952 | bytes 1000 | tf_op jit(solution)/shard_map/feed_back/pallas_call | solution.py:754
  22.7 1.0 add_split.12
  23.6 2.9 %collective-permute-start.9 = (bf16[256,1024]{1,0:T(8,128)(2,1)}, bf16[256,1024]{1,0:T(8,128)(2,1)}, u32[]{:S(2)}, u32[]{:S(2)}) collective-permute-start(bf16[256,1024]{1,0:T(8,128)(2,1)} %get-tuple-element.133.refs_3_), channel_id=1, source_target_pairs={{0,8},{2,10},{4,12},{6,14},{8,0},{10,2},{12,4},{14,6},{16,24},{18,... | collective-permute-start | bytes 1572872 | tf_op jit(solution)/shard_map/ppermute | solution.py:863
  26.6 0.7 feed_keep.1.refs_1_.refs_3_
  27.3 1.0 add_split.13
  28.3 1.5 %collective-permute-start.6 = (bf16[256,1024]{1,0:T(8,128)(2,1)}, bf16[256,1024]{1,0:T(8,128)(2,1)}, u32[]{:S(2)}, u32[]{:S(2)}) collective-permute-start(bf16[256,1024]{1,0:T(8,128)(2,1)} %get-tuple-element.134.refs_17_), channel_id=1, source_target_pairs={{0,2},{2,0},{4,6},{6,4},{8,10},{10,8},{12,14},{14,12},{16,18},{18,... | collective-permute-start | bytes 1572872 | tf_op jit(solution)/shard_map/ppermute | solution.py:863
  29.7 5.1 %cross.1 = (bf16[512,512]{1,0:T(8,128)(2,1)S(1)}, bf16[512,512]{1,0:T(8,128)(2,1)S(1)}, bf16[1024,512]{1,0:T(8,128)(2,1)S(1)}, f32[512,512]{1,0:T(8,128)S(1)}, f32[8,512]{1,0:T(8,128)S(1)}) custom-call(f32[512,512]{1,0:T(8,128)S(1)} %get-tuple-element.107.refs_0_, bf16[256,2048]{1,0:T(8,128)(2,1)S(1)} %get-tuple-element.108.refs_6_.refs_1_, ...), custom_call_target="tpu_custom_call" | custom-call | flops 99999997952 | bytes 1000 | tf_op jit(solution)/shard_map/cross/pallas_call | solution.py:754
  34.9 1.9 %cross_grads.1 = (bf16[768,1024]{1,0:T(8,128)(2,1)S(1)}, bf16[512,1024]{1,0:T(8,128)(2,1)S(1)}, bf16[2,128,512]{2,1,0:T(8,128)(2,1)S(1)}) custom-call(bf16[512,512]{1,0:T(8,128)(2,1)S(1)} %get-tuple-element.135.refs_0_, bf16[512,512]{1,0:T(8,128)(2,1)S(1)} %get-tuple-element.136.refs_1_, bf16[1024,512]{1,0:T(8,128)(2,1)S(1)} %get-tuple-element.137.refs_2_, ...), custom_call_target="tpu_custom_call" | custom-call | flops 99999997952 | bytes 1000 | tf_op jit(solution)/shard_map/cross_grads/pallas_call | solution.py:754
  36.9 2.8 %self.1 = (bf16[512,512]{1,0:T(8,128)(2,1)S(1)}, bf16[1536,512]{1,0:T(8,128)(2,1)S(1)}) custom-call(f32[512,512]{1,0:T(8,128)S(1)} %get-tuple-element.142.refs_8_.refs_0_.refs_1_, bf16[512,512]{1,0:T(8,128)(2,1)S(1)} %get-tuple-element.145.refs_1_, bf16[512,1536]{1,0:T(8,128)(2,1)S(1)} %get-tuple-element.146.refs_2_, ...), custom_call_target="tpu_custom_call" | custom-call | flops 99999997952 | bytes 1000 | tf_op jit(solution)/shard_map/self/pallas_call | solution.py:754
  39.7 1.2 add_split.14
  40.9 0.8 collective-permute-start.8
  41.7 1.0 add_split.15
  42.6 1.5 %collective-permute-start.13 = (bf16[256,1024]{1,0:T(8,128)(2,1)}, bf16[256,1024]{1,0:T(8,128)(2,1)}, u32[]{:S(2)}, u32[]{:S(2)}) collective-permute-start(bf16[256,1024]{1,0:T(8,128)(2,1)} %get-tuple-element.158.refs_8_), channel_id=1, source_target_pairs={{0,2},{2,0},{4,6},{6,4},{8,10},{10,8},{12,14},{14,12},{16,18},{18,... | collective-permute-start | bytes 1572872 | tf_op jit(solution)/shard_map/ppermute | solution.py:863
  44.1 2.9 %self_grads.1 = (bf16[656,1024]{1,0:T(8,128)(2,1)S(1)}, bf16[528,1024]{1,0:T(8,128)(2,1)S(1)}, bf16[2,128,512]{2,1,0:T(8,128)(2,1)S(1)}) custom-call(s32[2,5]{1,0:T(2,128)S(1)} %pad_add_fusion.refs_0_, f32[512,512]{1,0:T(8,128)S(1)} %get-tuple-element.142.refs_8_.refs_0_.refs_1_, f32[8,512]{1,0:T(8,128)S(1)} %get-tuple-element.144.refs_2_, ...), custom_call_target="tpu_custom_call" | custom-call | flops 99999997952 | bytes 1000 | tf_op jit(solution)/shard_map/self_grads/pallas_call | solution.py:754
  47.1 1.2 add_split.16
  48.3 0.6 collective-permute-start.11
  48.9 0.7 collective-permute-done.8.refs_2_
  49.7 1.6 %collective-permute-start.12 = (bf16[64,1024]{1,0:T(8,128)(2,1)S(1)}, bf16[64,1024]{1,0:T(8,128)(2,1)S(1)}, u32[]{:S(2)}, u32[]{:S(2)}) collective-permute-start(bf16[64,1024]{1,0:T(8,128)(2,1)S(1)} %get-tuple-element.165.refs_3_), channel_id=1, source_target_pairs={{0,4},{2,6},{4,0},{6,2},{8,12},{10,14},{12,8},{14,10},{16,20},{18,... | collective-permute-start | bytes 393224 | tf_op jit(solution)/shard_map/ppermute | solution.py:863
  51.6 0.8 copy-done
  52.4 0.5 collective-permute-start.10
  52.9 1.2 add_split.19
  54.1 0.7 collective-permute-start.15
  54.7 1.5 %collective-permute-done.12.refs_1_ = bf16[64,1024]{1,0:T(8,128)(2,1)S(1)} collective-permute-done((bf16[64,1024]{1,0:T(8,128)(2,1)S(1)}, bf16[64,1024]{1,0:T(8,128)(2,1)S(1)}, u32[]{:S(2)}, u32[]{:S(2)}) %collective-permute-start.12) | collective-permute-done | bytes 131104 | tf_op jit(solution)/shard_map/ppermute | solution.py:863
  56.2 2.7 %collective-permute-start.18 = (bf16[64,1024]{1,0:T(8,128)(2,1)S(1)}, bf16[64,1024]{1,0:T(8,128)(2,1)S(1)}, u32[]{:S(2)}, u32[]{:S(2)}) collective-permute-start(bf16[64,1024]{1,0:T(8,128)(2,1)S(1)} %add_all.4.refs_3_.refs_0_), channel_id=1, source_target_pairs={{0,16},{2,18},{4,20},{6,22},{8,24},{10,26},{12,28},{14,30},{16,0},... | collective-permute-start | bytes 393224 | tf_op jit(solution)/shard_map/ppermute | solution.py:863
  59.0 1.6 %collective-permute-start.16 = (bf16[64,1024]{1,0:T(8,128)(2,1)S(1)}, bf16[64,1024]{1,0:T(8,128)(2,1)S(1)}, u32[]{:S(2)}, u32[]{:S(2)}) collective-permute-start(bf16[64,1024]{1,0:T(8,128)(2,1)S(1)} %get-tuple-element.172.refs_3_), channel_id=1, source_target_pairs={{0,4},{2,6},{4,0},{6,2},{8,12},{10,14},{12,8},{14,10},{16,20},{18,... | collective-permute-start | bytes 393224 | tf_op jit(solution)/shard_map/ppermute | solution.py:863
  60.6 3.0 %collective-permute-done.10.refs_2_ = bf16[272,1024]{1,0:T(8,128)(2,1)S(1)} collective-permute-done((bf16[272,1024]{1,0:T(8,128)(2,1)S(1)}, bf16[272,1024]{1,0:T(8,128)(2,1)S(1)}, u32[]{:S(2)}, u32[]{:S(2)}) %collective-permute-start.10) | collective-permute-done | bytes 557088 | tf_op jit(solution)/shard_map/ppermute | solution.py:863
  63.8 1.4 %collective-permute-start.14 = (bf16[144,1024]{1,0:T(8,128)(2,1)S(1)}, bf16[144,1024]{1,0:T(8,128)(2,1)S(1)}, u32[]{:S(2)}, u32[]{:S(2)}) collective-permute-start(bf16[144,1024]{1,0:T(8,128)(2,1)S(1)} %get-tuple-element.174.refs_2_), channel_id=1, source_target_pairs={{0,4},{2,6},{4,0},{6,2},{8,12},{10,14},{12,8},{14,10},{16,20},{18,... | collective-permute-start | bytes 884744 | tf_op jit(solution)/shard_map/ppermute | solution.py:863
  65.2 2.7 %collective-permute-start.21 = (bf16[64,1024]{1,0:T(8,128)(2,1)S(1)}, bf16[64,1024]{1,0:T(8,128)(2,1)S(1)}, u32[]{:S(2)}, u32[]{:S(2)}) collective-permute-start(bf16[64,1024]{1,0:T(8,128)(2,1)S(1)} %add_all.5.refs_3_.refs_0_), channel_id=1, source_target_pairs={{0,16},{2,18},{4,20},{6,22},{8,24},{10,26},{12,28},{14,30},{16,0},... | collective-permute-start | bytes 393224 | tf_op jit(solution)/shard_map/ppermute | solution.py:863
  68.0 0.7 collective-permute-start.19
  68.6 1.9 %collective-permute-done.14.refs_2_ = bf16[144,1024]{1,0:T(8,128)(2,1)S(1)} collective-permute-done((bf16[144,1024]{1,0:T(8,128)(2,1)S(1)}, bf16[144,1024]{1,0:T(8,128)(2,1)S(1)}, u32[]{:S(2)}, u32[]{:S(2)}) %collective-permute-start.14) | collective-permute-done | bytes 294944 | tf_op jit(solution)/shard_map/ppermute | solution.py:863
  70.6 1.4 %collective-permute-start.17 = (bf16[80,1024]{1,0:T(8,128)(2,1)S(1)}, bf16[80,1024]{1,0:T(8,128)(2,1)S(1)}, u32[]{:S(2)}, u32[]{:S(2)}) collective-permute-start(bf16[80,1024]{1,0:T(8,128)(2,1)S(1)} %get-tuple-element.179.refs_2_), channel_id=1, source_target_pairs={{0,8},{2,10},{4,12},{6,14},{8,0},{10,2},{12,4},{14,6},{16,24},{18,... | collective-permute-start | bytes 491528 | tf_op jit(solution)/shard_map/ppermute | solution.py:863
  72.0 1.0 collective-permute-done.19.refs_1_
  73.0 1.6 %collective-permute-start.23 = (bf16[64,1024]{1,0:T(8,128)(2,1)S(1)}, bf16[64,1024]{1,0:T(8,128)(2,1)S(1)}, u32[]{:S(2)}, u32[]{:S(2)}) collective-permute-start(bf16[64,1024]{1,0:T(8,128)(2,1)S(1)} %add_all.6.refs_2_.refs_0_), channel_id=1, source_target_pairs={{0,16},{2,18},{4,20},{6,22},{8,24},{10,26},{12,28},{14,30},{16,0},... | collective-permute-start | bytes 393224 | tf_op jit(solution)/shard_map/ppermute | solution.py:863
  74.7 1.6 %collective-permute-start.24 = (bf16[64,1024]{1,0:T(8,128)(2,1)S(1)}, bf16[64,1024]{1,0:T(8,128)(2,1)S(1)}, u32[]{:S(2)}, u32[]{:S(2)}) collective-permute-start(bf16[64,1024]{1,0:T(8,128)(2,1)S(1)} %add_last.4.refs_2_.refs_1_), channel_id=1, source_target_pairs={{0,4},{2,6},{4,0},{6,2},{8,12},{10,14},{12,8},{14,10},{16,20},{18,... | collective-permute-start | bytes 393224 | tf_op jit(solution)/shard_map/ppermute | solution.py:863
  76.3 1.1 collective-permute-done.17.refs_1_
  77.4 2.4 %collective-permute-start.20 = (bf16[80,1024]{1,0:T(8,128)(2,1)S(1)}, bf16[80,1024]{1,0:T(8,128)(2,1)S(1)}, u32[]{:S(2)}, u32[]{:S(2)}) collective-permute-start(bf16[80,1024]{1,0:T(8,128)(2,1)S(1)} %add_all.7.refs_5_.refs_2_.refs_0_), channel_id=1, source_target_pairs={{0,16},{2,18},{4,20},{6,22},{8,24},{10,26},{12,28},{14,30},{16,0},... | collective-permute-start | bytes 491528 | tf_op jit(solution)/shard_map/ppermute | solution.py:863
  79.9 1.3 %collective-permute-start.22 = (bf16[64,1024]{1,0:T(8,128)(2,1)S(1)}, bf16[64,1024]{1,0:T(8,128)(2,1)S(1)}, u32[]{:S(2)}, u32[]{:S(2)}) collective-permute-start(bf16[64,1024]{1,0:T(8,128)(2,1)S(1)} %add_last.5.refs_3_.refs_1_), channel_id=1, source_target_pairs={{0,4},{2,6},{4,0},{6,2},{8,12},{10,14},{12,8},{14,10},{16,20},{18,... | collective-permute-start | bytes 393224 | tf_op jit(solution)/shard_map/ppermute | solution.py:863
  81.2 2.5 %collective-permute-start.26 = (bf16[128,1024]{1,0:T(8,128)(2,1)S(1)}, bf16[128,1024]{1,0:T(8,128)(2,1)S(1)}, u32[]{:S(2)}, u32[]{:S(2)}) collective-permute-start(bf16[128,1024]{1,0:T(8,128)(2,1)S(1)} %join.8.refs_2_.refs_1_), channel_id=1, source_target_pairs={{0,8},{2,10},{4,12},{6,14},{8,0},{10,2},{12,4},{14,6},{16,24},{18,... | collective-permute-start | bytes 786440 | tf_op jit(solution)/shard_map/ppermute | solution.py:863
  83.7 0.7 collective-permute-done.23.refs_1_
  84.5 1.2 %place.1 = (bf16[2,2,128,512]{3,2,1,0:T(8,128)(2,1)}, bf16[2,2,128,512]{3,2,1,0:T(8,128)(2,1)}, bf16[2,2,128,512]{3,2,1,0:T(8,128)(2,1)}) custom-call(bf16[2,128,512]{2,1,0:T(8,128)(2,1)S(1)} %get-tuple-element.106.refs_0_, bf16[2,128,512]{2,1,0:T(8,128)(2,1)S(1)} %get-tuple-element.143.refs_1_, bf16[2,128,512]{2,1,0:T(8,128)(2,1)S(1)} %get-tuple-element.159.refs_2_, ...), custom_call_target="tpu_custom_call" | custom-call | flops 20000000000 | bytes 400000000 | tf_op jit(solution)/shard_map/place/pallas_call | solution.py:754
  85.7 1.9 %collective-permute-start.31 = (bf16[128,1024]{1,0:T(8,128)(2,1)S(1)}, bf16[128,1024]{1,0:T(8,128)(2,1)S(1)}, u32[]{:S(2)}, u32[]{:S(2)}) collective-permute-start(bf16[128,1024]{1,0:T(8,128)(2,1)S(1)} %join.9.refs_2_.refs_1_), channel_id=1, source_target_pairs={{0,2},{2,0},{4,6},{6,4},{8,10},{10,8},{12,14},{14,12},{16,18},{18,... | collective-permute-start | bytes 786440 | tf_op jit(solution)/shard_map/ppermute | solution.py:863
  87.7 1.0 collective-permute-start.25
  88.7 0.7 collective-permute-done.27.refs_2_
  89.4 0.8 collective-permute-start.30
  90.3 1.9 %collective-permute-done.26.refs_2_ = bf16[128,1024]{1,0:T(8,128)(2,1)S(1)} collective-permute-done((bf16[128,1024]{1,0:T(8,128)(2,1)S(1)}, bf16[128,1024]{1,0:T(8,128)(2,1)S(1)}, u32[]{:S(2)}, u32[]{:S(2)}) %collective-permute-start.26) | collective-permute-done | bytes 262176 | tf_op jit(solution)/shard_map/ppermute | solution.py:863
  92.3 0.6 collective-permute-start.29
  92.8 2.2 %collective-permute-done.25.refs_2_ = bf16[64,1024]{1,0:T(8,128)(2,1)S(1)} collective-permute-done((bf16[64,1024]{1,0:T(8,128)(2,1)S(1)}, bf16[64,1024]{1,0:T(8,128)(2,1)S(1)}, u32[]{:S(2)}, u32[]{:S(2)}) %collective-permute-start.25) | collective-permute-done | bytes 131104 | tf_op jit(solution)/shard_map/ppermute | solution.py:863
  95.1 0.5 collective-permute-start.28
  95.6 1.4 %collective-permute-start.33 = (bf16[256,1024]{1,0:T(8,128)(2,1)S(1)}, bf16[256,1024]{1,0:T(8,128)(2,1)S(1)}, u32[]{:S(2)}, u32[]{:S(2)}) collective-permute-start(bf16[256,1024]{1,0:T(8,128)(2,1)S(1)} %join.13.refs_3_.refs_1_), channel_id=1, source_target_pairs={{0,8},{2,10},{4,12},{6,14},{8,0},{10,2},{12,4},{14,6},{16,24},{18,... | collective-permute-start | bytes 1572872 | tf_op jit(solution)/shard_map/ppermute | solution.py:863
  97.1 3.6 %collective-permute-done.30.refs_2_ = bf16[128,1024]{1,0:T(8,128)(2,1)S(1)} collective-permute-done((bf16[128,1024]{1,0:T(8,128)(2,1)S(1)}, bf16[128,1024]{1,0:T(8,128)(2,1)S(1)}, u32[]{:S(2)}, u32[]{:S(2)}) %collective-permute-start.30) | collective-permute-done | bytes 262176 | tf_op jit(solution)/shard_map/ppermute | solution.py:863
  101.1 2.3 %collective-permute-done.29.refs_2_ = bf16[256,1024]{1,0:T(8,128)(2,1)S(1)} collective-permute-done((bf16[256,1024]{1,0:T(8,128)(2,1)S(1)}, bf16[256,1024]{1,0:T(8,128)(2,1)S(1)}, u32[]{:S(2)}, u32[]{:S(2)}) %collective-permute-start.29) | collective-permute-done | bytes 524320 | tf_op jit(solution)/shard_map/ppermute | solution.py:863
  103.3 1.5 %unpack.4 = (f32[8,128]{1,0:T(8,128)S(1)}, f32[512,1024]{1,0:T(8,128)}) custom-call(s32[1]{0:T(128)} %bitcast.1.refs_0_, bf16[256,1024]{1,0:T(8,128)(2,1)S(1)} %join.11.refs_3_.refs_1_, bf16[256,1024]{1,0:T(8,128)(2,1)S(1)} %collective-permute-done.29.refs_2_, bf16[256,1024]{1,0:T(8,128)(2,1)S(1)} %join.14.refs_3_.refs_1_), custom_call_target="tpu_custom_call" | custom-call | flops 20000000000 | bytes 400000000 | tf_op jit(solution)/shard_map/unpack/pallas_call | solution.py:754
  105.2 4.7 %collective-permute-done.34.refs_2_ = bf16[256,1024]{1,0:T(8,128)(2,1)S(1)} collective-permute-done((bf16[256,1024]{1,0:T(8,128)(2,1)S(1)}, bf16[256,1024]{1,0:T(8,128)(2,1)S(1)}, u32[]{:S(2)}, u32[]{:S(2)}) %collective-permute-start.34) | collective-permute-done | bytes 524320 | tf_op jit(solution)/shard_map/ppermute | solution.py:863
  109.9 1.6 %unpack.5 = (f32[8,128]{1,0:T(8,128)S(1)}, f32[512,512]{1,0:T(8,128)}, f32[512,256]{1,0:T(8,128)}, f32[512,256]{1,0:T(8,128)}) custom-call(s32[1]{0:T(128)} %bitcast.1.refs_0_, bf16[256,1024]{1,0:T(8,128)(2,1)S(1)} %join.14.refs_3_.refs_1_, bf16[256,1024]{1,0:T(8,128)(2,1)S(1)} %collective-permute-done.34.refs_2_, bf16[256,1024]{1,0:T(8,128)(2,1)S(1)} %join.15.refs_3_.refs_1_), custom_call_target="tpu_custom_call" | custom-call | flops 20000000000 | bytes 400000000 | tf_op jit(solution)/shard_map/unpack/pallas_call | solution.py:754
  111.6 1.6 %unpack.6 = (f32[8,128]{1,0:T(8,128)S(1)}, f32[2048,256]{1,0:T(8,128)}) custom-call(s32[1]{0:T(128)} %bitcast.2.refs_0_, bf16[256,1024]{1,0:T(8,128)(2,1)S(1)} %join.13.refs_3_.refs_1_, bf16[256,1024]{1,0:T(8,128)(2,1)S(1)} %collective-permute-done.33.refs_2_, f32[8,128]{1,0:T(8,128)S(1)} %get-tuple-element.187.refs_3_), custom_call_target="tpu_custom_call" | custom-call | flops 20000000000 | bytes 400000000 | tf_op jit(solution)/shard_map/unpack/pallas_call | solution.py:754
  113.2 2.4 %collective-permute-done.32.refs_2_ = bf16[256,1024]{1,0:T(8,128)(2,1)S(1)} collective-permute-done((bf16[256,1024]{1,0:T(8,128)(2,1)S(1)}, bf16[256,1024]{1,0:T(8,128)(2,1)S(1)}, u32[]{:S(2)}, u32[]{:S(2)}) %collective-permute-start.32) | collective-permute-done | bytes 524320 | tf_op jit(solution)/shard_map/ppermute | solution.py:863
  115.6 1.6 %unpack.7 = (f32[8,128]{1,0:T(8,128)}, f32[512,768]{1,0:T(8,128)}, f32[512,256]{1,0:T(8,128)}, f32[3,256]{1,0:T(4,128)}, f32[3,256]{1,0:T(4,128)}, /*index=5*/f32[8,256]{1,0:T(8,128)}) custom-call(s32[1]{0:T(128)} %bitcast.1.refs_0_, bf16[256,1024]{1,0:T(8,128)(2,1)S(1)} %join.15.refs_3_.refs_1_, bf16[256,1024]{1,0:T(8,128)(2,1)S(1)} %collective-permute-done.32.refs_2_, ...), custom_call_target="tpu_custom_call" | custom-call | flops 20000000000 | bytes 400000000 | tf_op jit(solution)/shard_map/unpack/pallas_call | solution.py:754
  (52 shorter events, 2.9 us)
Async XLA Ops:
  0.6 2.5 %collective-permute-start = (bf16[2,2,128,512]{3,2,1,0:T(8,128)(2,1)}, bf16[2,2,128,512]{3,2,1,0:T(8,128)(2,1)S(1)}, u32[]{:S(2)}, u32[]{:S(2)}) collective-permute-start(bf16[2,2,128,512]{3,2,1,0:T(8,128)(2,1)} %refs_4_.1), channel_id=1, source_target_pairs={{0,1},{1,0},{2,3},{3,2},{4,5},{5,4},{6,7},{7,6},{8,9},{9,8},{10,11... | collective-permute-start | bytes 1572872 | tf_op jit(solution)/shard_map/ppermute | solution.py:791
  1.2 2.5 %collective-permute-start.1 = (bf16[2,2,128,512]{3,2,1,0:T(8,128)(2,1)}, bf16[2,2,128,512]{3,2,1,0:T(8,128)(2,1)S(1)}, u32[]{:S(2)}, u32[]{:S(2)}) collective-permute-start(bf16[2,2,128,512]{3,2,1,0:T(8,128)(2,1)} %refs_5_.1), channel_id=1, source_target_pairs={{0,1},{1,0},{2,3},{3,2},{4,5},{5,4},{6,7},{7,6},{8,9},{9,8},{10,11... | collective-permute-start | bytes 1572872 | tf_op jit(solution)/shard_map/ppermute | solution.py:792
  1.2 3.2 %collective-permute-start.2 = (bf16[2,2,128,512]{3,2,1,0:T(8,128)(2,1)}, bf16[2,2,128,512]{3,2,1,0:T(8,128)(2,1)S(1)}, u32[]{:S(2)}, u32[]{:S(2)}) collective-permute-start(bf16[2,2,128,512]{3,2,1,0:T(8,128)(2,1)} %refs_6_.1), channel_id=1, source_target_pairs={{0,1},{1,0},{2,3},{3,2},{4,5},{5,4},{6,7},{7,6},{8,9},{9,8},{10,11... | collective-permute-start | bytes 1572872 | tf_op jit(solution)/shard_map/ppermute | solution.py:793
  19.9 2.7 %collective-permute-start.3 = (bf16[512,1024]{1,0:T(8,128)(2,1)S(1)}, bf16[512,1024]{1,0:T(8,128)(2,1)S(1)}, u32[]{:S(2)}, u32[]{:S(2)}) collective-permute-start(bf16[512,1024]{1,0:T(8,128)(2,1)S(1)} %get-tuple-element.131), channel_id=1, source_target_pairs={{0,1},{1,0},{2,3},{3,2},{4,5},{5,4},{6,7},{7,6},{8,9},{9,8},{10,11... | collective-permute-start | bytes 3145736 | tf_op jit(solution)/shard_map/ppermute | solution.py:1022
  22.5 4.8 %collective-permute-start.4 = (bf16[512,1024]{1,0:T(8,128)(2,1)S(1)}, bf16[512,1024]{1,0:T(8,128)(2,1)S(1)}, u32[]{:S(2)}, u32[]{:S(2)}) collective-permute-start(bf16[512,1024]{1,0:T(8,128)(2,1)S(1)} %get-tuple-element.132.refs_3_), channel_id=1, source_target_pairs={{0,1},{1,0},{2,3},{3,2},{4,5},{5,4},{6,7},{7,6},{8,9},{9,8},{10,11... | collective-permute-start | bytes 3145736 | tf_op jit(solution)/shard_map/ppermute | solution.py:930
  23.6 23.5 %collective-permute-start.9 = (bf16[256,1024]{1,0:T(8,128)(2,1)}, bf16[256,1024]{1,0:T(8,128)(2,1)}, u32[]{:S(2)}, u32[]{:S(2)}) collective-permute-start(bf16[256,1024]{1,0:T(8,128)(2,1)} %get-tuple-element.133.refs_3_), channel_id=1, source_target_pairs={{0,8},{2,10},{4,12},{6,14},{8,0},{10,2},{12,4},{14,6},{16,24},{18,... | collective-permute-start | bytes 1572872 | tf_op jit(solution)/shard_map/ppermute | solution.py:863
  28.3 11.4 %collective-permute-start.6 = (bf16[256,1024]{1,0:T(8,128)(2,1)}, bf16[256,1024]{1,0:T(8,128)(2,1)}, u32[]{:S(2)}, u32[]{:S(2)}) collective-permute-start(bf16[256,1024]{1,0:T(8,128)(2,1)} %get-tuple-element.134.refs_17_), channel_id=1, source_target_pairs={{0,2},{2,0},{4,6},{6,4},{8,10},{10,8},{12,14},{14,12},{16,18},{18,... | collective-permute-start | bytes 1572872 | tf_op jit(solution)/shard_map/ppermute | solution.py:863
  36.8 4.9 %collective-permute-start.5 = (bf16[768,1024]{1,0:T(8,128)(2,1)S(1)}, bf16[768,1024]{1,0:T(8,128)(2,1)S(1)}, u32[]{:S(2)}, u32[]{:S(2)}) collective-permute-start(bf16[768,1024]{1,0:T(8,128)(2,1)S(1)} %get-tuple-element.150.refs_6_), channel_id=1, source_target_pairs={{0,1},{1,0},{2,3},{3,2},{4,5},{5,4},{6,7},{7,6},{8,9},{9,8},{10,11... | collective-permute-start | bytes 4718600 | tf_op jit(solution)/shard_map/ppermute | solution.py:975
  40.9 8.8 %collective-permute-start.8 = (bf16[128,1024]{1,0:T(8,128)(2,1)S(1)}, bf16[128,1024]{1,0:T(8,128)(2,1)S(1)}, u32[]{:S(2)}, u32[]{:S(2)}) collective-permute-start(bf16[128,1024]{1,0:T(8,128)(2,1)S(1)} %get-tuple-element.157.refs_3_), channel_id=1, source_target_pairs={{0,8},{2,10},{4,12},{6,14},{8,0},{10,2},{12,4},{14,6},{16,24},{18,... | collective-permute-start | bytes 786440 | tf_op jit(solution)/shard_map/ppermute | solution.py:863
  42.6 10.3 %collective-permute-start.13 = (bf16[256,1024]{1,0:T(8,128)(2,1)}, bf16[256,1024]{1,0:T(8,128)(2,1)}, u32[]{:S(2)}, u32[]{:S(2)}) collective-permute-start(bf16[256,1024]{1,0:T(8,128)(2,1)} %get-tuple-element.158.refs_8_), channel_id=1, source_target_pairs={{0,2},{2,0},{4,6},{6,4},{8,10},{10,8},{12,14},{14,12},{16,18},{18,... | collective-permute-start | bytes 1572872 | tf_op jit(solution)/shard_map/ppermute | solution.py:863
  47.0 4.3 %collective-permute-start.7 = (bf16[656,1024]{1,0:T(8,128)(2,1)S(1)}, bf16[656,1024]{1,0:T(8,128)(2,1)S(1)}, u32[]{:S(2)}, u32[]{:S(2)}) collective-permute-start(bf16[656,1024]{1,0:T(8,128)(2,1)S(1)} %get-tuple-element.160.refs_3_), channel_id=1, source_target_pairs={{0,1},{1,0},{2,3},{3,2},{4,5},{5,4},{6,7},{7,6},{8,9},{9,8},{10,11... | collective-permute-start | bytes 4030472 | tf_op jit(solution)/shard_map/ppermute | solution.py:1006
  48.3 10.6 %collective-permute-start.11 = (bf16[128,1024]{1,0:T(8,128)(2,1)S(1)}, bf16[128,1024]{1,0:T(8,128)(2,1)S(1)}, u32[]{:S(2)}, u32[]{:S(2)}) collective-permute-start(bf16[128,1024]{1,0:T(8,128)(2,1)S(1)} %get-tuple-element.164.refs_3_), channel_id=1, source_target_pairs={{0,2},{2,0},{4,6},{6,4},{8,10},{10,8},{12,14},{14,12},{16,18},{18,... | collective-permute-start | bytes 786440 | tf_op jit(solution)/shard_map/ppermute | solution.py:863
  49.7 6.5 %collective-permute-start.12 = (bf16[64,1024]{1,0:T(8,128)(2,1)S(1)}, bf16[64,1024]{1,0:T(8,128)(2,1)S(1)}, u32[]{:S(2)}, u32[]{:S(2)}) collective-permute-start(bf16[64,1024]{1,0:T(8,128)(2,1)S(1)} %get-tuple-element.165.refs_3_), channel_id=1, source_target_pairs={{0,4},{2,6},{4,0},{6,2},{8,12},{10,14},{12,8},{14,10},{16,20},{18,... | collective-permute-start | bytes 393224 | tf_op jit(solution)/shard_map/ppermute | solution.py:863
  51.3 1.1 copy-start
  52.4 11.2 %collective-permute-start.10 = (bf16[272,1024]{1,0:T(8,128)(2,1)S(1)}, bf16[272,1024]{1,0:T(8,128)(2,1)S(1)}, u32[]{:S(2)}, u32[]{:S(2)}) collective-permute-start(bf16[272,1024]{1,0:T(8,128)(2,1)S(1)} %get-tuple-element.167.refs_3_), channel_id=1, source_target_pairs={{0,2},{2,0},{4,6},{6,4},{8,10},{10,8},{12,14},{14,12},{16,18},{18,... | collective-permute-start | bytes 1671176 | tf_op jit(solution)/shard_map/ppermute | solution.py:863
  54.1 13.8 %collective-permute-start.15 = (bf16[128,1024]{1,0:T(8,128)(2,1)S(1)}, bf16[128,1024]{1,0:T(8,128)(2,1)S(1)}, u32[]{:S(2)}, u32[]{:S(2)}) collective-permute-start(bf16[128,1024]{1,0:T(8,128)(2,1)S(1)} %get-tuple-element.171.refs_2_), channel_id=1, source_target_pairs={{0,8},{2,10},{4,12},{6,14},{8,0},{10,2},{12,4},{14,6},{16,24},{18,... | collective-permute-start | bytes 786440 | tf_op jit(solution)/shard_map/ppermute | solution.py:863
  56.2 18.4 %collective-permute-start.18 = (bf16[64,1024]{1,0:T(8,128)(2,1)S(1)}, bf16[64,1024]{1,0:T(8,128)(2,1)S(1)}, u32[]{:S(2)}, u32[]{:S(2)}) collective-permute-start(bf16[64,1024]{1,0:T(8,128)(2,1)S(1)} %add_all.4.refs_3_.refs_0_), channel_id=1, source_target_pairs={{0,16},{2,18},{4,20},{6,22},{8,24},{10,26},{12,28},{14,30},{16,0},... | collective-permute-start | bytes 393224 | tf_op jit(solution)/shard_map/ppermute | solution.py:863
  59.0 6.2 %collective-permute-start.16 = (bf16[64,1024]{1,0:T(8,128)(2,1)S(1)}, bf16[64,1024]{1,0:T(8,128)(2,1)S(1)}, u32[]{:S(2)}, u32[]{:S(2)}) collective-permute-start(bf16[64,1024]{1,0:T(8,128)(2,1)S(1)} %get-tuple-element.172.refs_3_), channel_id=1, source_target_pairs={{0,4},{2,6},{4,0},{6,2},{8,12},{10,14},{12,8},{14,10},{16,20},{18,... | collective-permute-start | bytes 393224 | tf_op jit(solution)/shard_map/ppermute | solution.py:863
  63.8 6.8 %collective-permute-start.14 = (bf16[144,1024]{1,0:T(8,128)(2,1)S(1)}, bf16[144,1024]{1,0:T(8,128)(2,1)S(1)}, u32[]{:S(2)}, u32[]{:S(2)}) collective-permute-start(bf16[144,1024]{1,0:T(8,128)(2,1)S(1)} %get-tuple-element.174.refs_2_), channel_id=1, source_target_pairs={{0,4},{2,6},{4,0},{6,2},{8,12},{10,14},{12,8},{14,10},{16,20},{18,... | collective-permute-start | bytes 884744 | tf_op jit(solution)/shard_map/ppermute | solution.py:863
  65.2 14.6 %collective-permute-start.21 = (bf16[64,1024]{1,0:T(8,128)(2,1)S(1)}, bf16[64,1024]{1,0:T(8,128)(2,1)S(1)}, u32[]{:S(2)}, u32[]{:S(2)}) collective-permute-start(bf16[64,1024]{1,0:T(8,128)(2,1)S(1)} %add_all.5.refs_3_.refs_0_), channel_id=1, source_target_pairs={{0,16},{2,18},{4,20},{6,22},{8,24},{10,26},{12,28},{14,30},{16,0},... | collective-permute-start | bytes 393224 | tf_op jit(solution)/shard_map/ppermute | solution.py:863
  68.0 5.0 %collective-permute-start.19 = (bf16[64,1024]{1,0:T(8,128)(2,1)S(1)}, bf16[64,1024]{1,0:T(8,128)(2,1)S(1)}, u32[]{:S(2)}, u32[]{:S(2)}) collective-permute-start(bf16[64,1024]{1,0:T(8,128)(2,1)S(1)} %get-tuple-element.177.refs_3_), channel_id=1, source_target_pairs={{0,4},{2,6},{4,0},{6,2},{8,12},{10,14},{12,8},{14,10},{16,20},{18,... | collective-permute-start | bytes 393224 | tf_op jit(solution)/shard_map/ppermute | solution.py:863
  70.6 6.8 %collective-permute-start.17 = (bf16[80,1024]{1,0:T(8,128)(2,1)S(1)}, bf16[80,1024]{1,0:T(8,128)(2,1)S(1)}, u32[]{:S(2)}, u32[]{:S(2)}) collective-permute-start(bf16[80,1024]{1,0:T(8,128)(2,1)S(1)} %get-tuple-element.179.refs_2_), channel_id=1, source_target_pairs={{0,8},{2,10},{4,12},{6,14},{8,0},{10,2},{12,4},{14,6},{16,24},{18,... | collective-permute-start | bytes 491528 | tf_op jit(solution)/shard_map/ppermute | solution.py:863
  73.0 11.3 %collective-permute-start.23 = (bf16[64,1024]{1,0:T(8,128)(2,1)S(1)}, bf16[64,1024]{1,0:T(8,128)(2,1)S(1)}, u32[]{:S(2)}, u32[]{:S(2)}) collective-permute-start(bf16[64,1024]{1,0:T(8,128)(2,1)S(1)} %add_all.6.refs_2_.refs_0_), channel_id=1, source_target_pairs={{0,16},{2,18},{4,20},{6,22},{8,24},{10,26},{12,28},{14,30},{16,0},... | collective-permute-start | bytes 393224 | tf_op jit(solution)/shard_map/ppermute | solution.py:863
  74.7 6.4 %collective-permute-start.24 = (bf16[64,1024]{1,0:T(8,128)(2,1)S(1)}, bf16[64,1024]{1,0:T(8,128)(2,1)S(1)}, u32[]{:S(2)}, u32[]{:S(2)}) collective-permute-start(bf16[64,1024]{1,0:T(8,128)(2,1)S(1)} %add_last.4.refs_2_.refs_1_), channel_id=1, source_target_pairs={{0,4},{2,6},{4,0},{6,2},{8,12},{10,14},{12,8},{14,10},{16,20},{18,... | collective-permute-start | bytes 393224 | tf_op jit(solution)/shard_map/ppermute | solution.py:863
  77.4 10.2 %collective-permute-start.20 = (bf16[80,1024]{1,0:T(8,128)(2,1)S(1)}, bf16[80,1024]{1,0:T(8,128)(2,1)S(1)}, u32[]{:S(2)}, u32[]{:S(2)}) collective-permute-start(bf16[80,1024]{1,0:T(8,128)(2,1)S(1)} %add_all.7.refs_5_.refs_2_.refs_0_), channel_id=1, source_target_pairs={{0,16},{2,18},{4,20},{6,22},{8,24},{10,26},{12,28},{14,30},{16,0},... | collective-permute-start | bytes 491528 | tf_op jit(solution)/shard_map/ppermute | solution.py:863
  79.9 5.9 %collective-permute-start.22 = (bf16[64,1024]{1,0:T(8,128)(2,1)S(1)}, bf16[64,1024]{1,0:T(8,128)(2,1)S(1)}, u32[]{:S(2)}, u32[]{:S(2)}) collective-permute-start(bf16[64,1024]{1,0:T(8,128)(2,1)S(1)} %add_last.5.refs_3_.refs_1_), channel_id=1, source_target_pairs={{0,4},{2,6},{4,0},{6,2},{8,12},{10,14},{12,8},{14,10},{16,20},{18,... | collective-permute-start | bytes 393224 | tf_op jit(solution)/shard_map/ppermute | solution.py:863
  81.1 3.3 %copy-start.1 = (bf16[656,1024]{1,0:T(8,128)(2,1)S(1)}, bf16[656,1024]{1,0:T(8,128)(2,1)}, u32[]{:S(2)}) copy-start(bf16[656,1024]{1,0:T(8,128)(2,1)} %copy-done) | copy-start | bytes 4030468
  81.2 11.1 %collective-permute-start.26 = (bf16[128,1024]{1,0:T(8,128)(2,1)S(1)}, bf16[128,1024]{1,0:T(8,128)(2,1)S(1)}, u32[]{:S(2)}, u32[]{:S(2)}) collective-permute-start(bf16[128,1024]{1,0:T(8,128)(2,1)S(1)} %join.8.refs_2_.refs_1_), channel_id=1, source_target_pairs={{0,8},{2,10},{4,12},{6,14},{8,0},{10,2},{12,4},{14,6},{16,24},{18,... | collective-permute-start | bytes 786440 | tf_op jit(solution)/shard_map/ppermute | solution.py:863
  84.4 5.0 %collective-permute-start.27 = (bf16[64,1024]{1,0:T(8,128)(2,1)S(1)}, bf16[64,1024]{1,0:T(8,128)(2,1)S(1)}, u32[]{:S(2)}, u32[]{:S(2)}) collective-permute-start(bf16[64,1024]{1,0:T(8,128)(2,1)S(1)} %add_last.6.refs_3_.refs_1_), channel_id=1, source_target_pairs={{0,4},{2,6},{4,0},{6,2},{8,12},{10,14},{12,8},{14,10},{16,20},{18,... | collective-permute-start | bytes 393224 | tf_op jit(solution)/shard_map/ppermute | solution.py:863
  85.7 9.8 %collective-permute-start.31 = (bf16[128,1024]{1,0:T(8,128)(2,1)S(1)}, bf16[128,1024]{1,0:T(8,128)(2,1)S(1)}, u32[]{:S(2)}, u32[]{:S(2)}) collective-permute-start(bf16[128,1024]{1,0:T(8,128)(2,1)S(1)} %join.9.refs_2_.refs_1_), channel_id=1, source_target_pairs={{0,2},{2,0},{4,6},{6,4},{8,10},{10,8},{12,14},{14,12},{16,18},{18,... | collective-permute-start | bytes 786440 | tf_op jit(solution)/shard_map/ppermute | solution.py:863
  87.7 7.4 %collective-permute-start.25 = (bf16[64,1024]{1,0:T(8,128)(2,1)S(1)}, bf16[64,1024]{1,0:T(8,128)(2,1)S(1)}, u32[]{:S(2)}, u32[]{:S(2)}) collective-permute-start(bf16[64,1024]{1,0:T(8,128)(2,1)S(1)} %get-tuple-element.184.refs_3_.refs_1_), channel_id=1, source_target_pairs={{0,8},{2,10},{4,12},{6,14},{8,0},{10,2},{12,4},{14,6},{16,24},{18,... | collective-permute-start | bytes 393224 | tf_op jit(solution)/shard_map/ppermute | solution.py:863
  89.4 11.2 %collective-permute-start.30 = (bf16[128,1024]{1,0:T(8,128)(2,1)S(1)}, bf16[128,1024]{1,0:T(8,128)(2,1)S(1)}, u32[]{:S(2)}, u32[]{:S(2)}) collective-permute-start(bf16[128,1024]{1,0:T(8,128)(2,1)S(1)} %join.10.refs_3_.refs_1_), channel_id=1, source_target_pairs={{0,8},{2,10},{4,12},{6,14},{8,0},{10,2},{12,4},{14,6},{16,24},{18,... | collective-permute-start | bytes 786440 | tf_op jit(solution)/shard_map/ppermute | solution.py:863
  92.3 11.1 %collective-permute-start.29 = (bf16[256,1024]{1,0:T(8,128)(2,1)S(1)}, bf16[256,1024]{1,0:T(8,128)(2,1)S(1)}, u32[]{:S(2)}, u32[]{:S(2)}) collective-permute-start(bf16[256,1024]{1,0:T(8,128)(2,1)S(1)} %join.11.refs_3_.refs_1_), channel_id=1, source_target_pairs={{0,2},{2,0},{4,6},{6,4},{8,10},{10,8},{12,14},{14,12},{16,18},{18,... | collective-permute-start | bytes 1572872 | tf_op jit(solution)/shard_map/ppermute | solution.py:863
  95.1 9.8 %collective-permute-start.28 = (bf16[128,1024]{1,0:T(8,128)(2,1)S(1)}, bf16[128,1024]{1,0:T(8,128)(2,1)S(1)}, u32[]{:S(2)}, u32[]{:S(2)}) collective-permute-start(bf16[128,1024]{1,0:T(8,128)(2,1)S(1)} %join.12.refs_3_.refs_1_), channel_id=1, source_target_pairs={{0,4},{2,6},{4,0},{6,2},{8,12},{10,14},{12,8},{14,10},{16,20},{18,... | collective-permute-start | bytes 786440 | tf_op jit(solution)/shard_map/ppermute | solution.py:863
  95.6 15.9 %collective-permute-start.33 = (bf16[256,1024]{1,0:T(8,128)(2,1)S(1)}, bf16[256,1024]{1,0:T(8,128)(2,1)S(1)}, u32[]{:S(2)}, u32[]{:S(2)}) collective-permute-start(bf16[256,1024]{1,0:T(8,128)(2,1)S(1)} %join.13.refs_3_.refs_1_), channel_id=1, source_target_pairs={{0,8},{2,10},{4,12},{6,14},{8,0},{10,2},{12,4},{14,6},{16,24},{18,... | collective-permute-start | bytes 1572872 | tf_op jit(solution)/shard_map/ppermute | solution.py:863
  100.7 9.2 %collective-permute-start.34 = (bf16[256,1024]{1,0:T(8,128)(2,1)S(1)}, bf16[256,1024]{1,0:T(8,128)(2,1)S(1)}, u32[]{:S(2)}, u32[]{:S(2)}) collective-permute-start(bf16[256,1024]{1,0:T(8,128)(2,1)S(1)} %join.14.refs_3_.refs_1_), channel_id=1, source_target_pairs={{0,2},{2,0},{4,6},{6,4},{8,10},{10,8},{12,14},{14,12},{16,18},{18,... | collective-permute-start | bytes 1572872 | tf_op jit(solution)/shard_map/ppermute | solution.py:863
  104.9 10.7 %collective-permute-start.32 = (bf16[256,1024]{1,0:T(8,128)(2,1)S(1)}, bf16[256,1024]{1,0:T(8,128)(2,1)S(1)}, u32[]{:S(2)}, u32[]{:S(2)}) collective-permute-start(bf16[256,1024]{1,0:T(8,128)(2,1)S(1)} %join.15.refs_3_.refs_1_), channel_id=1, source_target_pairs={{0,2},{2,0},{4,6},{6,4},{8,10},{10,8},{12,14},{14,12},{16,18},{18,... | collective-permute-start | bytes 1572872 | tf_op jit(solution)/shard_map/ppermute | solution.py:863
